TPU v7x, 256 devices: a whole 4x4x8 slice. The times are simulated.
256 devices in a mesh: section: 32 (over y_lo, z, core), dp: 8 (over y_hi, x).
Axes of the slice: x: 4, y: 4 (y_hi: 2, y_lo: 2; y = y_hi * 2 + y_lo), z: 8, core: 2. Of those that a mesh axis runs over, the one named last changes fastest.
Arguments:
- forward_codes: int32 [32, 3072, 2048], P('section', 'dp'), may hold values from 0 to 4095
- forward_scales: bfloat16 [32, 3072, 192], P('section', 'dp'), may hold values from 0.019897461 to 0.25
- stored_base: bfloat16 [32, 256, 6144], P('section', 'dp'), may hold values from -6 to 6
- sample_ids: int32 [32, 3072], P('section', 'dp'), may hold values from 0 to 31
- backward_codes: bfloat16 [32, 3072, 6144], P('section', 'dp'), may hold values from 0 to 255
- backward_scales: bfloat16 [32, 3072, 192], P('section', 'dp'), may hold values from 4.9829483e-05 to 0.00049972534
- norm_gain: float32 [32, 6144], P('section'), may hold values from 0.5 to 2
- w_down: bfloat16 [32, 6144, 128], P('section'), may hold values from -0.078125 to 0.078125
- w_up: bfloat16 [32, 6144, 128], P('section'), may hold values from -0.5 to 0.5
Outputs:
- feedback: bfloat16 [32, 3072, 6144], P('section', 'dp')
- grad_down: float32 [32, 6144, 128], P('section', 'dp')
- grad_up: float32 [32, 6144, 128], P('section', 'dp')
Inputs may be any that keep to these rules, and one draw needn't show every extreme that they name: `forward_codes`: each word holds 3 codes of 4 bits of consecutive features, lowest bits first. sample_ids[s, t] counts from the first stored row of the dp block of token t.
All inputs are finite; a program needn't handle non-finite values.
Results may differ from a plain program's by a relative error of at most 0.0072.
Values may be sent and summed in bfloat16 or wider, within the bound.
No kernel may reach another device: no remote copies, remote signals or barrier semaphores. Data moves between devices by JAX's collectives and lax.ppermute only.
A program may use at most 192 MiB of HBM per device.

v0:
```python
import jax
import jax.numpy as jnp
from jax import lax
from jax.sharding import PartitionSpec as P


def passed_along(block, axis, distance):
    devices = range(lax.axis_size(axis))
    route = [((i - distance) % len(devices), i) for i in devices]
    return lax.ppermute(block, axis, route)


def unpack_codes(packed):
    offsets_bits = jnp.arange(3, dtype=jnp.int32) * 4
    unpacked = jnp.bitwise_and(jnp.right_shift(packed[..., None], offsets_bits), 15)
    return unpacked.reshape(packed.shape[0], -1)


def scale_blocks(values, scales):
    shaped = values.reshape(values.shape[0], scales.shape[-1], -1)
    return (shaped * scales.astype(jnp.float32)[:, :, None]).reshape(values.shape)


def build_message(base_rows, row_ids, packed, scales):
    picked = jnp.take(base_rows, row_ids, axis=0)
    codes = (unpack_codes(packed) - 8).astype(jnp.float32)
    return (picked.astype(jnp.float32) + scale_blocks(codes, scales)).astype(jnp.bfloat16)


def build_gradient(code_values, scales):
    return scale_blocks(code_values.astype(jnp.float32) - 128.0, scales).astype(jnp.bfloat16)


def transposed_product(left, right):
    return lax.dot_general(
        left, right, (((0,), (0,)), ((), ())), preferred_element_type=jnp.float32
    )


def body(
    forward_codes,
    forward_scales,
    stored_base,
    sample_ids,
    backward_codes,
    backward_scales,
    norm_gain,
    w_down,
    w_up,
):
    own_message = build_message(stored_base[0], sample_ids[0], forward_codes[0], forward_scales[0])
    sent_grad = build_gradient(backward_codes[0], backward_scales[0])
    incoming_raw = passed_along(own_message, "section", 1)
    out_grad = passed_along(sent_grad, "section", -1)
    incoming = incoming_raw.astype(jnp.float32)
    center = incoming - jnp.mean(incoming, axis=1, keepdims=True)
    variance = jnp.mean(center * center, axis=1, keepdims=True)
    hidden = (norm_gain[0] * center / jnp.sqrt(variance + 1e-05)).astype(jnp.bfloat16)
    pre = jnp.dot(hidden, w_down[0], preferred_element_type=jnp.float32)
    act_value, gelu_back = jax.vjp(jax.nn.gelu, pre)
    act = act_value.astype(jnp.bfloat16)
    lifted = lax.dot_general(
        act, w_up[0], (((1,), (1,)), ((), ())), preferred_element_type=jnp.float32
    )
    feedback = (incoming + lifted - own_message.astype(jnp.float32)).astype(jnp.bfloat16)
    dact = jnp.dot(out_grad, w_up[0], preferred_element_type=jnp.float32)
    dpre = gelu_back(dact)[0].astype(jnp.bfloat16)
    rank_units = w_down.shape[2]
    summed = lax.psum_scatter(
        jnp.concatenate(
            [transposed_product(hidden, dpre), transposed_product(out_grad, act)], axis=1
        ),
        "dp",
        scatter_dimension=0,
        tiled=True,
    )
    grad_down = summed[:, :rank_units]
    grad_up = summed[:, rank_units:]
    return (feedback[None], grad_down[None], grad_up[None])


def solution(mesh):
    in_specs = (
        P("section", "dp", None),
        P("section", "dp", None),
        P("section", "dp", None),
        P("section", "dp"),
        P("section", "dp", None),
        P("section", "dp", None),
        P("section", None),
        P("section", None, None),
        P("section", None, None),
    )
    out_specs = (P("section", "dp", None), P("section", "dp", None), P("section", "dp", None))
    return jax.shard_map(body, mesh=mesh, in_specs=in_specs, out_specs=out_specs, check_vma=False)
```

profile of v0, /device:TPU:1, one launch (start us, length us, event | category | flops | bytes accessed | tf_op | source)
XLA Modules:
  0.0 284.1 jit_solution(1587662544218835884)
XLA Ops:
  7.2 0.0 reduce-scatter.2.cloned.1.call-start
  7.2 3.7 %copy.16 = s32[384,2048]{0,1:T(8,128)} copy(s32[384,2048]{1,0:T(8,128)} %bitcast.44) | data formatting | bytes 6291456 | tf_op jit(solution)/shard_map/shift_right_arithmetic | solution.py:15
  10.9 7.9 %shift_right_arithmetic.25 = s32[384,2048,3]{0,2,1:T(4,128)} broadcast(s32[384,2048]{0,1:T(8,128)} %copy.16), dimensions={0,1} | broadcast | bytes 12582912 | tf_op jit(solution)/shard_map/shift_right_arithmetic | solution.py:15
  18.8 14.9 %shift_right_arithmetic.26 = s32[384,6144]{0,1:T(8,128)} reshape(s32[384,2048,3]{0,2,1:T(4,128)} %shift_right_arithmetic.25) | data formatting | bytes 18874368 | tf_op jit(solution)/shard_map/shift_right_arithmetic | solution.py:15
  33.7 9.7 %copy.17 = s32[384,6144]{1,0:T(8,128)} copy(s32[384,6144]{0,1:T(8,128)} %shift_right_arithmetic.26) | data formatting | bytes 18874368 | tf_op jit(solution)/shard_map/shift_right_arithmetic | solution.py:15
  43.4 4.3 %mul.87 = f32[384,192,32]{0,2,1:T(8,128)} broadcast(f32[384,192]{0,1:T(8,128)S(1)} %bitcast_convert_fusion.1), dimensions={0,1} | broadcast | bytes 9732096 | tf_op jit(solution)/shard_map/mul | solution.py:21
  47.7 9.6 %copy.18 = f32[384,6144]{1,0:T(8,128)} copy(f32[384,6144]{0,1:T(8,128)} %bitcast.43) | data formatting | bytes 18874368 | tf_op jit(solution)/shard_map/mul | solution.py:21
  57.4 0.1 shift_right_arithmetic.27
  57.5 0.7 shift_right_arithmetic.28
  58.2 0.2 copy-done.1
  58.4 5.5 %gather_fusion = bf16[384,6144]{1,0:T(8,128)(2,1)} fusion(bf16[32,6144]{1,0:T(8,128)(2,1)S(1)} %bitcast.42, s32[1024]{0:T(1024)S(1)} %pad_clamp_fusion), kind=kCustom, calls=%fused_computation | custom fusion | bytes 9438720 | tf_op jit(solution)/shard_map/jit(_take)/gather | solution.py:25
  63.9 11.2 %add_convert_fusion = bf16[384,6144]{1,0:T(8,128)(2,1)} fusion(f32[384,6144]{1,0:T(8,128)} %copy.18, s32[384,6144]{1,0:T(8,128)} %copy.17, s32[6144]{0:T(1024)S(1)} %shift_right_arithmetic.28, bf16[384,6144]{1,0:T(8,128)(2,1)} %gather_fusion, pred[384]{0:T(512)(128)(4,1)S(1)} %compare_and_fusion), kind=kLoop, calls=%fused_computation.13 | loop fusion | flops 21233664 | bytes 28336512 | tf_op jit(solution)/shard_map/convert_element_type | solution.py:27
  75.1 3.0 %collective-permute-start = (bf16[384,6144]{1,0:T(8,128)(2,1)}, bf16[384,6144]{1,0:T(8,128)(2,1)}, u32[]{:S(2)}, u32[]{:S(2)}) collective-permute-start(bf16[384,6144]{1,0:T(8,128)(2,1)} %add_convert_fusion), channel_id=1, source_target_pairs={{248,0},{0,8},{8,16},{16,24},{24,32},{32,40},{40,48},{48,56},{56,6... | collective-permute-start | bytes 14155784 | tf_op jit(solution)/shard_map/ppermute | solution.py:10
  78.1 6.6 %copy.19 = bf16[1,384,6144]{1,2,0:T(8,128)(2,1)} copy(bf16[1,384,6144]{2,1,0:T(8,128)(2,1)} %param.13) | data formatting | bytes 9437184 | tf_op args[4]
  84.8 3.5 %fusion.7 = bf16[384,6144]{0,1:T(8,128)(2,1)S(1)} fusion(bf16[1,384,6144]{1,2,0:T(8,128)(2,1)} %copy.19, f32[384,192]{0,1:T(8,128)S(1)} %bitcast_convert_fusion), kind=kLoop, calls=%fused_computation.12 | loop fusion | flops 9437184 | bytes 9732096 | tf_op jit(solution)/shard_map/convert_element_type | solution.py:31
  88.3 0.5 collective-permute-start.1
  88.8 40.7 %collective-permute-done = bf16[384,6144]{1,0:T(8,128)(2,1)} collective-permute-done((bf16[384,6144]{1,0:T(8,128)(2,1)}, bf16[384,6144]{1,0:T(8,128)(2,1)}, u32[]{:S(2)}, u32[]{:S(2)}) %collective-permute-start) | collective-permute-done | bytes 4718624 | tf_op jit(solution)/shard_map/ppermute | solution.py:10
  129.5 3.0 %convert_reduce_fusion = f32[384]{0:T(512)S(1)} fusion(bf16[384,6144]{1,0:T(8,128)(2,1)} %collective-permute-done), kind=kLoop, calls=%fused_computation.3 | loop fusion | flops 4718208 | bytes 4720128 | tf_op jit(solution)/shard_map/reduce_sum | solution.py:56
  132.5 3.7 %fusion.4 = f32[384]{0:T(512)S(1)} fusion(bf16[384,6144]{1,0:T(8,128)(2,1)} %collective-permute-done, f32[384]{0:T(512)S(1)} %broadcast_multiply_fusion), kind=kLoop, calls=%fused_computation.8 | loop fusion | flops 9436800 | bytes 4721664 | tf_op jit(solution)/shard_map/reduce_sum | solution.py:57
  136.3 5.1 %fusion.3 = bf16[384,6144]{1,0:T(8,128)(2,1)S(1)} fusion(bf16[384,6144]{1,0:T(8,128)(2,1)} %collective-permute-done, f32[384]{0:T(512)S(1)} %add_sqrt_fusion, f32[384]{0:T(512)S(1)} %broadcast_multiply_fusion, f32[6144]{0:T(1024)S(1)} %bitcast.45), kind=kLoop, calls=%fused_computation.7 | loop fusion | flops 11796480 | bytes 9464832 | tf_op jit(solution)/shard_map/convert_element_type | solution.py:58
  141.4 2.1 copy-done.2
  143.5 1.4 fusion.12
  144.9 2.2 copy-done.3
  147.1 3.3 %fusion.42 = f32[6144,128]{0,1:T(8,128)} fusion(bf16[384,6144]{0,1:T(8,128)(2,1)S(1)} %collective-permute-done.1, f32[384,128]{1,0:T(8,128)S(1)} %fusion.12), kind=kOutput, calls=%fused_computation.58 | convolution fusion | flops 604422144 | bytes 8060928 | tf_op jit(solution)/shard_map/dot_general | solution.py:35
  150.4 9.4 %fusion.24 = f32[6144,128]{0,1:T(8,128)} fusion(bf16[384,6144]{1,0:T(8,128)(2,1)} %copy-done.2, f32[384,128]{1,0:T(8,128)S(1)} %fusion.12, bf16[384,6144]{0,1:T(8,128)(2,1)} %copy-done.3, bf16[1,6144,128]{2,1,0:T(8,128)(2,1)S(1)} %copy-done), kind=kOutput, calls=%fused_computation.32 | convolution fusion | flops 1208942592 | bytes 14352384 | tf_op jit(solution)/shard_map/dot_general | solution.py:35
  159.8 6.2 %pad_maximum_fusion = f32[6144,256]{0,1:T(8,128)} fusion(f32[6144,128]{0,1:T(8,128)} %fusion.42, f32[6144,128]{0,1:T(8,128)} %fusion.24), kind=kLoop, calls=%fused_computation.15 | loop fusion | flops 1572864 | bytes 12582912 | tf_op jit(solution)/shard_map/concatenate | solution.py:70
  166.0 0.0 reduce-scatter.2.cloned.1.call-update
  166.0 7.6 %fusion.8 = bf16[1,384,6144]{2,1,0:T(8,128)(2,1)} fusion(bf16[384,6144]{1,0:T(8,128)(2,1)} %add_convert_fusion, bf16[384,6144]{1,0:T(8,128)(2,1)} %collective-permute-done, bf16[1,6144,128]{2,1,0:T(8,128)(2,1)S(1)} %copy-done, f32[384,128]{1,0:T(8,128)S(1)} %fusion.12), kind=kOutput, calls=%fused_computation.14 | convolution fusion | flops 616218624 | bytes 15925248 | tf_op jit(solution)/shard_map/dot_general | solution.py:62
  173.6 100.7 %reduce-scatter.2.cloned.1.call-done = f32[768,256]{0,1:T(8,128)} async-done(((f32[6144,256]{0,1:T(8,128)}), f32[768,256]{0,1:T(8,128)}) %reduce-scatter.2.cloned.1.call-update) | async-done | bytes 786448 | tf_op jit(solution)/shard_map/reduce_scatter | solution.py:69
  274.2 1.2 slice_bitcast_fusion
  275.4 0.9 copy.20
  276.3 0.9 copy.21
  (25 shorter events, 0.2 us)
Async XLA Ops:
  7.2 143.2 %copy-start = (bf16[1,6144,128]{2,1,0:T(8,128)(2,1)S(1)}, bf16[1,6144,128]{2,1,0:T(8,128)(2,1)}, u32[]{:S(2)}) copy-start(bf16[1,6144,128]{2,1,0:T(8,128)(2,1)} %param.17) | copy-start | bytes 4718596
  7.2 267.1 %reduce-scatter.2.cloned.1.call-start = ((), (), s32[]{:S(2)}) async-start(), calls=%async_computation.1 | async-start | bytes 7077888 | tf_op jit(solution)/shard_map/reduce_scatter | solution.py:69
  33.7 9.7 %copy-start.5 = (bf16[1,384,192]{1,2,0:T(8,128)(2,1)S(1)}, bf16[1,384,192]{1,2,0:T(8,128)(2,1)}, u32[]{:S(2)}) copy-start(bf16[1,384,192]{1,2,0:T(8,128)(2,1)} %param.10) | copy-start | bytes 442372
  47.7 9.6 %copy-start.8 = (s32[1,384]{1,0:T(1,128)S(1)}, s32[1,384]{1,0:T(1,128)}, u32[]{:S(2)}) copy-start(s32[1,384]{1,0:T(1,128)} %param.12) | copy-start | bytes 4612
  57.4 1.0 copy-start.1
  75.1 9.7 %copy-start.6 = (bf16[1,384,192]{1,2,0:T(8,128)(2,1)S(1)}, bf16[1,384,192]{1,2,0:T(8,128)(2,1)}, u32[]{:S(2)}) copy-start(bf16[1,384,192]{1,2,0:T(8,128)(2,1)} %param.14) | copy-start | bytes 442372
  75.1 54.4 %collective-permute-start = (bf16[384,6144]{1,0:T(8,128)(2,1)}, bf16[384,6144]{1,0:T(8,128)(2,1)}, u32[]{:S(2)}, u32[]{:S(2)}) collective-permute-start(bf16[384,6144]{1,0:T(8,128)(2,1)} %add_convert_fusion), channel_id=1, source_target_pairs={{248,0},{0,8},{8,16},{16,24},{24,32},{32,40},{40,48},{48,56},{56,6... | collective-permute-start | bytes 14155784 | tf_op jit(solution)/shard_map/ppermute | solution.py:10
  88.3 48.0 %copy-start.7 = (f32[1,6144]{1,0:T(1,128)S(1)}, f32[1,6144]{1,0:T(1,128)}, u32[]{:S(2)}) copy-start(f32[1,6144]{1,0:T(1,128)} %param.15) | copy-start | bytes 73732
  88.3 56.6 %collective-permute-start.1 = (bf16[384,6144]{0,1:T(8,128)(2,1)S(1)}, bf16[384,6144]{0,1:T(8,128)(2,1)S(1)}, u32[]{:S(2)}, u32[]{:S(2)}) collective-permute-start(bf16[384,6144]{0,1:T(8,128)(2,1)S(1)} %fusion.7), channel_id=1, source_target_pairs={{8,0},{16,8},{24,16},{32,24},{40,32},{48,40},{56,48},{64,56},{72,6... | collective-permute-start | bytes 14155784 | tf_op jit(solution)/shard_map/ppermute | solution.py:10
  136.3 7.2 %copy-start.4 = (bf16[1,6144,128]{2,1,0:T(8,128)(2,1)S(1)}, bf16[1,6144,128]{2,1,0:T(8,128)(2,1)}, u32[]{:S(2)}) copy-start(bf16[1,6144,128]{2,1,0:T(8,128)(2,1)} %param.16) | copy-start | bytes 4718596
  141.4 2.1 copy-start.2
  144.9 2.2 copy-start.3
Sparse Core Ops, SparseCore 0:
  166.1 108.0 reduce-scatter.1
where the time goes:
time: 285 us; the launch traced here: 284 us
  waiting for transfers between devices  141 us (49%)
  local copies, waits for them, and re-layouts  70.5 us (25%)
  other arithmetic  32.8 us (12%)
  matrix products  21.6 us (8%)
  between operations  14.1 us (5%)
  starting transfers between devices  3.57 us (1%)
    reduce_scatter x1, waiting for transfers between devices, body(): lax.psum_scatter(jnp.concatenate([transposed_product(hidden, dpre), trans...  101 us
    ppermute x2, waiting for transfers between devices, passed_along(): return lax.ppermute(block, axis, route)  40.7 us
    shift_right_arithmetic x6, local copies, waits for them, and re-layouts, unpack_codes(): jnp.right_shift(packed[..., None], offsets_bits)  36.9 us
    mul x2, local copies, waits for them, and re-layouts, scale_blocks(): shaped * scales.astype(jnp.float32)[:, :, None]  14 us
    unnamed x21, local copies, waits for them, and re-layouts  13 us
    dot_general x2, matrix products, transposed_product(): lax.dot_general(left, right, (((0,), (0,)), ((), ())), preferred_element_...  12.7 us
    convert_element_type x1, other arithmetic, build_message(): (picked.astype(jnp.float32) + scale_blocks(codes, scales)).astype(jnp.bfl...  11.2 us
    dot_general x1, matrix products, body(): lax.dot_general(act, w_up[0], (((1,), (1,)), ((), ())), preferred_element...  7.58 us
  transfers between devices with their start and end apart: 3, of which 2 were waited for; matrix products, arithmetic and copies ran while one was open for 11% of the time, Pallas kernels for 0%

commit v1 on v0

v1 whole, which is shorter than its diff:
```python
import functools
import math

import jax
import jax.numpy as jnp
from jax import lax
from jax.experimental import pallas as pl
from jax.experimental.pallas import tpu as pltpu
from jax.sharding import PartitionSpec as P

D = 6144
R = 128
TOK = 384
PIECE = D // 8
QUARTER = D // 4
F32 = jnp.float32
BF16 = jnp.bfloat16
ROWS = 32
CHUNK = 96
MIB = 1 << 20
ROOT_2_PI = math.sqrt(2.0 / math.pi)


def params(mib):
    return pltpu.CompilerParams(vmem_limit_bytes=mib * MIB)


def cost(flops, moved):
    return pl.CostEstimate(flops=flops, bytes_accessed=moved, transcendentals=0)


def lanes(shape):
    return lax.broadcasted_iota(jnp.int32, shape, 1)


def spread_scales(scales, tile, rows):
    part = scales[:, : 128] if tile < 32 else scales[:, 128 : 256]
    at = lanes((rows, 128)) // 32 + 4 * (tile % 32)
    return jnp.take_along_axis(part, at, axis=1)


def message_kernel(codes_ref, scales_ref, base_ref, ids_ref, out_ref):
    rows = codes_ref.shape[0]
    scales = jnp.concatenate(
        [scales_ref[...].astype(F32), jnp.zeros((rows, 64), F32)], axis=1
    )
    picks = (ids_ref[...] == lanes((rows, 32))).astype(BF16)
    lane = lanes((rows, 128))
    for block in range(16):
        words = codes_ref[:, block * 128 : (block + 1) * 128]
        base = jnp.dot(
            picks, base_ref[:, block * 384 : (block + 1) * 384], preferred_element_type=F32
        )
        for j in range(3):
            spot = lane + 128 * j
            word = jnp.take_along_axis(words, spot // 3, axis=1)
            code = jnp.right_shift(word, (spot % 3) * 4) & 15
            step = spread_scales(scales, block * 3 + j, rows)
            value = base[:, j * 128 : (j + 1) * 128] + step * (code - 8).astype(F32)
            out_ref[:, (block * 3 + j) * 128 : (block * 3 + j + 1) * 128] = value.astype(BF16)


def make_message(codes, scales, base, ids, first, count):
    skip = first // ROWS
    return pl.pallas_call(
        message_kernel,
        grid=(count // ROWS,),
        in_specs=[
            pl.BlockSpec((ROWS, D // 3), lambda i: (i + skip, 0)),
            pl.BlockSpec((ROWS, D // 32), lambda i: (i + skip, 0)),
            pl.BlockSpec((32, D), lambda i: (0, 0)),
            pl.BlockSpec((ROWS, 1), lambda i: (i + skip, 0)),
        ],
        out_specs=pl.BlockSpec((ROWS, D), lambda i: (i, 0)),
        out_shape=jax.ShapeDtypeStruct((count, D), BF16),
        compiler_params=params(16),
        cost_estimate=cost(count * D * 80, count * D * 4),
        name="message",
    )(codes, scales, base, ids)


def gradient_kernel(codes_ref, scales_ref, out_ref):
    rows = codes_ref.shape[0]
    scales = jnp.concatenate(
        [scales_ref[...].astype(F32), jnp.zeros((rows, 64), F32)], axis=1
    )
    for tile in range(48):
        part = slice(tile * 128, (tile + 1) * 128)
        step = spread_scales(scales, tile, rows)
        out_ref[:, part] = (step * (codes_ref[:, part].astype(F32) - 128.0)).astype(BF16)


def make_gradient(codes, scales):
    return pl.pallas_call(
        gradient_kernel,
        grid=(TOK // ROWS,),
        in_specs=[
            pl.BlockSpec((ROWS, D), lambda i: (i, 0)),
            pl.BlockSpec((ROWS, D // 32), lambda i: (i, 0)),
        ],
        out_specs=pl.BlockSpec((ROWS, D), lambda i: (i, 0)),
        out_shape=jax.ShapeDtypeStruct((TOK, D), BF16),
        compiler_params=params(16),
        cost_estimate=cost(TOK * D * 20, TOK * D * 4),
        name="gradient",
    )(codes, scales)


def hidden_kernel(first, message_ref, gain_ref, out_ref):
    x = message_ref[...].astype(F32)
    center = x - jnp.sum(x, axis=1, keepdims=True) * (1.0 / D)
    variance = jnp.sum(center * center, axis=1, keepdims=True) * (1.0 / D)
    out_ref[...] = (gain_ref[...] * center * lax.rsqrt(variance + 1e-05)).astype(BF16)


def make_hidden(message, gain):
    count = message.shape[0]
    return pl.pallas_call(
        functools.partial(hidden_kernel, 0),
        grid=(count // ROWS,),
        in_specs=[
            pl.BlockSpec((ROWS, D), lambda i: (i, 0)),
            pl.BlockSpec((1, D), lambda i: (0, 0)),
        ],
        out_specs=pl.BlockSpec((ROWS, D), lambda i: (i, 0)),
        out_shape=jax.ShapeDtypeStruct((count, D), BF16),
        compiler_params=params(16),
        cost_estimate=cost(count * D * 20, count * D * 4),
        name="hidden",
    )(message, gain)


def tanh_of(pre):
    return jnp.tanh(ROOT_2_PI * (pre + 0.044715 * (pre * pre * pre)))


def down_kernel(*refs):
    *hidden_refs, weight_ref, pre_ref, act_ref = refs
    weight = weight_ref[...]
    at = 0
    for hidden_ref in hidden_refs:
        rows = hidden_ref.shape[0]
        pre = jnp.dot(hidden_ref[...], weight, preferred_element_type=F32)
        pre_ref[at : at + rows, :] = pre
        act_ref[at : at + rows, :] = (0.5 * pre * (1.0 + tanh_of(pre))).astype(BF16)
        at += rows


def project_down(hiddens, weight):
    return pl.pallas_call(
        down_kernel,
        out_shape=(
            jax.ShapeDtypeStruct((TOK, R), F32),
            jax.ShapeDtypeStruct((TOK, R), BF16),
        ),
        compiler_params=params(24),
        cost_estimate=cost(2 * TOK * D * R, TOK * D * 2 + D * R * 2),
        name="down",
    )(*hiddens, weight)


def back_kernel(place_ref, grad_ref, chip_ref, *refs):
    *quarter_refs, out_ref = refs
    total = jnp.zeros((TOK, R), F32)
    for j, quarter_ref in enumerate(quarter_refs):
        quarter = lax.rem(place_ref[0] + j, 4)
        at = pl.multiple_of(quarter * QUARTER, QUARTER)
        weight = quarter_ref[...] + chip_ref[pl.ds(at, QUARTER), :]
        total += jnp.dot(
            grad_ref[:, pl.ds(at, QUARTER)], weight, preferred_element_type=F32
        )
    out_ref[...] = total.astype(BF16)


def project_back(place, grad, chip, quarters):
    whole = pl.BlockSpec(memory_space=pltpu.VMEM)
    return pl.pallas_call(
        back_kernel,
        in_specs=[pl.BlockSpec(memory_space=pltpu.SMEM)] + [whole] * 6,
        out_specs=whole,
        out_shape=jax.ShapeDtypeStruct((TOK, R), BF16),
        compiler_params=params(24),
        cost_estimate=cost(2 * TOK * D * R, TOK * D * 2 + D * R * 4),
        name="back",
    )(place, grad, chip, *quarters)


def transposed(left, right):
    return lax.dot_general(left, right, (((0,), (0,)), ((), ())), preferred_element_type=F32)


def grad_up_kernel(place_ref, act_ref, grad_ref, kept_ref, sent_ref):
    act = act_ref[...]
    for half, out_ref in ((0, kept_ref), (1, sent_ref)):
        for j in range(4):
            piece = (place_ref[1] ^ half) * 4 + lax.rem(place_ref[0] + j, 4)
            at = pl.multiple_of(piece * PIECE, PIECE)
            out_ref[j] = transposed(act, grad_ref[:, pl.ds(at, PIECE)]).astype(BF16)


def partial_grad_up(place, act, grad):
    whole = pl.BlockSpec(memory_space=pltpu.VMEM)
    shape = jax.ShapeDtypeStruct((4, R, PIECE), BF16)
    return pl.pallas_call(
        grad_up_kernel,
        in_specs=[pl.BlockSpec(memory_space=pltpu.SMEM)] + [whole] * 2,
        out_specs=(whole,) * 2,
        out_shape=(shape,) * 2,
        compiler_params=params(24),
        cost_estimate=cost(2 * TOK * D * R, TOK * D * 2 + D * R * 2),
        name="grad_up",
    )(place, act, grad)


def grad_down_kernel(place_ref, pre_ref, dact_ref, *refs):
    *hidden_refs, out0, out1, out2, out3 = refs
    pre = pre_ref[...]
    t = tanh_of(pre)
    slope = 0.5 * (1.0 + t) + (0.5 * ROOT_2_PI) * pre * (1.0 - t * t) * (
        1.0 + (3.0 * 0.044715) * (pre * pre)
    )
    dpre = (dact_ref[...].astype(F32) * slope).astype(BF16)
    for j, out_ref in enumerate((out0, out1, out2, out3)):
        for half in range(2):
            piece = (place_ref[1] ^ half) * 4 + lax.rem(place_ref[0] + j, 4)
            at = pl.multiple_of(piece * PIECE, PIECE)
            total = jnp.zeros((R, PIECE), F32)
            row = 0
            for hidden_ref in hidden_refs:
                rows = hidden_ref.shape[0]
                total += transposed(
                    dpre[row : row + rows], hidden_ref[:, pl.ds(at, PIECE)]
                )
                row += rows
            out_ref[half] = total.astype(BF16)


def partial_grad_down(place, pre, dact, hiddens):
    whole = pl.BlockSpec(memory_space=pltpu.VMEM)
    shape = jax.ShapeDtypeStruct((2, R, PIECE), BF16)
    return pl.pallas_call(
        grad_down_kernel,
        in_specs=[pl.BlockSpec(memory_space=pltpu.SMEM)] + [whole] * (2 + len(hiddens)),
        out_specs=(whole,) * 4,
        out_shape=(shape,) * 4,
        compiler_params=params(24),
        cost_estimate=cost(2 * TOK * D * R, TOK * D * 2 + D * R * 2),
        name="grad_down",
    )(place, pre, dact, *hiddens)


def add_kernel(*refs):
    *in_refs, out_ref = refs
    total = in_refs[0][...].astype(F32)
    for ref in in_refs[1:]:
        total += ref[...].astype(F32)
    out_ref[...] = total.astype(BF16)


def add_parts(parts):
    return pl.pallas_call(
        add_kernel,
        out_shape=jax.ShapeDtypeStruct(parts[0].shape, BF16),
        compiler_params=params(16),
        cost_estimate=cost(parts[0].size, parts[0].size * 2 * (len(parts) + 1)),
        name="add",
    )(*parts)


def finish_kernel(*refs):
    *in_refs, out_ref = refs
    total = in_refs[0][...].astype(F32)
    for ref in in_refs[1:]:
        total += ref[...].astype(F32)
    out_ref[...] = total.T


def finish(parts):
    return pl.pallas_call(
        finish_kernel,
        out_shape=jax.ShapeDtypeStruct((PIECE, R), F32),
        compiler_params=params(16),
        cost_estimate=cost(R * PIECE, R * PIECE * 8),
        name="finish",
    )(*parts)


def feedback_kernel(x_ref, own_ref, act_ref, weight_ref, *refs):
    out_ref = refs[-1]
    act = act_ref[...]
    for part in range(4):
        at = slice(part * QUARTER, (part + 1) * QUARTER)
        lifted = lax.dot_general(
            act, weight_ref[at, :], (((1,), (1,)), ((), ())), preferred_element_type=F32
        )
        value = x_ref[:, at].astype(F32) + lifted - own_ref[:, at].astype(F32)
        out_ref[:, at] = value.astype(BF16)


def make_feedback(x, own, own_first, act, weight, first, before):
    count = x.shape[0]
    rows = 48
    skip, own_skip = first // rows, own_first // rows
    specs = [
        pl.BlockSpec((rows, D), lambda i: (i, 0)),
        pl.BlockSpec((rows, D), lambda i: (i + own_skip, 0)),
        pl.BlockSpec((rows, R), lambda i: (i + skip, 0)),
        pl.BlockSpec((D, R), lambda i: (0, 0)),
    ]
    operands = [x, own, act, weight]
    if before is not None:
        specs.append(pl.BlockSpec(memory_space=pl.ANY))
        operands.append(before)
    return pl.pallas_call(
        feedback_kernel,
        grid=(count // rows,),
        in_specs=specs,
        out_specs=pl.BlockSpec((rows, D), lambda i: (i + skip, 0)),
        out_shape=jax.ShapeDtypeStruct((TOK, D), BF16),
        input_output_aliases={} if before is None else {4: 0},
        compiler_params=params(16),
        cost_estimate=cost(2 * count * D * R, count * D * 6 + D * R * 2),
        name="feedback",
    )(*operands)


def body(
    forward_codes,
    forward_scales,
    stored_base,
    sample_ids,
    backward_codes,
    backward_scales,
    norm_gain,
    w_down,
    w_up,
):
    sections = lax.axis_size("section")
    replicas = lax.axis_size("dp")
    across = replicas // 2
    both = ("section", "dp")

    def along(value, distance):
        pairs = [(s, (s + distance) % sections) for s in range(sections)]
        return lax.ppermute(value, "section", pairs)

    def among(value, flip_y, step_x, section_step=0, only_even=False):
        pairs = []
        for s in range(sections):
            if only_even and s % 2:
                continue
            for d in range(replicas):
                y, x = divmod(d, across)
                source = (y ^ flip_y) * across + (x + step_x) % across
                goal = ((s + section_step) % sections) * replicas + d
                pairs.append((s * replicas + source, goal))
        return lax.ppermute(value, both, pairs)

    replica = lax.axis_index("dp")
    place = jnp.stack([replica % across, replica // across]).astype(jnp.int32)

    up = w_up[0]
    quarter = lax.dynamic_slice(up, ((replica % across) * QUARTER, 0), (QUARTER, R))
    quarter0 = lax.ppermute(
        quarter, "section", [(s, (s + 1) % sections) for s in range(1, sections, 2)]
    )
    chip = lax.ppermute(up, "section", [(s, s + 1) for s in range(0, sections, 2)])
    down_next = along(w_down[0], -1)
    gain_next = along(norm_gain, -1)

    codes, scales, base = forward_codes[0], forward_scales[0], stored_base[0]
    ids = sample_ids.reshape(TOK, 1)
    spans = [(0, CHUNK), (CHUNK, TOK - CHUNK)]
    messages = [make_message(codes, scales, base, ids, a, n) for a, n in spans]
    pieces = [
        (messages[0], 0, 0),
        (messages[1], 0, CHUNK),
        (messages[1], CHUNK, 2 * CHUNK),
        (messages[1], 2 * CHUNK, 3 * CHUNK),
    ]
    arrived = [along(m[at : at + CHUNK], 1) for m, at, _ in pieces]
    quarters = [quarter0] + [among(quarter0, 0, j, only_even=True) for j in range(1, 4)]
    gradient = make_gradient(backward_codes[0], backward_scales[0])
    hiddens = [make_hidden(m, gain_next) for m in messages]

    dact_before = project_back(place, gradient, chip, quarters)
    pre_next, act_next = project_down(hiddens, down_next)
    dact_next = along(dact_before, -2)
    act_own = along(act_next, 1)
    act_before = along(act_next, 2)

    kept, sent = partial_grad_up(place, act_before, gradient)
    to_x = partial_grad_down(place, pre_next, dact_next, hiddens)
    up_half = add_parts([kept, among(sent, 1, 0)])
    down_half = add_parts([to_x[0]] + [among(to_x[j], 0, -j) for j in range(1, 4)])
    grad_up = finish([among(up_half[j], 0, -j, section_step=-1) for j in range(4)])
    grad_down = finish(
        [among(down_half[half], half, 0, section_step=1) for half in range(2)]
    )

    feedback = None
    for (own, own_first, first), x in zip(pieces, arrived):
        feedback = make_feedback(x, own, own_first, act_own, up, first, feedback)
    return (feedback[None], grad_down[None], grad_up[None])


def solution(mesh):
    in_specs = (
        P("section", "dp", None),
        P("section", "dp", None),
        P("section", "dp", None),
        P("section", "dp"),
        P("section", "dp", None),
        P("section", "dp", None),
        P("section", None),
        P("section", None, None),
        P("section", None, None),
    )
    out_specs = (P("section", "dp", None), P("section", "dp", None), P("section", "dp", None))
    return jax.shard_map(body, mesh=mesh, in_specs=in_specs, out_specs=out_specs, check_vma=False)
```

time: 285 us -> 167 us (0.59)
  waiting for transfers between devices: 141 us -> 63.3 us
  local copies, waits for them, and re-layouts: 70.5 us -> 15.5 us
  starting transfers between devices: 3.57 us -> 46.1 us
  Pallas kernels: 0 us -> 38.9 us
  other arithmetic: 32.8 us -> 0.08 us
  matrix products: 21.6 us -> 0 us
  between operations: 14.1 us -> 0.97 us
    reduce_scatter x1 -> x0, waiting for transfers between devices: 101 us -> none  [body(): lax.psum_scatter(jnp.concatenate([transposed_product(hidden, dpre), trans...]
    ppermute x2 -> x24, starting transfers between devices: 3.54 us -> 46.1 us  [the longest x9 26.5 us: along(): return lax.ppermute(value, 'section', pairs)]
    pallas_call x0 -> x17, Pallas kernels: none -> 38.9 us  [the longest x4 8.66 us: make_feedback(): pl.pallas_call(feedback_kernel, grid=(count // rows,), in_specs=specs, ou...]
    shift_right_arithmetic x6 -> x0, local copies, waits for them, and re-layouts: 36.9 us -> none  [unpack_codes(): jnp.right_shift(packed[..., None], offsets_bits)]
    ppermute x2 -> x24, waiting for transfers between devices: 40.7 us -> 63.3 us  [the longest x13 58.4 us: among(): return lax.ppermute(value, both, pairs)]
    dot_general x4 -> x0, matrix products: 21.6 us -> none  [the longest x2 12.7 us: transposed_product(): lax.dot_general(left, right, (((0,), (0,)), ((), ())), preferred_element_...]
    convert_element_type x5 -> x0, other arithmetic: 19.8 us -> none  [the longest x1 11.2 us: build_message(): (picked.astype(jnp.float32) + scale_blocks(codes, scales)).astype(jnp.bfl...]
    mul x2 -> x0, local copies, waits for them, and re-layouts: 14 us -> none  [scale_blocks(): shaped * scales.astype(jnp.float32)[:, :, None]]
  transfers between devices with their start and end apart: 3 -> 24, of which waited for: 2 -> 4; matrix products, arithmetic and copies ran while one was open for 11% -> 2% of each run, Pallas kernels for 0% -> 23%
where the time goes in v1:
time: 167 us; the launch traced here: 165 us
  waiting for transfers between devices  63.3 us (38%)
  starting transfers between devices  46.1 us (28%)
  Pallas kernels  38.9 us (23%)
  local copies, waits for them, and re-layouts  15.5 us (9%)
    ppermute x13, waiting for transfers between devices, among(): return lax.ppermute(value, both, pairs)  58.4 us
    ppermute x9, starting transfers between devices, along(): return lax.ppermute(value, 'section', pairs)  26.5 us
    ppermute x13, starting transfers between devices, among(): return lax.ppermute(value, both, pairs)  16.1 us
    unnamed x34, local copies, waits for them, and re-layouts  13.9 us
    pallas_call x4, Pallas kernels, make_feedback(): pl.pallas_call(feedback_kernel, grid=(count // rows,), in_specs=specs, ou...  8.66 us
    pallas_call x2, Pallas kernels, make_message(): pl.pallas_call(message_kernel, grid=(count // ROWS,), in_specs=[pl.BlockS...  8.56 us
    pallas_call x2, Pallas kernels, make_hidden(): pl.pallas_call(functools.partial(hidden_kernel, 0), grid=(count // ROWS,)...  6.15 us
    ppermute x1, waiting for transfers between devices, body(): lax.ppermute(quarter, 'section', [(s, (s + 1) % sections) for s in range(...  4.68 us
  transfers between devices with their start and end apart: 24, of which 4 were waited for; matrix products, arithmetic and copies ran while one was open for 2% of the time, Pallas kernels for 23%

profile of v1, /device:TPU:1, one launch (start us, length us, event | category | flops | bytes accessed | tf_op | source)
XLA Modules:
  0.0 164.9 jit_solution(4222118802384491169)
XLA Ops:
  0.6 1.3 collective-permute-start.7
  1.9 3.4 %collective-permute-start.2 = (bf16[6144,128]{1,0:T(8,128)(2,1)}, bf16[6144,128]{1,0:T(8,128)(2,1)}, u32[]{:S(2)}, u32[]{:S(2)}) collective-permute-start(bf16[6144,128]{1,0:T(8,128)(2,1)} %bitcast.46), channel_id=1, source_target_pairs={{0,248},{8,0},{16,8},{24,16},{32,24},{40,32},{48,40},{56,48},{64,5... | collective-permute-start | bytes 4718600 | tf_op jit(solution)/shard_map/ppermute | solution.py:345
  6.4 2.2 %collective-permute-start.8 = (bf16[1536,128]{1,0:T(8,128)(2,1)S(1)}, bf16[1536,128]{1,0:T(8,128)(2,1)S(1)}, u32[]{:S(2)}, u32[]{:S(2)}) collective-permute-start(bf16[1536,128]{1,0:T(8,128)(2,1)S(1)} %dynamic-slice_bitcast_fusion), channel_id=1, source_target_pairs={{8,16},{24,32},{40,48},{56,64},{72,80},{88,96},{104,112},{120,128}... | collective-permute-start | bytes 1179656 | tf_op jit(solution)/shard_map/ppermute | solution.py:364
  8.6 4.7 %collective-permute-done.8.refs_0_ = bf16[1536,128]{1,0:T(8,128)(2,1)S(1)} collective-permute-done((bf16[1536,128]{1,0:T(8,128)(2,1)S(1)}, bf16[1536,128]{1,0:T(8,128)(2,1)S(1)}, u32[]{:S(2)}, u32[]{:S(2)}) %collective-permute-start.8) | collective-permute-done | bytes 393248 | tf_op jit(solution)/shard_map/ppermute | solution.py:364
  16.4 2.3 %copy-done.3 = bf16[1,384,6144]{2,1,0:T(8,128)(2,1)S(1)} copy-done((bf16[1,384,6144]{2,1,0:T(8,128)(2,1)S(1)}, bf16[1,384,6144]{2,1,0:T(8,128)(2,1)}, u32[]{:S(2)}) %copy-start.3) | copy-done | bytes 4718616
  18.7 3.7 %gradient.1.grad_ref = bf16[384,6144]{1,0:T(8,128)(2,1)S(1)} custom-call(bf16[384,6144]{1,0:T(8,128)(2,1)S(1)} %bitcast.36, bf16[384,192]{1,0:T(8,128)(2,1)S(1)} %bitcast.41), custom_call_target="tpu_custom_call" | custom-call | flops 47185920 | bytes 9437184 | tf_op jit(solution)/shard_map/gradient/pallas_call | solution.py:94
  23.4 1.3 copy-done.9
  25.5 1.2 copy-done.5
  26.6 1.4 copy-done.6
  31.0 2.6 %back.1 = bf16[384,128]{1,0:T(8,128)(2,1)} custom-call(s32[2]{0:T(128)S(1)} %pad_add_fusion.place_ref, bf16[384,6144]{1,0:T(8,128)(2,1)S(1)} %gradient.1.grad_ref, bf16[6144,128]{1,0:T(8,128)(2,1)S(1)} %copy-done.6, bf16[1536,128]{1,0:T(8,128)(2,1)S(1)} %collective-permute-done.8.refs_0_, bf16[1536,128]{1,0:T(8,128)(2,1)S(1)} %copy-done.12, ...), custom_call_target="tpu_custom_call" | custom-call | flops 603979776 | bytes 7864320 | tf_op jit(solution)/shard_map/back/pallas_call | solution.py:177
  33.7 7.7 %collective-permute-start.12 = (bf16[384,128]{1,0:T(8,128)(2,1)}, bf16[384,128]{1,0:T(8,128)(2,1)}, u32[]{:S(2)}, u32[]{:S(2)}) collective-permute-start(bf16[384,128]{1,0:T(8,128)(2,1)} %back.1), channel_id=1, source_target_pairs={{0,240},{8,248},{16,0},{24,8},{32,16},{40,24},{48,32},{56,40},{64,... | collective-permute-start | bytes 294920 | tf_op jit(solution)/shard_map/ppermute | solution.py:345
  41.3 11.1 %collective-permute-start.1 = (f32[1,6144]{1,0:T(1,128)}, f32[1,6144]{1,0:T(1,128)}, u32[]{:S(2)}, u32[]{:S(2)}) collective-permute-start(f32[1,6144]{1,0:T(1,128)} %param.15), channel_id=1, source_target_pairs={{0,248},{8,0},{16,8},{24,16},{32,24},{40,32},{48,40},{56,48},{64,5... | collective-permute-start | bytes 73736 | tf_op jit(solution)/shard_map/ppermute | solution.py:345
  54.6 2.1 %message.3.message_ref.own_ref = bf16[96,6144]{1,0:T(8,128)(2,1)S(1)} custom-call(s32[384,2048]{1,0:T(8,128)S(1)} %bitcast.34, bf16[384,192]{1,0:T(8,128)(2,1)S(1)} %bitcast.37, bf16[32,6144]{1,0:T(8,128)(2,1)S(1)} %bitcast.39, s32[384,1]{1,0:T(8,128)S(1)} %copy.18.ids_ref), custom_call_target="tpu_custom_call" | custom-call | flops 47185920 | bytes 2359296 | tf_op jit(solution)/shard_map/message/pallas_call | solution.py:65
  56.7 1.7 %collective-permute-start.6 = (bf16[96,6144]{1,0:T(8,128)(2,1)S(1)}, bf16[96,6144]{1,0:T(8,128)(2,1)S(1)}, u32[]{:S(2)}, u32[]{:S(2)}) collective-permute-start(bf16[96,6144]{1,0:T(8,128)(2,1)S(1)} %message.3.message_ref.own_ref), channel_id=1, source_target_pairs={{0,8},{8,16},{16,24},{24,32},{32,40},{40,48},{48,56},{56,64},{64,7... | collective-permute-start | bytes 3538952 | tf_op jit(solution)/shard_map/ppermute | solution.py:345
  58.4 6.4 %message.2.message_ref.own_ref = bf16[288,6144]{1,0:T(8,128)(2,1)S(1)} custom-call(s32[384,2048]{1,0:T(8,128)S(1)} %bitcast.35, bf16[384,192]{1,0:T(8,128)(2,1)S(1)} %bitcast.38, bf16[32,6144]{1,0:T(8,128)(2,1)S(1)} %bitcast.40, s32[384,1]{1,0:T(8,128)S(1)} %copy.18.ids_ref), custom_call_target="tpu_custom_call" | custom-call | flops 141557760 | bytes 7077888 | tf_op jit(solution)/shard_map/message/pallas_call | solution.py:65
  64.9 1.9 %hidden.2.refs_0_ = bf16[96,6144]{1,0:T(8,128)(2,1)S(1)} custom-call(bf16[96,6144]{1,0:T(8,128)(2,1)S(1)} %message.3.message_ref.own_ref, f32[1,6144]{1,0:T(1,128)} %collective-permute-done.1.gain_ref), custom_call_target="tpu_custom_call" | custom-call | flops 11796480 | bytes 2359296 | tf_op jit(solution)/shard_map/hidden/pallas_call | solution.py:118
  66.8 4.2 %hidden.3.refs_1_ = bf16[288,6144]{1,0:T(8,128)(2,1)S(1)} custom-call(bf16[288,6144]{1,0:T(8,128)(2,1)S(1)} %message.2.message_ref.own_ref, f32[1,6144]{1,0:T(1,128)} %collective-permute-done.1.gain_ref), custom_call_target="tpu_custom_call" | custom-call | flops 35389440 | bytes 7077888 | tf_op jit(solution)/shard_map/hidden/pallas_call | solution.py:118
  71.1 3.0 %down.1 = (f32[384,128]{1,0:T(8,128)S(1)}, bf16[384,128]{1,0:T(8,128)(2,1)S(1)}) custom-call(bf16[96,6144]{1,0:T(8,128)(2,1)S(1)} %hidden.2.refs_0_, bf16[288,6144]{1,0:T(8,128)(2,1)S(1)} %hidden.3.refs_1_, bf16[6144,128]{1,0:T(8,128)(2,1)} %collective-permute-done.2.refs_2_), custom_call_target="tpu_custom_call" | custom-call | flops 603979776 | bytes 6291456 | tf_op jit(solution)/shard_map/down/pallas_call | solution.py:150
  74.3 2.5 %grad_down.1 = (bf16[2,128,768]{2,1,0:T(8,128)(2,1)S(1)}, bf16[2,128,768]{2,1,0:T(8,128)(2,1)S(1)}, bf16[2,128,768]{2,1,0:T(8,128)(2,1)S(1)}, bf16[2,128,768]{2,1,0:T(8,128)(2,1)S(1)}) custom-call(s32[2]{0:T(128)S(1)} %pad_add_fusion.place_ref, f32[384,128]{1,0:T(8,128)S(1)} %get-tuple-element.12.pre_ref, bf16[384,128]{1,0:T(8,128)(2,1)} %collective-permute-done.12.dact_ref, ...), custom_call_target="tpu_custom_call" | custom-call | flops 603979776 | bytes 6291456 | tf_op jit(solution)/shard_map/grad_down/pallas_call | solution.py:241
  77.7 1.8 %collective-permute-start.15 = (bf16[2,128,768]{2,1,0:T(8,128)(2,1)S(1)}, bf16[2,128,768]{2,1,0:T(8,128)(2,1)S(1)}, u32[]{:S(2)}, u32[]{:S(2)}) collective-permute-start(bf16[2,128,768]{2,1,0:T(8,128)(2,1)S(1)} %get-tuple-element.16), channel_id=1, source_target_pairs={{1,0},{2,1},{3,2},{0,3},{5,4},{6,5},{7,6},{4,7},{9,8},{10,9},{11,1... | collective-permute-start | bytes 1179656 | tf_op jit(solution)/shard_map/ppermute | solution.py:357
  80.9 15.4 %collective-permute-done.13.refs_1_ = bf16[2,128,768]{2,1,0:T(8,128)(2,1)S(1)} collective-permute-done((bf16[2,128,768]{2,1,0:T(8,128)(2,1)S(1)}, bf16[2,128,768]{2,1,0:T(8,128)(2,1)S(1)}, u32[]{:S(2)}, u32[]{:S(2)}) %collective-permute-start.13) | collective-permute-done | bytes 393248 | tf_op jit(solution)/shard_map/ppermute | solution.py:357
  96.3 1.6 collective-permute-start.4
  98.0 1.5 grad_up.1
  99.5 2.7 %collective-permute-start.19 = (bf16[4,128,768]{2,1,0:T(8,128)(2,1)S(1)}, bf16[4,128,768]{2,1,0:T(8,128)(2,1)S(1)}, u32[]{:S(2)}, u32[]{:S(2)}) collective-permute-start(bf16[4,128,768]{2,1,0:T(8,128)(2,1)S(1)} %get-tuple-element.18), channel_id=1, source_target_pairs={{4,0},{5,1},{6,2},{7,3},{0,4},{1,5},{2,6},{3,7},{12,8},{13,9},{14,... | collective-permute-start | bytes 2359304 | tf_op jit(solution)/shard_map/ppermute | solution.py:357
  102.4 42.9 %collective-permute-done.19.refs_1_ = bf16[4,128,768]{2,1,0:T(8,128)(2,1)S(1)} collective-permute-done((bf16[4,128,768]{2,1,0:T(8,128)(2,1)S(1)}, bf16[4,128,768]{2,1,0:T(8,128)(2,1)S(1)}, u32[]{:S(2)}, u32[]{:S(2)}) %collective-permute-start.19) | collective-permute-done | bytes 786464 | tf_op jit(solution)/shard_map/ppermute | solution.py:357
  145.8 1.4 collective-permute-start.20
  147.6 4.1 %collective-permute-start.22 = (bf16[128,768]{1,0:T(8,128)(2,1)S(1)}, bf16[128,768]{1,0:T(8,128)(2,1)S(1)}, u32[]{:S(2)}, u32[]{:S(2)}) collective-permute-start(bf16[128,768]{1,0:T(8,128)(2,1)S(1)} %get-tuple-element.23), channel_id=1, source_target_pairs={{2,248},{3,249},{0,250},{1,251},{6,252},{7,253},{4,254},{5,255},{1... | collective-permute-start | bytes 589832 | tf_op jit(solution)/shard_map/ppermute | solution.py:357
  151.8 2.6 %collective-permute-start.23 = (bf16[128,768]{1,0:T(8,128)(2,1)S(1)}, bf16[128,768]{1,0:T(8,128)(2,1)S(1)}, u32[]{:S(2)}, u32[]{:S(2)}) collective-permute-start(bf16[128,768]{1,0:T(8,128)(2,1)S(1)} %get-tuple-element.22), channel_id=1, source_target_pairs={{1,248},{2,249},{3,250},{0,251},{5,252},{6,253},{7,254},{4,255},{9... | collective-permute-start | bytes 589832 | tf_op jit(solution)/shard_map/ppermute | solution.py:357
  154.3 2.2 %feedback.4.refs_0_ = bf16[384,6144]{1,0:T(8,128)(2,1)} custom-call(bf16[96,6144]{1,0:T(8,128)(2,1)S(1)} %collective-permute-done.6.x_ref, bf16[96,6144]{1,0:T(8,128)(2,1)S(1)} %message.3.message_ref.own_ref, bf16[384,128]{1,0:T(8,128)(2,1)S(1)} %collective-permute-done.3.act_ref, bf16[6144,128]{1,0:T(8,128)(2,1)S(1)} %bitcast.30), custom_call_target="tpu_custom_call" | custom-call | flops 150994944 | bytes 5111808 | tf_op jit(solution)/shard_map/feedback/pallas_call | solution.py:314
  156.5 2.2 %feedback.5.refs_0_ = bf16[384,6144]{1,0:T(8,128)(2,1)} custom-call(bf16[96,6144]{1,0:T(8,128)(2,1)S(1)} %collective-permute-done.5.x_ref, bf16[288,6144]{1,0:T(8,128)(2,1)S(1)} %message.2.message_ref.own_ref, bf16[384,128]{1,0:T(8,128)(2,1)S(1)} %collective-permute-done.3.act_ref, bf16[6144,128]{1,0:T(8,128)(2,1)S(1)} %bitcast.31, ...), custom_call_target="tpu_custom_call", output_to_operand_aliasing={{}: (4, {})} | custom-call | flops 150994944 | bytes 5111808 | tf_op jit(solution)/shard_map/feedback/pallas_call | solution.py:314
  158.7 2.2 %feedback.6.refs_0_ = bf16[384,6144]{1,0:T(8,128)(2,1)} custom-call(bf16[96,6144]{1,0:T(8,128)(2,1)S(1)} %collective-permute-done.4.x_ref, bf16[288,6144]{1,0:T(8,128)(2,1)S(1)} %message.2.message_ref.own_ref, bf16[384,128]{1,0:T(8,128)(2,1)S(1)} %collective-permute-done.3.act_ref, bf16[6144,128]{1,0:T(8,128)(2,1)S(1)} %bitcast.32, ...), custom_call_target="tpu_custom_call", output_to_operand_aliasing={{}: (4, {})} | custom-call | flops 150994944 | bytes 5111808 | tf_op jit(solution)/shard_map/feedback/pallas_call | solution.py:314
  160.8 2.2 %feedback.7 = bf16[384,6144]{1,0:T(8,128)(2,1)} custom-call(bf16[96,6144]{1,0:T(8,128)(2,1)S(1)} %collective-permute-done.x_ref, bf16[288,6144]{1,0:T(8,128)(2,1)S(1)} %message.2.message_ref.own_ref, bf16[384,128]{1,0:T(8,128)(2,1)S(1)} %collective-permute-done.3.act_ref, bf16[6144,128]{1,0:T(8,128)(2,1)S(1)} %bitcast.33, ...), custom_call_target="tpu_custom_call", output_to_operand_aliasing={{}: (4, {})} | custom-call | flops 150994944 | bytes 5111808 | tf_op jit(solution)/shard_map/feedback/pallas_call | solution.py:314
  (74 shorter events, 16.5 us)
Async XLA Ops:
  0.6 24.8 %collective-permute-start.7 = (bf16[6144,128]{1,0:T(8,128)(2,1)}, bf16[6144,128]{1,0:T(8,128)(2,1)S(1)}, u32[]{:S(2)}, u32[]{:S(2)}) collective-permute-start(bf16[6144,128]{1,0:T(8,128)(2,1)} %bitcast.29), channel_id=1, source_target_pairs={{0,8},{16,24},{32,40},{48,56},{64,72},{80,88},{96,104},{112,120},{... | collective-permute-start | bytes 4718600 | tf_op jit(solution)/shard_map/ppermute | solution.py:367
  1.9 69.1 %collective-permute-start.2 = (bf16[6144,128]{1,0:T(8,128)(2,1)}, bf16[6144,128]{1,0:T(8,128)(2,1)}, u32[]{:S(2)}, u32[]{:S(2)}) collective-permute-start(bf16[6144,128]{1,0:T(8,128)(2,1)} %bitcast.46), channel_id=1, source_target_pairs={{0,248},{8,0},{16,8},{24,16},{32,24},{40,32},{48,40},{56,48},{64,5... | collective-permute-start | bytes 4718600 | tf_op jit(solution)/shard_map/ppermute | solution.py:345
  6.4 6.9 %collective-permute-start.8 = (bf16[1536,128]{1,0:T(8,128)(2,1)S(1)}, bf16[1536,128]{1,0:T(8,128)(2,1)S(1)}, u32[]{:S(2)}, u32[]{:S(2)}) collective-permute-start(bf16[1536,128]{1,0:T(8,128)(2,1)S(1)} %dynamic-slice_bitcast_fusion), channel_id=1, source_target_pairs={{8,16},{24,32},{40,48},{56,64},{72,80},{88,96},{104,112},{120,128}... | collective-permute-start | bytes 1179656 | tf_op jit(solution)/shard_map/ppermute | solution.py:364
  13.3 9.3 %collective-permute-start.10 = (bf16[1536,128]{1,0:T(8,128)(2,1)S(1)}, bf16[1536,128]{1,0:T(8,128)(2,1)S(1)}, u32[]{:S(2)}, u32[]{:S(2)}) collective-permute-start(bf16[1536,128]{1,0:T(8,128)(2,1)S(1)} %collective-permute-done.8.refs_0_), channel_id=1, source_target_pairs={{2,0},{3,1},{0,2},{1,3},{6,4},{7,5},{4,6},{5,7},{18,16},{19,17},{1... | collective-permute-start | bytes 1179656 | tf_op jit(solution)/shard_map/ppermute | solution.py:357
  13.9 9.5 %collective-permute-start.11 = (bf16[1536,128]{1,0:T(8,128)(2,1)S(1)}, bf16[1536,128]{1,0:T(8,128)(2,1)S(1)}, u32[]{:S(2)}, u32[]{:S(2)}) collective-permute-start(bf16[1536,128]{1,0:T(8,128)(2,1)S(1)} %collective-permute-done.8.refs_0_), channel_id=1, source_target_pairs={{3,0},{0,1},{1,2},{2,3},{7,4},{4,5},{5,6},{6,7},{19,16},{16,17},{1... | collective-permute-start | bytes 1179656 | tf_op jit(solution)/shard_map/ppermute | solution.py:357
  14.6 10.1 %collective-permute-start.9 = (bf16[1536,128]{1,0:T(8,128)(2,1)S(1)}, bf16[1536,128]{1,0:T(8,128)(2,1)S(1)}, u32[]{:S(2)}, u32[]{:S(2)}) collective-permute-start(bf16[1536,128]{1,0:T(8,128)(2,1)S(1)} %collective-permute-done.8.refs_0_), channel_id=1, source_target_pairs={{1,0},{2,1},{3,2},{0,3},{5,4},{6,5},{7,6},{4,7},{17,16},{18,17},{1... | collective-permute-start | bytes 1179656 | tf_op jit(solution)/shard_map/ppermute | solution.py:357
  16.4 2.3 %copy-start.3 = (bf16[1,384,6144]{2,1,0:T(8,128)(2,1)S(1)}, bf16[1,384,6144]{2,1,0:T(8,128)(2,1)}, u32[]{:S(2)}) copy-start(bf16[1,384,6144]{2,1,0:T(8,128)(2,1)} %param.13) | copy-start | bytes 14155780
  22.5 11.2 %copy-start = (bf16[384,6144]{1,0:T(8,128)(2,1)}, bf16[384,6144]{1,0:T(8,128)(2,1)S(1)}, u32[]{:S(2)}) copy-start(bf16[384,6144]{1,0:T(8,128)(2,1)S(1)} %gradient.1.grad_ref) | copy-start | bytes 14155780
  22.5 30.9 %copy-start.13 = (s32[1,384]{1,0:T(1,128)S(1)}, s32[1,384]{1,0:T(1,128)}, u32[]{:S(2)}) copy-start(s32[1,384]{1,0:T(1,128)} %param.12) | copy-start | bytes 4612
  26.6 1.4 copy-start.6
  31.0 22.5 %copy-start.2 = (s32[1,384,2048]{2,1,0:T(8,128)S(1)}, s32[1,384,2048]{2,1,0:T(8,128)}, u32[]{:S(2)}) copy-start(s32[1,384,2048]{2,1,0:T(8,128)} %param.9) | copy-start | bytes 9437188
  33.7 40.6 %collective-permute-start.12 = (bf16[384,128]{1,0:T(8,128)(2,1)}, bf16[384,128]{1,0:T(8,128)(2,1)}, u32[]{:S(2)}, u32[]{:S(2)}) collective-permute-start(bf16[384,128]{1,0:T(8,128)(2,1)} %back.1), channel_id=1, source_target_pairs={{0,240},{8,248},{16,0},{24,8},{32,16},{40,24},{48,32},{56,40},{64,... | collective-permute-start | bytes 294920 | tf_op jit(solution)/shard_map/ppermute | solution.py:345
  41.3 23.6 %collective-permute-start.1 = (f32[1,6144]{1,0:T(1,128)}, f32[1,6144]{1,0:T(1,128)}, u32[]{:S(2)}, u32[]{:S(2)}) collective-permute-start(f32[1,6144]{1,0:T(1,128)} %param.15), channel_id=1, source_target_pairs={{0,248},{8,0},{16,8},{24,16},{32,24},{40,32},{48,40},{56,48},{64,5... | collective-permute-start | bytes 73736 | tf_op jit(solution)/shard_map/ppermute | solution.py:345
  56.7 88.8 %collective-permute-start.6 = (bf16[96,6144]{1,0:T(8,128)(2,1)S(1)}, bf16[96,6144]{1,0:T(8,128)(2,1)S(1)}, u32[]{:S(2)}, u32[]{:S(2)}) collective-permute-start(bf16[96,6144]{1,0:T(8,128)(2,1)S(1)} %message.3.message_ref.own_ref), channel_id=1, source_target_pairs={{0,8},{8,16},{16,24},{24,32},{32,40},{40,48},{48,56},{56,64},{64,7... | collective-permute-start | bytes 3538952 | tf_op jit(solution)/shard_map/ppermute | solution.py:345
  71.1 26.9 %slice-start = ((s8[4718592]{0:T(1024)(128)(4,1)}), s8[4194304]{0:T(1024)(128)(4,1)S(1)}, s32[]{:S(2)}) async-start(s8[4718592]{0:T(1024)(128)(4,1)} %bitcast.27), calls=%async_computation | async-start | bytes 8388608
  74.1 6.0 %collective-permute-start.18 = (bf16[384,128]{1,0:T(8,128)(2,1)S(1)}, bf16[384,128]{1,0:T(8,128)(2,1)S(1)}, u32[]{:S(2)}, u32[]{:S(2)}) collective-permute-start(bf16[384,128]{1,0:T(8,128)(2,1)S(1)} %get-tuple-element.11), channel_id=1, source_target_pairs={{0,16},{8,24},{16,32},{24,40},{32,48},{40,56},{48,64},{56,72},{64,... | collective-permute-start | bytes 294920 | tf_op jit(solution)/shard_map/ppermute | solution.py:345
  74.3 23.7 %slice-start.1 = ((s8[4718592]{0:T(1024)(128)(4,1)}), s8[524288]{0:T(1024)(128)(4,1)S(1)}, s32[]{:S(2)}) async-start(s8[4718592]{0:T(1024)(128)(4,1)} %bitcast.27), calls=%async_computation.1 | async-start | bytes 1048576
  76.8 19.6 %collective-permute-start.13 = (bf16[2,128,768]{2,1,0:T(8,128)(2,1)S(1)}, bf16[2,128,768]{2,1,0:T(8,128)(2,1)S(1)}, u32[]{:S(2)}, u32[]{:S(2)}) collective-permute-start(bf16[2,128,768]{2,1,0:T(8,128)(2,1)S(1)} %get-tuple-element.14), channel_id=1, source_target_pairs={{3,0},{0,1},{1,2},{2,3},{7,4},{4,5},{5,6},{6,7},{11,8},{8,9},{9,10... | collective-permute-start | bytes 1179656 | tf_op jit(solution)/shard_map/ppermute | solution.py:357
  76.8 21.1 %collective-permute-start.14 = (bf16[2,128,768]{2,1,0:T(8,128)(2,1)S(1)}, bf16[2,128,768]{2,1,0:T(8,128)(2,1)S(1)}, u32[]{:S(2)}, u32[]{:S(2)}) collective-permute-start(bf16[2,128,768]{2,1,0:T(8,128)(2,1)S(1)} %get-tuple-element.15), channel_id=1, source_target_pairs={{2,0},{3,1},{0,2},{1,3},{6,4},{7,5},{4,6},{5,7},{10,8},{11,9},{8,1... | collective-permute-start | bytes 1179656 | tf_op jit(solution)/shard_map/ppermute | solution.py:357
  77.7 21.8 %collective-permute-start.15 = (bf16[2,128,768]{2,1,0:T(8,128)(2,1)S(1)}, bf16[2,128,768]{2,1,0:T(8,128)(2,1)S(1)}, u32[]{:S(2)}, u32[]{:S(2)}) collective-permute-start(bf16[2,128,768]{2,1,0:T(8,128)(2,1)S(1)} %get-tuple-element.16), channel_id=1, source_target_pairs={{1,0},{2,1},{3,2},{0,3},{5,4},{6,5},{7,6},{4,7},{9,8},{10,9},{11,1... | collective-permute-start | bytes 1179656 | tf_op jit(solution)/shard_map/ppermute | solution.py:357
  80.1 65.6 %collective-permute-start.5 = (bf16[96,6144]{1,0:T(8,128)(2,1)S(1)}, bf16[96,6144]{1,0:T(8,128)(2,1)S(1)}, u32[]{:S(2)}, u32[]{:S(2)}) collective-permute-start(bf16[96,6144]{1,0:T(8,128)(2,1)S(1)} %get-tuple-element.19), channel_id=1, source_target_pairs={{0,8},{8,16},{16,24},{24,32},{32,40},{40,48},{48,56},{56,64},{64,7... | collective-permute-start | bytes 3538952 | tf_op jit(solution)/shard_map/ppermute | solution.py:345
  96.3 49.5 %collective-permute-start.4 = (bf16[96,6144]{1,0:T(8,128)(2,1)S(1)}, bf16[96,6144]{1,0:T(8,128)(2,1)S(1)}, u32[]{:S(2)}, u32[]{:S(2)}) collective-permute-start(bf16[96,6144]{1,0:T(8,128)(2,1)S(1)} %get-tuple-element.20), channel_id=1, source_target_pairs={{0,8},{8,16},{16,24},{24,32},{32,40},{40,48},{48,56},{56,64},{64,7... | collective-permute-start | bytes 3538952 | tf_op jit(solution)/shard_map/ppermute | solution.py:345
  97.9 49.3 %collective-permute-start = (bf16[96,6144]{1,0:T(8,128)(2,1)S(1)}, bf16[96,6144]{1,0:T(8,128)(2,1)S(1)}, u32[]{:S(2)}, u32[]{:S(2)}) collective-permute-start(bf16[96,6144]{1,0:T(8,128)(2,1)S(1)} %get-tuple-element.21), channel_id=1, source_target_pairs={{0,8},{8,16},{16,24},{24,32},{32,40},{40,48},{48,56},{56,64},{64,7... | collective-permute-start | bytes 3538952 | tf_op jit(solution)/shard_map/ppermute | solution.py:345
  99.5 45.9 %collective-permute-start.19 = (bf16[4,128,768]{2,1,0:T(8,128)(2,1)S(1)}, bf16[4,128,768]{2,1,0:T(8,128)(2,1)S(1)}, u32[]{:S(2)}, u32[]{:S(2)}) collective-permute-start(bf16[4,128,768]{2,1,0:T(8,128)(2,1)S(1)} %get-tuple-element.18), channel_id=1, source_target_pairs={{4,0},{5,1},{6,2},{7,3},{0,4},{1,5},{2,6},{3,7},{12,8},{13,9},{14,... | collective-permute-start | bytes 2359304 | tf_op jit(solution)/shard_map/ppermute | solution.py:357
  145.4 2.3 %collective-permute-start.3 = (bf16[384,128]{1,0:T(8,128)(2,1)S(1)}, bf16[384,128]{1,0:T(8,128)(2,1)S(1)}, u32[]{:S(2)}, u32[]{:S(2)}) collective-permute-start(bf16[384,128]{1,0:T(8,128)(2,1)S(1)} %get-tuple-element.11), channel_id=1, source_target_pairs={{0,8},{8,16},{16,24},{24,32},{32,40},{40,48},{48,56},{56,64},{64,7... | collective-permute-start | bytes 294920 | tf_op jit(solution)/shard_map/ppermute | solution.py:345
  145.4 9.0 %copy-start.1 = (bf16[1,6144,128]{2,1,0:T(8,128)(2,1)S(1)}, bf16[1,6144,128]{2,1,0:T(8,128)(2,1)}, u32[]{:S(2)}) copy-start(bf16[1,6144,128]{2,1,0:T(8,128)(2,1)} %param.17) | copy-start | bytes 4718596
  145.6 6.2 %collective-permute-start.16 = (bf16[128,768]{1,0:T(8,128)(2,1)S(1)}, bf16[128,768]{1,0:T(8,128)(2,1)S(1)}, u32[]{:S(2)}, u32[]{:S(2)}) collective-permute-start(bf16[128,768]{1,0:T(8,128)(2,1)S(1)} %get-tuple-element.27), channel_id=1, source_target_pairs={{0,8},{1,9},{2,10},{3,11},{4,12},{5,13},{6,14},{7,15},{8,16},{9,17... | collective-permute-start | bytes 589832 | tf_op jit(solution)/shard_map/ppermute | solution.py:357
  145.7 17.3 %collective-permute-start.17 = (bf16[128,768]{1,0:T(8,128)(2,1)S(1)}, bf16[128,768]{1,0:T(8,128)(2,1)S(1)}, u32[]{:S(2)}, u32[]{:S(2)}) collective-permute-start(bf16[128,768]{1,0:T(8,128)(2,1)S(1)} %get-tuple-element.26), channel_id=1, source_target_pairs={{4,8},{5,9},{6,10},{7,11},{0,12},{1,13},{2,14},{3,15},{12,16},{13,... | collective-permute-start | bytes 589832 | tf_op jit(solution)/shard_map/ppermute | solution.py:357
  145.8 18.1 %collective-permute-start.20 = (bf16[128,768]{1,0:T(8,128)(2,1)S(1)}, bf16[128,768]{1,0:T(8,128)(2,1)S(1)}, u32[]{:S(2)}, u32[]{:S(2)}) collective-permute-start(bf16[128,768]{1,0:T(8,128)(2,1)S(1)} %get-tuple-element.25), channel_id=1, source_target_pairs={{0,248},{1,249},{2,250},{3,251},{4,252},{5,253},{6,254},{7,255},{8... | collective-permute-start | bytes 589832 | tf_op jit(solution)/shard_map/ppermute | solution.py:357
  147.3 16.7 %collective-permute-start.21 = (bf16[128,768]{1,0:T(8,128)(2,1)S(1)}, bf16[128,768]{1,0:T(8,128)(2,1)S(1)}, u32[]{:S(2)}, u32[]{:S(2)}) collective-permute-start(bf16[128,768]{1,0:T(8,128)(2,1)S(1)} %get-tuple-element.24), channel_id=1, source_target_pairs={{3,248},{0,249},{1,250},{2,251},{7,252},{4,253},{5,254},{6,255},{1... | collective-permute-start | bytes 589832 | tf_op jit(solution)/shard_map/ppermute | solution.py:357
  147.6 16.3 %collective-permute-start.22 = (bf16[128,768]{1,0:T(8,128)(2,1)S(1)}, bf16[128,768]{1,0:T(8,128)(2,1)S(1)}, u32[]{:S(2)}, u32[]{:S(2)}) collective-permute-start(bf16[128,768]{1,0:T(8,128)(2,1)S(1)} %get-tuple-element.23), channel_id=1, source_target_pairs={{2,248},{3,249},{0,250},{1,251},{6,252},{7,253},{4,254},{5,255},{1... | collective-permute-start | bytes 589832 | tf_op jit(solution)/shard_map/ppermute | solution.py:357
  151.8 12.2 %collective-permute-start.23 = (bf16[128,768]{1,0:T(8,128)(2,1)S(1)}, bf16[128,768]{1,0:T(8,128)(2,1)S(1)}, u32[]{:S(2)}, u32[]{:S(2)}) collective-permute-start(bf16[128,768]{1,0:T(8,128)(2,1)S(1)} %get-tuple-element.22), channel_id=1, source_target_pairs={{1,248},{2,249},{3,250},{0,251},{5,252},{6,253},{7,254},{4,255},{9... | collective-permute-start | bytes 589832 | tf_op jit(solution)/shard_map/ppermute | solution.py:357
  (8 other events, 8.0 us)

commit v2 on v0

v2 whole, which is shorter than its diff:
```python
import functools
import math

import jax
import jax.numpy as jnp
from jax import lax
from jax.experimental import pallas as pl
from jax.experimental.pallas import tpu as pltpu
from jax.sharding import PartitionSpec as P

D = 6144
R = 128
TOK = 384
PIECE = D // 8
QUARTER = D // 4
F32 = jnp.float32
BF16 = jnp.bfloat16
ROWS = 48
SPANS = (96, 144, 96, 48)
VMEM = 14
MIB = 1 << 20
ROOT_2_PI = math.sqrt(2.0 / math.pi)


def launch(
    kernel, name, operands, specs, shapes, out_specs,
    grid=(1,), prefetch=0, scratch=(), aliases=None, needs=(), carried=(),
):
    n_in, n_out = len(operands), len(shapes)
    first_carried = n_in + len(needs)
    n_all = first_carried + len(carried)
    anywhere = pl.BlockSpec(memory_space=pl.ANY)
    aliases = dict(aliases or {})
    for k in range(len(carried)):
        aliases[first_carried + k] = n_out + k

    def wrapped(*refs):
        rest = refs[n_all + n_out + len(carried) :]
        kernel(*refs[:n_in], *refs[n_all : n_all + n_out], *rest)

    out = pl.pallas_call(
        wrapped,
        grid_spec=pltpu.PrefetchScalarGridSpec(
            num_scalar_prefetch=prefetch,
            grid=grid,
            in_specs=[*specs, *[anywhere] * (len(needs) + len(carried))],
            out_specs=[*out_specs, *[anywhere] * len(carried)],
            scratch_shapes=scratch,
        ),
        out_shape=[
            *shapes, *[jax.ShapeDtypeStruct(c.shape, c.dtype) for c in carried]
        ],
        input_output_aliases=aliases,
        compiler_params=pltpu.CompilerParams(vmem_limit_bytes=VMEM * MIB),
        cost_estimate=pl.CostEstimate(flops=1, bytes_accessed=1, transcendentals=0),
        name=name,
    )(*operands, *needs, *carried)
    return list(out)


def array(shape, dtype):
    return jax.ShapeDtypeStruct(shape, dtype)


def rows_of(rows, width, skip=0):
    return pl.BlockSpec((rows, width), lambda i, *_: (i + skip, 0))


def whole(*shape):
    return pl.BlockSpec(shape, lambda i, *_: (0,) * len(shape))


def lanes(shape):
    return lax.broadcasted_iota(jnp.int32, shape, 1)


def spread_scales(scales, tile, rows):
    part = scales[:, : 128] if tile < 32 else scales[:, 128 : 256]
    at = lanes((rows, 128)) // 32 + 4 * (tile % 32)
    return jnp.take_along_axis(part, at, axis=1)


def message_kernel(codes_ref, scales_ref, base_ref, ids_ref, out_ref):
    rows = codes_ref.shape[0]
    scales = jnp.concatenate(
        [scales_ref[...].astype(F32), jnp.zeros((rows, 64), F32)], axis=1
    )
    picks = (ids_ref[...] == lanes((rows, 32))).astype(BF16)
    lane = lanes((rows, 128))
    for block in range(16):
        words = codes_ref[:, block * 128 : (block + 1) * 128]
        base = jnp.dot(
            picks, base_ref[:, block * 384 : (block + 1) * 384], preferred_element_type=F32
        )
        for j in range(3):
            spot = lane + 128 * j
            word = jnp.take_along_axis(words, spot // 3, axis=1)
            code = jnp.right_shift(word, (spot % 3) * 4) & 15
            step = spread_scales(scales, block * 3 + j, rows)
            value = base[:, j * 128 : (j + 1) * 128] + step * (code - 8).astype(F32)
            out_ref[:, (block * 3 + j) * 128 : (block * 3 + j + 1) * 128] = value.astype(BF16)


def make_message(codes, scales, base, ids, first, count):
    skip = first // ROWS
    return launch(
        message_kernel, "message", [codes, scales, base, ids],
        [
            rows_of(ROWS, D // 3, skip), rows_of(ROWS, D // 32, skip),
            whole(32, D), rows_of(ROWS, 1, skip),
        ],
        [array((count, D), BF16)], [rows_of(ROWS, D)], grid=(count // ROWS,),
    )[0]


def gradient_kernel(codes_ref, scales_ref, out_ref):
    rows = codes_ref.shape[0]
    scales = jnp.concatenate(
        [scales_ref[...].astype(F32), jnp.zeros((rows, 64), F32)], axis=1
    )
    for tile in range(48):
        part = slice(tile * 128, (tile + 1) * 128)
        step = spread_scales(scales, tile, rows)
        out_ref[:, part] = (step * (codes_ref[:, part].astype(F32) - 128.0)).astype(BF16)


def make_gradient(codes, scales):
    return launch(
        gradient_kernel, "gradient", [codes, scales],
        [rows_of(ROWS, D), rows_of(ROWS, D // 32)],
        [array((TOK, D), BF16)], [rows_of(ROWS, D)], grid=(TOK // ROWS,),
    )[0]


def hidden_kernel(ends, gain_ref, *refs):
    *message_refs, out_ref = refs
    step = pl.program_id(0)
    start = 0
    for end, message_ref in zip(ends, message_refs):

        @pl.when((step >= start) & (step < end))
        def _(message_ref=message_ref):
            x = message_ref[...].astype(F32)
            center = x - jnp.sum(x, axis=1, keepdims=True) * (1.0 / D)
            variance = jnp.sum(center * center, axis=1, keepdims=True) * (1.0 / D)
            out_ref[...] = (gain_ref[...] * center * lax.rsqrt(variance + 1e-05)).astype(BF16)

        start = end


def make_hidden(messages, gain):
    specs, ends, start = [], [], 0
    for message in messages:
        tiles = message.shape[0] // ROWS
        specs.append(
            pl.BlockSpec(
                (ROWS, D), lambda i, a=start, n=tiles: (jnp.clip(i - a, 0, n - 1), 0)
            )
        )
        start += tiles
        ends.append(start)
    return launch(
        functools.partial(hidden_kernel, tuple(ends)), "hidden", [gain, *messages],
        [whole(1, D), *specs],
        [array((TOK, D), BF16)], [rows_of(ROWS, D)], grid=(TOK // ROWS,),
    )[0]


def tanh_of(pre):
    return jnp.tanh(ROOT_2_PI * (pre + 0.044715 * (pre * pre * pre)))


def down_kernel(hidden_ref, weight_ref, pre_ref, act_ref):
    pre = jnp.dot(hidden_ref[...], weight_ref[...], preferred_element_type=F32)
    pre_ref[...] = pre
    act_ref[...] = (0.5 * pre * (1.0 + tanh_of(pre))).astype(BF16)


def project_down(hidden, weight, **ties):
    rows = TOK // 2
    return launch(
        down_kernel, "down", [hidden, weight],
        [rows_of(rows, D), whole(D, R)],
        [array((TOK, R), F32), array((TOK, R), BF16)], [rows_of(rows, R)] * 2, grid=(2,), **ties,
    )


def back_kernel(grad_ref, weight_ref, out_ref):
    out_ref[...] = jnp.dot(
        grad_ref[...], weight_ref[...], preferred_element_type=F32
    ).astype(BF16)


def project_back(grad, weight, **ties):
    rows = TOK // 2
    return launch(
        back_kernel, "back", [grad, weight],
        [rows_of(rows, D), whole(D, R)],
        [array((TOK, R), BF16)], [rows_of(rows, R)], grid=(2,), **ties,
    )


def transposed(left, right):
    return lax.dot_general(left, right, (((0,), (0,)), ((), ())), preferred_element_type=F32)


def store_partial(total, kept_ref, sent_ref):
    step = pl.program_id(0)

    @pl.when(step < 4)
    def _():
        kept_ref[0] = total

    @pl.when(step >= 4)
    def _():
        sent_ref[0] = total.astype(BF16)


def grad_up_kernel(order_ref, wide_ref, act_ref, kept_ref, sent_ref):
    store_partial(transposed(act_ref[...], wide_ref[...]), kept_ref, sent_ref)


def grad_down_kernel(order_ref, wide_ref, pre_ref, dact_ref, kept_ref, sent_ref, dpre_ref):
    @pl.when(pl.program_id(0) == 0)
    def _():
        pre = pre_ref[...]
        t = tanh_of(pre)
        slope = 0.5 * (1.0 + t) + (0.5 * ROOT_2_PI) * pre * (1.0 - t * t) * (
            1.0 + (3.0 * 0.044715) * (pre * pre)
        )
        dpre_ref[...] = (dact_ref[...].astype(F32) * slope).astype(BF16)

    store_partial(transposed(dpre_ref[...], wide_ref[...]), kept_ref, sent_ref)


def partial_grad(kernel, name, order, wide, *narrow, **ties):
    return launch(
        kernel, name, [order, wide, *narrow],
        [
            pl.BlockSpec((TOK, PIECE), lambda i, order: (0, order[i])),
            *[whole(TOK, R)] * len(narrow),
        ],
        [array((4, R, PIECE), F32), array((4, R, PIECE), BF16)],
        [
            pl.BlockSpec((1, R, PIECE), lambda i, order: (jnp.minimum(i, 3), 0, 0)),
            pl.BlockSpec((1, R, PIECE), lambda i, order: (jnp.maximum(i - 4, 0), 0, 0)),
        ],
        grid=(8,), prefetch=1, **ties,
    )


def halve_kernel(kept_ref, came_ref, keep_ref, send_ref):
    keep_ref[...] = kept_ref[:2] + came_ref[:2].astype(F32)
    send_ref[...] = (kept_ref[2:] + came_ref[2:].astype(F32)).astype(BF16)


def halve(kept, came, **ties):
    return launch(
        halve_kernel, "halve", [kept, came], [whole(4, R, PIECE)] * 2,
        [array((2, R, PIECE), F32), array((2, R, PIECE), BF16)], [whole(2, R, PIECE)] * 2,
        **ties,
    )


def split_kernel(kept_ref, came_ref, *out_refs):
    for half, out_ref in enumerate(out_refs):
        out_ref[...] = (kept_ref[half] + came_ref[half].astype(F32)).astype(BF16)


def split(kept, came, **ties):
    return launch(
        split_kernel, "split", [kept, came], [whole(2, R, PIECE)] * 2,
        [array((R, PIECE), BF16)] * 2, [whole(R, PIECE)] * 2, **ties,
    )


def finish_kernel(*refs):
    *in_refs, out_ref = refs
    total = in_refs[0][...].astype(F32)
    for ref in in_refs[1:]:
        total += ref[...].astype(F32)
    out_ref[...] = total.T


def finish(parts):
    return launch(
        finish_kernel, "finish", parts, [whole(R, PIECE)] * len(parts),
        [array((PIECE, R), F32)], [whole(PIECE, R)],
    )[0]


def feedback_kernel(x_ref, own_ref, act_ref, weight_ref, out_ref, done_ref):
    done_ref[...] = jnp.zeros_like(done_ref)
    act = act_ref[...]
    for part in range(4):
        at = slice(part * QUARTER, (part + 1) * QUARTER)
        lifted = lax.dot_general(
            act, weight_ref[at, :], (((1,), (1,)), ((), ())), preferred_element_type=F32
        )
        value = x_ref[:, at].astype(F32) + lifted - own_ref[:, at].astype(F32)
        out_ref[:, at] = value.astype(BF16)


def make_feedback(x, own, act, weight, first, before):
    skip = first // ROWS
    shape = array((TOK, D), BF16)
    operands = [x, own, act, weight]
    specs = [rows_of(ROWS, D), rows_of(ROWS, D), rows_of(ROWS, R, skip), whole(D, R)]
    kernel, aliases = feedback_kernel, {}
    if before is not None:
        operands, aliases = [*operands, before], {4: 0}
        specs = [*specs, pl.BlockSpec(memory_space=pl.ANY)]

        def kernel(x_ref, own_ref, act_ref, weight_ref, before_ref, out_ref, done_ref):
            feedback_kernel(x_ref, own_ref, act_ref, weight_ref, out_ref, done_ref)

    return launch(
        kernel, "feedback", operands, specs, [shape, array((8, 128), F32)],
        [rows_of(ROWS, D, skip), whole(8, 128)],
        grid=(x.shape[0] // ROWS,), aliases=aliases,
    )


def body(
    forward_codes,
    forward_scales,
    stored_base,
    sample_ids,
    backward_codes,
    backward_scales,
    norm_gain,
    w_down,
    w_up,
):
    sections = lax.axis_size("section")
    replicas = lax.axis_size("dp")
    across = replicas // 2
    both = ("section", "dp")

    def along(value, distance):
        pairs = [(s, (s + distance) % sections) for s in range(sections)]
        return lax.ppermute(value, "section", pairs)

    def among(value, flip_x, flip_y=0, section_step=0):
        pairs = []
        for s in range(sections):
            for d in range(replicas):
                y, x = divmod(d, across)
                source = (y ^ flip_y) * across + (x ^ flip_x)
                goal = ((s + section_step) % sections) * replicas + d
                pairs.append((s * replicas + source, goal))
        return lax.ppermute(value, both, pairs)

    replica = lax.axis_index("dp")
    x_at, y_at = replica % across, replica // across

    def order_of(flips):
        return jnp.stack(
            [((y_at ^ half) * across + (x_at ^ flip)) for flip in flips for half in range(2)]
        ).astype(jnp.int32)

    up = w_up[0]
    up_before = along(up, 1)
    down_next = along(w_down[0], -1)
    gain_next = along(norm_gain, -1)

    codes, scales, base = forward_codes[0], forward_scales[0], stored_base[0]
    ids = sample_ids.reshape(TOK, 1)
    firsts = [sum(SPANS[:k]) for k in range(len(SPANS))]
    messages = [make_message(codes, scales, base, ids, a, n) for a, n in zip(firsts, SPANS)]
    gradient = make_gradient(backward_codes[0], backward_scales[0])
    hidden = make_hidden(messages, gain_next)

    pre_next, act_next = project_down(hidden, down_next, needs=[up_before])
    act_before = along(act_next, 2)
    act_own = along(act_next, 1)
    arrived0 = along(messages[0], 1)
    dact_before = project_back(gradient, up_before, needs=[act_next])[0]
    dact_next = along(dact_before, -2)

    def feedback_of(own, x, at, before):
        return make_feedback(x, own, act_own, up, firsts[at], before)

    up_kept, up_sent, message1, message2 = partial_grad(
        grad_up_kernel, "grad_up", order_of((0, 1, 3, 2)), gradient, act_before,
        needs=[act_own, arrived0, dact_next], carried=messages[1:3],
    )
    arrived1 = along(message1, 1)
    arrived2 = along(message2, 1)
    down_kept, down_sent = partial_grad(
        grad_down_kernel, "grad_down", order_of((0, 3, 1, 2)), hidden, pre_next, dact_next,
        scratch=[pltpu.VMEM((TOK, R), BF16)],
    )
    feedback, done = feedback_of(messages[0], arrived0, 0, None)
    up_kept, up_sent, message3 = halve(
        up_kept, among(up_sent, 3), needs=[arrived1, done], carried=messages[3:4]
    )
    arrived3 = along(message3, 1)
    down_kept, down_sent = halve(down_kept, among(down_sent, 1))
    feedback, done = feedback_of(message1, arrived1, 1, feedback)
    up_parts = split(up_kept, among(up_sent, 1), needs=[arrived2, done])
    down_parts = split(down_kept, among(down_sent, 3))
    grad_up = finish([among(up_parts[half], 0, half, -1) for half in range(2)])
    grad_down = finish([among(down_parts[half], 0, half, 1) for half in range(2)])
    feedback, _ = feedback_of(message2, arrived2, 2, feedback)
    feedback, _ = feedback_of(message3, arrived3, 3, feedback)
    return (feedback[None], grad_down[None], grad_up[None])


def solution(mesh):
    in_specs = (
        P("section", "dp", None),
        P("section", "dp", None),
        P("section", "dp", None),
        P("section", "dp"),
        P("section", "dp", None),
        P("section", "dp", None),
        P("section", None),
        P("section", None, None),
        P("section", None, None),
    )
    out_specs = (P("section", "dp", None), P("section", "dp", None), P("section", "dp", None))
    return jax.shard_map(body, mesh=mesh, in_specs=in_specs, out_specs=out_specs, check_vma=False)
```

time: 285 us -> 130 us (0.46)
  waiting for transfers between devices: 141 us -> 30.2 us
  local copies, waits for them, and re-layouts: 70.5 us -> 19.6 us
  Pallas kernels: 0 us -> 49.2 us
  other arithmetic: 32.8 us -> 0 us
  starting transfers between devices: 3.57 us -> 29.1 us
  matrix products: 21.6 us -> 0 us
  between operations: 14.1 us -> 0.89 us
    reduce_scatter x1 -> x0, waiting for transfers between devices: 101 us -> none  [body(): lax.psum_scatter(jnp.concatenate([transposed_product(hidden, dpre), trans...]
    pallas_call x0 -> x20, Pallas kernels: none -> 49.2 us  [launch(): pl.pallas_call(wrapped, grid_spec=pltpu.PrefetchScalarGridSpec(num_scalar...]
    shift_right_arithmetic x6 -> x0, local copies, waits for them, and re-layouts: 36.9 us -> none  [unpack_codes(): jnp.right_shift(packed[..., None], offsets_bits)]
    ppermute x2 -> x18, starting transfers between devices: 3.54 us -> 29.1 us  [the longest x8 14.6 us: among(): return lax.ppermute(value, both, pairs)]
    dot_general x4 -> x0, matrix products: 21.6 us -> none  [the longest x2 12.7 us: transposed_product(): lax.dot_general(left, right, (((0,), (0,)), ((), ())), preferred_element_...]
    convert_element_type x5 -> x0, other arithmetic: 19.8 us -> none  [the longest x1 11.2 us: build_message(): (picked.astype(jnp.float32) + scale_blocks(codes, scales)).astype(jnp.bfl...]
    mul x2 -> x0, local copies, waits for them, and re-layouts: 14 us -> none  [scale_blocks(): shaped * scales.astype(jnp.float32)[:, :, None]]
    ppermute x2 -> x18, waiting for transfers between devices: 40.7 us -> 30.2 us  [the longest x8 23.7 us: among(): return lax.ppermute(value, both, pairs)]
  transfers between devices with their start and end apart: 3 -> 18, of which waited for: 2 -> 6; matrix products, arithmetic and copies ran while one was open for 11% -> 3% of each run, Pallas kernels for 0% -> 34%
where the time goes in v2:
time: 130 us; the launch traced here: 129 us
  Pallas kernels  49.2 us (38%)
  waiting for transfers between devices  30.2 us (23%)
  starting transfers between devices  29.1 us (22%)
  local copies, waits for them, and re-layouts  19.6 us (15%)
    pallas_call x20, Pallas kernels, launch(): pl.pallas_call(wrapped, grid_spec=pltpu.PrefetchScalarGridSpec(num_scalar...  49.2 us
    ppermute x8, waiting for transfers between devices, among(): return lax.ppermute(value, both, pairs)  23.7 us
    unnamed x40, local copies, waits for them, and re-layouts  18.7 us
    ppermute x8, starting transfers between devices, among(): return lax.ppermute(value, both, pairs)  14.6 us
    ppermute x10, starting transfers between devices, along(): return lax.ppermute(value, 'section', pairs)  14.5 us
    ppermute x10, waiting for transfers between devices, along(): return lax.ppermute(value, 'section', pairs)  6.57 us
  transfers between devices with their start and end apart: 18, of which 6 were waited for; matrix products, arithmetic and copies ran while one was open for 3% of the time, Pallas kernels for 34%

profile of v2, /device:TPU:1, one launch (start us, length us, event | category | flops | bytes accessed | tf_op | source)
XLA Modules:
  0.0 129.1 jit_solution(3315438986705423550)
XLA Ops:
  0.6 3.3 %collective-permute-start.1 = (bf16[6144,128]{1,0:T(8,128)(2,1)}, bf16[6144,128]{1,0:T(8,128)(2,1)}, u32[]{:S(2)}, u32[]{:S(2)}) collective-permute-start(bf16[6144,128]{1,0:T(8,128)(2,1)} %bitcast.42), channel_id=1, source_target_pairs={{0,248},{8,0},{16,8},{24,16},{32,24},{40,32},{48,40},{56,48},{64,5... | collective-permute-start | bytes 4718600 | tf_op jit(solution)/shard_map/ppermute | solution.py:342
  5.9 2.0 %copy-done = s32[1,384,2048]{2,1,0:T(8,128)S(1)} copy-done((s32[1,384,2048]{2,1,0:T(8,128)S(1)}, s32[1,384,2048]{2,1,0:T(8,128)}, u32[]{:S(2)}) %copy-start) | copy-done | bytes 3145752
  8.9 2.6 %message.4.refs_1_ = bf16[96,6144]{1,0:T(8,128)(2,1)} custom-call(s32[384,2048]{1,0:T(8,128)S(1)} %bitcast.19, bf16[384,192]{1,0:T(8,128)(2,1)S(1)} %bitcast.32, bf16[32,6144]{1,0:T(8,128)(2,1)S(1)} %bitcast.28, s32[384,1]{1,0:T(8,128)S(1)} %copy.22.refs_3_), custom_call_target="tpu_custom_call" | custom-call | flops 1 | bytes 1 | tf_op jit(solution)/shard_map/message/pallas_call | solution.py:41
  11.7 4.3 %collective-permute-start = (f32[1,6144]{1,0:T(1,128)}, f32[1,6144]{1,0:T(1,128)}, u32[]{:S(2)}, u32[]{:S(2)}) collective-permute-start(f32[1,6144]{1,0:T(1,128)} %param.15), channel_id=1, source_target_pairs={{0,248},{8,0},{16,8},{24,16},{32,24},{40,32},{48,40},{56,48},{64,5... | collective-permute-start | bytes 73736 | tf_op jit(solution)/shard_map/ppermute | solution.py:342
  16.9 1.8 %message.6.refs_3_.refs_7_ = bf16[96,6144]{1,0:T(8,128)(2,1)S(1)} custom-call(s32[384,2048]{1,0:T(8,128)S(1)} %bitcast.21, bf16[384,192]{1,0:T(8,128)(2,1)S(1)} %bitcast.34, bf16[32,6144]{1,0:T(8,128)(2,1)S(1)} %bitcast.30, s32[384,1]{1,0:T(8,128)S(1)} %copy.22.refs_3_), custom_call_target="tpu_custom_call" | custom-call | flops 1 | bytes 1 | tf_op jit(solution)/shard_map/message/pallas_call | solution.py:41
  20.6 2.6 %message.5.refs_2_.refs_6_ = bf16[144,6144]{1,0:T(8,128)(2,1)S(1)} custom-call(s32[384,2048]{1,0:T(8,128)S(1)} %bitcast.22, bf16[384,192]{1,0:T(8,128)(2,1)S(1)} %bitcast.35, bf16[32,6144]{1,0:T(8,128)(2,1)S(1)} %bitcast.31, s32[384,1]{1,0:T(8,128)S(1)} %copy-done.8), custom_call_target="tpu_custom_call" | custom-call | flops 1 | bytes 1 | tf_op jit(solution)/shard_map/message/pallas_call | solution.py:41
  23.2 1.7 %copy.20 = bf16[1,384,192]{2,1,0:T(8,128)(2,1)} copy(bf16[1,384,192]{1,2,0:T(8,128)(2,1)} %param.14) | data formatting | bytes 294912 | tf_op args[5]
  24.9 2.3 %copy-done.11 = bf16[1,384,6144]{2,1,0:T(8,128)(2,1)S(1)} copy-done((bf16[1,384,6144]{2,1,0:T(8,128)(2,1)S(1)}, bf16[1,384,6144]{2,1,0:T(8,128)(2,1)}, u32[]{:S(2)}) %copy-start.11) | copy-done | bytes 4718616
  28.2 3.0 %gradient.1.refs_0_.refs_1_ = bf16[384,6144]{1,0:T(8,128)(2,1)S(1)} custom-call(bf16[384,6144]{1,0:T(8,128)(2,1)S(1)} %bitcast.36, bf16[384,192]{1,0:T(8,128)(2,1)S(1)} %bitcast.37), custom_call_target="tpu_custom_call" | custom-call | flops 1 | bytes 1 | tf_op jit(solution)/shard_map/gradient/pallas_call | solution.py:41
  31.2 5.9 %hidden.1.refs_0_.refs_1_ = bf16[384,6144]{1,0:T(8,128)(2,1)S(1)} custom-call(f32[1,6144]{1,0:T(1,128)} %collective-permute-done.refs_0_, bf16[96,6144]{1,0:T(8,128)(2,1)} %message.4.refs_1_, bf16[144,6144]{1,0:T(8,128)(2,1)S(1)} %message.5.refs_2_.refs_6_, bf16[96,6144]{1,0:T(8,128)(2,1)S(1)} %message.6.refs_3_.refs_7_, bf16[48,6144]{1,0:T(8,128)(2,1)S(1)} %message.7.refs_4_), custom_call_target="tpu_custom_call" | custom-call | flops 1 | bytes 1 | tf_op jit(solution)/shard_map/hidden/pallas_call | solution.py:41
  37.2 4.8 %down.1 = (f32[384,128]{1,0:T(8,128)S(1)}, bf16[384,128]{1,0:T(8,128)(2,1)}) custom-call(bf16[384,6144]{1,0:T(8,128)(2,1)S(1)} %hidden.1.refs_0_.refs_1_, bf16[6144,128]{1,0:T(8,128)(2,1)} %collective-permute-done.1.refs_1_, bf16[6144,128]{1,0:T(8,128)(2,1)} %collective-permute-done.2.refs_2_.refs_1_), custom_call_target="tpu_custom_call" | custom-call | flops 1 | bytes 1 | tf_op jit(solution)/shard_map/down/pallas_call | solution.py:41
  42.0 3.6 %back.1 = bf16[384,128]{1,0:T(8,128)(2,1)} custom-call(bf16[384,6144]{1,0:T(8,128)(2,1)S(1)} %gradient.1.refs_0_.refs_1_, bf16[6144,128]{1,0:T(8,128)(2,1)} %collective-permute-done.2.refs_2_.refs_1_, bf16[384,128]{1,0:T(8,128)(2,1)} %get-tuple-element.26.refs_2_), custom_call_target="tpu_custom_call" | custom-call | flops 1 | bytes 1 | tf_op jit(solution)/shard_map/back/pallas_call | solution.py:41
  45.7 4.0 %collective-permute-start.6 = (bf16[384,128]{1,0:T(8,128)(2,1)}, bf16[384,128]{1,0:T(8,128)(2,1)}, u32[]{:S(2)}, u32[]{:S(2)}) collective-permute-start(bf16[384,128]{1,0:T(8,128)(2,1)} %back.1), channel_id=1, source_target_pairs={{0,240},{8,248},{16,0},{24,8},{32,16},{40,24},{48,32},{56,40},{64,... | collective-permute-start | bytes 294920 | tf_op jit(solution)/shard_map/ppermute | solution.py:342
  49.6 1.5 %collective-permute-start.4 = (bf16[384,128]{1,0:T(8,128)(2,1)}, bf16[384,128]{1,0:T(8,128)(2,1)}, u32[]{:S(2)}, u32[]{:S(2)}) collective-permute-start(bf16[384,128]{1,0:T(8,128)(2,1)} %get-tuple-element.26.refs_2_), channel_id=1, source_target_pairs={{0,8},{8,16},{16,24},{24,32},{32,40},{40,48},{48,56},{56,64},{64,7... | collective-permute-start | bytes 294920 | tf_op jit(solution)/shard_map/ppermute | solution.py:342
  52.2 1.3 %collective-permute-done.4.refs_3_.refs_2_ = bf16[384,128]{1,0:T(8,128)(2,1)} collective-permute-done((bf16[384,128]{1,0:T(8,128)(2,1)}, bf16[384,128]{1,0:T(8,128)(2,1)}, u32[]{:S(2)}, u32[]{:S(2)}) %collective-permute-start.4) | collective-permute-done | bytes 98336 | tf_op jit(solution)/shard_map/ppermute | solution.py:342
  53.5 4.3 %collective-permute-done.3.refs_2_ = bf16[384,128]{1,0:T(8,128)(2,1)} collective-permute-done((bf16[384,128]{1,0:T(8,128)(2,1)}, bf16[384,128]{1,0:T(8,128)(2,1)}, u32[]{:S(2)}, u32[]{:S(2)}) %collective-permute-start.3) | collective-permute-done | bytes 98336 | tf_op jit(solution)/shard_map/ppermute | solution.py:342
  57.8 2.3 %copy-done.2 = bf16[384,6144]{1,0:T(8,128)(2,1)S(1)} copy-done((bf16[384,6144]{1,0:T(8,128)(2,1)S(1)}, bf16[384,6144]{1,0:T(8,128)(2,1)}, u32[]{:S(2)}) %copy-start.2) | copy-done | bytes 4718616
  60.1 4.3 %grad_up.1 = (f32[4,128,768]{2,1,0:T(8,128)S(1)}, bf16[4,128,768]{2,1,0:T(8,128)(2,1)S(1)}, bf16[144,6144]{1,0:T(8,128)(2,1)S(1)}, bf16[96,6144]{1,0:T(8,128)(2,1)S(1)}) custom-call(s32[8]{0:T(128)S(1)} %stack.46.refs_0_, bf16[384,6144]{1,0:T(8,128)(2,1)S(1)} %copy-done.2, ...), custom_call_target="tpu_custom_call", output_to_operand_aliasing={{2}: (6, {}), {3}: (7, {})} | custom-call | flops 1 | bytes 1 | tf_op jit(solution)/shard_map/grad_up/pallas_call | solution.py:41
  66.7 2.3 %copy-done.4 = bf16[384,6144]{1,0:T(8,128)(2,1)S(1)} copy-done((bf16[384,6144]{1,0:T(8,128)(2,1)S(1)}, bf16[384,6144]{1,0:T(8,128)(2,1)}, u32[]{:S(2)}) %copy-start.4) | copy-done | bytes 4718616
  70.0 4.5 %grad_down.1 = (f32[4,128,768]{2,1,0:T(8,128)S(1)}, bf16[4,128,768]{2,1,0:T(8,128)(2,1)S(1)}) custom-call(s32[8]{0:T(128)S(1)} %stack.47.refs_0_, bf16[384,6144]{1,0:T(8,128)(2,1)S(1)} %copy-done.4, f32[384,128]{1,0:T(8,128)S(1)} %copy-done.16, bf16[384,128]{1,0:T(8,128)(2,1)} %collective-permute-done.6.refs_5_.refs_3_), custom_call_target="tpu_custom_call" | custom-call | flops 1 | bytes 1 | tf_op jit(solution)/shard_map/grad_down/pallas_call | solution.py:41
  75.8 1.8 %collective-permute-start.7 = (bf16[4,128,768]{2,1,0:T(8,128)(2,1)S(1)}, bf16[4,128,768]{2,1,0:T(8,128)(2,1)S(1)}, u32[]{:S(2)}, u32[]{:S(2)}) collective-permute-start(bf16[4,128,768]{2,1,0:T(8,128)(2,1)S(1)} %copy-done.18), channel_id=1, source_target_pairs={{3,0},{2,1},{1,2},{0,3},{7,4},{6,5},{5,6},{4,7},{11,8},{10,9},{9,1... | collective-permute-start | bytes 2359304 | tf_op jit(solution)/shard_map/ppermute | solution.py:352
  77.8 15.4 %collective-permute-done.11.refs_1_ = bf16[4,128,768]{2,1,0:T(8,128)(2,1)S(1)} collective-permute-done((bf16[4,128,768]{2,1,0:T(8,128)(2,1)S(1)}, bf16[4,128,768]{2,1,0:T(8,128)(2,1)S(1)}, u32[]{:S(2)}, u32[]{:S(2)}) %collective-permute-start.11) | collective-permute-done | bytes 786464 | tf_op jit(solution)/shard_map/ppermute | solution.py:352
  93.3 2.6 %collective-permute-start.12 = (bf16[2,128,768]{2,1,0:T(8,128)(2,1)S(1)}, bf16[2,128,768]{2,1,0:T(8,128)(2,1)S(1)}, u32[]{:S(2)}, u32[]{:S(2)}) collective-permute-start(bf16[2,128,768]{2,1,0:T(8,128)(2,1)S(1)} %get-tuple-element.41), channel_id=1, source_target_pairs={{3,0},{2,1},{1,2},{0,3},{7,4},{6,5},{5,6},{4,7},{11,8},{10,9},{9,1... | collective-permute-start | bytes 1179656 | tf_op jit(solution)/shard_map/ppermute | solution.py:352
  95.9 3.4 %feedback.4 = (bf16[384,6144]{1,0:T(8,128)(2,1)}, f32[8,128]{1,0:T(8,128)S(1)}) custom-call(bf16[96,6144]{1,0:T(8,128)(2,1)} %collective-permute-done.5.refs_4_.refs_0_, bf16[96,6144]{1,0:T(8,128)(2,1)} %message.4.refs_1_, bf16[384,128]{1,0:T(8,128)(2,1)} %collective-permute-done.4.refs_3_.refs_2_, bf16[6144,128]{1,0:T(8,128)(2,1)S(1)} %bitcast.24), custom_call_target="tpu_custom_call" | custom-call | flops 1 | bytes 1 | tf_op jit(solution)/shard_map/feedback/pallas_call | solution.py:41
  100.5 3.4 %collective-permute-done.12.refs_1_ = bf16[2,128,768]{2,1,0:T(8,128)(2,1)S(1)} collective-permute-done((bf16[2,128,768]{2,1,0:T(8,128)(2,1)S(1)}, bf16[2,128,768]{2,1,0:T(8,128)(2,1)S(1)}, u32[]{:S(2)}, u32[]{:S(2)}) %collective-permute-start.12) | collective-permute-done | bytes 393248 | tf_op jit(solution)/shard_map/ppermute | solution.py:352
  103.9 1.5 %collective-permute-start.13 = (bf16[128,768]{1,0:T(8,128)(2,1)S(1)}, bf16[128,768]{1,0:T(8,128)(2,1)S(1)}, u32[]{:S(2)}, u32[]{:S(2)}) collective-permute-start(bf16[128,768]{1,0:T(8,128)(2,1)S(1)} %get-tuple-element.42), channel_id=1, source_target_pairs={{0,8},{1,9},{2,10},{3,11},{4,12},{5,13},{6,14},{7,15},{8,16},{9,17... | collective-permute-start | bytes 589832 | tf_op jit(solution)/shard_map/ppermute | solution.py:352
  105.4 2.4 %collective-permute-start.14 = (bf16[128,768]{1,0:T(8,128)(2,1)S(1)}, bf16[128,768]{1,0:T(8,128)(2,1)S(1)}, u32[]{:S(2)}, u32[]{:S(2)}) collective-permute-start(bf16[128,768]{1,0:T(8,128)(2,1)S(1)} %get-tuple-element.43), channel_id=1, source_target_pairs={{4,8},{5,9},{6,10},{7,11},{0,12},{1,13},{2,14},{3,15},{12,16},{13,... | collective-permute-start | bytes 589832 | tf_op jit(solution)/shard_map/ppermute | solution.py:352
  107.9 4.5 %feedback.5 = (bf16[384,6144]{1,0:T(8,128)(2,1)}, f32[8,128]{1,0:T(8,128)S(1)}) custom-call(bf16[144,6144]{1,0:T(8,128)(2,1)} %collective-permute-done.8.refs_2_.refs_0_, bf16[144,6144]{1,0:T(8,128)(2,1)S(1)} %get-tuple-element.29.refs_1_, bf16[384,128]{1,0:T(8,128)(2,1)} %collective-permute-done.4.refs_3_.refs_2_, ...), custom_call_target="tpu_custom_call", output_to_operand_aliasing={{0}: (4, {})} | custom-call | flops 1 | bytes 1 | tf_op jit(solution)/shard_map/feedback/pallas_call | solution.py:41
  113.1 4.2 %collective-permute-start.17 = (bf16[128,768]{1,0:T(8,128)(2,1)S(1)}, bf16[128,768]{1,0:T(8,128)(2,1)S(1)}, u32[]{:S(2)}, u32[]{:S(2)}) collective-permute-start(bf16[128,768]{1,0:T(8,128)(2,1)S(1)} %get-tuple-element.48), channel_id=1, source_target_pairs={{4,248},{5,249},{6,250},{7,251},{0,252},{1,253},{2,254},{3,255},{1... | collective-permute-start | bytes 589832 | tf_op jit(solution)/shard_map/ppermute | solution.py:352
  117.3 4.9 %collective-permute-done.14.refs_1_ = bf16[128,768]{1,0:T(8,128)(2,1)S(1)} collective-permute-done((bf16[128,768]{1,0:T(8,128)(2,1)S(1)}, bf16[128,768]{1,0:T(8,128)(2,1)S(1)}, u32[]{:S(2)}, u32[]{:S(2)}) %collective-permute-start.14) | collective-permute-done | bytes 196640 | tf_op jit(solution)/shard_map/ppermute | solution.py:352
  123.2 2.9 %feedback.6 = (bf16[384,6144]{1,0:T(8,128)(2,1)}, f32[8,128]{1,0:T(8,128)}) custom-call(bf16[96,6144]{1,0:T(8,128)(2,1)S(1)} %collective-permute-done.10.refs_0_.refs_2_, bf16[96,6144]{1,0:T(8,128)(2,1)S(1)} %get-tuple-element.32.refs_1_, bf16[384,128]{1,0:T(8,128)(2,1)} %collective-permute-done.4.refs_3_.refs_2_, ...), custom_call_target="tpu_custom_call", output_to_operand_aliasing={{0}: (4, {})} | custom-call | flops 1 | bytes 1 | tf_op jit(solution)/shard_map/feedback/pallas_call | solution.py:41
  126.0 2.2 %feedback.7 = (bf16[384,6144]{1,0:T(8,128)(2,1)}, f32[8,128]{1,0:T(8,128)}) custom-call(bf16[48,6144]{1,0:T(8,128)(2,1)S(1)} %collective-permute-done.9.refs_0_, bf16[48,6144]{1,0:T(8,128)(2,1)S(1)} %get-tuple-element.31.refs_1_, bf16[384,128]{1,0:T(8,128)(2,1)} %collective-permute-done.4.refs_3_.refs_2_, ...), custom_call_target="tpu_custom_call", output_to_operand_aliasing={{0}: (4, {})} | custom-call | flops 1 | bytes 1 | tf_op jit(solution)/shard_map/feedback/pallas_call | solution.py:41
  (67 shorter events, 16.5 us)
Async XLA Ops:
  0.6 36.6 %collective-permute-start.1 = (bf16[6144,128]{1,0:T(8,128)(2,1)}, bf16[6144,128]{1,0:T(8,128)(2,1)}, u32[]{:S(2)}, u32[]{:S(2)}) collective-permute-start(bf16[6144,128]{1,0:T(8,128)(2,1)} %bitcast.42), channel_id=1, source_target_pairs={{0,248},{8,0},{16,8},{24,16},{32,24},{40,32},{48,40},{56,48},{64,5... | collective-permute-start | bytes 4718600 | tf_op jit(solution)/shard_map/ppermute | solution.py:342
  3.9 33.3 %collective-permute-start.2 = (bf16[6144,128]{1,0:T(8,128)(2,1)}, bf16[6144,128]{1,0:T(8,128)(2,1)}, u32[]{:S(2)}, u32[]{:S(2)}) collective-permute-start(bf16[6144,128]{1,0:T(8,128)(2,1)} %bitcast.23), channel_id=1, source_target_pairs={{0,8},{8,16},{16,24},{24,32},{32,40},{40,48},{48,56},{56,64},{64,7... | collective-permute-start | bytes 4718600 | tf_op jit(solution)/shard_map/ppermute | solution.py:342
  4.8 12.1 %copy-start.7 = (s32[384,1]{1,0:T(8,128)}, s32[384,1]{1,0:T(8,128)S(1)}, u32[]{:S(2)}) copy-start(s32[384,1]{1,0:T(8,128)S(1)} %copy.22.refs_3_) | copy-start | bytes 4612
  5.9 11.0 %copy-start.9 = (bf16[1,384,192]{2,1,0:T(8,128)(2,1)}, bf16[1,384,192]{2,1,0:T(8,128)(2,1)S(1)}, u32[]{:S(2)}) copy-start(bf16[1,384,192]{2,1,0:T(8,128)(2,1)S(1)} %copy.21) | copy-start | bytes 442372
  5.9 2.0 %copy-start = (s32[1,384,2048]{2,1,0:T(8,128)S(1)}, s32[1,384,2048]{2,1,0:T(8,128)}, u32[]{:S(2)}) copy-start(s32[1,384,2048]{2,1,0:T(8,128)} %param.9) | copy-start | bytes 9437188
  7.9 1.0 copy-start.6
  11.4 39.8 %collective-permute-start.5 = (bf16[96,6144]{1,0:T(8,128)(2,1)}, bf16[96,6144]{1,0:T(8,128)(2,1)}, u32[]{:S(2)}, u32[]{:S(2)}) collective-permute-start(bf16[96,6144]{1,0:T(8,128)(2,1)} %message.4.refs_1_), channel_id=1, source_target_pairs={{0,8},{8,16},{16,24},{24,32},{32,40},{40,48},{48,56},{56,64},{64,7... | collective-permute-start | bytes 3538952 | tf_op jit(solution)/shard_map/ppermute | solution.py:342
  11.7 19.5 %collective-permute-start = (f32[1,6144]{1,0:T(1,128)}, f32[1,6144]{1,0:T(1,128)}, u32[]{:S(2)}, u32[]{:S(2)}) collective-permute-start(f32[1,6144]{1,0:T(1,128)} %param.15), channel_id=1, source_target_pairs={{0,248},{8,0},{16,8},{24,16},{32,24},{40,32},{48,40},{56,48},{64,5... | collective-permute-start | bytes 73736 | tf_op jit(solution)/shard_map/ppermute | solution.py:342
  24.9 2.3 %copy-start.11 = (bf16[1,384,6144]{2,1,0:T(8,128)(2,1)S(1)}, bf16[1,384,6144]{2,1,0:T(8,128)(2,1)}, u32[]{:S(2)}) copy-start(bf16[1,384,6144]{2,1,0:T(8,128)(2,1)} %param.13) | copy-start | bytes 14155780
  31.2 10.8 %copy-start.1 = (bf16[384,6144]{1,0:T(8,128)(2,1)}, bf16[384,6144]{1,0:T(8,128)(2,1)S(1)}, u32[]{:S(2)}) copy-start(bf16[384,6144]{1,0:T(8,128)(2,1)S(1)} %gradient.1.refs_0_.refs_1_) | copy-start | bytes 14155780
  37.2 4.8 %copy-start.3 = (bf16[384,6144]{1,0:T(8,128)(2,1)}, bf16[384,6144]{1,0:T(8,128)(2,1)S(1)}, u32[]{:S(2)}) copy-start(bf16[384,6144]{1,0:T(8,128)(2,1)S(1)} %hidden.1.refs_0_.refs_1_) | copy-start | bytes 14155780
  42.0 3.7 %copy-start.15 = (f32[384,128]{1,0:T(8,128)}, f32[384,128]{1,0:T(8,128)S(1)}, u32[]{:S(2)}) copy-start(f32[384,128]{1,0:T(8,128)S(1)} %get-tuple-element.37.refs_2_) | copy-start | bytes 589828
  45.7 6.5 %collective-permute-start.6 = (bf16[384,128]{1,0:T(8,128)(2,1)}, bf16[384,128]{1,0:T(8,128)(2,1)}, u32[]{:S(2)}, u32[]{:S(2)}) collective-permute-start(bf16[384,128]{1,0:T(8,128)(2,1)} %back.1), channel_id=1, source_target_pairs={{0,240},{8,248},{16,0},{24,8},{32,16},{40,24},{48,32},{56,40},{64,... | collective-permute-start | bytes 294920 | tf_op jit(solution)/shard_map/ppermute | solution.py:342
  49.6 3.9 %collective-permute-start.4 = (bf16[384,128]{1,0:T(8,128)(2,1)}, bf16[384,128]{1,0:T(8,128)(2,1)}, u32[]{:S(2)}, u32[]{:S(2)}) collective-permute-start(bf16[384,128]{1,0:T(8,128)(2,1)} %get-tuple-element.26.refs_2_), channel_id=1, source_target_pairs={{0,8},{8,16},{16,24},{24,32},{32,40},{40,48},{48,56},{56,64},{64,7... | collective-permute-start | bytes 294920 | tf_op jit(solution)/shard_map/ppermute | solution.py:342
  51.1 6.6 %collective-permute-start.3 = (bf16[384,128]{1,0:T(8,128)(2,1)}, bf16[384,128]{1,0:T(8,128)(2,1)}, u32[]{:S(2)}, u32[]{:S(2)}) collective-permute-start(bf16[384,128]{1,0:T(8,128)(2,1)} %get-tuple-element.26.refs_2_), channel_id=1, source_target_pairs={{0,16},{8,24},{16,32},{24,40},{32,48},{40,56},{48,64},{56,72},{64,... | collective-permute-start | bytes 294920 | tf_op jit(solution)/shard_map/ppermute | solution.py:342
  57.8 2.3 %copy-start.2 = (bf16[384,6144]{1,0:T(8,128)(2,1)S(1)}, bf16[384,6144]{1,0:T(8,128)(2,1)}, u32[]{:S(2)}) copy-start(bf16[384,6144]{1,0:T(8,128)(2,1)} %copy-done.1) | copy-start | bytes 14155780
  64.5 1.2 copy-start.12
  66.6 32.7 %collective-permute-start.8 = (bf16[144,6144]{1,0:T(8,128)(2,1)S(1)}, bf16[144,6144]{1,0:T(8,128)(2,1)}, u32[]{:S(2)}, u32[]{:S(2)}) collective-permute-start(bf16[144,6144]{1,0:T(8,128)(2,1)S(1)} %get-tuple-element.29.refs_1_), channel_id=1, source_target_pairs={{0,8},{8,16},{16,24},{24,32},{32,40},{40,48},{48,56},{56,64},{64,7... | collective-permute-start | bytes 5308424 | tf_op jit(solution)/shard_map/ppermute | solution.py:342
  66.7 2.3 %copy-start.4 = (bf16[384,6144]{1,0:T(8,128)(2,1)S(1)}, bf16[384,6144]{1,0:T(8,128)(2,1)}, u32[]{:S(2)}) copy-start(bf16[384,6144]{1,0:T(8,128)(2,1)} %copy-done.3) | copy-start | bytes 14155780
  70.0 5.8 %copy-start.18 = (bf16[4,128,768]{2,1,0:T(8,128)(2,1)S(1)}, bf16[4,128,768]{2,1,0:T(8,128)(2,1)}, u32[]{:S(2)}) copy-start(bf16[4,128,768]{2,1,0:T(8,128)(2,1)} %copy-done.17) | copy-start | bytes 2359300
  74.5 21.4 %copy-start.5 = (bf16[1,6144,128]{2,1,0:T(8,128)(2,1)S(1)}, bf16[1,6144,128]{2,1,0:T(8,128)(2,1)}, u32[]{:S(2)}) copy-start(bf16[1,6144,128]{2,1,0:T(8,128)(2,1)} %param.17) | copy-start | bytes 4718596
  74.5 18.7 %collective-permute-start.11 = (bf16[4,128,768]{2,1,0:T(8,128)(2,1)S(1)}, bf16[4,128,768]{2,1,0:T(8,128)(2,1)S(1)}, u32[]{:S(2)}, u32[]{:S(2)}) collective-permute-start(bf16[4,128,768]{2,1,0:T(8,128)(2,1)S(1)} %get-tuple-element.39), channel_id=1, source_target_pairs={{1,0},{0,1},{3,2},{2,3},{5,4},{4,5},{7,6},{6,7},{9,8},{8,9},{11,10... | collective-permute-start | bytes 2359304 | tf_op jit(solution)/shard_map/ppermute | solution.py:352
  75.8 23.5 %collective-permute-start.7 = (bf16[4,128,768]{2,1,0:T(8,128)(2,1)S(1)}, bf16[4,128,768]{2,1,0:T(8,128)(2,1)S(1)}, u32[]{:S(2)}, u32[]{:S(2)}) collective-permute-start(bf16[4,128,768]{2,1,0:T(8,128)(2,1)S(1)} %copy-done.18), channel_id=1, source_target_pairs={{3,0},{2,1},{1,2},{0,3},{7,4},{6,5},{5,6},{4,7},{11,8},{10,9},{9,1... | collective-permute-start | bytes 2359304 | tf_op jit(solution)/shard_map/ppermute | solution.py:352
  77.6 34.7 %collective-permute-start.10 = (bf16[96,6144]{1,0:T(8,128)(2,1)S(1)}, bf16[96,6144]{1,0:T(8,128)(2,1)S(1)}, u32[]{:S(2)}, u32[]{:S(2)}) collective-permute-start(bf16[96,6144]{1,0:T(8,128)(2,1)S(1)} %get-tuple-element.32.refs_1_), channel_id=1, source_target_pairs={{0,8},{8,16},{16,24},{24,32},{32,40},{40,48},{48,56},{56,64},{64,7... | collective-permute-start | bytes 3538952 | tf_op jit(solution)/shard_map/ppermute | solution.py:342
  93.3 6.0 %copy-start.13 = (f32[4,128,768]{2,1,0:T(8,128)S(1)}, f32[4,128,768]{2,1,0:T(8,128)}, u32[]{:S(2)}) copy-start(f32[4,128,768]{2,1,0:T(8,128)} %copy-done.12) | copy-start | bytes 4718596
  93.3 10.6 %collective-permute-start.12 = (bf16[2,128,768]{2,1,0:T(8,128)(2,1)S(1)}, bf16[2,128,768]{2,1,0:T(8,128)(2,1)S(1)}, u32[]{:S(2)}, u32[]{:S(2)}) collective-permute-start(bf16[2,128,768]{2,1,0:T(8,128)(2,1)S(1)} %get-tuple-element.41), channel_id=1, source_target_pairs={{3,0},{2,1},{1,2},{0,3},{7,4},{6,5},{5,6},{4,7},{11,8},{10,9},{9,1... | collective-permute-start | bytes 1179656 | tf_op jit(solution)/shard_map/ppermute | solution.py:352
  99.5 12.9 %collective-permute-start.15 = (bf16[2,128,768]{2,1,0:T(8,128)(2,1)S(1)}, bf16[2,128,768]{2,1,0:T(8,128)(2,1)S(1)}, u32[]{:S(2)}, u32[]{:S(2)}) collective-permute-start(bf16[2,128,768]{2,1,0:T(8,128)(2,1)S(1)} %get-tuple-element.45), channel_id=1, source_target_pairs={{1,0},{0,1},{3,2},{2,3},{5,4},{4,5},{7,6},{6,7},{9,8},{8,9},{11,10... | collective-permute-start | bytes 1179656 | tf_op jit(solution)/shard_map/ppermute | solution.py:352
  99.6 26.5 %collective-permute-start.9 = (bf16[48,6144]{1,0:T(8,128)(2,1)S(1)}, bf16[48,6144]{1,0:T(8,128)(2,1)S(1)}, u32[]{:S(2)}, u32[]{:S(2)}) collective-permute-start(bf16[48,6144]{1,0:T(8,128)(2,1)S(1)} %get-tuple-element.31.refs_1_), channel_id=1, source_target_pairs={{0,8},{8,16},{16,24},{24,32},{32,40},{40,48},{48,56},{56,64},{64,7... | collective-permute-start | bytes 1769480 | tf_op jit(solution)/shard_map/ppermute | solution.py:342
  103.9 13.4 %collective-permute-start.13 = (bf16[128,768]{1,0:T(8,128)(2,1)S(1)}, bf16[128,768]{1,0:T(8,128)(2,1)S(1)}, u32[]{:S(2)}, u32[]{:S(2)}) collective-permute-start(bf16[128,768]{1,0:T(8,128)(2,1)S(1)} %get-tuple-element.42), channel_id=1, source_target_pairs={{0,8},{1,9},{2,10},{3,11},{4,12},{5,13},{6,14},{7,15},{8,16},{9,17... | collective-permute-start | bytes 589832 | tf_op jit(solution)/shard_map/ppermute | solution.py:352
  105.4 16.8 %collective-permute-start.14 = (bf16[128,768]{1,0:T(8,128)(2,1)S(1)}, bf16[128,768]{1,0:T(8,128)(2,1)S(1)}, u32[]{:S(2)}, u32[]{:S(2)}) collective-permute-start(bf16[128,768]{1,0:T(8,128)(2,1)S(1)} %get-tuple-element.43), channel_id=1, source_target_pairs={{4,8},{5,9},{6,10},{7,11},{0,12},{1,13},{2,14},{3,15},{12,16},{13,... | collective-permute-start | bytes 589832 | tf_op jit(solution)/shard_map/ppermute | solution.py:352
  112.4 15.8 %collective-permute-start.16 = (bf16[128,768]{1,0:T(8,128)(2,1)S(1)}, bf16[128,768]{1,0:T(8,128)(2,1)S(1)}, u32[]{:S(2)}, u32[]{:S(2)}) collective-permute-start(bf16[128,768]{1,0:T(8,128)(2,1)S(1)} %get-tuple-element.47), channel_id=1, source_target_pairs={{0,248},{1,249},{2,250},{3,251},{4,252},{5,253},{6,254},{7,255},{8... | collective-permute-start | bytes 589832 | tf_op jit(solution)/shard_map/ppermute | solution.py:352
  113.1 15.1 %collective-permute-start.17 = (bf16[128,768]{1,0:T(8,128)(2,1)S(1)}, bf16[128,768]{1,0:T(8,128)(2,1)S(1)}, u32[]{:S(2)}, u32[]{:S(2)}) collective-permute-start(bf16[128,768]{1,0:T(8,128)(2,1)S(1)} %get-tuple-element.48), channel_id=1, source_target_pairs={{4,248},{5,249},{6,250},{7,251},{0,252},{1,253},{2,254},{3,255},{1... | collective-permute-start | bytes 589832 | tf_op jit(solution)/shard_map/ppermute | solution.py:352
  (5 other events, 4.6 us)

commit v3 on v0

v3 whole, which is shorter than its diff:
```python
import functools
import math

import jax
import jax.numpy as jnp
from jax import lax
from jax.experimental import pallas as pl
from jax.experimental.pallas import tpu as pltpu
from jax.sharding import PartitionSpec as P

D = 6144
R = 128
TOK = 384
PIECE = D // 8
F32 = jnp.float32
BF16 = jnp.bfloat16
TILE = 48
SPANS = (96, 144, 96, 48)
MIB = 1 << 20
ROOT_2_PI = math.sqrt(2.0 / math.pi)
HBM = pl.BlockSpec(memory_space=pltpu.HBM)
VMEM = pl.BlockSpec(memory_space=pltpu.VMEM)
SMEM = pl.BlockSpec(memory_space=pltpu.SMEM)
ANY = pl.BlockSpec(memory_space=pl.ANY)


def array(shape, dtype):
    return jax.ShapeDtypeStruct(shape, dtype)


def launch(kernel, name, ins, outs, scratch=(), aliases=None, needs=(), carried=(), grant=63):
    n_in, n_out = len(ins), len(outs)
    first_carried = n_in + len(needs)
    n_all = first_carried + len(carried)
    aliases = dict(aliases or {})
    for k in range(len(carried)):
        aliases[first_carried + k] = n_out + k

    def wrapped(*refs):
        rest = refs[n_all + n_out + len(carried) :]
        kernel(*refs[:n_in], *refs[n_all : n_all + n_out], *rest)

    return pl.pallas_call(
        wrapped,
        in_specs=[where for _, where in ins] + [ANY] * (len(needs) + len(carried)),
        out_specs=[where for _, where in outs] + [ANY] * len(carried),
        out_shape=[out for out, _ in outs] + [array(c.shape, c.dtype) for c in carried],
        scratch_shapes=scratch,
        input_output_aliases=aliases,
        compiler_params=pltpu.CompilerParams(vmem_limit_bytes=grant * MIB),
        cost_estimate=pl.CostEstimate(flops=1, bytes_accessed=1, transcendentals=0),
        name=name,
    )(*[value for value, _ in ins], *needs, *carried)


def sems(count):
    return pltpu.SemaphoreType.DMA((count,))


def tile_at(i, base=0):
    return pl.ds(pl.multiple_of(base + i * TILE, 16), TILE)


def lanes(shape):
    return lax.broadcasted_iota(jnp.int32, shape, 1)


def spread_scales(scales_ref, rows, tile):
    half, at = divmod(tile, 32)
    part = scales_ref[rows, half * 128 : half * 128 + 128]
    return jnp.take_along_axis(part, lanes((TILE, 128)) // 32 + 4 * at, axis=1)


def turn_scales(scales_ref, turned_ref):
    turned_ref[:, : D // 32] = scales_ref[...].astype(F32).T


def message_kernel(
    first, spans, codes_hbm, scales_hbm, base_hbm, ids_hbm, *refs
):
    n = len(spans)
    out_hbms, stats_hbm = refs[:n], refs[n]
    (codes_ref, scales_ref, base_ref, ids_ref, turned_ref, picks_ref, out_ref, stats_ref,
     code_sems, in_sems, out_sems, stats_sem) = refs[n + 1 :]
    count = sum(spans)
    tiles = count // TILE
    small = [
        pltpu.make_async_copy(src, dst, in_sems.at[k])
        for k, (src, dst) in enumerate(
            ((scales_hbm, scales_ref), (ids_hbm, ids_ref), (base_hbm, base_ref))
        )
    ]

    def codes_copy(i):
        return pltpu.make_async_copy(
            codes_hbm.at[tile_at(i, first)], codes_ref.at[tile_at(i)], code_sems.at[i]
        )

    def out_copy(i, out_hbm, start):
        return pltpu.make_async_copy(
            out_ref.at[tile_at(i)], out_hbm.at[tile_at(i, -start)], out_sems.at[i]
        )

    for copy in small:
        copy.start()
    for i in range(tiles):
        codes_copy(i).start()
    for copy in small:
        copy.wait()
    turn_scales(scales_ref, turned_ref)
    hits = lax.broadcasted_iota(jnp.int32, (32, TOK), 0) == ids_ref[...]
    picks_ref[...] = hits.astype(F32).T.astype(BF16)
    lane = lanes((TILE, 128))
    bounds = [sum(spans[:k]) for k in range(n + 1)]

    def one_tile(i, carry):
        codes_copy(i).wait()
        here, rows = tile_at(i), tile_at(i, first)
        picks = picks_ref[rows, :]
        total = jnp.zeros((TILE, 128), F32)
        for block in range(16):
            words = codes_ref[here, block * 128 : (block + 1) * 128]
            base = jnp.dot(
                picks, base_ref[:, block * 384 : (block + 1) * 384], preferred_element_type=F32
            )
            for j in range(3):
                spot = lane + 128 * j
                word = jnp.take_along_axis(words, spot // 3, axis=1)
                code = jnp.right_shift(word, (spot % 3) * 4) & 15
                tile = block * 3 + j
                step = spread_scales(turned_ref, rows, tile)
                value = base[:, j * 128 : (j + 1) * 128] + step * (code - 8).astype(F32)
                value = value.astype(BF16)
                out_ref[here, tile * 128 : (tile + 1) * 128] = value
                total += value.astype(F32)
        for out_hbm, start, end in zip(out_hbms, bounds, bounds[1:]):

            @pl.when((i >= start // TILE) & (i < end // TILE))
            def _(out_hbm=out_hbm, start=start):
                out_copy(i, out_hbm, start).start()

        mean = jnp.sum(total, axis=1, keepdims=True) * (1.0 / D)
        total = jnp.zeros((TILE, 128), F32)
        for tile in range(48):
            center = out_ref[here, tile * 128 : (tile + 1) * 128].astype(F32) - mean
            total += center * center
        variance = jnp.sum(total, axis=1, keepdims=True) * (1.0 / D)
        stats_ref[here, :128] = jnp.broadcast_to(mean, (TILE, 128))
        stats_ref[here, 128:] = jnp.broadcast_to(lax.rsqrt(variance + 1e-05), (TILE, 128))
        return carry

    lax.fori_loop(0, tiles, one_tile, 0)
    stats_copy = pltpu.make_async_copy(stats_ref, stats_hbm, stats_sem.at[0])
    stats_copy.start()
    for out_hbm, start, end in zip(out_hbms, bounds, bounds[1:]):
        for i in range(start // TILE, end // TILE):
            out_copy(i, out_hbm, start).wait()
    stats_copy.wait()


def make_messages(codes, scales, base, ids, first, spans, **ties):
    count = sum(spans)
    return launch(
        functools.partial(message_kernel, first, spans), "message",
        [(codes, HBM), (scales, HBM), (base, HBM), (ids, HBM)],
        [(array((span, D), BF16), HBM) for span in spans] + [(array((count, 256), F32), HBM)],
        [
            pltpu.VMEM((count, D // 3), jnp.int32), pltpu.VMEM((D // 32, TOK), BF16),
            pltpu.VMEM((32, D), BF16), pltpu.VMEM((1, TOK), jnp.int32),
            pltpu.VMEM((TOK, 256), F32), pltpu.VMEM((TOK, 32), BF16),
            pltpu.VMEM((count, D), BF16), pltpu.VMEM((count, 256), F32),
            sems(count // TILE), sems(3), sems(count // TILE), sems(1),
        ],
        **ties,
    )


def gradient_kernel(
    codes_hbm, scales_hbm, out_hbm,
    codes_ref, scales_ref, turned_ref, out_ref, code_sems, in_sem, out_sems,
):
    tiles = TOK // TILE
    scales_copy = pltpu.make_async_copy(scales_hbm, scales_ref, in_sem.at[0])
    scales_copy.start()

    def codes_copy(i):
        return pltpu.make_async_copy(
            codes_hbm.at[tile_at(i)], codes_ref.at[tile_at(i)], code_sems.at[i]
        )

    def out_copy(i):
        return pltpu.make_async_copy(
            out_ref.at[:, tile_at(i)], out_hbm.at[:, tile_at(i)], out_sems.at[i]
        )

    for i in range(tiles):
        codes_copy(i).start()
    scales_copy.wait()
    turn_scales(scales_ref, turned_ref)

    def one_tile(i, carry):
        codes_copy(i).wait()
        rows = tile_at(i)
        for tile in range(48):
            step = spread_scales(turned_ref, rows, tile)
            codes = codes_ref[rows, tile * 128 : (tile + 1) * 128].astype(F32)
            piece, at = divmod(tile, 6)
            out_ref[piece, rows, at * 128 : (at + 1) * 128] = (step * (codes - 128.0)).astype(
                BF16
            )
        out_copy(i).start()
        return carry

    lax.fori_loop(0, tiles, one_tile, 0)
    for i in range(tiles):
        out_copy(i).wait()


def make_gradient(codes, scales, **ties):
    return launch(
        gradient_kernel, "gradient", [(codes, HBM), (scales, HBM)],
        [(array((8, TOK, PIECE), BF16), HBM)],
        [
            pltpu.VMEM((TOK, D), BF16), pltpu.VMEM((D // 32, TOK), BF16),
            pltpu.VMEM((TOK, 256), F32), pltpu.VMEM((8, TOK, PIECE), BF16),
            sems(TOK // TILE), sems(1), sems(TOK // TILE),
        ],
        **ties,
    )[0]


def tanh_of(pre):
    return jnp.tanh(ROOT_2_PI * (pre + 0.044715 * (pre * pre * pre)))


def down_kernel(spans, n_stats, weight_hbm, gain_ref, *refs):
    n = len(spans)
    message_hbms, stats_hbms = refs[:n], refs[n : n + n_stats]
    (pre_ref, act_ref, hidden_hbm, message_ref, stats_ref, weight_ref, hidden_ref,
     message_sems, stats_sems, weight_sems, out_sems) = refs[n + n_stats :]
    bounds = [sum(spans[:k]) for k in range(n + 1)]
    stats_copies, row = [], 0
    for k, stats_hbm in enumerate(stats_hbms):
        count = stats_hbm.shape[0]
        stats_copies.append(
            pltpu.make_async_copy(
                stats_hbm, stats_ref.at[pl.ds(row, count)], stats_sems.at[k]
            )
        )
        row += count
    copies = []
    for p in range(8):
        columns = pl.ds(p * PIECE, PIECE)
        copies.append([
            pltpu.make_async_copy(
                weight_hbm.at[columns], weight_ref.at[columns], weight_sems.at[p]
            )
        ] + [
            pltpu.make_async_copy(
                hbm.at[:, columns], message_ref.at[p, pl.ds(start, span)],
                message_sems.at[p * n + k],
            )
            for k, (hbm, start, span) in enumerate(zip(message_hbms, bounds, spans))
        ])
    for copy in stats_copies + [c for group in copies for c in group]:
        copy.start()
    for copy in stats_copies:
        copy.wait()
    out_copies = []
    for p in range(8):
        for copy in copies[p]:
            copy.wait()
        columns = slice(p * PIECE, (p + 1) * PIECE)
        for t in range(TOK // TILE):
            rows = slice(t * TILE, (t + 1) * TILE)
            for c in range(PIECE // 128):
                at = slice(c * 128, (c + 1) * 128)
                center = message_ref[p, rows, at].astype(F32) - stats_ref[rows, :128]
                gain = gain_ref[:, p * PIECE + c * 128 : p * PIECE + (c + 1) * 128]
                hidden_ref[p, rows, at] = (gain * center * stats_ref[rows, 128:]).astype(BF16)
        copy = pltpu.make_async_copy(hidden_ref.at[p], hidden_hbm.at[p], out_sems.at[p])
        copy.start()
        out_copies.append(copy)
        part = jnp.dot(hidden_ref[p], weight_ref[columns, :], preferred_element_type=F32)
        if p == 0:
            pre_ref[...] = part
        else:
            pre_ref[...] += part
    pre = pre_ref[...]
    act_ref[...] = (0.5 * pre * (1.0 + tanh_of(pre))).astype(BF16)
    for copy in out_copies:
        copy.wait()


def project_down(messages, stats, gain, weight, **ties):
    spans = tuple(m.shape[0] for m in messages)
    return launch(
        functools.partial(down_kernel, spans, len(stats)), "down",
        [(weight, HBM), (gain, VMEM)] + [(v, HBM) for v in (*messages, *stats)],
        [
            (array((TOK, R), F32), VMEM), (array((TOK, R), BF16), VMEM),
            (array((8, TOK, PIECE), BF16), HBM),
        ],
        [
            pltpu.VMEM((8, TOK, PIECE), BF16), pltpu.VMEM((TOK, 256), F32),
            pltpu.VMEM((D, R), BF16), pltpu.VMEM((8, TOK, PIECE), BF16),
            sems(8 * len(spans)), sems(len(stats)), sems(8), sems(8),
        ],
        **ties,
    )


def back_kernel(grad_hbm, weight_hbm, out_ref, grad_ref, weight_ref, grad_sems, weight_sems):
    copies = []
    for p in range(8):
        columns = pl.ds(p * PIECE, PIECE)
        copies.append((
            pltpu.make_async_copy(
                weight_hbm.at[columns], weight_ref.at[columns], weight_sems.at[p]
            ),
            pltpu.make_async_copy(grad_hbm.at[p], grad_ref.at[p], grad_sems.at[p]),
        ))
    for group in copies:
        for copy in group:
            copy.start()
    total = jnp.zeros((TOK, R), F32)
    for p in range(8):
        for copy in copies[p]:
            copy.wait()
        total += jnp.dot(
            grad_ref[p], weight_ref[p * PIECE : (p + 1) * PIECE, :], preferred_element_type=F32
        )
    out_ref[...] = total.astype(BF16)


def project_back(grad, weight, **ties):
    return launch(
        back_kernel, "back", [(grad, HBM), (weight, HBM)], [(array((TOK, R), BF16), VMEM)],
        [pltpu.VMEM((8, TOK, PIECE), BF16), pltpu.VMEM((D, R), BF16), sems(8), sems(8)],
        **ties,
    )


def transposed(left, right):
    return lax.dot_general(left, right, (((0,), (0,)), ((), ())), preferred_element_type=F32)


def grad_kernel(narrow_of, order_ref, wide_hbm, *refs):
    (*narrow_refs, kept_hbm, sent_hbm,
     wide_ref, kept_ref, sent_ref, wide_sems, out_sems) = refs
    copies = [
        pltpu.make_async_copy(wide_hbm.at[order_ref[i]], wide_ref.at[i], wide_sems.at[i])
        for i in range(8)
    ]
    for copy in copies:
        copy.start()
    narrow = narrow_of(*narrow_refs)
    out_copies = []
    for i, copy in enumerate(copies):
        copy.wait()
        total = transposed(narrow, wide_ref[i])
        if i < 4:
            sent_ref[i] = total.astype(BF16)
            pair = sent_ref.at[i], sent_hbm.at[i]
        else:
            kept_ref[i - 4] = total
            pair = kept_ref.at[i - 4], kept_hbm.at[i - 4]
        out_copies.append(pltpu.make_async_copy(*pair, out_sems.at[i]))
        out_copies[-1].start()
    for copy in out_copies:
        copy.wait()


def read_act(act_ref):
    return act_ref[...]


def make_dpre(pre_ref, dact_ref):
    pre = pre_ref[...]
    t = tanh_of(pre)
    slope = 0.5 * (1.0 + t) + (0.5 * ROOT_2_PI) * pre * (1.0 - t * t) * (
        1.0 + (3.0 * 0.044715) * (pre * pre)
    )
    return (dact_ref[...].astype(F32) * slope).astype(BF16)


def partial_grad(narrow_of, name, order, wide, *narrow, **ties):
    return launch(
        functools.partial(grad_kernel, narrow_of), name,
        [(order, SMEM), (wide, HBM)] + [(value, VMEM) for value in narrow],
        [(array((4, R, PIECE), F32), HBM), (array((4, R, PIECE), BF16), HBM)],
        [
            pltpu.VMEM((8, TOK, PIECE), BF16), pltpu.VMEM((4, R, PIECE), F32),
            pltpu.VMEM((4, R, PIECE), BF16), sems(8), sems(8),
        ],
        **ties,
    )


def halve_kernel(kept_ref, came_ref, keep_ref, send_ref):
    keep_ref[...] = kept_ref[:2] + came_ref[:2].astype(F32)
    send_ref[...] = (kept_ref[2:] + came_ref[2:].astype(F32)).astype(BF16)


def halve(kept, came, **ties):
    return launch(
        halve_kernel, "halve", [(kept, VMEM), (came, VMEM)],
        [(array((2, R, PIECE), F32), VMEM), (array((2, R, PIECE), BF16), VMEM)], grant=8, **ties,
    )


def split_kernel(kept_ref, came_ref, *out_refs):
    for half, out_ref in enumerate(out_refs):
        out_ref[...] = (kept_ref[half] + came_ref[half].astype(F32)).astype(BF16)


def split(kept, came, **ties):
    return launch(
        split_kernel, "split", [(kept, VMEM), (came, VMEM)],
        [(array((R, PIECE), BF16), VMEM)] * 2, grant=8, **ties,
    )


def finish_kernel(one_ref, two_ref, out_ref):
    out_ref[...] = (one_ref[...].astype(F32) + two_ref[...].astype(F32)).T


def finish(parts):
    return pl.pallas_call(
        finish_kernel,
        out_shape=array((PIECE, R), F32),
        in_specs=[VMEM] * 2,
        cost_estimate=pl.CostEstimate(flops=1, bytes_accessed=1, transcendentals=0),
        name="finish",
    )(*parts)


def feedback_kernel(
    first, count, x_hbm, own_hbm, act_ref, weight_hbm, *refs
):
    (out_hbm, done_ref, x_ref, own_ref, out_ref, weight_ref,
     x_sems, own_sems, out_sems, weight_sems) = refs[-10:]
    done_ref[...] = jnp.zeros_like(done_ref)
    weight_copies = []
    for part in range(8):
        at = pl.ds(part * PIECE, PIECE)
        weight_copies.append(
            pltpu.make_async_copy(weight_hbm.at[at], weight_ref.at[at], weight_sems.at[part])
        )
    copies = []
    for i in range(count // TILE):
        rows = pl.ds(i * TILE, TILE)
        copies.append((
            pltpu.make_async_copy(x_hbm.at[rows], x_ref.at[rows], x_sems.at[i]),
            pltpu.make_async_copy(own_hbm.at[rows], own_ref.at[rows], own_sems.at[i]),
        ))
    for copy in [*copies[0], *weight_copies, *(c for group in copies[1:] for c in group)]:
        copy.start()
    out_copies = []
    for i in range(count // TILE):
        for copy in copies[i]:
            copy.wait()
        rows = slice(i * TILE, (i + 1) * TILE)
        act = act_ref[first + i * TILE : first + (i + 1) * TILE, :]
        for part in range(8):
            at = slice(part * PIECE, (part + 1) * PIECE)
            if i == 0:
                weight_copies[part].wait()
            lifted = lax.dot_general(
                act, weight_ref[at, :], (((1,), (1,)), ((), ())), preferred_element_type=F32
            )
            value = x_ref[rows, at].astype(F32) + lifted - own_ref[rows, at].astype(F32)
            out_ref[rows, at] = value.astype(BF16)
        copy = pltpu.make_async_copy(
            out_ref.at[pl.ds(i * TILE, TILE)],
            out_hbm.at[pl.ds(first + i * TILE, TILE)],
            out_sems.at[i],
        )
        copy.start()
        out_copies.append(copy)
    for copy in out_copies:
        copy.wait()


def make_feedback(x, own, act, weight, first, before):
    count = x.shape[0]
    ins = [(x, HBM), (own, HBM), (act, VMEM), (weight, HBM)]
    if before is not None:
        ins.append((before, HBM))
    return launch(
        functools.partial(feedback_kernel, first, count), "feedback", ins,
        [(array((TOK, D), BF16), HBM), (array((8, 128), F32), VMEM)],
        [pltpu.VMEM((count, D), BF16)] * 3
        + [pltpu.VMEM((D, R), BF16)] + [sems(count // TILE)] * 3 + [sems(8)],
        aliases={} if before is None else {4: 0},
    )


def body(
    forward_codes,
    forward_scales,
    stored_base,
    sample_ids,
    backward_codes,
    backward_scales,
    norm_gain,
    w_down,
    w_up,
):
    sections = lax.axis_size("section")
    replicas = lax.axis_size("dp")
    across = replicas // 2
    both = ("section", "dp")

    def along(value, distance):
        pairs = [(s, (s + distance) % sections) for s in range(sections)]
        return lax.ppermute(value, "section", pairs)

    def among(value, flip_x, flip_y=0, section_step=0):
        pairs = []
        for s in range(sections):
            for d in range(replicas):
                y, x = divmod(d, across)
                source = (y ^ flip_y) * across + (x ^ flip_x)
                goal = ((s + section_step) % sections) * replicas + d
                pairs.append((s * replicas + source, goal))
        return lax.ppermute(value, both, pairs)

    replica = lax.axis_index("dp")
    x_at, y_at = replica % across, replica // across

    def order_of(flips):
        return jnp.stack(
            [((y_at ^ half) * across + (x_at ^ flip)) for flip in flips for half in range(2)]
        ).astype(jnp.int32)

    up = w_up[0]
    up_before = along(up, 1)
    down_next = along(w_down[0], -1)
    gain_next = along(norm_gain, -1)

    codes, base = forward_codes[0], stored_base[0]
    scales = forward_scales[0].T
    firsts = [sum(SPANS[:k]) for k in range(len(SPANS))]
    message0, stats0 = make_messages(codes, scales, base, sample_ids, 0, SPANS[:1])
    *later, stats1 = make_messages(
        codes, scales, base, sample_ids, SPANS[0], SPANS[1:], needs=[stats0]
    )
    messages = [message0, *later]
    gradient = make_gradient(backward_codes[0], backward_scales[0].T, needs=[stats1])

    pre_next, act_next, hidden = project_down(
        messages, [stats0, stats1], gain_next, down_next, needs=[up_before, gradient]
    )
    act_before = along(act_next, 2)
    act_own = along(act_next, 1)
    arrived0 = along(messages[0], 1)
    dact_before = project_back(gradient, up_before, needs=[act_next])[0]
    dact_next = along(dact_before, -2)

    def feedback_of(own, x, at, before):
        return make_feedback(x, own, act_own, up, firsts[at], before)

    up_kept, up_sent, message1, message2 = partial_grad(
        read_act, "grad_up", order_of((3, 2, 0, 1)), gradient, act_before,
        needs=[act_own, arrived0, dact_next], carried=messages[1:3],
    )
    arrived1 = along(message1, 1)
    arrived2 = along(message2, 1)
    down_kept, down_sent = partial_grad(
        make_dpre, "grad_down", order_of((1, 2, 0, 3)), hidden, pre_next, dact_next,
    )
    feedback, done = feedback_of(messages[0], arrived0, 0, None)
    up_kept, up_sent, message3 = halve(
        up_kept, among(up_sent, 3), needs=[arrived1, done], carried=messages[3:4]
    )
    arrived3 = along(message3, 1)
    down_kept, down_sent = halve(down_kept, among(down_sent, 1))
    feedback, done = feedback_of(message1, arrived1, 1, feedback)
    up_parts = split(up_kept, among(up_sent, 1), needs=[arrived2, done])
    down_parts = split(down_kept, among(down_sent, 3))
    grad_up = finish([among(up_parts[half], 0, half, -1) for half in range(2)])
    grad_down = finish([among(down_parts[half], 0, half, 1) for half in range(2)])
    feedback, _ = feedback_of(message2, arrived2, 2, feedback)
    feedback, _ = feedback_of(message3, arrived3, 3, feedback)
    return (feedback[None], grad_down[None], grad_up[None])


def solution(mesh):
    in_specs = (
        P("section", "dp", None),
        P("section", "dp", None),
        P("section", "dp", None),
        P("section", "dp"),
        P("section", "dp", None),
        P("section", "dp", None),
        P("section", None),
        P("section", None, None),
        P("section", None, None),
    )
    out_specs = (P("section", "dp", None), P("section", "dp", None), P("section", "dp", None))
    return jax.shard_map(body, mesh=mesh, in_specs=in_specs, out_specs=out_specs, check_vma=False)
```

time: 285 us -> 144 us (0.51)
  waiting for transfers between devices: 141 us -> 21.6 us
  Pallas kernels: 0 us -> 82.4 us
  local copies, waits for them, and re-layouts: 70.5 us -> 10.9 us
  other arithmetic: 32.8 us -> 0 us
  starting transfers between devices: 3.57 us -> 27.7 us
  matrix products: 21.6 us -> 0 us
  between operations: 14.1 us -> 0.89 us
    reduce_scatter x1 -> x0, waiting for transfers between devices: 101 us -> none  [body(): lax.psum_scatter(jnp.concatenate([transposed_product(hidden, dpre), trans...]
    pallas_call x0 -> x17, Pallas kernels: none -> 82.4 us  [the longest x15 78.5 us: launch(): pl.pallas_call(wrapped, in_specs=[where for _, where in ins] + [ANY] * (l...]
    shift_right_arithmetic x6 -> x0, local copies, waits for them, and re-layouts: 36.9 us -> none  [unpack_codes(): jnp.right_shift(packed[..., None], offsets_bits)]
    ppermute x2 -> x18, starting transfers between devices: 3.54 us -> 27.7 us  [the longest x10 14.9 us: along(): return lax.ppermute(value, 'section', pairs)]
    dot_general x4 -> x0, matrix products: 21.6 us -> none  [the longest x2 12.7 us: transposed_product(): lax.dot_general(left, right, (((0,), (0,)), ((), ())), preferred_element_...]
    convert_element_type x5 -> x0, other arithmetic: 19.8 us -> none  [the longest x1 11.2 us: build_message(): (picked.astype(jnp.float32) + scale_blocks(codes, scales)).astype(jnp.bfl...]
    ppermute x2 -> x18, waiting for transfers between devices: 40.7 us -> 21.6 us  [the longest x8 16.1 us: among(): return lax.ppermute(value, both, pairs)]
    mul x2 -> x0, local copies, waits for them, and re-layouts: 14 us -> none  [scale_blocks(): shaped * scales.astype(jnp.float32)[:, :, None]]
  transfers between devices with their start and end apart: 3 -> 18, of which waited for: 2 -> 5; matrix products, arithmetic and copies ran while one was open for 11% -> 1% of each run, Pallas kernels for 0% -> 52%
where the time goes in v3:
time: 144 us
  Pallas kernels  82.4 us (57%)
  starting transfers between devices  27.7 us (19%)
  waiting for transfers between devices  21.6 us (15%)
  local copies, waits for them, and re-layouts  10.9 us (8%)
    pallas_call x15, Pallas kernels, launch(): pl.pallas_call(wrapped, in_specs=[where for _, where in ins] + [ANY] * (l...  78.5 us
    ppermute x8, waiting for transfers between devices, among(): return lax.ppermute(value, both, pairs)  16.1 us
    ppermute x10, starting transfers between devices, along(): return lax.ppermute(value, 'section', pairs)  14.9 us
    ppermute x8, starting transfers between devices, among(): return lax.ppermute(value, both, pairs)  12.7 us
    unnamed x36, local copies, waits for them, and re-layouts  9.67 us
    ppermute x10, waiting for transfers between devices, along(): return lax.ppermute(value, 'section', pairs)  5.58 us
    pallas_call x2, Pallas kernels, finish(): pl.pallas_call(finish_kernel, out_shape=array((PIECE, R), F32), in_specs=...  3.87 us
  transfers between devices with their start and end apart: 18, of which 5 were waited for; matrix products, arithmetic and copies ran while one was open for 1% of the time, Pallas kernels for 52%

profile of v3, /device:TPU:1, one launch (start us, length us, event | category | flops | bytes accessed | tf_op | source)
XLA Modules:
  0.0 143.5 jit_solution(6612074530406280188)
XLA Ops:
  0.6 3.3 %collective-permute-start = (bf16[6144,128]{1,0:T(8,128)(2,1)}, bf16[6144,128]{1,0:T(8,128)(2,1)}, u32[]{:S(2)}, u32[]{:S(2)}) collective-permute-start(bf16[6144,128]{1,0:T(8,128)(2,1)} %bitcast.38), channel_id=1, source_target_pairs={{0,248},{8,0},{16,8},{24,16},{32,24},{40,32},{48,40},{56,48},{64,5... | collective-permute-start | bytes 4718600 | tf_op jit(solution)/shard_map/ppermute | solution.py:517
  4.0 4.8 %message.2 = (bf16[96,6144]{1,0:T(8,128)(2,1)}, f32[96,256]{1,0:T(8,128)}) custom-call(s32[384,2048]{1,0:T(8,128)} %bitcast.28, bf16[192,384]{1,0:T(8,128)(2,1)} %bitcast.33, bf16[32,6144]{1,0:T(8,128)(2,1)} %bitcast.31, s32[1,384]{1,0:T(1,128)} %refs_3_.3), custom_call_target="tpu_custom_call" | custom-call | flops 1 | bytes 1 | tf_op jit(solution)/shard_map/message/pallas_call | solution.py:43
  9.1 4.4 %collective-permute-start.1 = (f32[1,6144]{1,0:T(1,128)S(1)}, f32[1,6144]{1,0:T(1,128)S(1)}, u32[]{:S(2)}, u32[]{:S(2)}) collective-permute-start(f32[1,6144]{1,0:T(1,128)S(1)} %copy-done.17), channel_id=1, source_target_pairs={{0,248},{8,0},{16,8},{24,16},{32,24},{40,32},{48,40},{56,48},{64,5... | collective-permute-start | bytes 73736 | tf_op jit(solution)/shard_map/ppermute | solution.py:517
  13.5 10.7 %message.3 = (bf16[144,6144]{1,0:T(8,128)(2,1)}, bf16[96,6144]{1,0:T(8,128)(2,1)}, bf16[48,6144]{1,0:T(8,128)(2,1)}, f32[288,256]{1,0:T(8,128)}) custom-call(s32[384,2048]{1,0:T(8,128)} %bitcast.29, bf16[192,384]{1,0:T(8,128)(2,1)} %bitcast.34, bf16[32,6144]{1,0:T(8,128)(2,1)} %bitcast.32, s32[1,384]{1,0:T(1,128)} %refs_3_.3, ...), custom_call_target="tpu_custom_call" | custom-call | flops 1 | bytes 1 | tf_op jit(solution)/shard_map/message/pallas_call | solution.py:43
  24.2 7.5 %gradient.1.refs_9_.refs_0_.refs_1_ = bf16[8,384,768]{2,1,0:T(8,128)(2,1)} custom-call(bf16[384,6144]{1,0:T(8,128)(2,1)} %bitcast.30, bf16[192,384]{1,0:T(8,128)(2,1)} %bitcast.37, f32[288,256]{1,0:T(8,128)} %get-tuple-element.34.refs_2_.refs_7_), custom_call_target="tpu_custom_call" | custom-call | flops 1 | bytes 1 | tf_op jit(solution)/shard_map/gradient/pallas_call | solution.py:43
  32.3 8.5 %down.1 = (f32[384,128]{1,0:T(8,128)}, bf16[384,128]{1,0:T(8,128)(2,1)}, bf16[8,384,768]{2,1,0:T(8,128)(2,1)}) custom-call(bf16[6144,128]{1,0:T(8,128)(2,1)} %collective-permute-done.refs_0_, f32[1,6144]{1,0:T(1,128)} %copy-done.16, bf16[96,6144]{1,0:T(8,128)(2,1)} %get-tuple-element.35.refs_2_.refs_1_, bf16[144,6144]{1,0:T(8,128)(2,1)} %get-tuple-element.36.refs_3_.refs_6_, ...), custom_call_target="tpu_custom_call" | custom-call | flops 1 | bytes 1 | tf_op jit(solution)/shard_map/down/pallas_call | solution.py:43
  40.9 5.1 %back.1 = bf16[384,128]{1,0:T(8,128)(2,1)} custom-call(bf16[8,384,768]{2,1,0:T(8,128)(2,1)} %gradient.1.refs_9_.refs_0_.refs_1_, bf16[6144,128]{1,0:T(8,128)(2,1)} %collective-permute-done.2.refs_8_.refs_1_, bf16[384,128]{1,0:T(8,128)(2,1)} %get-tuple-element.39.refs_2_), custom_call_target="tpu_custom_call" | custom-call | flops 1 | bytes 1 | tf_op jit(solution)/shard_map/back/pallas_call | solution.py:43
  46.0 3.9 %collective-permute-start.6 = (bf16[384,128]{1,0:T(8,128)(2,1)}, bf16[384,128]{1,0:T(8,128)(2,1)S(1)}, u32[]{:S(2)}, u32[]{:S(2)}) collective-permute-start(bf16[384,128]{1,0:T(8,128)(2,1)} %back.1), channel_id=1, source_target_pairs={{0,240},{8,248},{16,0},{24,8},{32,16},{40,24},{48,32},{56,40},{64,... | collective-permute-start | bytes 294920 | tf_op jit(solution)/shard_map/ppermute | solution.py:517
  49.9 1.6 %collective-permute-start.4 = (bf16[384,128]{1,0:T(8,128)(2,1)S(1)}, bf16[384,128]{1,0:T(8,128)(2,1)S(1)}, u32[]{:S(2)}, u32[]{:S(2)}) collective-permute-start(bf16[384,128]{1,0:T(8,128)(2,1)S(1)} %copy-done.15), channel_id=1, source_target_pairs={{0,8},{8,16},{16,24},{24,32},{32,40},{40,48},{48,56},{56,64},{64,7... | collective-permute-start | bytes 294920 | tf_op jit(solution)/shard_map/ppermute | solution.py:517
  52.5 1.1 collective-permute-done.4.refs_3_.refs_2_
  53.6 4.2 %collective-permute-done.3.refs_2_ = bf16[384,128]{1,0:T(8,128)(2,1)S(1)} collective-permute-done((bf16[384,128]{1,0:T(8,128)(2,1)S(1)}, bf16[384,128]{1,0:T(8,128)(2,1)S(1)}, u32[]{:S(2)}, u32[]{:S(2)}) %collective-permute-start.3) | collective-permute-done | bytes 98336 | tf_op jit(solution)/shard_map/ppermute | solution.py:517
  58.4 5.3 %grad_up.1 = (f32[4,128,768]{2,1,0:T(8,128)}, bf16[4,128,768]{2,1,0:T(8,128)(2,1)}, bf16[144,6144]{1,0:T(8,128)(2,1)}, bf16[96,6144]{1,0:T(8,128)(2,1)}) custom-call(s32[8]{0:T(128)} %stack.46.refs_0_, bf16[8,384,768]{2,1,0:T(8,128)(2,1)} %gradient.1.refs_9_.refs_0_.refs_1_, ...), custom_call_target="tpu_custom_call", output_to_operand_aliasing={{2}: (6, {}), {3}: (7, {})} | custom-call | flops 1 | bytes 1 | tf_op jit(solution)/shard_map/grad_up/pallas_call | solution.py:43
  64.4 5.4 %grad_down.1 = (f32[4,128,768]{2,1,0:T(8,128)}, bf16[4,128,768]{2,1,0:T(8,128)(2,1)}) custom-call(s32[8]{0:T(128)} %stack.47.refs_0_, bf16[8,384,768]{2,1,0:T(8,128)(2,1)} %get-tuple-element.50.refs_1_, f32[384,128]{1,0:T(8,128)} %get-tuple-element.51.refs_2_, bf16[384,128]{1,0:T(8,128)(2,1)} %copy-done.11), custom_call_target="tpu_custom_call" | custom-call | flops 1 | bytes 1 | tf_op jit(solution)/shard_map/grad_down/pallas_call | solution.py:43
  69.8 1.3 collective-permute-start.11
  71.1 1.8 %collective-permute-start.7 = (bf16[4,128,768]{2,1,0:T(8,128)(2,1)}, bf16[4,128,768]{2,1,0:T(8,128)(2,1)}, u32[]{:S(2)}, u32[]{:S(2)}) collective-permute-start(bf16[4,128,768]{2,1,0:T(8,128)(2,1)} %get-tuple-element.41), channel_id=1, source_target_pairs={{3,0},{2,1},{1,2},{0,3},{7,4},{6,5},{5,6},{4,7},{11,8},{10,9},{9,1... | collective-permute-start | bytes 2359304 | tf_op jit(solution)/shard_map/ppermute | solution.py:527
  73.2 15.6 %collective-permute-done.11.refs_1_ = bf16[4,128,768]{2,1,0:T(8,128)(2,1)S(1)} collective-permute-done((bf16[4,128,768]{2,1,0:T(8,128)(2,1)}, bf16[4,128,768]{2,1,0:T(8,128)(2,1)S(1)}, u32[]{:S(2)}, u32[]{:S(2)}) %collective-permute-start.11) | collective-permute-done | bytes 786464 | tf_op jit(solution)/shard_map/ppermute | solution.py:527
  88.9 1.4 copy-done.2
  92.0 2.5 %collective-permute-start.12 = (bf16[2,128,768]{2,1,0:T(8,128)(2,1)}, bf16[2,128,768]{2,1,0:T(8,128)(2,1)}, u32[]{:S(2)}, u32[]{:S(2)}) collective-permute-start(bf16[2,128,768]{2,1,0:T(8,128)(2,1)} %get-tuple-element.55), channel_id=1, source_target_pairs={{3,0},{2,1},{1,2},{0,3},{7,4},{6,5},{5,6},{4,7},{11,8},{10,9},{9,1... | collective-permute-start | bytes 1179656 | tf_op jit(solution)/shard_map/ppermute | solution.py:527
  94.5 6.4 %feedback.4 = (bf16[384,6144]{1,0:T(8,128)(2,1)}, f32[8,128]{1,0:T(8,128)}) custom-call(bf16[96,6144]{1,0:T(8,128)(2,1)} %collective-permute-done.5.refs_4_.refs_0_, bf16[96,6144]{1,0:T(8,128)(2,1)} %get-tuple-element.35.refs_2_.refs_1_, bf16[384,128]{1,0:T(8,128)(2,1)} %copy-done.10, bf16[6144,128]{1,0:T(8,128)(2,1)} %bitcast.24), custom_call_target="tpu_custom_call" | custom-call | flops 1 | bytes 1 | tf_op jit(solution)/shard_map/feedback/pallas_call | solution.py:43
  101.0 1.4 copy-done.3
  103.1 2.1 %halve.2 = (f32[2,128,768]{2,1,0:T(8,128)S(1)}, bf16[2,128,768]{2,1,0:T(8,128)(2,1)}, bf16[48,6144]{1,0:T(8,128)(2,1)S(1)}) custom-call(f32[4,128,768]{2,1,0:T(8,128)S(1)} %copy-done.3, bf16[4,128,768]{2,1,0:T(8,128)(2,1)} %collective-permute-done.7.refs_1_, ...), custom_call_target="tpu_custom_call", output_to_operand_aliasing={{2}: (4, {})} | custom-call | flops 1 | bytes 1 | tf_op jit(solution)/shard_map/halve/pallas_call | solution.py:43
  105.1 0.9 copy-done.6
  106.0 1.0 collective-permute-start.9
  107.0 1.8 %split.2 = (bf16[128,768]{1,0:T(8,128)(2,1)}, bf16[128,768]{1,0:T(8,128)(2,1)}) custom-call(f32[2,128,768]{2,1,0:T(8,128)S(1)} %copy-done.5, bf16[2,128,768]{2,1,0:T(8,128)(2,1)} %collective-permute-done.12.refs_1_), custom_call_target="tpu_custom_call" | custom-call | flops 1 | bytes 1 | tf_op jit(solution)/shard_map/split/pallas_call | solution.py:43
  108.8 2.3 %collective-permute-start.14 = (bf16[128,768]{1,0:T(8,128)(2,1)}, bf16[128,768]{1,0:T(8,128)(2,1)}, u32[]{:S(2)}, u32[]{:S(2)}) collective-permute-start(bf16[128,768]{1,0:T(8,128)(2,1)} %get-tuple-element.57), channel_id=1, source_target_pairs={{4,8},{5,9},{6,10},{7,11},{0,12},{1,13},{2,14},{3,15},{12,16},{13,... | collective-permute-start | bytes 589832 | tf_op jit(solution)/shard_map/ppermute | solution.py:527
  111.1 7.0 %feedback.5 = (bf16[384,6144]{1,0:T(8,128)(2,1)}, f32[8,128]{1,0:T(8,128)}) custom-call(bf16[144,6144]{1,0:T(8,128)(2,1)} %collective-permute-done.8.refs_2_.refs_0_, bf16[144,6144]{1,0:T(8,128)(2,1)} %get-tuple-element.42.refs_1_, bf16[384,128]{1,0:T(8,128)(2,1)} %copy-done.10, bf16[6144,128]{1,0:T(8,128)(2,1)} %bitcast.25, ...), custom_call_target="tpu_custom_call", output_to_operand_aliasing={{0}: (4, {})} | custom-call | flops 1 | bytes 1 | tf_op jit(solution)/shard_map/feedback/pallas_call | solution.py:43
  118.2 1.1 copy-done.7
  121.5 4.1 %collective-permute-start.17 = (bf16[128,768]{1,0:T(8,128)(2,1)}, bf16[128,768]{1,0:T(8,128)(2,1)S(1)}, u32[]{:S(2)}, u32[]{:S(2)}) collective-permute-start(bf16[128,768]{1,0:T(8,128)(2,1)} %get-tuple-element.62), channel_id=1, source_target_pairs={{4,248},{5,249},{6,250},{7,251},{0,252},{1,253},{2,254},{3,255},{1... | collective-permute-start | bytes 589832 | tf_op jit(solution)/shard_map/ppermute | solution.py:527
  126.1 1.9 %finish.2 = f32[768,128]{1,0:T(8,128)} custom-call(bf16[128,768]{1,0:T(8,128)(2,1)} %collective-permute-done.13.one_ref, bf16[128,768]{1,0:T(8,128)(2,1)} %collective-permute-done.14.two_ref), custom_call_target="tpu_custom_call" | custom-call | flops 1 | bytes 1 | tf_op jit(solution)/shard_map/finish/pallas_call | solution.py:429
  128.0 6.4 %feedback.6 = (bf16[384,6144]{1,0:T(8,128)(2,1)}, f32[8,128]{1,0:T(8,128)}) custom-call(bf16[96,6144]{1,0:T(8,128)(2,1)} %collective-permute-done.10.refs_0_.refs_2_, bf16[96,6144]{1,0:T(8,128)(2,1)} %get-tuple-element.45.refs_1_, bf16[384,128]{1,0:T(8,128)(2,1)} %copy-done.10, bf16[6144,128]{1,0:T(8,128)(2,1)} %bitcast.26, ...), custom_call_target="tpu_custom_call", output_to_operand_aliasing={{0}: (4, {})} | custom-call | flops 1 | bytes 1 | tf_op jit(solution)/shard_map/feedback/pallas_call | solution.py:43
  134.4 5.8 %feedback.7 = (bf16[384,6144]{1,0:T(8,128)(2,1)}, f32[8,128]{1,0:T(8,128)}) custom-call(bf16[48,6144]{1,0:T(8,128)(2,1)} %collective-permute-done.9.refs_0_, bf16[48,6144]{1,0:T(8,128)(2,1)} %copy-done.1, bf16[384,128]{1,0:T(8,128)(2,1)} %copy-done.10, bf16[6144,128]{1,0:T(8,128)(2,1)} %bitcast.27, ...), custom_call_target="tpu_custom_call", output_to_operand_aliasing={{0}: (4, {})} | custom-call | flops 1 | bytes 1 | tf_op jit(solution)/shard_map/feedback/pallas_call | solution.py:43
  141.6 1.9 %finish.3 = f32[768,128]{1,0:T(8,128)} custom-call(bf16[128,768]{1,0:T(8,128)(2,1)} %copy-done.12, bf16[128,768]{1,0:T(8,128)(2,1)} %copy-done.13), custom_call_target="tpu_custom_call" | custom-call | flops 1 | bytes 1 | tf_op jit(solution)/shard_map/finish/pallas_call | solution.py:429
  (59 shorter events, 9.9 us)
Async XLA Ops:
  0.6 31.1 %collective-permute-start = (bf16[6144,128]{1,0:T(8,128)(2,1)}, bf16[6144,128]{1,0:T(8,128)(2,1)}, u32[]{:S(2)}, u32[]{:S(2)}) collective-permute-start(bf16[6144,128]{1,0:T(8,128)(2,1)} %bitcast.38), channel_id=1, source_target_pairs={{0,248},{8,0},{16,8},{24,16},{32,24},{40,32},{48,40},{56,48},{64,5... | collective-permute-start | bytes 4718600 | tf_op jit(solution)/shard_map/ppermute | solution.py:517
  3.9 27.8 %collective-permute-start.2 = (bf16[6144,128]{1,0:T(8,128)(2,1)}, bf16[6144,128]{1,0:T(8,128)(2,1)}, u32[]{:S(2)}, u32[]{:S(2)}) collective-permute-start(bf16[6144,128]{1,0:T(8,128)(2,1)} %bitcast.23), channel_id=1, source_target_pairs={{0,8},{8,16},{16,24},{24,32},{32,40},{40,48},{48,56},{56,64},{64,7... | collective-permute-start | bytes 4718600 | tf_op jit(solution)/shard_map/ppermute | solution.py:517
  4.0 5.2 %copy-start.17 = (f32[1,6144]{1,0:T(1,128)S(1)}, f32[1,6144]{1,0:T(1,128)}, u32[]{:S(2)}) copy-start(f32[1,6144]{1,0:T(1,128)} %param.15) | copy-start | bytes 73732
  8.7 43.5 %collective-permute-start.5 = (bf16[96,6144]{1,0:T(8,128)(2,1)}, bf16[96,6144]{1,0:T(8,128)(2,1)}, u32[]{:S(2)}, u32[]{:S(2)}) collective-permute-start(bf16[96,6144]{1,0:T(8,128)(2,1)} %get-tuple-element.35.refs_2_.refs_1_), channel_id=1, source_target_pairs={{0,8},{8,16},{16,24},{24,32},{32,40},{40,48},{48,56},{56,64},{64,7... | collective-permute-start | bytes 3538952 | tf_op jit(solution)/shard_map/ppermute | solution.py:517
  9.1 22.6 %collective-permute-start.1 = (f32[1,6144]{1,0:T(1,128)S(1)}, f32[1,6144]{1,0:T(1,128)S(1)}, u32[]{:S(2)}, u32[]{:S(2)}) collective-permute-start(f32[1,6144]{1,0:T(1,128)S(1)} %copy-done.17), channel_id=1, source_target_pairs={{0,248},{8,0},{16,8},{24,16},{32,24},{40,32},{48,40},{56,48},{64,5... | collective-permute-start | bytes 73736 | tf_op jit(solution)/shard_map/ppermute | solution.py:517
  40.8 9.1 %copy-start.15 = (bf16[384,128]{1,0:T(8,128)(2,1)S(1)}, bf16[384,128]{1,0:T(8,128)(2,1)}, u32[]{:S(2)}) copy-start(bf16[384,128]{1,0:T(8,128)(2,1)} %get-tuple-element.39.refs_2_) | copy-start | bytes 294916
  46.0 6.5 %collective-permute-start.6 = (bf16[384,128]{1,0:T(8,128)(2,1)}, bf16[384,128]{1,0:T(8,128)(2,1)S(1)}, u32[]{:S(2)}, u32[]{:S(2)}) collective-permute-start(bf16[384,128]{1,0:T(8,128)(2,1)} %back.1), channel_id=1, source_target_pairs={{0,240},{8,248},{16,0},{24,8},{32,16},{40,24},{48,32},{56,40},{64,... | collective-permute-start | bytes 294920 | tf_op jit(solution)/shard_map/ppermute | solution.py:517
  49.9 3.7 %collective-permute-start.4 = (bf16[384,128]{1,0:T(8,128)(2,1)S(1)}, bf16[384,128]{1,0:T(8,128)(2,1)S(1)}, u32[]{:S(2)}, u32[]{:S(2)}) collective-permute-start(bf16[384,128]{1,0:T(8,128)(2,1)S(1)} %copy-done.15), channel_id=1, source_target_pairs={{0,8},{8,16},{16,24},{24,32},{32,40},{40,48},{48,56},{56,64},{64,7... | collective-permute-start | bytes 294920 | tf_op jit(solution)/shard_map/ppermute | solution.py:517
  51.5 6.2 %collective-permute-start.3 = (bf16[384,128]{1,0:T(8,128)(2,1)S(1)}, bf16[384,128]{1,0:T(8,128)(2,1)S(1)}, u32[]{:S(2)}, u32[]{:S(2)}) collective-permute-start(bf16[384,128]{1,0:T(8,128)(2,1)S(1)} %copy-done.15), channel_id=1, source_target_pairs={{0,16},{8,24},{16,32},{24,40},{32,48},{40,56},{48,64},{56,72},{64,... | collective-permute-start | bytes 294920 | tf_op jit(solution)/shard_map/ppermute | solution.py:517
  52.5 5.3 %copy-start.11 = (bf16[384,128]{1,0:T(8,128)(2,1)}, bf16[384,128]{1,0:T(8,128)(2,1)S(1)}, u32[]{:S(2)}) copy-start(bf16[384,128]{1,0:T(8,128)(2,1)S(1)} %collective-permute-done.6.refs_5_.refs_3_) | copy-start | bytes 294916
  53.6 4.2 %copy-start.10 = (bf16[384,128]{1,0:T(8,128)(2,1)}, bf16[384,128]{1,0:T(8,128)(2,1)S(1)}, u32[]{:S(2)}) copy-start(bf16[384,128]{1,0:T(8,128)(2,1)S(1)} %collective-permute-done.4.refs_3_.refs_2_) | copy-start | bytes 294916
  63.7 37.2 %collective-permute-start.8 = (bf16[144,6144]{1,0:T(8,128)(2,1)}, bf16[144,6144]{1,0:T(8,128)(2,1)}, u32[]{:S(2)}, u32[]{:S(2)}) collective-permute-start(bf16[144,6144]{1,0:T(8,128)(2,1)} %get-tuple-element.42.refs_1_), channel_id=1, source_target_pairs={{0,8},{8,16},{16,24},{24,32},{32,40},{40,48},{48,56},{56,64},{64,7... | collective-permute-start | bytes 5308424 | tf_op jit(solution)/shard_map/ppermute | solution.py:517
  69.8 19.0 %collective-permute-start.11 = (bf16[4,128,768]{2,1,0:T(8,128)(2,1)}, bf16[4,128,768]{2,1,0:T(8,128)(2,1)S(1)}, u32[]{:S(2)}, u32[]{:S(2)}) collective-permute-start(bf16[4,128,768]{2,1,0:T(8,128)(2,1)} %get-tuple-element.53), channel_id=1, source_target_pairs={{1,0},{0,1},{3,2},{2,3},{5,4},{4,5},{7,6},{6,7},{9,8},{8,9},{11,10... | collective-permute-start | bytes 2359304 | tf_op jit(solution)/shard_map/ppermute | solution.py:527
  71.1 29.8 %collective-permute-start.7 = (bf16[4,128,768]{2,1,0:T(8,128)(2,1)}, bf16[4,128,768]{2,1,0:T(8,128)(2,1)}, u32[]{:S(2)}, u32[]{:S(2)}) collective-permute-start(bf16[4,128,768]{2,1,0:T(8,128)(2,1)} %get-tuple-element.41), channel_id=1, source_target_pairs={{3,0},{2,1},{1,2},{0,3},{7,4},{6,5},{5,6},{4,7},{11,8},{10,9},{9,1... | collective-permute-start | bytes 2359304 | tf_op jit(solution)/shard_map/ppermute | solution.py:527
  73.0 45.2 %collective-permute-start.10 = (bf16[96,6144]{1,0:T(8,128)(2,1)}, bf16[96,6144]{1,0:T(8,128)(2,1)}, u32[]{:S(2)}, u32[]{:S(2)}) collective-permute-start(bf16[96,6144]{1,0:T(8,128)(2,1)} %get-tuple-element.45.refs_1_), channel_id=1, source_target_pairs={{0,8},{8,16},{16,24},{24,32},{32,40},{40,48},{48,56},{56,64},{64,7... | collective-permute-start | bytes 3538952 | tf_op jit(solution)/shard_map/ppermute | solution.py:517
  88.9 1.4 copy-start.2
  91.1 0.9 copy-start.4
  92.0 8.9 %copy-start = (bf16[48,6144]{1,0:T(8,128)(2,1)S(1)}, bf16[48,6144]{1,0:T(8,128)(2,1)}, u32[]{:S(2)}) copy-start(bf16[48,6144]{1,0:T(8,128)(2,1)} %get-tuple-element.38.refs_5_.refs_4_) | copy-start | bytes 1769476
  92.0 15.0 %collective-permute-start.12 = (bf16[2,128,768]{2,1,0:T(8,128)(2,1)}, bf16[2,128,768]{2,1,0:T(8,128)(2,1)}, u32[]{:S(2)}, u32[]{:S(2)}) collective-permute-start(bf16[2,128,768]{2,1,0:T(8,128)(2,1)} %get-tuple-element.55), channel_id=1, source_target_pairs={{3,0},{2,1},{1,2},{0,3},{7,4},{6,5},{5,6},{4,7},{11,8},{10,9},{9,1... | collective-permute-start | bytes 1179656 | tf_op jit(solution)/shard_map/ppermute | solution.py:527
  101.0 1.4 copy-start.3
  102.4 0.7 copy-start.9
  103.1 3.9 %copy-start.5 = (f32[2,128,768]{2,1,0:T(8,128)S(1)}, f32[2,128,768]{2,1,0:T(8,128)}, u32[]{:S(2)}) copy-start(f32[2,128,768]{2,1,0:T(8,128)} %copy-done.4) | copy-start | bytes 2359300
  105.1 0.9 copy-start.6
  106.0 12.2 %copy-start.1 = (bf16[48,6144]{1,0:T(8,128)(2,1)}, bf16[48,6144]{1,0:T(8,128)(2,1)S(1)}, u32[]{:S(2)}) copy-start(bf16[48,6144]{1,0:T(8,128)(2,1)S(1)} %get-tuple-element.44.refs_1_) | copy-start | bytes 1769476
  106.0 12.2 %collective-permute-start.15 = (bf16[2,128,768]{2,1,0:T(8,128)(2,1)}, bf16[2,128,768]{2,1,0:T(8,128)(2,1)S(1)}, u32[]{:S(2)}, u32[]{:S(2)}) collective-permute-start(bf16[2,128,768]{2,1,0:T(8,128)(2,1)} %get-tuple-element.59), channel_id=1, source_target_pairs={{1,0},{0,1},{3,2},{2,3},{5,4},{4,5},{7,6},{6,7},{9,8},{8,9},{11,10... | collective-permute-start | bytes 1179656 | tf_op jit(solution)/shard_map/ppermute | solution.py:527
  106.0 28.4 %collective-permute-start.9 = (bf16[48,6144]{1,0:T(8,128)(2,1)S(1)}, bf16[48,6144]{1,0:T(8,128)(2,1)}, u32[]{:S(2)}, u32[]{:S(2)}) collective-permute-start(bf16[48,6144]{1,0:T(8,128)(2,1)S(1)} %get-tuple-element.44.refs_1_), channel_id=1, source_target_pairs={{0,8},{8,16},{16,24},{24,32},{32,40},{40,48},{48,56},{56,64},{64,7... | collective-permute-start | bytes 1769480 | tf_op jit(solution)/shard_map/ppermute | solution.py:517
  108.8 16.8 %collective-permute-start.13 = (bf16[128,768]{1,0:T(8,128)(2,1)}, bf16[128,768]{1,0:T(8,128)(2,1)}, u32[]{:S(2)}, u32[]{:S(2)}) collective-permute-start(bf16[128,768]{1,0:T(8,128)(2,1)} %get-tuple-element.56), channel_id=1, source_target_pairs={{0,8},{1,9},{2,10},{3,11},{4,12},{5,13},{6,14},{7,15},{8,16},{9,17... | collective-permute-start | bytes 589832 | tf_op jit(solution)/shard_map/ppermute | solution.py:527
  108.8 17.3 %collective-permute-start.14 = (bf16[128,768]{1,0:T(8,128)(2,1)}, bf16[128,768]{1,0:T(8,128)(2,1)}, u32[]{:S(2)}, u32[]{:S(2)}) collective-permute-start(bf16[128,768]{1,0:T(8,128)(2,1)} %get-tuple-element.57), channel_id=1, source_target_pairs={{4,8},{5,9},{6,10},{7,11},{0,12},{1,13},{2,14},{3,15},{12,16},{13,... | collective-permute-start | bytes 589832 | tf_op jit(solution)/shard_map/ppermute | solution.py:527
  118.2 1.1 copy-start.7
  119.4 0.7 copy-start.8
  120.8 19.4 %collective-permute-start.16 = (bf16[128,768]{1,0:T(8,128)(2,1)}, bf16[128,768]{1,0:T(8,128)(2,1)S(1)}, u32[]{:S(2)}, u32[]{:S(2)}) collective-permute-start(bf16[128,768]{1,0:T(8,128)(2,1)} %get-tuple-element.61), channel_id=1, source_target_pairs={{0,248},{1,249},{2,250},{3,251},{4,252},{5,253},{6,254},{7,255},{8... | collective-permute-start | bytes 589832 | tf_op jit(solution)/shard_map/ppermute | solution.py:527
  121.5 18.7 %collective-permute-start.17 = (bf16[128,768]{1,0:T(8,128)(2,1)}, bf16[128,768]{1,0:T(8,128)(2,1)S(1)}, u32[]{:S(2)}, u32[]{:S(2)}) collective-permute-start(bf16[128,768]{1,0:T(8,128)(2,1)} %get-tuple-element.62), channel_id=1, source_target_pairs={{4,248},{5,249},{6,250},{7,251},{0,252},{1,253},{2,254},{3,255},{1... | collective-permute-start | bytes 589832 | tf_op jit(solution)/shard_map/ppermute | solution.py:527
  (4 other events, 2.6 us)

commit v4 on v0

v4 whole, which is shorter than its diff:
```python
import functools
import math

import jax
import jax.numpy as jnp
from jax import lax
from jax.experimental import pallas as pl
from jax.experimental.pallas import tpu as pltpu
from jax.sharding import PartitionSpec as P

D = 6144
R = 128
TOK = 384
PIECE = D // 8
F32 = jnp.float32
BF16 = jnp.bfloat16
TILE = 48
SPANS = (96, 144, 96, 48)
MIB = 1 << 20
ROOT_2_PI = math.sqrt(2.0 / math.pi)
VMEM = pl.BlockSpec(memory_space=pltpu.VMEM)
ANY = pl.BlockSpec(memory_space=pl.ANY)


def array(shape, dtype):
    return jax.ShapeDtypeStruct(shape, dtype)


def launch(
    kernel, name, ins, outs, scratch=(), grid=(), aliases=None, needs=(), carried=(), grant=14
):
    n_in, n_out = len(ins), len(outs)
    first_carried = n_in + len(needs)
    n_all = first_carried + len(carried)
    aliases = dict(aliases or {})
    for k in range(len(carried)):
        aliases[first_carried + k] = n_out + k

    def wrapped(*refs):
        rest = refs[n_all + n_out + len(carried) :]
        kernel(*refs[:n_in], *refs[n_all : n_all + n_out], *rest)

    return pl.pallas_call(
        wrapped,
        grid=grid,
        in_specs=[spec for _, spec in ins] + [ANY] * (len(needs) + len(carried)),
        out_specs=[spec for _, spec in outs] + [ANY] * len(carried),
        out_shape=[out for out, _ in outs] + [array(c.shape, c.dtype) for c in carried],
        scratch_shapes=scratch,
        input_output_aliases=aliases,
        compiler_params=pltpu.CompilerParams(vmem_limit_bytes=grant * MIB),
        cost_estimate=pl.CostEstimate(flops=1, bytes_accessed=1, transcendentals=0),
        name=name,
    )(*[value for value, _ in ins], *needs, *carried)


def rows_of(width, skip=0):
    return pl.BlockSpec((TILE, width), lambda i: (i + skip, 0))


def rows_between(start, end, width):
    return pl.BlockSpec((TILE, width), lambda i: (jnp.clip(i - start, 0, end - start - 1), 0))


def whole(*shape):
    return pl.BlockSpec(shape, lambda i: (0,) * len(shape))


def lanes(shape):
    return lax.broadcasted_iota(jnp.int32, shape, 1)


def spread_scales(scales_ref, rows, tile):
    half, at = divmod(tile, 32)
    part = scales_ref[rows, half * 128 : half * 128 + 128]
    return jnp.take_along_axis(part, lanes((TILE, 128)) // 32 + 4 * at, axis=1)


def turn_scales(scales_ref, turned_ref):
    turned_ref[:, : D // 32] = scales_ref[...].astype(F32).T


def tile_at(i):
    return pl.ds(pl.multiple_of(i * TILE, 16), TILE)


def message_kernel(first, bounds, codes_ref, scales_ref, base_ref, ids_ref, *refs):
    *out_refs, turned_ref, picks_ref = refs
    step = pl.program_id(0)

    @pl.when(step == 0)
    def _():
        turn_scales(scales_ref, turned_ref)
        hits = lax.broadcasted_iota(jnp.int32, (32, TOK), 0) == ids_ref[...]
        picks_ref[...] = hits.astype(F32).T.astype(BF16)

    def fill(out_ref):
        rows = tile_at(step + first // TILE)
        picks = picks_ref[rows, :]
        lane = lanes((TILE, 128))
        for block in range(16):
            words = codes_ref[:, block * 128 : (block + 1) * 128]
            base = jnp.dot(
                picks, base_ref[:, block * 384 : (block + 1) * 384], preferred_element_type=F32
            )
            for j in range(3):
                spot = lane + 128 * j
                word = jnp.take_along_axis(words, spot // 3, axis=1)
                code = jnp.right_shift(word, (spot % 3) * 4) & 15
                tile = block * 3 + j
                scale = spread_scales(turned_ref, rows, tile)
                value = base[:, j * 128 : (j + 1) * 128] + scale * (code - 8).astype(F32)
                out_ref[:, tile * 128 : (tile + 1) * 128] = value.astype(BF16)

    if len(out_refs) == 1:
        fill(out_refs[0])
        return
    for out_ref, (start, end) in zip(out_refs, bounds):

        @pl.when((step >= start) & (step < end))
        def _(out_ref=out_ref):
            fill(out_ref)


def make_messages(codes, scales, base, ids, first, spans, **ties):
    ends = [sum(spans[: k + 1]) // TILE for k in range(len(spans))]
    bounds = list(zip([0, *ends], ends))
    return launch(
        functools.partial(message_kernel, first, bounds), "message",
        [
            (codes, rows_of(D // 3, first // TILE)), (scales, whole(D // 32, TOK)),
            (base, whole(32, D)), (ids, whole(1, TOK)),
        ],
        [
            (array((span, D), BF16), rows_between(start, end, D))
            for span, (start, end) in zip(spans, bounds)
        ],
        [pltpu.VMEM((TOK, 256), F32), pltpu.VMEM((TOK, 32), BF16)],
        grid=(ends[-1],), **ties,
    )


def gradient_kernel(codes_ref, scales_ref, out_ref, turned_ref):
    step = pl.program_id(0)

    @pl.when(step == 0)
    def _():
        turn_scales(scales_ref, turned_ref)

    for tile in range(48):
        part = slice(tile * 128, (tile + 1) * 128)
        scale = spread_scales(turned_ref, tile_at(step), tile)
        out_ref[:, part] = (scale * (codes_ref[:, part].astype(F32) - 128.0)).astype(BF16)


def make_gradient(codes, scales, **ties):
    return launch(
        gradient_kernel, "gradient",
        [(codes, rows_of(D)), (scales, whole(D // 32, TOK))],
        [(array((TOK, D), BF16), rows_of(D))], [pltpu.VMEM((TOK, 256), F32)],
        grid=(TOK // TILE,), **ties,
    )[0]


def hidden_kernel(bounds, gain_ref, *refs):
    *message_refs, out_ref = refs
    step = pl.program_id(0)
    for message_ref, (start, end) in zip(message_refs, bounds):

        @pl.when((step >= start) & (step < end))
        def _(message_ref=message_ref):
            x = message_ref[...].astype(F32)
            center = x - jnp.sum(x, axis=1, keepdims=True) * (1.0 / D)
            variance = jnp.sum(center * center, axis=1, keepdims=True) * (1.0 / D)
            out_ref[...] = (gain_ref[...] * center * lax.rsqrt(variance + 1e-05)).astype(BF16)


def make_hidden(messages, gain, **ties):
    ends = [sum(m.shape[0] for m in messages[: k + 1]) // TILE for k in range(len(messages))]
    bounds = list(zip([0, *ends], ends))
    return launch(
        functools.partial(hidden_kernel, bounds), "hidden",
        [(gain, whole(1, D))]
        + [(m, rows_between(start, end, D)) for m, (start, end) in zip(messages, bounds)],
        [(array((TOK, D), BF16), rows_of(D))], grid=(TOK // TILE,), **ties,
    )[0]


def tanh_of(pre):
    return jnp.tanh(ROOT_2_PI * (pre + 0.044715 * (pre * pre * pre)))


def down_kernel(hidden_ref, weight_ref, pre_ref, act_ref):
    pre = jnp.dot(hidden_ref[...], weight_ref[...], preferred_element_type=F32)
    pre_ref[...] = pre
    act_ref[...] = (0.5 * pre * (1.0 + tanh_of(pre))).astype(BF16)


def project_down(hidden, weight, **ties):
    return launch(
        down_kernel, "down", [(hidden, VMEM), (weight, VMEM)],
        [(array((TOK, R), F32), VMEM), (array((TOK, R), BF16), VMEM)], **ties,
    )


def back_kernel(grad_ref, weight_ref, out_ref):
    out_ref[...] = jnp.dot(
        grad_ref[...], weight_ref[...], preferred_element_type=F32
    ).astype(BF16)


def project_back(grad, weight, **ties):
    return launch(
        back_kernel, "back", [(grad, VMEM), (weight, VMEM)],
        [(array((TOK, R), BF16), VMEM)], **ties,
    )


def transposed(left, right):
    return lax.dot_general(left, right, (((0,), (0,)), ((), ())), preferred_element_type=F32)


def grad_kernel(narrow_of, flips, wide_ref, *refs):
    *narrow_refs, kept_ref, sent_ref = refs
    narrow = narrow_of(*narrow_refs)
    replica = lax.axis_index("dp")
    x_at, y_at = lax.rem(replica, 4), lax.div(replica, 4)
    for i, flip in enumerate(flips):
        for half in range(2):
            piece = (y_at ^ half) * 4 + (x_at ^ flip)
            columns = pl.ds(pl.multiple_of(piece * PIECE, 128), PIECE)
            total = transposed(narrow, wide_ref[:, columns])
            if i < 2:
                kept_ref[2 * i + half] = total
            else:
                sent_ref[2 * i - 4 + half] = total.astype(BF16)


def read_act(act_ref):
    return act_ref[...]


def make_dpre(pre_ref, dact_ref):
    pre = pre_ref[...]
    t = tanh_of(pre)
    slope = 0.5 * (1.0 + t) + (0.5 * ROOT_2_PI) * pre * (1.0 - t * t) * (
        1.0 + (3.0 * 0.044715) * (pre * pre)
    )
    return (dact_ref[...].astype(F32) * slope).astype(BF16)


def partial_grad(narrow_of, name, flips, wide, *narrow, **ties):
    return launch(
        functools.partial(grad_kernel, narrow_of, flips), name,
        [(value, VMEM) for value in (wide, *narrow)],
        [(array((4, R, PIECE), F32), VMEM), (array((4, R, PIECE), BF16), VMEM)], **ties,
    )


def halve_kernel(kept_ref, came_ref, keep_ref, send_ref):
    keep_ref[...] = kept_ref[:2] + came_ref[:2].astype(F32)
    send_ref[...] = (kept_ref[2:] + came_ref[2:].astype(F32)).astype(BF16)


def halve(kept, came, **ties):
    return launch(
        halve_kernel, "halve", [(kept, VMEM), (came, VMEM)],
        [(array((2, R, PIECE), F32), VMEM), (array((2, R, PIECE), BF16), VMEM)], **ties,
    )


def split_kernel(kept_ref, came_ref, *out_refs):
    for half, out_ref in enumerate(out_refs):
        out_ref[...] = (kept_ref[half] + came_ref[half].astype(F32)).astype(BF16)


def split(kept, came, **ties):
    return launch(
        split_kernel, "split", [(kept, VMEM), (came, VMEM)],
        [(array((R, PIECE), BF16), VMEM)] * 2, **ties,
    )


def finish_kernel(one_ref, two_ref, out_ref):
    out_ref[...] = (one_ref[...].astype(F32) + two_ref[...].astype(F32)).T


def finish(parts):
    return launch(
        finish_kernel, "finish", [(part, VMEM) for part in parts],
        [(array((PIECE, R), F32), pl.BlockSpec((PIECE, R)))],
    )[0]


def feedback_kernel(first, count, before, x_ref, own_ref, act_ref, weight_ref, *refs):
    *rest, out_ref, out_sems = refs
    if before:
        rest = rest[1:]
    out_hbm = rest[0]
    for done_ref in rest[1:]:
        done_ref[...] = jnp.zeros_like(done_ref)
    copies = []
    for i in range(count // TILE):
        rows = slice(i * TILE, (i + 1) * TILE)
        act = act_ref[first + i * TILE : first + (i + 1) * TILE, :]
        for part in range(4):
            at = slice(part * 2 * PIECE, (part + 1) * 2 * PIECE)
            lifted = lax.dot_general(
                act, weight_ref[at, :], (((1,), (1,)), ((), ())), preferred_element_type=F32
            )
            value = x_ref[rows, at].astype(F32) + lifted - own_ref[rows, at].astype(F32)
            out_ref[rows, at] = value.astype(BF16)
        copies.append(
            pltpu.make_async_copy(
                out_ref.at[pl.ds(i * TILE, TILE)],
                out_hbm.at[pl.ds(first + i * TILE, TILE)],
                out_sems.at[i],
            )
        )
        copies[-1].start()
    for copy in copies:
        copy.wait()


def make_feedback(x, own, act, weight, first, before, marked):
    count = x.shape[0]
    ins = [(x, VMEM), (own, VMEM), (act, VMEM), (weight, VMEM)]
    if before is not None:
        ins.append((before, ANY))
    return launch(
        functools.partial(feedback_kernel, first, count, before is not None), "feedback", ins,
        [(array((TOK, D), BF16), ANY)] + [(array((8, 128), F32), VMEM)] * marked,
        [pltpu.VMEM((count, D), BF16), pltpu.SemaphoreType.DMA((count // TILE,))],
        aliases={} if before is None else {4: 0},
    )


def body(
    forward_codes,
    forward_scales,
    stored_base,
    sample_ids,
    backward_codes,
    backward_scales,
    norm_gain,
    w_down,
    w_up,
):
    sections = lax.axis_size("section")
    replicas = lax.axis_size("dp")
    across = replicas // 2
    both = ("section", "dp")

    def along(value, distance):
        pairs = [(s, (s + distance) % sections) for s in range(sections)]
        return lax.ppermute(value, "section", pairs)

    def among(value, flip_x, flip_y=0, section_step=0):
        pairs = []
        for s in range(sections):
            for d in range(replicas):
                y, x = divmod(d, across)
                source = (y ^ flip_y) * across + (x ^ flip_x)
                goal = ((s + section_step) % sections) * replicas + d
                pairs.append((s * replicas + source, goal))
        return lax.ppermute(value, both, pairs)

    up = w_up[0]
    up_before = along(up, 1)
    down_next = along(w_down[0], -1)
    gain_next = along(norm_gain, -1)

    codes, base = forward_codes[0], stored_base[0]
    scales = forward_scales[0].T
    firsts = [sum(SPANS[:k]) for k in range(len(SPANS))]
    message0 = make_messages(codes, scales, base, sample_ids, 0, SPANS[:1])[0]
    later = make_messages(codes, scales, base, sample_ids, SPANS[0], SPANS[1:], needs=[message0])
    messages = [message0, *later]
    gradient = make_gradient(backward_codes[0], backward_scales[0].T, needs=[later[0]])
    hidden = make_hidden(messages, gain_next, needs=[gradient])

    pre_next, act_next = project_down(hidden, down_next, needs=[up_before])
    act_before = along(act_next, 2)
    act_own = along(act_next, 1)
    arrived0 = along(messages[0], 1)
    dact_before = project_back(gradient, up_before, needs=[act_next])[0]
    dact_next = along(dact_before, -2)

    def feedback_of(own, x, at, before, marked=False):
        return make_feedback(x, own, act_own, up, firsts[at], before, marked)

    up_kept, up_sent, message1, message2 = partial_grad(
        read_act, "grad_up", (0, 1, 3, 2), gradient, act_before,
        needs=[act_own, arrived0, dact_next], carried=messages[1:3],
    )
    arrived1 = along(message1, 1)
    arrived2 = along(message2, 1)
    down_kept, down_sent = partial_grad(
        make_dpre, "grad_down", (0, 3, 1, 2), hidden, pre_next, dact_next,
    )
    feedback, done = feedback_of(messages[0], arrived0, 0, None, True)
    up_kept, up_sent, message3 = halve(
        up_kept, among(up_sent, 3), needs=[arrived1, done], carried=messages[3:4]
    )
    arrived3 = along(message3, 1)
    down_kept, down_sent = halve(down_kept, among(down_sent, 1))
    feedback, done = feedback_of(message1, arrived1, 1, feedback, True)
    up_parts = split(up_kept, among(up_sent, 1), needs=[arrived2, done])
    down_parts = split(down_kept, among(down_sent, 3))
    grad_up = finish([among(up_parts[half], 0, half, -1) for half in range(2)])
    grad_down = finish([among(down_parts[half], 0, half, 1) for half in range(2)])
    feedback = feedback_of(message2, arrived2, 2, feedback)[0]
    feedback = feedback_of(message3, arrived3, 3, feedback)[0]
    return (feedback[None], grad_down[None], grad_up[None])


def solution(mesh):
    in_specs = (
        P("section", "dp", None),
        P("section", "dp", None),
        P("section", "dp", None),
        P("section", "dp"),
        P("section", "dp", None),
        P("section", "dp", None),
        P("section", None),
        P("section", None, None),
        P("section", None, None),
    )
    out_specs = (P("section", "dp", None), P("section", "dp", None), P("section", "dp", None))
    return jax.shard_map(body, mesh=mesh, in_specs=in_specs, out_specs=out_specs, check_vma=False)
```

time: 285 us -> 107 us (0.38)
  waiting for transfers between devices: 141 us -> 39.3 us
  local copies, waits for them, and re-layouts: 70.5 us -> 4.5 us
  Pallas kernels: 0 us -> 32.8 us
  other arithmetic: 32.8 us -> 0 us
  starting transfers between devices: 3.57 us -> 29.1 us
  matrix products: 21.6 us -> 0 us
  between operations: 14.1 us -> 0.9 us
    reduce_scatter x1 -> x0, waiting for transfers between devices: 101 us -> none  [body(): lax.psum_scatter(jnp.concatenate([transposed_product(hidden, dpre), trans...]
    shift_right_arithmetic x6 -> x0, local copies, waits for them, and re-layouts: 36.9 us -> none  [unpack_codes(): jnp.right_shift(packed[..., None], offsets_bits)]
    pallas_call x0 -> x18, Pallas kernels: none -> 32.8 us  [launch(): pl.pallas_call(wrapped, grid=grid, in_specs=[spec for _, spec in ins] + [...]
    ppermute x2 -> x18, starting transfers between devices: 3.54 us -> 29.1 us  [the longest x10 14.6 us: along(): return lax.ppermute(value, 'section', pairs)]
    dot_general x4 -> x0, matrix products: 21.6 us -> none  [the longest x2 12.7 us: transposed_product(): lax.dot_general(left, right, (((0,), (0,)), ((), ())), preferred_element_...]
    convert_element_type x5 -> x0, other arithmetic: 19.8 us -> none  [the longest x1 11.2 us: build_message(): (picked.astype(jnp.float32) + scale_blocks(codes, scales)).astype(jnp.bfl...]
    mul x2 -> x0, local copies, waits for them, and re-layouts: 14 us -> none  [scale_blocks(): shaped * scales.astype(jnp.float32)[:, :, None]]
    unnamed x21 -> x18, local copies, waits for them, and re-layouts: 13 us -> 4.5 us
  transfers between devices with their start and end apart: 3 -> 18, of which waited for: 2 -> 6; matrix products, arithmetic and copies ran while one was open for 11% -> 0% of each run, Pallas kernels for 0% -> 29%
where the time goes in v4:
time: 107 us
  waiting for transfers between devices  39.3 us (37%)
  Pallas kernels  32.8 us (31%)
  starting transfers between devices  29.1 us (27%)
  local copies, waits for them, and re-layouts  4.5 us (4%)
    pallas_call x18, Pallas kernels, launch(): pl.pallas_call(wrapped, grid=grid, in_specs=[spec for _, spec in ins] + [...  32.8 us
    ppermute x8, waiting for transfers between devices, among(): return lax.ppermute(value, both, pairs)  32.6 us
    ppermute x10, starting transfers between devices, along(): return lax.ppermute(value, 'section', pairs)  14.6 us
    ppermute x8, starting transfers between devices, among(): return lax.ppermute(value, both, pairs)  14.5 us
    ppermute x10, waiting for transfers between devices, along(): return lax.ppermute(value, 'section', pairs)  6.64 us
    unnamed x18, local copies, waits for them, and re-layouts  4.5 us
  transfers between devices with their start and end apart: 18, of which 6 were waited for; matrix products, arithmetic and copies ran while one was open for 0% of the time, Pallas kernels for 29%

profile of v4, /device:TPU:1, one launch (start us, length us, event | category | flops | bytes accessed | tf_op | source)
XLA Modules:
  0.0 106.5 jit_solution(3018959347422285244)
XLA Ops:
  0.6 3.3 %collective-permute-start.1 = (bf16[6144,128]{1,0:T(8,128)(2,1)}, bf16[6144,128]{1,0:T(8,128)(2,1)S(1)}, u32[]{:S(2)}, u32[]{:S(2)}) collective-permute-start(bf16[6144,128]{1,0:T(8,128)(2,1)} %bitcast.30), channel_id=1, source_target_pairs={{0,248},{8,0},{16,8},{24,16},{32,24},{40,32},{48,40},{56,48},{64,5... | collective-permute-start | bytes 4718600 | tf_op jit(solution)/shard_map/ppermute | solution.py:356
  4.0 1.9 %copy-done.1 = s32[1,384,2048]{2,1,0:T(8,128)S(1)} copy-done((s32[1,384,2048]{2,1,0:T(8,128)S(1)}, s32[1,384,2048]{2,1,0:T(8,128)}, u32[]{:S(2)}) %copy-start.1) | copy-done | bytes 3145752
  5.8 1.0 copy-done.3
  8.4 2.2 %message.2.refs_4_.refs_1_ = bf16[96,6144]{1,0:T(8,128)(2,1)S(1)} custom-call(s32[384,2048]{1,0:T(8,128)S(1)} %bitcast.19, bf16[192,384]{1,0:T(8,128)(2,1)S(1)} %bitcast.24, bf16[32,6144]{1,0:T(8,128)(2,1)S(1)} %bitcast.22, s32[1,384]{1,0:T(1,128)S(1)} %copy-done.6), custom_call_target="tpu_custom_call" | custom-call | flops 1 | bytes 1 | tf_op jit(solution)/shard_map/message/pallas_call | solution.py:43
  11.1 4.4 %collective-permute-start = (f32[1,6144]{1,0:T(1,128)S(1)}, f32[1,6144]{1,0:T(1,128)S(1)}, u32[]{:S(2)}, u32[]{:S(2)}) collective-permute-start(f32[1,6144]{1,0:T(1,128)S(1)} %copy-done.8), channel_id=1, source_target_pairs={{0,248},{8,0},{16,8},{24,16},{32,24},{40,32},{48,40},{56,48},{64,5... | collective-permute-start | bytes 73736 | tf_op jit(solution)/shard_map/ppermute | solution.py:356
  15.5 6.4 %message.3 = (bf16[144,6144]{1,0:T(8,128)(2,1)S(1)}, bf16[96,6144]{1,0:T(8,128)(2,1)S(1)}, bf16[48,6144]{1,0:T(8,128)(2,1)S(1)}) custom-call(s32[384,2048]{1,0:T(8,128)S(1)} %bitcast.20, bf16[192,384]{1,0:T(8,128)(2,1)S(1)} %bitcast.25, bf16[32,6144]{1,0:T(8,128)(2,1)S(1)} %bitcast.23, s32[1,384]{1,0:T(1,128)S(1)} %copy-done.7, ...), custom_call_target="tpu_custom_call" | custom-call | flops 1 | bytes 1 | tf_op jit(solution)/shard_map/message/pallas_call | solution.py:43
  21.9 4.4 %gradient.1.refs_5_.refs_0_ = bf16[384,6144]{1,0:T(8,128)(2,1)S(1)} custom-call(bf16[384,6144]{1,0:T(8,128)(2,1)S(1)} %bitcast.21, bf16[192,384]{1,0:T(8,128)(2,1)S(1)} %bitcast.26, bf16[144,6144]{1,0:T(8,128)(2,1)S(1)} %get-tuple-element.27.refs_2_.refs_5_), custom_call_target="tpu_custom_call" | custom-call | flops 1 | bytes 1 | tf_op jit(solution)/shard_map/gradient/pallas_call | solution.py:43
  26.4 4.2 %hidden.1.refs_0_ = bf16[384,6144]{1,0:T(8,128)(2,1)S(1)} custom-call(f32[1,6144]{1,0:T(1,128)S(1)} %collective-permute-done.refs_0_, bf16[96,6144]{1,0:T(8,128)(2,1)S(1)} %message.2.refs_4_.refs_1_, bf16[144,6144]{1,0:T(8,128)(2,1)S(1)} %get-tuple-element.27.refs_2_.refs_5_, bf16[96,6144]{1,0:T(8,128)(2,1)S(1)} %get-tuple-element.28.refs_3_.refs_6_, ...), custom_call_target="tpu_custom_call" | custom-call | flops 1 | bytes 1 | tf_op jit(solution)/shard_map/hidden/pallas_call | solution.py:43
  30.6 1.4 %down.1 = (f32[384,128]{1,0:T(8,128)S(1)}, bf16[384,128]{1,0:T(8,128)(2,1)S(1)}) custom-call(bf16[384,6144]{1,0:T(8,128)(2,1)S(1)} %hidden.1.refs_0_, bf16[6144,128]{1,0:T(8,128)(2,1)S(1)} %collective-permute-done.1.refs_1_, bf16[6144,128]{1,0:T(8,128)(2,1)S(1)} %collective-permute-done.2.refs_2_.refs_1_), custom_call_target="tpu_custom_call" | custom-call | flops 1 | bytes 1 | tf_op jit(solution)/shard_map/down/pallas_call | solution.py:43
  32.0 1.4 %back.1 = bf16[384,128]{1,0:T(8,128)(2,1)S(1)} custom-call(bf16[384,6144]{1,0:T(8,128)(2,1)S(1)} %gradient.1.refs_5_.refs_0_, bf16[6144,128]{1,0:T(8,128)(2,1)S(1)} %collective-permute-done.2.refs_2_.refs_1_, bf16[384,128]{1,0:T(8,128)(2,1)S(1)} %get-tuple-element.30.refs_2_), custom_call_target="tpu_custom_call" | custom-call | flops 1 | bytes 1 | tf_op jit(solution)/shard_map/back/pallas_call | solution.py:43
  33.4 4.4 %collective-permute-start.6 = (bf16[384,128]{1,0:T(8,128)(2,1)S(1)}, bf16[384,128]{1,0:T(8,128)(2,1)S(1)}, u32[]{:S(2)}, u32[]{:S(2)}) collective-permute-start(bf16[384,128]{1,0:T(8,128)(2,1)S(1)} %back.1), channel_id=1, source_target_pairs={{0,240},{8,248},{16,0},{24,8},{32,16},{40,24},{48,32},{56,40},{64,... | collective-permute-start | bytes 294920 | tf_op jit(solution)/shard_map/ppermute | solution.py:356
  37.8 1.3 %collective-permute-start.4 = (bf16[384,128]{1,0:T(8,128)(2,1)S(1)}, bf16[384,128]{1,0:T(8,128)(2,1)S(1)}, u32[]{:S(2)}, u32[]{:S(2)}) collective-permute-start(bf16[384,128]{1,0:T(8,128)(2,1)S(1)} %get-tuple-element.30.refs_2_), channel_id=1, source_target_pairs={{0,8},{8,16},{16,24},{24,32},{32,40},{40,48},{48,56},{56,64},{64,7... | collective-permute-start | bytes 294920 | tf_op jit(solution)/shard_map/ppermute | solution.py:356
  39.2 1.1 collective-permute-done.6.refs_4_.refs_2_
  40.2 1.0 collective-permute-done.4.refs_2_
  41.2 4.6 %collective-permute-done.3.refs_1_ = bf16[384,128]{1,0:T(8,128)(2,1)S(1)} collective-permute-done((bf16[384,128]{1,0:T(8,128)(2,1)S(1)}, bf16[384,128]{1,0:T(8,128)(2,1)S(1)}, u32[]{:S(2)}, u32[]{:S(2)}) %collective-permute-start.3) | collective-permute-done | bytes 98336 | tf_op jit(solution)/shard_map/ppermute | solution.py:356
  45.8 1.0 grad_up.1
  46.9 1.1 %grad_down.1 = (f32[4,128,768]{2,1,0:T(8,128)S(1)}, bf16[4,128,768]{2,1,0:T(8,128)(2,1)S(1)}) custom-call(bf16[384,6144]{1,0:T(8,128)(2,1)S(1)} %hidden.1.refs_0_, f32[384,128]{1,0:T(8,128)S(1)} %get-tuple-element.39.refs_1_, bf16[384,128]{1,0:T(8,128)(2,1)S(1)} %collective-permute-done.6.refs_4_.refs_2_), custom_call_target="tpu_custom_call" | custom-call | flops 1 | bytes 1 | tf_op jit(solution)/shard_map/grad_down/pallas_call | solution.py:43
  48.0 1.3 %collective-permute-start.11 = (bf16[4,128,768]{2,1,0:T(8,128)(2,1)S(1)}, bf16[4,128,768]{2,1,0:T(8,128)(2,1)S(1)}, u32[]{:S(2)}, u32[]{:S(2)}) collective-permute-start(bf16[4,128,768]{2,1,0:T(8,128)(2,1)S(1)} %get-tuple-element.41), channel_id=1, source_target_pairs={{1,0},{0,1},{3,2},{2,3},{5,4},{4,5},{7,6},{6,7},{9,8},{8,9},{11,10... | collective-permute-start | bytes 2359304 | tf_op jit(solution)/shard_map/ppermute | solution.py:366
  49.3 1.8 %collective-permute-start.7 = (bf16[4,128,768]{2,1,0:T(8,128)(2,1)S(1)}, bf16[4,128,768]{2,1,0:T(8,128)(2,1)S(1)}, u32[]{:S(2)}, u32[]{:S(2)}) collective-permute-start(bf16[4,128,768]{2,1,0:T(8,128)(2,1)S(1)} %get-tuple-element.32), channel_id=1, source_target_pairs={{3,0},{2,1},{1,2},{0,3},{7,4},{6,5},{5,6},{4,7},{11,8},{10,9},{9,1... | collective-permute-start | bytes 2359304 | tf_op jit(solution)/shard_map/ppermute | solution.py:366
  51.1 15.6 %collective-permute-done.11.refs_1_ = bf16[4,128,768]{2,1,0:T(8,128)(2,1)S(1)} collective-permute-done((bf16[4,128,768]{2,1,0:T(8,128)(2,1)S(1)}, bf16[4,128,768]{2,1,0:T(8,128)(2,1)S(1)}, u32[]{:S(2)}, u32[]{:S(2)}) %collective-permute-start.11) | collective-permute-done | bytes 786464 | tf_op jit(solution)/shard_map/ppermute | solution.py:366
  66.8 2.6 %collective-permute-start.12 = (bf16[2,128,768]{2,1,0:T(8,128)(2,1)S(1)}, bf16[2,128,768]{2,1,0:T(8,128)(2,1)S(1)}, u32[]{:S(2)}, u32[]{:S(2)}) collective-permute-start(bf16[2,128,768]{2,1,0:T(8,128)(2,1)S(1)} %get-tuple-element.43), channel_id=1, source_target_pairs={{3,0},{2,1},{1,2},{0,3},{7,4},{6,5},{5,6},{4,7},{11,8},{10,9},{9,1... | collective-permute-start | bytes 1179656 | tf_op jit(solution)/shard_map/ppermute | solution.py:366
  69.4 2.1 %feedback.4 = (bf16[384,6144]{1,0:T(8,128)(2,1)}, f32[8,128]{1,0:T(8,128)S(1)}) custom-call(bf16[96,6144]{1,0:T(8,128)(2,1)S(1)} %collective-permute-done.5.refs_3_.refs_0_, bf16[96,6144]{1,0:T(8,128)(2,1)S(1)} %message.2.refs_4_.refs_1_, bf16[384,128]{1,0:T(8,128)(2,1)S(1)} %collective-permute-done.4.refs_2_, bf16[6144,128]{1,0:T(8,128)(2,1)S(1)} %bitcast.15), custom_call_target="tpu_custom_call" | custom-call | flops 1 | bytes 1 | tf_op jit(solution)/shard_map/feedback/pallas_call | solution.py:43
  72.4 5.0 %collective-permute-done.12.refs_1_ = bf16[2,128,768]{2,1,0:T(8,128)(2,1)S(1)} collective-permute-done((bf16[2,128,768]{2,1,0:T(8,128)(2,1)S(1)}, bf16[2,128,768]{2,1,0:T(8,128)(2,1)S(1)}, u32[]{:S(2)}, u32[]{:S(2)}) %collective-permute-start.12) | collective-permute-done | bytes 393248 | tf_op jit(solution)/shard_map/ppermute | solution.py:366
  77.5 1.2 %collective-permute-start.13 = (bf16[128,768]{1,0:T(8,128)(2,1)S(1)}, bf16[128,768]{1,0:T(8,128)(2,1)S(1)}, u32[]{:S(2)}, u32[]{:S(2)}) collective-permute-start(bf16[128,768]{1,0:T(8,128)(2,1)S(1)} %get-tuple-element.44), channel_id=1, source_target_pairs={{0,8},{1,9},{2,10},{3,11},{4,12},{5,13},{6,14},{7,15},{8,16},{9,17... | collective-permute-start | bytes 589832 | tf_op jit(solution)/shard_map/ppermute | solution.py:366
  78.6 2.4 %collective-permute-start.14 = (bf16[128,768]{1,0:T(8,128)(2,1)S(1)}, bf16[128,768]{1,0:T(8,128)(2,1)S(1)}, u32[]{:S(2)}, u32[]{:S(2)}) collective-permute-start(bf16[128,768]{1,0:T(8,128)(2,1)S(1)} %get-tuple-element.45), channel_id=1, source_target_pairs={{4,8},{5,9},{6,10},{7,11},{0,12},{1,13},{2,14},{3,15},{12,16},{13,... | collective-permute-start | bytes 589832 | tf_op jit(solution)/shard_map/ppermute | solution.py:366
  81.1 2.6 %feedback.5 = (bf16[384,6144]{1,0:T(8,128)(2,1)}, f32[8,128]{1,0:T(8,128)S(1)}) custom-call(bf16[144,6144]{1,0:T(8,128)(2,1)S(1)} %collective-permute-done.8.refs_2_.refs_0_, bf16[144,6144]{1,0:T(8,128)(2,1)S(1)} %get-tuple-element.33.refs_1_, bf16[384,128]{1,0:T(8,128)(2,1)S(1)} %collective-permute-done.4.refs_2_, ...), custom_call_target="tpu_custom_call", output_to_operand_aliasing={{0}: (4, {})} | custom-call | flops 1 | bytes 1 | tf_op jit(solution)/shard_map/feedback/pallas_call | solution.py:43
  84.5 4.5 %collective-permute-start.17 = (bf16[128,768]{1,0:T(8,128)(2,1)S(1)}, bf16[128,768]{1,0:T(8,128)(2,1)S(1)}, u32[]{:S(2)}, u32[]{:S(2)}) collective-permute-start(bf16[128,768]{1,0:T(8,128)(2,1)S(1)} %get-tuple-element.50), channel_id=1, source_target_pairs={{4,248},{5,249},{6,250},{7,251},{0,252},{1,253},{2,254},{3,255},{1... | collective-permute-start | bytes 589832 | tf_op jit(solution)/shard_map/ppermute | solution.py:366
  89.0 12.1 %collective-permute-done.14.refs_1_ = bf16[128,768]{1,0:T(8,128)(2,1)S(1)} collective-permute-done((bf16[128,768]{1,0:T(8,128)(2,1)S(1)}, bf16[128,768]{1,0:T(8,128)(2,1)S(1)}, u32[]{:S(2)}, u32[]{:S(2)}) %collective-permute-start.14) | collective-permute-done | bytes 196640 | tf_op jit(solution)/shard_map/ppermute | solution.py:366
  101.1 0.9 finish.2
  102.0 2.1 %feedback.6.refs_4_ = bf16[384,6144]{1,0:T(8,128)(2,1)} custom-call(bf16[96,6144]{1,0:T(8,128)(2,1)S(1)} %collective-permute-done.10.refs_0_.refs_2_, bf16[96,6144]{1,0:T(8,128)(2,1)S(1)} %get-tuple-element.36.refs_1_, bf16[384,128]{1,0:T(8,128)(2,1)S(1)} %collective-permute-done.4.refs_2_, ...), custom_call_target="tpu_custom_call", output_to_operand_aliasing={{}: (4, {})} | custom-call | flops 1 | bytes 1 | tf_op jit(solution)/shard_map/feedback/pallas_call | solution.py:43
  104.1 1.5 %feedback.7 = bf16[384,6144]{1,0:T(8,128)(2,1)} custom-call(bf16[48,6144]{1,0:T(8,128)(2,1)S(1)} %collective-permute-done.9.refs_0_, bf16[48,6144]{1,0:T(8,128)(2,1)S(1)} %get-tuple-element.35.refs_1_, bf16[384,128]{1,0:T(8,128)(2,1)S(1)} %collective-permute-done.4.refs_2_, bf16[6144,128]{1,0:T(8,128)(2,1)S(1)} %bitcast.18, ...), custom_call_target="tpu_custom_call", output_to_operand_aliasing={{}: (4, {})} | custom-call | flops 1 | bytes 1 | tf_op jit(solution)/shard_map/feedback/pallas_call | solution.py:43
  105.6 0.9 finish.3
  (40 shorter events, 4.0 us)
Async XLA Ops:
  0.6 30.0 %collective-permute-start.1 = (bf16[6144,128]{1,0:T(8,128)(2,1)}, bf16[6144,128]{1,0:T(8,128)(2,1)S(1)}, u32[]{:S(2)}, u32[]{:S(2)}) collective-permute-start(bf16[6144,128]{1,0:T(8,128)(2,1)} %bitcast.30), channel_id=1, source_target_pairs={{0,248},{8,0},{16,8},{24,16},{32,24},{40,32},{48,40},{56,48},{64,5... | collective-permute-start | bytes 4718600 | tf_op jit(solution)/shard_map/ppermute | solution.py:356
  4.0 26.7 %collective-permute-start.2 = (bf16[6144,128]{1,0:T(8,128)(2,1)}, bf16[6144,128]{1,0:T(8,128)(2,1)S(1)}, u32[]{:S(2)}, u32[]{:S(2)}) collective-permute-start(bf16[6144,128]{1,0:T(8,128)(2,1)} %bitcast.14), channel_id=1, source_target_pairs={{0,8},{8,16},{16,24},{24,32},{32,40},{40,48},{48,56},{56,64},{64,7... | collective-permute-start | bytes 4718600 | tf_op jit(solution)/shard_map/ppermute | solution.py:356
  4.0 1.9 %copy-start.1 = (s32[1,384,2048]{2,1,0:T(8,128)S(1)}, s32[1,384,2048]{2,1,0:T(8,128)}, u32[]{:S(2)}) copy-start(s32[1,384,2048]{2,1,0:T(8,128)} %param.9) | copy-start | bytes 9437188
  5.8 1.0 copy-start.3
  6.8 0.9 copy-start.4
  7.8 0.7 copy-start.6
  8.4 2.6 %copy-start.8 = (f32[1,6144]{1,0:T(1,128)S(1)}, f32[1,6144]{1,0:T(1,128)}, u32[]{:S(2)}) copy-start(f32[1,6144]{1,0:T(1,128)} %param.15) | copy-start | bytes 73732
  8.4 7.0 %copy-start.7 = (s32[1,384]{1,0:T(1,128)S(1)}, s32[1,384]{1,0:T(1,128)}, u32[]{:S(2)}) copy-start(s32[1,384]{1,0:T(1,128)} %refs_3_.3) | copy-start | bytes 4612
  10.7 11.2 %copy-start.2 = (bf16[1,384,6144]{2,1,0:T(8,128)(2,1)S(1)}, bf16[1,384,6144]{2,1,0:T(8,128)(2,1)}, u32[]{:S(2)}) copy-start(bf16[1,384,6144]{2,1,0:T(8,128)(2,1)} %param.13) | copy-start | bytes 14155780
  10.7 11.2 %copy-start.5 = (bf16[1,384,192]{1,2,0:T(8,128)(2,1)S(1)}, bf16[1,384,192]{1,2,0:T(8,128)(2,1)}, u32[]{:S(2)}) copy-start(bf16[1,384,192]{1,2,0:T(8,128)(2,1)} %param.14) | copy-start | bytes 442372
  10.7 28.5 %collective-permute-start.5 = (bf16[96,6144]{1,0:T(8,128)(2,1)S(1)}, bf16[96,6144]{1,0:T(8,128)(2,1)S(1)}, u32[]{:S(2)}, u32[]{:S(2)}) collective-permute-start(bf16[96,6144]{1,0:T(8,128)(2,1)S(1)} %message.2.refs_4_.refs_1_), channel_id=1, source_target_pairs={{0,8},{8,16},{16,24},{24,32},{32,40},{40,48},{48,56},{56,64},{64,7... | collective-permute-start | bytes 3538952 | tf_op jit(solution)/shard_map/ppermute | solution.py:356
  11.1 15.3 %collective-permute-start = (f32[1,6144]{1,0:T(1,128)S(1)}, f32[1,6144]{1,0:T(1,128)S(1)}, u32[]{:S(2)}, u32[]{:S(2)}) collective-permute-start(f32[1,6144]{1,0:T(1,128)S(1)} %copy-done.8), channel_id=1, source_target_pairs={{0,248},{8,0},{16,8},{24,16},{32,24},{40,32},{48,40},{56,48},{64,5... | collective-permute-start | bytes 73736 | tf_op jit(solution)/shard_map/ppermute | solution.py:356
  33.4 6.8 %collective-permute-start.6 = (bf16[384,128]{1,0:T(8,128)(2,1)S(1)}, bf16[384,128]{1,0:T(8,128)(2,1)S(1)}, u32[]{:S(2)}, u32[]{:S(2)}) collective-permute-start(bf16[384,128]{1,0:T(8,128)(2,1)S(1)} %back.1), channel_id=1, source_target_pairs={{0,240},{8,248},{16,0},{24,8},{32,16},{40,24},{48,32},{56,40},{64,... | collective-permute-start | bytes 294920 | tf_op jit(solution)/shard_map/ppermute | solution.py:356
  37.8 3.4 %collective-permute-start.4 = (bf16[384,128]{1,0:T(8,128)(2,1)S(1)}, bf16[384,128]{1,0:T(8,128)(2,1)S(1)}, u32[]{:S(2)}, u32[]{:S(2)}) collective-permute-start(bf16[384,128]{1,0:T(8,128)(2,1)S(1)} %get-tuple-element.30.refs_2_), channel_id=1, source_target_pairs={{0,8},{8,16},{16,24},{24,32},{32,40},{40,48},{48,56},{56,64},{64,7... | collective-permute-start | bytes 294920 | tf_op jit(solution)/shard_map/ppermute | solution.py:356
  39.2 6.6 %collective-permute-start.3 = (bf16[384,128]{1,0:T(8,128)(2,1)S(1)}, bf16[384,128]{1,0:T(8,128)(2,1)S(1)}, u32[]{:S(2)}, u32[]{:S(2)}) collective-permute-start(bf16[384,128]{1,0:T(8,128)(2,1)S(1)} %get-tuple-element.30.refs_2_), channel_id=1, source_target_pairs={{0,16},{8,24},{16,32},{24,40},{32,48},{40,56},{48,64},{56,72},{64,... | collective-permute-start | bytes 294920 | tf_op jit(solution)/shard_map/ppermute | solution.py:356
  46.8 24.7 %collective-permute-start.8 = (bf16[144,6144]{1,0:T(8,128)(2,1)S(1)}, bf16[144,6144]{1,0:T(8,128)(2,1)S(1)}, u32[]{:S(2)}, u32[]{:S(2)}) collective-permute-start(bf16[144,6144]{1,0:T(8,128)(2,1)S(1)} %get-tuple-element.33.refs_1_), channel_id=1, source_target_pairs={{0,8},{8,16},{16,24},{24,32},{32,40},{40,48},{48,56},{56,64},{64,7... | collective-permute-start | bytes 5308424 | tf_op jit(solution)/shard_map/ppermute | solution.py:356
  48.0 21.4 %copy-start = (bf16[1,6144,128]{2,1,0:T(8,128)(2,1)S(1)}, bf16[1,6144,128]{2,1,0:T(8,128)(2,1)}, u32[]{:S(2)}) copy-start(bf16[1,6144,128]{2,1,0:T(8,128)(2,1)} %param.17) | copy-start | bytes 4718596
  48.0 18.7 %collective-permute-start.11 = (bf16[4,128,768]{2,1,0:T(8,128)(2,1)S(1)}, bf16[4,128,768]{2,1,0:T(8,128)(2,1)S(1)}, u32[]{:S(2)}, u32[]{:S(2)}) collective-permute-start(bf16[4,128,768]{2,1,0:T(8,128)(2,1)S(1)} %get-tuple-element.41), channel_id=1, source_target_pairs={{1,0},{0,1},{3,2},{2,3},{5,4},{4,5},{7,6},{6,7},{9,8},{8,9},{11,10... | collective-permute-start | bytes 2359304 | tf_op jit(solution)/shard_map/ppermute | solution.py:366
  49.3 22.2 %collective-permute-start.7 = (bf16[4,128,768]{2,1,0:T(8,128)(2,1)S(1)}, bf16[4,128,768]{2,1,0:T(8,128)(2,1)S(1)}, u32[]{:S(2)}, u32[]{:S(2)}) collective-permute-start(bf16[4,128,768]{2,1,0:T(8,128)(2,1)S(1)} %get-tuple-element.32), channel_id=1, source_target_pairs={{3,0},{2,1},{1,2},{0,3},{7,4},{6,5},{5,6},{4,7},{11,8},{10,9},{9,1... | collective-permute-start | bytes 2359304 | tf_op jit(solution)/shard_map/ppermute | solution.py:366
  51.1 32.6 %collective-permute-start.10 = (bf16[96,6144]{1,0:T(8,128)(2,1)S(1)}, bf16[96,6144]{1,0:T(8,128)(2,1)S(1)}, u32[]{:S(2)}, u32[]{:S(2)}) collective-permute-start(bf16[96,6144]{1,0:T(8,128)(2,1)S(1)} %get-tuple-element.36.refs_1_), channel_id=1, source_target_pairs={{0,8},{8,16},{16,24},{24,32},{32,40},{40,48},{48,56},{56,64},{64,7... | collective-permute-start | bytes 3538952 | tf_op jit(solution)/shard_map/ppermute | solution.py:356
  66.8 10.6 %collective-permute-start.12 = (bf16[2,128,768]{2,1,0:T(8,128)(2,1)S(1)}, bf16[2,128,768]{2,1,0:T(8,128)(2,1)S(1)}, u32[]{:S(2)}, u32[]{:S(2)}) collective-permute-start(bf16[2,128,768]{2,1,0:T(8,128)(2,1)S(1)} %get-tuple-element.43), channel_id=1, source_target_pairs={{3,0},{2,1},{1,2},{0,3},{7,4},{6,5},{5,6},{4,7},{11,8},{10,9},{9,1... | collective-permute-start | bytes 1179656 | tf_op jit(solution)/shard_map/ppermute | solution.py:366
  71.7 12.0 %collective-permute-start.15 = (bf16[2,128,768]{2,1,0:T(8,128)(2,1)S(1)}, bf16[2,128,768]{2,1,0:T(8,128)(2,1)S(1)}, u32[]{:S(2)}, u32[]{:S(2)}) collective-permute-start(bf16[2,128,768]{2,1,0:T(8,128)(2,1)S(1)} %get-tuple-element.47), channel_id=1, source_target_pairs={{1,0},{0,1},{3,2},{2,3},{5,4},{4,5},{7,6},{6,7},{9,8},{8,9},{11,10... | collective-permute-start | bytes 1179656 | tf_op jit(solution)/shard_map/ppermute | solution.py:366
  71.8 32.3 %collective-permute-start.9 = (bf16[48,6144]{1,0:T(8,128)(2,1)S(1)}, bf16[48,6144]{1,0:T(8,128)(2,1)S(1)}, u32[]{:S(2)}, u32[]{:S(2)}) collective-permute-start(bf16[48,6144]{1,0:T(8,128)(2,1)S(1)} %get-tuple-element.35.refs_1_), channel_id=1, source_target_pairs={{0,8},{8,16},{16,24},{24,32},{32,40},{40,48},{48,56},{56,64},{64,7... | collective-permute-start | bytes 1769480 | tf_op jit(solution)/shard_map/ppermute | solution.py:356
  77.5 11.5 %collective-permute-start.13 = (bf16[128,768]{1,0:T(8,128)(2,1)S(1)}, bf16[128,768]{1,0:T(8,128)(2,1)S(1)}, u32[]{:S(2)}, u32[]{:S(2)}) collective-permute-start(bf16[128,768]{1,0:T(8,128)(2,1)S(1)} %get-tuple-element.44), channel_id=1, source_target_pairs={{0,8},{1,9},{2,10},{3,11},{4,12},{5,13},{6,14},{7,15},{8,16},{9,17... | collective-permute-start | bytes 589832 | tf_op jit(solution)/shard_map/ppermute | solution.py:366
  78.6 22.4 %collective-permute-start.14 = (bf16[128,768]{1,0:T(8,128)(2,1)S(1)}, bf16[128,768]{1,0:T(8,128)(2,1)S(1)}, u32[]{:S(2)}, u32[]{:S(2)}) collective-permute-start(bf16[128,768]{1,0:T(8,128)(2,1)S(1)} %get-tuple-element.45), channel_id=1, source_target_pairs={{4,8},{5,9},{6,10},{7,11},{0,12},{1,13},{2,14},{3,15},{12,16},{13,... | collective-permute-start | bytes 589832 | tf_op jit(solution)/shard_map/ppermute | solution.py:366
  83.8 21.8 %collective-permute-start.16 = (bf16[128,768]{1,0:T(8,128)(2,1)S(1)}, bf16[128,768]{1,0:T(8,128)(2,1)S(1)}, u32[]{:S(2)}, u32[]{:S(2)}) collective-permute-start(bf16[128,768]{1,0:T(8,128)(2,1)S(1)} %get-tuple-element.49), channel_id=1, source_target_pairs={{0,248},{1,249},{2,250},{3,251},{4,252},{5,253},{6,254},{7,255},{8... | collective-permute-start | bytes 589832 | tf_op jit(solution)/shard_map/ppermute | solution.py:366
  84.5 21.1 %collective-permute-start.17 = (bf16[128,768]{1,0:T(8,128)(2,1)S(1)}, bf16[128,768]{1,0:T(8,128)(2,1)S(1)}, u32[]{:S(2)}, u32[]{:S(2)}) collective-permute-start(bf16[128,768]{1,0:T(8,128)(2,1)S(1)} %get-tuple-element.50), channel_id=1, source_target_pairs={{4,248},{5,249},{6,250},{7,251},{0,252},{1,253},{2,254},{3,255},{1... | collective-permute-start | bytes 589832 | tf_op jit(solution)/shard_map/ppermute | solution.py:366

commit v5 on v4

--- a/solution.py
+++ b/solution.py
@@ -15,6 +15,8 @@
 F32 = jnp.float32
 BF16 = jnp.bfloat16
 TILE = 48
+BLOCK = 384
+HALF = D // 2
 SPANS = (96, 144, 96, 48)
 MIB = 1 << 20
 ROOT_2_PI = math.sqrt(2.0 / math.pi)
@@ -54,135 +56,157 @@
     )(*[value for value, _ in ins], *needs, *carried)
 
 
-def rows_of(width, skip=0):
-    return pl.BlockSpec((TILE, width), lambda i: (i + skip, 0))
-
-
-def rows_between(start, end, width):
-    return pl.BlockSpec((TILE, width), lambda i: (jnp.clip(i - start, 0, end - start - 1), 0))
-
-
-def whole(*shape):
-    return pl.BlockSpec(shape, lambda i: (0,) * len(shape))
+def hand_on(value, after):
+    return launch(lambda: None, "hand_on", [], [], needs=[after], carried=[value], grant=1)[0]
 
 
 def lanes(shape):
     return lax.broadcasted_iota(jnp.int32, shape, 1)
 
 
-def spread_scales(scales_ref, rows, tile):
-    half, at = divmod(tile, 32)
-    part = scales_ref[rows, half * 128 : half * 128 + 128]
-    return jnp.take_along_axis(part, lanes((TILE, 128)) // 32 + 4 * at, axis=1)
-
-
-def turn_scales(scales_ref, turned_ref):
-    turned_ref[:, : D // 32] = scales_ref[...].astype(F32).T
-
-
-def tile_at(i):
-    return pl.ds(pl.multiple_of(i * TILE, 16), TILE)
-
-
-def message_kernel(first, bounds, codes_ref, scales_ref, base_ref, ids_ref, *refs):
-    *out_refs, turned_ref, picks_ref = refs
-    step = pl.program_id(0)
-
-    @pl.when(step == 0)
-    def _():
-        turn_scales(scales_ref, turned_ref)
-        hits = lax.broadcasted_iota(jnp.int32, (32, TOK), 0) == ids_ref[...]
-        picks_ref[...] = hits.astype(F32).T.astype(BF16)
-
-    def fill(out_ref):
-        rows = tile_at(step + first // TILE)
-        picks = picks_ref[rows, :]
-        lane = lanes((TILE, 128))
-        for block in range(16):
-            words = codes_ref[:, block * 128 : (block + 1) * 128]
-            base = jnp.dot(
-                picks, base_ref[:, block * 384 : (block + 1) * 384], preferred_element_type=F32
-            )
+def block_at(b):
+    return pl.ds(pl.multiple_of(b * BLOCK, 128), BLOCK)
+
+
+def one_hot_blocks(b):
+    shape = (D // 32, BLOCK)
+    spot = lax.broadcasted_iota(jnp.int32, shape, 0) - b * (BLOCK // 32)
+    return (spot == lanes(shape) // 32).astype(F32).astype(BF16)
+
+
+def exact(left, right):
+    return jnp.dot(left, right, preferred_element_type=F32)
+
+
+def chunks_of(out_refs):
+    found, start = [], 0
+    for ref in out_refs:
+        count = ref.shape[0]
+        for row in range(0, count, 96):
+            found.append((ref, row, start + row, min(96, count - row)))
+        start += count
+    return found
+
+
+def message_kernel(first, codes_ref, scales_ref, base_ref, ids_ref, *refs):
+    *out_refs, stats_ref, turned_ref, picks_ref, pivot_ref, sum_ref, square_ref = refs
+    count = stats_ref.shape[0]
+    mine = slice(first, first + count)
+    turned_ref[...] = scales_ref[...].astype(F32).T[mine].astype(BF16)
+    hits = lax.broadcasted_iota(jnp.int32, (32, TOK), 0) == ids_ref[...]
+    picks_ref[...] = hits.astype(F32).T[mine].astype(BF16)
+    chunks = chunks_of(out_refs)
+
+    def decode(b, take):
+        spread = one_hot_blocks(b)
+        base_block = base_ref[:, block_at(b)]
+        words_at = pl.ds(pl.multiple_of(b * 128, 128), 128)
+        for ref, row, at, n in chunks:
+            rows = slice(at, at + n)
+            scale = exact(turned_ref[rows, :], spread)
+            base = exact(picks_ref[rows, :], base_block)
+            words = codes_ref[first + at : first + at + n, words_at]
+            lane = lanes((n, 128))
+            values = []
             for j in range(3):
                 spot = lane + 128 * j
                 word = jnp.take_along_axis(words, spot // 3, axis=1)
                 code = jnp.right_shift(word, (spot % 3) * 4) & 15
-                tile = block * 3 + j
-                scale = spread_scales(turned_ref, rows, tile)
-                value = base[:, j * 128 : (j + 1) * 128] + scale * (code - 8).astype(F32)
-                out_ref[:, tile * 128 : (tile + 1) * 128] = value.astype(BF16)
-
-    if len(out_refs) == 1:
-        fill(out_refs[0])
-        return
-    for out_ref, (start, end) in zip(out_refs, bounds):
-
-        @pl.when((step >= start) & (step < end))
-        def _(out_ref=out_ref):
-            fill(out_ref)
+                part = slice(j * 128, (j + 1) * 128)
+                value = base[:, part] + scale[:, part] * (code - 8).astype(F32)
+                value = value.astype(BF16)
+                ref[row : row + n, pl.ds(pl.multiple_of(b * BLOCK + j * 128, 128), 128)] = value
+                values.append(value.astype(F32))
+            take(rows, n, values)
+
+    def begin(rows, n, values):
+        pivot = jnp.sum(values[0] + values[1] + values[2], axis=1, keepdims=True) / BLOCK
+        pivot = jnp.broadcast_to(pivot, (n, 128))
+        pivot_ref[rows, :] = pivot
+        away = [value - pivot for value in values]
+        sum_ref[rows, :] = away[0] + away[1] + away[2]
+        square_ref[rows, :] = away[0] * away[0] + away[1] * away[1] + away[2] * away[2]
+
+    def go_on(rows, n, values):
+        pivot = pivot_ref[rows, :]
+        away = [value - pivot for value in values]
+        sum_ref[rows, :] += away[0] + away[1] + away[2]
+        square_ref[rows, :] += away[0] * away[0] + away[1] * away[1] + away[2] * away[2]
+
+    def one_block(b, carry):
+        decode(b, go_on)
+        return carry
+
+    decode(0, begin)
+    lax.fori_loop(1, D // BLOCK, one_block, 0)
+    shift = jnp.sum(sum_ref[...], axis=1, keepdims=True) * (1.0 / D)
+    square = jnp.sum(square_ref[...], axis=1, keepdims=True) * (1.0 / D)
+    variance = jnp.maximum(square - shift * shift, 0.0)
+    stats_ref[:, :128] = pivot_ref[...] + shift
+    stats_ref[:, 128:] = jnp.broadcast_to(lax.rsqrt(variance + 1e-05), (count, 128))
 
 
 def make_messages(codes, scales, base, ids, first, spans, **ties):
-    ends = [sum(spans[: k + 1]) // TILE for k in range(len(spans))]
-    bounds = list(zip([0, *ends], ends))
-    return launch(
-        functools.partial(message_kernel, first, bounds), "message",
-        [
-            (codes, rows_of(D // 3, first // TILE)), (scales, whole(D // 32, TOK)),
-            (base, whole(32, D)), (ids, whole(1, TOK)),
-        ],
-        [
-            (array((span, D), BF16), rows_between(start, end, D))
-            for span, (start, end) in zip(spans, bounds)
-        ],
-        [pltpu.VMEM((TOK, 256), F32), pltpu.VMEM((TOK, 32), BF16)],
-        grid=(ends[-1],), **ties,
+    count = sum(spans)
+    return launch(
+        functools.partial(message_kernel, first), "message",
+        [(value, VMEM) for value in (codes, scales, base, ids)],
+        [(array((span, D), BF16), VMEM) for span in spans] + [(array((count, 256), F32), VMEM)],
+        [pltpu.VMEM((count, D // 32), BF16), pltpu.VMEM((count, 32), BF16)]
+        + [pltpu.VMEM((count, 128), F32)] * 3,
+        **ties,
     )
 
 
 def gradient_kernel(codes_ref, scales_ref, out_ref, turned_ref):
-    step = pl.program_id(0)
-
-    @pl.when(step == 0)
-    def _():
-        turn_scales(scales_ref, turned_ref)
-
-    for tile in range(48):
-        part = slice(tile * 128, (tile + 1) * 128)
-        scale = spread_scales(turned_ref, tile_at(step), tile)
-        out_ref[:, part] = (scale * (codes_ref[:, part].astype(F32) - 128.0)).astype(BF16)
+    turned_ref[...] = scales_ref[...].astype(F32).T.astype(BF16)
+
+    def one_block(b, carry):
+        spread = one_hot_blocks(b)
+        for at in range(0, TOK, 96):
+            rows = slice(at, at + 96)
+            scale = exact(turned_ref[rows, :], spread)
+            codes = codes_ref[rows, block_at(b)].astype(F32)
+            out_ref[rows, block_at(b)] = (scale * (codes - 128.0)).astype(BF16)
+        return carry
+
+    lax.fori_loop(0, D // BLOCK, one_block, 0)
 
 
 def make_gradient(codes, scales, **ties):
     return launch(
-        gradient_kernel, "gradient",
-        [(codes, rows_of(D)), (scales, whole(D // 32, TOK))],
-        [(array((TOK, D), BF16), rows_of(D))], [pltpu.VMEM((TOK, 256), F32)],
-        grid=(TOK // TILE,), **ties,
+        gradient_kernel, "gradient", [(codes, VMEM), (scales, VMEM)],
+        [(array((TOK, D), BF16), VMEM)], [pltpu.VMEM((TOK, D // 32), BF16)], **ties,
     )[0]
 
 
-def hidden_kernel(bounds, gain_ref, *refs):
-    *message_refs, out_ref = refs
-    step = pl.program_id(0)
-    for message_ref, (start, end) in zip(message_refs, bounds):
-
-        @pl.when((step >= start) & (step < end))
-        def _(message_ref=message_ref):
-            x = message_ref[...].astype(F32)
-            center = x - jnp.sum(x, axis=1, keepdims=True) * (1.0 / D)
-            variance = jnp.sum(center * center, axis=1, keepdims=True) * (1.0 / D)
-            out_ref[...] = (gain_ref[...] * center * lax.rsqrt(variance + 1e-05)).astype(BF16)
-
-
-def make_hidden(messages, gain, **ties):
-    ends = [sum(m.shape[0] for m in messages[: k + 1]) // TILE for k in range(len(messages))]
-    bounds = list(zip([0, *ends], ends))
-    return launch(
-        functools.partial(hidden_kernel, bounds), "hidden",
-        [(gain, whole(1, D))]
-        + [(m, rows_between(start, end, D)) for m, (start, end) in zip(messages, bounds)],
-        [(array((TOK, D), BF16), rows_of(D))], grid=(TOK // TILE,), **ties,
+def hidden_kernel(n, gain_ref, *refs):
+    message_refs, stats_refs, out_ref = refs[:n], refs[n:-1], refs[-1]
+    stats = [
+        (ref, row) for ref, row, _, rows in chunks_of(stats_refs) for row in range(row, row + rows, TILE)
+    ]
+    messages = [
+        (ref, row) for ref, row, _, rows in chunks_of(message_refs) for row in range(row, row + rows, TILE)
+    ]
+
+    def one_block(b, carry):
+        at = pl.ds(pl.multiple_of(b * 128, 128), 128)
+        gain = gain_ref[:, at]
+        for t, ((ref, row), (stats_ref, stats_row)) in enumerate(zip(messages, stats)):
+            x = ref[row : row + TILE, at].astype(F32)
+            mean = stats_ref[stats_row : stats_row + TILE, :128]
+            scale = stats_ref[stats_row : stats_row + TILE, 128:]
+            out_ref[t * TILE : (t + 1) * TILE, at] = (gain * (x - mean) * scale).astype(BF16)
+        return carry
+
+    lax.fori_loop(0, D // 128, one_block, 0)
+
+
+def make_hidden(messages, stats, gain, **ties):
+    return launch(
+        functools.partial(hidden_kernel, len(messages)), "hidden",
+        [(value, VMEM) for value in (gain, *messages, *stats)],
+        [(array((TOK, D), BF16), VMEM)], **ties,
     )[0]
 
 
@@ -203,15 +227,34 @@
     )
 
 
-def back_kernel(grad_ref, weight_ref, out_ref):
-    out_ref[...] = jnp.dot(
-        grad_ref[...], weight_ref[...], preferred_element_type=F32
-    ).astype(BF16)
-
-
-def project_back(grad, weight, **ties):
-    return launch(
-        back_kernel, "back", [(grad, VMEM), (weight, VMEM)],
+def pick_half_kernel(weight_ref, out_ref, sem):
+    half = lax.rem(lax.axis_index("dp"), 2)
+    rows = pl.ds(pl.multiple_of(half * HALF, HALF), HALF)
+    copy = pltpu.make_async_copy(weight_ref.at[rows], out_ref, sem.at[0])
+    copy.start()
+    copy.wait()
+
+
+def pick_half(weight):
+    return launch(
+        pick_half_kernel, "pick_half", [(weight, ANY)], [(array((HALF, R), BF16), VMEM)],
+        [pltpu.SemaphoreType.DMA((1,))],
+    )[0]
+
+
+def back_kernel(grad_ref, chip_ref, mine_ref, other_ref, out_ref):
+    half = lax.rem(lax.axis_index("dp"), 2)
+    total = jnp.zeros((TOK, R), F32)
+    for where, part_ref in ((half, mine_ref), (1 - half, other_ref)):
+        at = pl.ds(pl.multiple_of(where * HALF, HALF), HALF)
+        weight = part_ref[...] + chip_ref[at, :]
+        total += jnp.dot(grad_ref[:, at], weight, preferred_element_type=F32)
+    out_ref[...] = total.astype(BF16)
+
+
+def project_back(grad, chip, mine, other, **ties):
+    return launch(
+        back_kernel, "back", [(value, VMEM) for value in (grad, chip, mine, other)],
         [(array((TOK, R), BF16), VMEM)], **ties,
     )
 
@@ -355,9 +398,9 @@
         pairs = [(s, (s + distance) % sections) for s in range(sections)]
         return lax.ppermute(value, "section", pairs)
 
-    def among(value, flip_x, flip_y=0, section_step=0):
+    def among(value, flip_x, flip_y=0, section_step=0, stride=1):
         pairs = []
-        for s in range(sections):
+        for s in range(0, sections, stride):
             for d in range(replicas):
                 y, x = divmod(d, across)
                 source = (y ^ flip_y) * across + (x ^ flip_x)
@@ -366,24 +409,36 @@
         return lax.ppermute(value, both, pairs)
 
     up = w_up[0]
-    up_before = along(up, 1)
+    odd_to_even = [(s, (s + 1) % sections) for s in range(1, sections, 2)]
+    even_to_odd = [(s, s + 1) for s in range(0, sections, 2)]
+    up_mine = lax.ppermute(pick_half(up), "section", odd_to_even)
+    up_chip = lax.ppermute(up, "section", even_to_odd)
     down_next = along(w_down[0], -1)
     gain_next = along(norm_gain, -1)
 
     codes, base = forward_codes[0], stored_base[0]
     scales = forward_scales[0].T
     firsts = [sum(SPANS[:k]) for k in range(len(SPANS))]
-    message0 = make_messages(codes, scales, base, sample_ids, 0, SPANS[:1])[0]
-    later = make_messages(codes, scales, base, sample_ids, SPANS[0], SPANS[1:], needs=[message0])
-    messages = [message0, *later]
+    message0, stats0 = make_messages(codes, scales, base, sample_ids, 0, SPANS[:1])
+    message1, stats1 = make_messages(
+        codes, scales, base, sample_ids, firsts[1], SPANS[1:2], needs=[message0]
+    )
+    up_mine = hand_on(up_mine, message1)
+    up_other = among(up_mine, 1, stride=2)
+    *later, stats2 = make_messages(
+        codes, scales, base, sample_ids, firsts[2], SPANS[2:], needs=[message1]
+    )
+    messages = [message0, message1, *later]
     gradient = make_gradient(backward_codes[0], backward_scales[0].T, needs=[later[0]])
-    hidden = make_hidden(messages, gain_next, needs=[gradient])
-
-    pre_next, act_next = project_down(hidden, down_next, needs=[up_before])
+    hidden = make_hidden(messages, [stats0, stats1, stats2], gain_next, needs=[gradient])
+
+    pre_next, act_next = project_down(hidden, down_next, needs=[up_chip, up_other])
     act_before = along(act_next, 2)
     act_own = along(act_next, 1)
     arrived0 = along(messages[0], 1)
-    dact_before = project_back(gradient, up_before, needs=[act_next])[0]
+    dact_before = project_back(
+        gradient, up_chip, up_mine, up_other, needs=[act_next]
+    )[0]
     dact_next = along(dact_before, -2)
 
     def feedback_of(own, x, at, before, marked=False):
@@ -400,13 +455,13 @@
     )
     feedback, done = feedback_of(messages[0], arrived0, 0, None, True)
     up_kept, up_sent, message3 = halve(
-        up_kept, among(up_sent, 3), needs=[arrived1, done], carried=messages[3:4]
+        up_kept, among(up_sent, 3), needs=[arrived1], carried=messages[3:4]
     )
     arrived3 = along(message3, 1)
-    down_kept, down_sent = halve(down_kept, among(down_sent, 1))
+    down_kept, down_sent = halve(down_kept, among(down_sent, 1), needs=[done])
     feedback, done = feedback_of(message1, arrived1, 1, feedback, True)
-    up_parts = split(up_kept, among(up_sent, 1), needs=[arrived2, done])
-    down_parts = split(down_kept, among(down_sent, 3))
+    up_parts = split(up_kept, among(up_sent, 1), needs=[arrived2])
+    down_parts = split(down_kept, among(down_sent, 3), needs=[done])
     grad_up = finish([among(up_parts[half], 0, half, -1) for half in range(2)])
     grad_down = finish([among(down_parts[half], 0, half, 1) for half in range(2)])
     feedback = feedback_of(message2, arrived2, 2, feedback)[0]

time: 107 us -> 112 us (1.047)
  Pallas kernels: 32.8 us -> 42.4 us
  waiting for transfers between devices: 39.3 us -> 34.8 us
  starting transfers between devices: 29.1 us -> 31.7 us
  local copies, waits for them, and re-layouts: 4.5 us -> 1.93 us
    pallas_call x18 -> x21, Pallas kernels: 32.8 us -> 42.4 us  [launch(): pl.pallas_call(wrapped, grid=grid, in_specs=[spec for _, spec in ins] + [...]
    ppermute x0 -> x2, starting transfers between devices: none -> 6.27 us  [the longest x1 4.98 us: body(): up_mine = lax.ppermute(pick_half(up), 'section', odd_to_even)]
    ppermute x8 -> x9, waiting for transfers between devices: 32.6 us -> 27 us  [among(): return lax.ppermute(value, both, pairs)]
    ppermute x10 -> x9, starting transfers between devices: 14.6 us -> 10.2 us  [along(): return lax.ppermute(value, 'section', pairs)]
    unnamed x18, local copies, waits for them, and re-layouts: 4.5 us -> 1.93 us
    ppermute x10 -> x9, waiting for transfers between devices: 6.64 us -> 7.74 us  [along(): return lax.ppermute(value, 'section', pairs)]
    ppermute x8 -> x9, starting transfers between devices: 14.5 us -> 15.2 us  [among(): return lax.ppermute(value, both, pairs)]
  transfers between devices with their start and end apart: 18 -> 20, of which waited for: 6 -> 5; matrix products, arithmetic and copies ran while one was open for 0% -> 0% of each run, Pallas kernels for 29% -> 35%
where the time goes in v5:
time: 112 us
  Pallas kernels  42.4 us (38%)
  waiting for transfers between devices  34.8 us (31%)
  starting transfers between devices  31.7 us (28%)
  local copies, waits for them, and re-layouts  1.93 us (2%)
    pallas_call x21, Pallas kernels, launch(): pl.pallas_call(wrapped, grid=grid, in_specs=[spec for _, spec in ins] + [...  42.4 us
    ppermute x9, waiting for transfers between devices, among(): return lax.ppermute(value, both, pairs)  27 us
    ppermute x9, starting transfers between devices, among(): return lax.ppermute(value, both, pairs)  15.2 us
    ppermute x9, starting transfers between devices, along(): return lax.ppermute(value, 'section', pairs)  10.2 us
    ppermute x9, waiting for transfers between devices, along(): return lax.ppermute(value, 'section', pairs)  7.74 us
    ppermute x1, starting transfers between devices, body(): up_mine = lax.ppermute(pick_half(up), 'section', odd_to_even)  4.98 us
  transfers between devices with their start and end apart: 20, of which 5 were waited for; matrix products, arithmetic and copies ran while one was open for 0% of the time, Pallas kernels for 35%

profile of v5, /device:TPU:1, one launch (start us, length us, event | category | flops | bytes accessed | tf_op | source)
XLA Modules:
  0.0 111.8 jit_solution(1376694625327886901)
XLA Ops:
  0.7 1.3 %pick_half.1 = bf16[3072,128]{1,0:T(8,128)(2,1)S(1)} custom-call(bf16[6144,128]{1,0:T(8,128)(2,1)} %bitcast.9.refs_0_.refs_3_), custom_call_target="tpu_custom_call" | custom-call | flops 1 | bytes 1 | tf_op jit(solution)/shard_map/pick_half/pallas_call | solution.py:45
  2.0 5.0 %collective-permute-start.3 = (bf16[3072,128]{1,0:T(8,128)(2,1)S(1)}, bf16[3072,128]{1,0:T(8,128)(2,1)S(1)}, u32[]{:S(2)}, u32[]{:S(2)}) collective-permute-start(bf16[3072,128]{1,0:T(8,128)(2,1)S(1)} %pick_half.1), channel_id=1, source_target_pairs={{8,16},{24,32},{40,48},{56,64},{72,80},{88,96},{104,112},{120,128}... | collective-permute-start | bytes 2359304 | tf_op jit(solution)/shard_map/ppermute | solution.py:414
  7.1 1.3 %collective-permute-start.2 = (bf16[6144,128]{1,0:T(8,128)(2,1)}, bf16[6144,128]{1,0:T(8,128)(2,1)S(1)}, u32[]{:S(2)}, u32[]{:S(2)}) collective-permute-start(bf16[6144,128]{1,0:T(8,128)(2,1)} %bitcast.9.refs_0_.refs_3_), channel_id=1, source_target_pairs={{0,8},{16,24},{32,40},{48,56},{64,72},{80,88},{96,104},{112,120},{... | collective-permute-start | bytes 4718600 | tf_op jit(solution)/shard_map/ppermute | solution.py:415
  8.4 1.9 %copy-done = s32[1,384,2048]{2,1,0:T(8,128)S(1)} copy-done((s32[1,384,2048]{2,1,0:T(8,128)S(1)}, s32[1,384,2048]{2,1,0:T(8,128)}, u32[]{:S(2)}) %copy-start) | copy-done | bytes 3145752
  10.3 4.0 %message.3 = (bf16[96,6144]{1,0:T(8,128)(2,1)S(1)}, f32[96,256]{1,0:T(8,128)S(1)}) custom-call(s32[384,2048]{1,0:T(8,128)S(1)} %bitcast.14, bf16[192,384]{1,0:T(8,128)(2,1)S(1)} %bitcast.23, bf16[32,6144]{1,0:T(8,128)(2,1)S(1)} %bitcast.20, s32[1,384]{1,0:T(1,128)S(1)} %copy-done.4), custom_call_target="tpu_custom_call" | custom-call | flops 1 | bytes 1 | tf_op jit(solution)/shard_map/message/pallas_call | solution.py:45
  14.3 2.8 %collective-permute-start.7 = (bf16[96,6144]{1,0:T(8,128)(2,1)S(1)}, bf16[96,6144]{1,0:T(8,128)(2,1)S(1)}, u32[]{:S(2)}, u32[]{:S(2)}) collective-permute-start(bf16[96,6144]{1,0:T(8,128)(2,1)S(1)} %get-tuple-element.31.refs_4_.refs_1_), channel_id=1, source_target_pairs={{0,8},{8,16},{16,24},{24,32},{32,40},{40,48},{48,56},{56,64},{64,7... | collective-permute-start | bytes 3538952 | tf_op jit(solution)/shard_map/ppermute | solution.py:399
  17.1 4.5 %message.4 = (bf16[144,6144]{1,0:T(8,128)(2,1)S(1)}, f32[144,256]{1,0:T(8,128)S(1)}) custom-call(s32[384,2048]{1,0:T(8,128)S(1)} %bitcast.15, bf16[192,384]{1,0:T(8,128)(2,1)S(1)} %bitcast.24, bf16[32,6144]{1,0:T(8,128)(2,1)S(1)} %bitcast.21, s32[1,384]{1,0:T(1,128)S(1)} %copy-done.4, bf16[96,6144]{1,0:T(8,128)(2,1)S(1)} %get-tuple-element.31.refs_4_.refs_1_), custom_call_target="tpu_custom_call" | custom-call | flops 1 | bytes 1 | tf_op jit(solution)/shard_map/message/pallas_call | solution.py:45
  22.6 4.3 %collective-permute-start = (f32[1,6144]{1,0:T(1,128)S(1)}, f32[1,6144]{1,0:T(1,128)S(1)}, u32[]{:S(2)}, u32[]{:S(2)}) collective-permute-start(f32[1,6144]{1,0:T(1,128)S(1)} %copy-done.6), channel_id=1, source_target_pairs={{0,248},{8,0},{16,8},{24,16},{32,24},{40,32},{48,40},{56,48},{64,5... | collective-permute-start | bytes 73736 | tf_op jit(solution)/shard_map/ppermute | solution.py:399
  26.9 4.5 %message.5 = (bf16[96,6144]{1,0:T(8,128)(2,1)S(1)}, bf16[48,6144]{1,0:T(8,128)(2,1)S(1)}, f32[144,256]{1,0:T(8,128)S(1)}) custom-call(s32[384,2048]{1,0:T(8,128)S(1)} %bitcast.16, bf16[192,384]{1,0:T(8,128)(2,1)S(1)} %bitcast.25, bf16[32,6144]{1,0:T(8,128)(2,1)S(1)} %bitcast.22, s32[1,384]{1,0:T(1,128)S(1)} %copy-done.4, ...), custom_call_target="tpu_custom_call" | custom-call | flops 1 | bytes 1 | tf_op jit(solution)/shard_map/message/pallas_call | solution.py:45
  31.4 4.5 %gradient.1.refs_8_.refs_0_ = bf16[384,6144]{1,0:T(8,128)(2,1)S(1)} custom-call(bf16[384,6144]{1,0:T(8,128)(2,1)S(1)} %bitcast.19, bf16[192,384]{1,0:T(8,128)(2,1)S(1)} %bitcast.26, bf16[96,6144]{1,0:T(8,128)(2,1)S(1)} %get-tuple-element.33.refs_2_.refs_3_.refs_6_), custom_call_target="tpu_custom_call" | custom-call | flops 1 | bytes 1 | tf_op jit(solution)/shard_map/gradient/pallas_call | solution.py:45
  35.9 2.5 %hidden.1.refs_0_ = bf16[384,6144]{1,0:T(8,128)(2,1)S(1)} custom-call(f32[1,6144]{1,0:T(1,128)S(1)} %collective-permute-done.refs_0_, bf16[96,6144]{1,0:T(8,128)(2,1)S(1)} %get-tuple-element.31.refs_4_.refs_1_, bf16[144,6144]{1,0:T(8,128)(2,1)S(1)} %get-tuple-element.32.refs_4_.refs_2_.refs_0_.refs_5_, ...), custom_call_target="tpu_custom_call" | custom-call | flops 1 | bytes 1 | tf_op jit(solution)/shard_map/hidden/pallas_call | solution.py:45
  38.4 1.4 %down.1 = (f32[384,128]{1,0:T(8,128)S(1)}, bf16[384,128]{1,0:T(8,128)(2,1)S(1)}) custom-call(bf16[384,6144]{1,0:T(8,128)(2,1)S(1)} %hidden.1.refs_0_, bf16[6144,128]{1,0:T(8,128)(2,1)S(1)} %collective-permute-done.1.refs_1_, bf16[6144,128]{1,0:T(8,128)(2,1)S(1)} %collective-permute-done.2.refs_2_.refs_1_, bf16[3072,128]{1,0:T(8,128)(2,1)S(1)} %collective-permute-done.4.refs_3_), custom_call_target="tpu_custom_call" | custom-call | flops 1 | bytes 1 | tf_op jit(solution)/shard_map/down/pallas_call | solution.py:45
  39.8 1.5 %back.1 = bf16[384,128]{1,0:T(8,128)(2,1)S(1)} custom-call(bf16[384,6144]{1,0:T(8,128)(2,1)S(1)} %gradient.1.refs_8_.refs_0_, bf16[6144,128]{1,0:T(8,128)(2,1)S(1)} %collective-permute-done.2.refs_2_.refs_1_, bf16[3072,128]{1,0:T(8,128)(2,1)S(1)} %hand_on.1.refs_2_, bf16[3072,128]{1,0:T(8,128)(2,1)S(1)} %collective-permute-done.4.refs_3_, ...), custom_call_target="tpu_custom_call" | custom-call | flops 1 | bytes 1 | tf_op jit(solution)/shard_map/back/pallas_call | solution.py:45
  41.3 2.7 %collective-permute-start.8 = (bf16[384,128]{1,0:T(8,128)(2,1)S(1)}, bf16[384,128]{1,0:T(8,128)(2,1)S(1)}, u32[]{:S(2)}, u32[]{:S(2)}) collective-permute-start(bf16[384,128]{1,0:T(8,128)(2,1)S(1)} %back.1), channel_id=1, source_target_pairs={{0,240},{8,248},{16,0},{24,8},{32,16},{40,24},{48,32},{56,40},{64,... | collective-permute-start | bytes 294920 | tf_op jit(solution)/shard_map/ppermute | solution.py:399
  44.2 2.1 %collective-permute-done.8.refs_4_.refs_2_ = bf16[384,128]{1,0:T(8,128)(2,1)S(1)} collective-permute-done((bf16[384,128]{1,0:T(8,128)(2,1)S(1)}, bf16[384,128]{1,0:T(8,128)(2,1)S(1)}, u32[]{:S(2)}, u32[]{:S(2)}) %collective-permute-start.8) | collective-permute-done | bytes 98336 | tf_op jit(solution)/shard_map/ppermute | solution.py:399
  46.2 5.7 %collective-permute-done.5.refs_1_ = bf16[384,128]{1,0:T(8,128)(2,1)S(1)} collective-permute-done((bf16[384,128]{1,0:T(8,128)(2,1)S(1)}, bf16[384,128]{1,0:T(8,128)(2,1)S(1)}, u32[]{:S(2)}, u32[]{:S(2)}) %collective-permute-start.5) | collective-permute-done | bytes 98336 | tf_op jit(solution)/shard_map/ppermute | solution.py:399
  51.9 1.0 grad_up.1
  53.0 1.1 grad_down.1
  54.6 2.5 %collective-permute-start.9 = (bf16[4,128,768]{2,1,0:T(8,128)(2,1)S(1)}, bf16[4,128,768]{2,1,0:T(8,128)(2,1)S(1)}, u32[]{:S(2)}, u32[]{:S(2)}) collective-permute-start(bf16[4,128,768]{2,1,0:T(8,128)(2,1)S(1)} %get-tuple-element.40), channel_id=1, source_target_pairs={{3,0},{2,1},{1,2},{0,3},{7,4},{6,5},{5,6},{4,7},{11,8},{10,9},{9,1... | collective-permute-start | bytes 2359304 | tf_op jit(solution)/shard_map/ppermute | solution.py:409
  57.1 3.5 %feedback.4 = (bf16[384,6144]{1,0:T(8,128)(2,1)}, f32[8,128]{1,0:T(8,128)S(1)}) custom-call(bf16[96,6144]{1,0:T(8,128)(2,1)S(1)} %collective-permute-done.7.refs_3_.refs_0_, bf16[96,6144]{1,0:T(8,128)(2,1)S(1)} %get-tuple-element.31.refs_4_.refs_1_, bf16[384,128]{1,0:T(8,128)(2,1)S(1)} %collective-permute-done.6.refs_2_, ...), custom_call_target="tpu_custom_call" | custom-call | flops 1 | bytes 1 | tf_op jit(solution)/shard_map/feedback/pallas_call | solution.py:45
  60.6 12.4 %collective-permute-done.13.refs_1_ = bf16[4,128,768]{2,1,0:T(8,128)(2,1)S(1)} collective-permute-done((bf16[4,128,768]{2,1,0:T(8,128)(2,1)S(1)}, bf16[4,128,768]{2,1,0:T(8,128)(2,1)S(1)}, u32[]{:S(2)}, u32[]{:S(2)}) %collective-permute-start.13) | collective-permute-done | bytes 786464 | tf_op jit(solution)/shard_map/ppermute | solution.py:409
  73.1 1.9 %collective-permute-start.14 = (bf16[2,128,768]{2,1,0:T(8,128)(2,1)S(1)}, bf16[2,128,768]{2,1,0:T(8,128)(2,1)S(1)}, u32[]{:S(2)}, u32[]{:S(2)}) collective-permute-start(bf16[2,128,768]{2,1,0:T(8,128)(2,1)S(1)} %get-tuple-element.51), channel_id=1, source_target_pairs={{3,0},{2,1},{1,2},{0,3},{7,4},{6,5},{5,6},{4,7},{11,8},{10,9},{9,1... | collective-permute-start | bytes 1179656 | tf_op jit(solution)/shard_map/ppermute | solution.py:409
  75.7 4.0 %feedback.5 = (bf16[384,6144]{1,0:T(8,128)(2,1)}, f32[8,128]{1,0:T(8,128)S(1)}) custom-call(bf16[144,6144]{1,0:T(8,128)(2,1)S(1)} %collective-permute-done.10.refs_2_.refs_0_, bf16[144,6144]{1,0:T(8,128)(2,1)S(1)} %get-tuple-element.41.refs_1_, bf16[384,128]{1,0:T(8,128)(2,1)S(1)} %collective-permute-done.6.refs_2_, ...), custom_call_target="tpu_custom_call", output_to_operand_aliasing={{0}: (4, {})} | custom-call | flops 1 | bytes 1 | tf_op jit(solution)/shard_map/feedback/pallas_call | solution.py:45
  79.8 3.9 %collective-permute-done.14.refs_1_ = bf16[2,128,768]{2,1,0:T(8,128)(2,1)S(1)} collective-permute-done((bf16[2,128,768]{2,1,0:T(8,128)(2,1)S(1)}, bf16[2,128,768]{2,1,0:T(8,128)(2,1)S(1)}, u32[]{:S(2)}, u32[]{:S(2)}) %collective-permute-start.14) | collective-permute-done | bytes 393248 | tf_op jit(solution)/shard_map/ppermute | solution.py:409
  83.9 2.4 %collective-permute-start.16 = (bf16[128,768]{1,0:T(8,128)(2,1)S(1)}, bf16[128,768]{1,0:T(8,128)(2,1)S(1)}, u32[]{:S(2)}, u32[]{:S(2)}) collective-permute-start(bf16[128,768]{1,0:T(8,128)(2,1)S(1)} %get-tuple-element.54), channel_id=1, source_target_pairs={{4,8},{5,9},{6,10},{7,11},{0,12},{1,13},{2,14},{3,15},{12,16},{13,... | collective-permute-start | bytes 589832 | tf_op jit(solution)/shard_map/ppermute | solution.py:409
  86.3 4.0 %collective-permute-start.18 = (bf16[128,768]{1,0:T(8,128)(2,1)S(1)}, bf16[128,768]{1,0:T(8,128)(2,1)S(1)}, u32[]{:S(2)}, u32[]{:S(2)}) collective-permute-start(bf16[128,768]{1,0:T(8,128)(2,1)S(1)} %get-tuple-element.57), channel_id=1, source_target_pairs={{0,248},{1,249},{2,250},{3,251},{4,252},{5,253},{6,254},{7,255},{8... | collective-permute-start | bytes 589832 | tf_op jit(solution)/shard_map/ppermute | solution.py:409
  90.3 2.6 %collective-permute-start.19 = (bf16[128,768]{1,0:T(8,128)(2,1)S(1)}, bf16[128,768]{1,0:T(8,128)(2,1)S(1)}, u32[]{:S(2)}, u32[]{:S(2)}) collective-permute-start(bf16[128,768]{1,0:T(8,128)(2,1)S(1)} %get-tuple-element.58), channel_id=1, source_target_pairs={{4,248},{5,249},{6,250},{7,251},{0,252},{1,253},{2,254},{3,255},{1... | collective-permute-start | bytes 589832 | tf_op jit(solution)/shard_map/ppermute | solution.py:409
  92.9 3.4 %feedback.6.refs_4_ = bf16[384,6144]{1,0:T(8,128)(2,1)} custom-call(bf16[96,6144]{1,0:T(8,128)(2,1)S(1)} %collective-permute-done.12.refs_0_.refs_2_, bf16[96,6144]{1,0:T(8,128)(2,1)S(1)} %get-tuple-element.43.refs_1_, bf16[384,128]{1,0:T(8,128)(2,1)S(1)} %collective-permute-done.6.refs_2_, ...), custom_call_target="tpu_custom_call", output_to_operand_aliasing={{}: (4, {})} | custom-call | flops 1 | bytes 1 | tf_op jit(solution)/shard_map/feedback/pallas_call | solution.py:45
  96.4 10.7 %collective-permute-done.16.refs_1_ = bf16[128,768]{1,0:T(8,128)(2,1)S(1)} collective-permute-done((bf16[128,768]{1,0:T(8,128)(2,1)S(1)}, bf16[128,768]{1,0:T(8,128)(2,1)S(1)}, u32[]{:S(2)}, u32[]{:S(2)}) %collective-permute-start.16) | collective-permute-done | bytes 196640 | tf_op jit(solution)/shard_map/ppermute | solution.py:409
  107.1 0.9 finish.2
  108.0 2.9 %feedback.7 = bf16[384,6144]{1,0:T(8,128)(2,1)} custom-call(bf16[48,6144]{1,0:T(8,128)(2,1)S(1)} %collective-permute-done.11.refs_0_, bf16[48,6144]{1,0:T(8,128)(2,1)S(1)} %get-tuple-element.42.refs_1_, bf16[384,128]{1,0:T(8,128)(2,1)S(1)} %collective-permute-done.6.refs_2_, ...), custom_call_target="tpu_custom_call", output_to_operand_aliasing={{}: (4, {})} | custom-call | flops 1 | bytes 1 | tf_op jit(solution)/shard_map/feedback/pallas_call | solution.py:45
  110.9 0.9 finish.3
  (48 shorter events, 2.9 us)
Async XLA Ops:
  0.6 6.3 %copy-start.5 = (bf16[1,6144,128]{2,1,0:T(8,128)(2,1)S(1)}, bf16[1,6144,128]{2,1,0:T(8,128)(2,1)}, u32[]{:S(2)}) copy-start(bf16[1,6144,128]{2,1,0:T(8,128)(2,1)} %param.16) | copy-start | bytes 4718596
  0.6 7.7 %copy-start.4 = (s32[1,384]{1,0:T(1,128)S(1)}, s32[1,384]{1,0:T(1,128)}, u32[]{:S(2)}) copy-start(s32[1,384]{1,0:T(1,128)} %refs_3_.5) | copy-start | bytes 4612
  0.7 7.7 %copy-start.1 = (bf16[1,32,6144]{2,1,0:T(8,128)(2,1)S(1)}, bf16[1,32,6144]{2,1,0:T(8,128)(2,1)}, u32[]{:S(2)}) copy-start(bf16[1,32,6144]{2,1,0:T(8,128)(2,1)} %param.11) | copy-start | bytes 1179652
  0.7 7.7 %copy-start.2 = (bf16[1,384,192]{1,2,0:T(8,128)(2,1)S(1)}, bf16[1,384,192]{1,2,0:T(8,128)(2,1)}, u32[]{:S(2)}) copy-start(bf16[1,384,192]{1,2,0:T(8,128)(2,1)} %param.10) | copy-start | bytes 442372
  2.0 19.7 %collective-permute-start.3 = (bf16[3072,128]{1,0:T(8,128)(2,1)S(1)}, bf16[3072,128]{1,0:T(8,128)(2,1)S(1)}, u32[]{:S(2)}, u32[]{:S(2)}) collective-permute-start(bf16[3072,128]{1,0:T(8,128)(2,1)S(1)} %pick_half.1), channel_id=1, source_target_pairs={{8,16},{24,32},{40,48},{56,64},{72,80},{88,96},{104,112},{120,128}... | collective-permute-start | bytes 2359304 | tf_op jit(solution)/shard_map/ppermute | solution.py:414
  7.0 31.4 %collective-permute-start.1 = (bf16[6144,128]{1,0:T(8,128)(2,1)S(1)}, bf16[6144,128]{1,0:T(8,128)(2,1)S(1)}, u32[]{:S(2)}, u32[]{:S(2)}) collective-permute-start(bf16[6144,128]{1,0:T(8,128)(2,1)S(1)} %bitcast.30), channel_id=1, source_target_pairs={{0,248},{8,0},{16,8},{24,16},{32,24},{40,32},{48,40},{56,48},{64,5... | collective-permute-start | bytes 4718600 | tf_op jit(solution)/shard_map/ppermute | solution.py:399
  7.1 31.4 %collective-permute-start.2 = (bf16[6144,128]{1,0:T(8,128)(2,1)}, bf16[6144,128]{1,0:T(8,128)(2,1)S(1)}, u32[]{:S(2)}, u32[]{:S(2)}) collective-permute-start(bf16[6144,128]{1,0:T(8,128)(2,1)} %bitcast.9.refs_0_.refs_3_), channel_id=1, source_target_pairs={{0,8},{16,24},{32,40},{48,56},{64,72},{80,88},{96,104},{112,120},{... | collective-permute-start | bytes 4718600 | tf_op jit(solution)/shard_map/ppermute | solution.py:415
  8.4 1.9 %copy-start = (s32[1,384,2048]{2,1,0:T(8,128)S(1)}, s32[1,384,2048]{2,1,0:T(8,128)}, u32[]{:S(2)}) copy-start(s32[1,384,2048]{2,1,0:T(8,128)} %param.9) | copy-start | bytes 9437188
  14.3 29.9 %collective-permute-start.7 = (bf16[96,6144]{1,0:T(8,128)(2,1)S(1)}, bf16[96,6144]{1,0:T(8,128)(2,1)S(1)}, u32[]{:S(2)}, u32[]{:S(2)}) collective-permute-start(bf16[96,6144]{1,0:T(8,128)(2,1)S(1)} %get-tuple-element.31.refs_4_.refs_1_), channel_id=1, source_target_pairs={{0,8},{8,16},{16,24},{24,32},{32,40},{40,48},{48,56},{56,64},{64,7... | collective-permute-start | bytes 3538952 | tf_op jit(solution)/shard_map/ppermute | solution.py:399
  17.1 14.3 %slice-start = ((s8[4718592]{0:T(1024)(128)(4,1)}), s8[4194304]{0:T(1024)(128)(4,1)S(1)}, s32[]{:S(2)}) async-start(s8[4718592]{0:T(1024)(128)(4,1)} %bitcast.17), calls=%async_computation | async-start | bytes 8388608
  21.7 0.9 copy-start.6
  21.7 9.7 %slice-start.1 = ((s8[4718592]{0:T(1024)(128)(4,1)}), s8[524288]{0:T(1024)(128)(4,1)S(1)}, s32[]{:S(2)}) async-start(s8[4718592]{0:T(1024)(128)(4,1)} %bitcast.17), calls=%async_computation.1 | async-start | bytes 1048576
  21.7 9.7 %copy-start.3 = (bf16[1,384,192]{1,2,0:T(8,128)(2,1)S(1)}, bf16[1,384,192]{1,2,0:T(8,128)(2,1)}, u32[]{:S(2)}) copy-start(bf16[1,384,192]{1,2,0:T(8,128)(2,1)} %param.14) | copy-start | bytes 442372
  21.7 16.7 %collective-permute-start.4 = (bf16[3072,128]{1,0:T(8,128)(2,1)S(1)}, bf16[3072,128]{1,0:T(8,128)(2,1)S(1)}, u32[]{:S(2)}, u32[]{:S(2)}) collective-permute-start(bf16[3072,128]{1,0:T(8,128)(2,1)S(1)} %hand_on.1.refs_2_), channel_id=1, source_target_pairs={{1,0},{0,1},{3,2},{2,3},{5,4},{4,5},{7,6},{6,7},{17,16},{16,17},{1... | collective-permute-start | bytes 2359304 | tf_op jit(solution)/shard_map/ppermute | solution.py:409
  22.6 13.3 %collective-permute-start = (f32[1,6144]{1,0:T(1,128)S(1)}, f32[1,6144]{1,0:T(1,128)S(1)}, u32[]{:S(2)}, u32[]{:S(2)}) collective-permute-start(f32[1,6144]{1,0:T(1,128)S(1)} %copy-done.6), channel_id=1, source_target_pairs={{0,248},{8,0},{16,8},{24,16},{32,24},{40,32},{48,40},{56,48},{64,5... | collective-permute-start | bytes 73736 | tf_op jit(solution)/shard_map/ppermute | solution.py:399
  41.3 4.9 %collective-permute-start.8 = (bf16[384,128]{1,0:T(8,128)(2,1)S(1)}, bf16[384,128]{1,0:T(8,128)(2,1)S(1)}, u32[]{:S(2)}, u32[]{:S(2)}) collective-permute-start(bf16[384,128]{1,0:T(8,128)(2,1)S(1)} %back.1), channel_id=1, source_target_pairs={{0,240},{8,248},{16,0},{24,8},{32,16},{40,24},{48,32},{56,40},{64,... | collective-permute-start | bytes 294920 | tf_op jit(solution)/shard_map/ppermute | solution.py:399
  44.0 2.2 %collective-permute-start.6 = (bf16[384,128]{1,0:T(8,128)(2,1)S(1)}, bf16[384,128]{1,0:T(8,128)(2,1)S(1)}, u32[]{:S(2)}, u32[]{:S(2)}) collective-permute-start(bf16[384,128]{1,0:T(8,128)(2,1)S(1)} %get-tuple-element.38.refs_4_), channel_id=1, source_target_pairs={{0,8},{8,16},{16,24},{24,32},{32,40},{40,48},{48,56},{56,64},{64,7... | collective-permute-start | bytes 294920 | tf_op jit(solution)/shard_map/ppermute | solution.py:399
  44.2 7.7 %collective-permute-start.5 = (bf16[384,128]{1,0:T(8,128)(2,1)S(1)}, bf16[384,128]{1,0:T(8,128)(2,1)S(1)}, u32[]{:S(2)}, u32[]{:S(2)}) collective-permute-start(bf16[384,128]{1,0:T(8,128)(2,1)S(1)} %get-tuple-element.38.refs_4_), channel_id=1, source_target_pairs={{0,16},{8,24},{16,32},{24,40},{32,48},{40,56},{48,64},{56,72},{64,... | collective-permute-start | bytes 294920 | tf_op jit(solution)/shard_map/ppermute | solution.py:399
  52.9 22.1 %collective-permute-start.10 = (bf16[144,6144]{1,0:T(8,128)(2,1)S(1)}, bf16[144,6144]{1,0:T(8,128)(2,1)S(1)}, u32[]{:S(2)}, u32[]{:S(2)}) collective-permute-start(bf16[144,6144]{1,0:T(8,128)(2,1)S(1)} %get-tuple-element.41.refs_1_), channel_id=1, source_target_pairs={{0,8},{8,16},{16,24},{24,32},{32,40},{40,48},{48,56},{56,64},{64,7... | collective-permute-start | bytes 5308424 | tf_op jit(solution)/shard_map/ppermute | solution.py:399
  54.1 18.9 %collective-permute-start.13 = (bf16[4,128,768]{2,1,0:T(8,128)(2,1)S(1)}, bf16[4,128,768]{2,1,0:T(8,128)(2,1)S(1)}, u32[]{:S(2)}, u32[]{:S(2)}) collective-permute-start(bf16[4,128,768]{2,1,0:T(8,128)(2,1)S(1)} %get-tuple-element.48), channel_id=1, source_target_pairs={{1,0},{0,1},{3,2},{2,3},{5,4},{4,5},{7,6},{6,7},{9,8},{8,9},{11,10... | collective-permute-start | bytes 2359304 | tf_op jit(solution)/shard_map/ppermute | solution.py:409
  54.6 20.4 %collective-permute-start.9 = (bf16[4,128,768]{2,1,0:T(8,128)(2,1)S(1)}, bf16[4,128,768]{2,1,0:T(8,128)(2,1)S(1)}, u32[]{:S(2)}, u32[]{:S(2)}) collective-permute-start(bf16[4,128,768]{2,1,0:T(8,128)(2,1)S(1)} %get-tuple-element.40), channel_id=1, source_target_pairs={{3,0},{2,1},{1,2},{0,3},{7,4},{6,5},{5,6},{4,7},{11,8},{10,9},{9,1... | collective-permute-start | bytes 2359304 | tf_op jit(solution)/shard_map/ppermute | solution.py:409
  57.1 29.2 %collective-permute-start.12 = (bf16[96,6144]{1,0:T(8,128)(2,1)S(1)}, bf16[96,6144]{1,0:T(8,128)(2,1)S(1)}, u32[]{:S(2)}, u32[]{:S(2)}) collective-permute-start(bf16[96,6144]{1,0:T(8,128)(2,1)S(1)} %get-tuple-element.43.refs_1_), channel_id=1, source_target_pairs={{0,8},{8,16},{16,24},{24,32},{32,40},{40,48},{48,56},{56,64},{64,7... | collective-permute-start | bytes 3538952 | tf_op jit(solution)/shard_map/ppermute | solution.py:399
  73.1 10.6 %collective-permute-start.14 = (bf16[2,128,768]{2,1,0:T(8,128)(2,1)S(1)}, bf16[2,128,768]{2,1,0:T(8,128)(2,1)S(1)}, u32[]{:S(2)}, u32[]{:S(2)}) collective-permute-start(bf16[2,128,768]{2,1,0:T(8,128)(2,1)S(1)} %get-tuple-element.51), channel_id=1, source_target_pairs={{3,0},{2,1},{1,2},{0,3},{7,4},{6,5},{5,6},{4,7},{11,8},{10,9},{9,1... | collective-permute-start | bytes 1179656 | tf_op jit(solution)/shard_map/ppermute | solution.py:409
  75.2 11.0 %collective-permute-start.17 = (bf16[2,128,768]{2,1,0:T(8,128)(2,1)S(1)}, bf16[2,128,768]{2,1,0:T(8,128)(2,1)S(1)}, u32[]{:S(2)}, u32[]{:S(2)}) collective-permute-start(bf16[2,128,768]{2,1,0:T(8,128)(2,1)S(1)} %get-tuple-element.56), channel_id=1, source_target_pairs={{1,0},{0,1},{3,2},{2,3},{5,4},{4,5},{7,6},{6,7},{9,8},{8,9},{11,10... | collective-permute-start | bytes 1179656 | tf_op jit(solution)/shard_map/ppermute | solution.py:409
  75.6 32.3 %collective-permute-start.11 = (bf16[48,6144]{1,0:T(8,128)(2,1)S(1)}, bf16[48,6144]{1,0:T(8,128)(2,1)S(1)}, u32[]{:S(2)}, u32[]{:S(2)}) collective-permute-start(bf16[48,6144]{1,0:T(8,128)(2,1)S(1)} %get-tuple-element.42.refs_1_), channel_id=1, source_target_pairs={{0,8},{8,16},{16,24},{24,32},{32,40},{40,48},{48,56},{56,64},{64,7... | collective-permute-start | bytes 1769480 | tf_op jit(solution)/shard_map/ppermute | solution.py:399
  83.8 12.6 %collective-permute-start.15 = (bf16[128,768]{1,0:T(8,128)(2,1)S(1)}, bf16[128,768]{1,0:T(8,128)(2,1)S(1)}, u32[]{:S(2)}, u32[]{:S(2)}) collective-permute-start(bf16[128,768]{1,0:T(8,128)(2,1)S(1)} %get-tuple-element.53), channel_id=1, source_target_pairs={{0,8},{1,9},{2,10},{3,11},{4,12},{5,13},{6,14},{7,15},{8,16},{9,17... | collective-permute-start | bytes 589832 | tf_op jit(solution)/shard_map/ppermute | solution.py:409
  83.9 23.2 %collective-permute-start.16 = (bf16[128,768]{1,0:T(8,128)(2,1)S(1)}, bf16[128,768]{1,0:T(8,128)(2,1)S(1)}, u32[]{:S(2)}, u32[]{:S(2)}) collective-permute-start(bf16[128,768]{1,0:T(8,128)(2,1)S(1)} %get-tuple-element.54), channel_id=1, source_target_pairs={{4,8},{5,9},{6,10},{7,11},{0,12},{1,13},{2,14},{3,15},{12,16},{13,... | collective-permute-start | bytes 589832 | tf_op jit(solution)/shard_map/ppermute | solution.py:409
  86.3 24.5 %collective-permute-start.18 = (bf16[128,768]{1,0:T(8,128)(2,1)S(1)}, bf16[128,768]{1,0:T(8,128)(2,1)S(1)}, u32[]{:S(2)}, u32[]{:S(2)}) collective-permute-start(bf16[128,768]{1,0:T(8,128)(2,1)S(1)} %get-tuple-element.57), channel_id=1, source_target_pairs={{0,248},{1,249},{2,250},{3,251},{4,252},{5,253},{6,254},{7,255},{8... | collective-permute-start | bytes 589832 | tf_op jit(solution)/shard_map/ppermute | solution.py:409
  90.3 20.6 %collective-permute-start.19 = (bf16[128,768]{1,0:T(8,128)(2,1)S(1)}, bf16[128,768]{1,0:T(8,128)(2,1)S(1)}, u32[]{:S(2)}, u32[]{:S(2)}) collective-permute-start(bf16[128,768]{1,0:T(8,128)(2,1)S(1)} %get-tuple-element.58), channel_id=1, source_target_pairs={{4,248},{5,249},{6,250},{7,251},{0,252},{1,253},{2,254},{3,255},{1... | collective-permute-start | bytes 589832 | tf_op jit(solution)/shard_map/ppermute | solution.py:409

commit v6 on v5

--- a/solution.py
+++ b/solution.py
@@ -15,9 +15,11 @@
 F32 = jnp.float32
 BF16 = jnp.bfloat16
 TILE = 48
-BLOCK = 384
+BLOCK = 768
+WORDS = BLOCK // 3
+CODES = BLOCK // 32
 HALF = D // 2
-SPANS = (96, 144, 96, 48)
+SPANS = (96, 48, 96, 96, 48)
 MIB = 1 << 20
 ROOT_2_PI = math.sqrt(2.0 / math.pi)
 VMEM = pl.BlockSpec(memory_space=pltpu.VMEM)
@@ -56,10 +58,6 @@
     )(*[value for value, _ in ins], *needs, *carried)
 
 
-def hand_on(value, after):
-    return launch(lambda: None, "hand_on", [], [], needs=[after], carried=[value], grant=1)[0]
-
-
 def lanes(shape):
     return lax.broadcasted_iota(jnp.int32, shape, 1)
 
@@ -68,10 +66,18 @@
     return pl.ds(pl.multiple_of(b * BLOCK, 128), BLOCK)
 
 
-def one_hot_blocks(b):
-    shape = (D // 32, BLOCK)
-    spot = lax.broadcasted_iota(jnp.int32, shape, 0) - b * (BLOCK // 32)
-    return (spot == lanes(shape) // 32).astype(F32).astype(BF16)
+def spreader():
+    shape = (32, BLOCK)
+    return (lax.broadcasted_iota(jnp.int32, shape, 0) == lanes(shape) // 32).astype(F32).astype(
+        BF16
+    )
+
+
+def turn_scales(scales_ref, turned_ref, rows):
+    padding = jnp.zeros((32 - CODES, TOK), F32)
+    for b in range(D // BLOCK):
+        part = scales_ref[b * CODES : (b + 1) * CODES, :].astype(F32)
+        turned_ref[b] = jnp.concatenate([part, padding], axis=0).T[rows].astype(BF16)
 
 
 def exact(left, right):
@@ -92,46 +98,49 @@
     *out_refs, stats_ref, turned_ref, picks_ref, pivot_ref, sum_ref, square_ref = refs
     count = stats_ref.shape[0]
     mine = slice(first, first + count)
-    turned_ref[...] = scales_ref[...].astype(F32).T[mine].astype(BF16)
+    turn_scales(scales_ref, turned_ref, mine)
+    spread = spreader()
     hits = lax.broadcasted_iota(jnp.int32, (32, TOK), 0) == ids_ref[...]
     picks_ref[...] = hits.astype(F32).T[mine].astype(BF16)
     chunks = chunks_of(out_refs)
 
     def decode(b, take):
-        spread = one_hot_blocks(b)
         base_block = base_ref[:, block_at(b)]
-        words_at = pl.ds(pl.multiple_of(b * 128, 128), 128)
         for ref, row, at, n in chunks:
             rows = slice(at, at + n)
-            scale = exact(turned_ref[rows, :], spread)
+            scale = exact(turned_ref[b, rows, :], spread)
             base = exact(picks_ref[rows, :], base_block)
-            words = codes_ref[first + at : first + at + n, words_at]
             lane = lanes((n, 128))
             values = []
-            for j in range(3):
-                spot = lane + 128 * j
-                word = jnp.take_along_axis(words, spot // 3, axis=1)
-                code = jnp.right_shift(word, (spot % 3) * 4) & 15
-                part = slice(j * 128, (j + 1) * 128)
-                value = base[:, part] + scale[:, part] * (code - 8).astype(F32)
-                value = value.astype(BF16)
-                ref[row : row + n, pl.ds(pl.multiple_of(b * BLOCK + j * 128, 128), 128)] = value
-                values.append(value.astype(F32))
+            for k in range(WORDS // 128):
+                words_at = pl.ds(pl.multiple_of(b * WORDS + k * 128, 128), 128)
+                words = codes_ref[first + at : first + at + n, words_at]
+                for j in range(3):
+                    spot = lane + 128 * j
+                    word = jnp.take_along_axis(words, spot // 3, axis=1)
+                    code = jnp.right_shift(word, (spot % 3) * 4) & 15
+                    tile = 3 * k + j
+                    part = slice(tile * 128, (tile + 1) * 128)
+                    value = base[:, part] + scale[:, part] * (code - 8).astype(F32)
+                    value = value.astype(BF16)
+                    to = pl.ds(pl.multiple_of(b * BLOCK + tile * 128, 128), 128)
+                    ref[row : row + n, to] = value
+                    values.append(value.astype(F32))
             take(rows, n, values)
 
     def begin(rows, n, values):
-        pivot = jnp.sum(values[0] + values[1] + values[2], axis=1, keepdims=True) / BLOCK
+        pivot = jnp.sum(sum(values), axis=1, keepdims=True) / BLOCK
         pivot = jnp.broadcast_to(pivot, (n, 128))
         pivot_ref[rows, :] = pivot
         away = [value - pivot for value in values]
-        sum_ref[rows, :] = away[0] + away[1] + away[2]
-        square_ref[rows, :] = away[0] * away[0] + away[1] * away[1] + away[2] * away[2]
+        sum_ref[rows, :] = sum(away)
+        square_ref[rows, :] = sum(v * v for v in away)
 
     def go_on(rows, n, values):
         pivot = pivot_ref[rows, :]
         away = [value - pivot for value in values]
-        sum_ref[rows, :] += away[0] + away[1] + away[2]
-        square_ref[rows, :] += away[0] * away[0] + away[1] * away[1] + away[2] * away[2]
+        sum_ref[rows, :] += sum(away)
+        square_ref[rows, :] += sum(v * v for v in away)
 
     def one_block(b, carry):
         decode(b, go_on)
@@ -152,20 +161,20 @@
         functools.partial(message_kernel, first), "message",
         [(value, VMEM) for value in (codes, scales, base, ids)],
         [(array((span, D), BF16), VMEM) for span in spans] + [(array((count, 256), F32), VMEM)],
-        [pltpu.VMEM((count, D // 32), BF16), pltpu.VMEM((count, 32), BF16)]
+        [pltpu.VMEM((D // BLOCK, count, 32), BF16), pltpu.VMEM((count, 32), BF16)]
         + [pltpu.VMEM((count, 128), F32)] * 3,
         **ties,
     )
 
 
 def gradient_kernel(codes_ref, scales_ref, out_ref, turned_ref):
-    turned_ref[...] = scales_ref[...].astype(F32).T.astype(BF16)
+    turn_scales(scales_ref, turned_ref, slice(0, TOK))
+    spread = spreader()
 
     def one_block(b, carry):
-        spread = one_hot_blocks(b)
         for at in range(0, TOK, 96):
             rows = slice(at, at + 96)
-            scale = exact(turned_ref[rows, :], spread)
+            scale = exact(turned_ref[b, rows, :], spread)
             codes = codes_ref[rows, block_at(b)].astype(F32)
             out_ref[rows, block_at(b)] = (scale * (codes - 128.0)).astype(BF16)
         return carry
@@ -176,37 +185,7 @@
 def make_gradient(codes, scales, **ties):
     return launch(
         gradient_kernel, "gradient", [(codes, VMEM), (scales, VMEM)],
-        [(array((TOK, D), BF16), VMEM)], [pltpu.VMEM((TOK, D // 32), BF16)], **ties,
-    )[0]
-
-
-def hidden_kernel(n, gain_ref, *refs):
-    message_refs, stats_refs, out_ref = refs[:n], refs[n:-1], refs[-1]
-    stats = [
-        (ref, row) for ref, row, _, rows in chunks_of(stats_refs) for row in range(row, row + rows, TILE)
-    ]
-    messages = [
-        (ref, row) for ref, row, _, rows in chunks_of(message_refs) for row in range(row, row + rows, TILE)
-    ]
-
-    def one_block(b, carry):
-        at = pl.ds(pl.multiple_of(b * 128, 128), 128)
-        gain = gain_ref[:, at]
-        for t, ((ref, row), (stats_ref, stats_row)) in enumerate(zip(messages, stats)):
-            x = ref[row : row + TILE, at].astype(F32)
-            mean = stats_ref[stats_row : stats_row + TILE, :128]
-            scale = stats_ref[stats_row : stats_row + TILE, 128:]
-            out_ref[t * TILE : (t + 1) * TILE, at] = (gain * (x - mean) * scale).astype(BF16)
-        return carry
-
-    lax.fori_loop(0, D // 128, one_block, 0)
-
-
-def make_hidden(messages, stats, gain, **ties):
-    return launch(
-        functools.partial(hidden_kernel, len(messages)), "hidden",
-        [(value, VMEM) for value in (gain, *messages, *stats)],
-        [(array((TOK, D), BF16), VMEM)], **ties,
+        [(array((TOK, D), BF16), VMEM)], [pltpu.VMEM((D // BLOCK, TOK, 32), BF16)], **ties,
     )[0]
 
 
@@ -214,32 +193,91 @@
     return jnp.tanh(ROOT_2_PI * (pre + 0.044715 * (pre * pre * pre)))
 
 
-def down_kernel(hidden_ref, weight_ref, pre_ref, act_ref):
-    pre = jnp.dot(hidden_ref[...], weight_ref[...], preferred_element_type=F32)
-    pre_ref[...] = pre
+def stage_down_kernel(weight_hbm, gain_ref, out_ref, rows_ref, sems):
+    copy = pltpu.make_async_copy(weight_hbm, out_ref.at[pl.ds(0, D)], sems.at[0])
+    copy.start()
+    for k in range(D // 128):
+        rows_ref[k : k + 1, :] = gain_ref[:, k * 128 : (k + 1) * 128]
+    gain = rows_ref[...]
+    high = gain.astype(BF16)
+    out_ref[D : D + D // 128, :] = high
+    out_ref[D + D // 128 :, :] = (gain - high.astype(F32)).astype(BF16)
+    copy.wait()
+
+
+def stage_down(weight, gain):
+    return launch(
+        stage_down_kernel, "stage_down", [(weight, ANY), (gain, VMEM)],
+        [(array((D + D // 64, R), BF16), VMEM)],
+        [pltpu.VMEM((D // 128, 128), F32), pltpu.SemaphoreType.DMA((1,))],
+    )[0]
+
+
+def down_kernel(n, weight_ref, *refs):
+    message_refs, stats_refs = refs[:n], refs[n:-4]
+    hidden_ref, pre_ref, act_ref, gain_ref = refs[-4:]
+    gain_ref[...] = weight_ref[D : D + D // 128, :].astype(F32) + weight_ref[
+        D + D // 128 :, :
+    ].astype(F32)
+    messages, stats = [
+        [(ref, at) for ref, row, _, rows in chunks_of(found) for at in range(row, row + rows, TILE)]
+        for found in (message_refs, stats_refs)
+    ]
+
+    def one_block(b, carry):
+        for c in range(BLOCK // 128):
+            at = pl.ds(pl.multiple_of(b * BLOCK + c * 128, 128), 128)
+            gain = gain_ref[pl.ds(b * (BLOCK // 128) + c, 1), :]
+            for t, ((ref, row), (stats_ref, stats_row)) in enumerate(zip(messages, stats)):
+                x = ref[row : row + TILE, at].astype(F32)
+                mean = stats_ref[stats_row : stats_row + TILE, :128]
+                scale = stats_ref[stats_row : stats_row + TILE, 128:]
+                hidden_ref[t * TILE : (t + 1) * TILE, at] = (gain * (x - mean) * scale).astype(
+                    BF16
+                )
+        weight = weight_ref[pl.ds(pl.multiple_of(b * BLOCK, 128), BLOCK), :]
+        pre_ref[...] += jnp.dot(
+            hidden_ref[:, block_at(b)], weight, preferred_element_type=F32
+        )
+        return carry
+
+    pre_ref[...] = jnp.zeros_like(pre_ref)
+    lax.fori_loop(0, D // BLOCK, one_block, 0)
+    pre = pre_ref[...]
     act_ref[...] = (0.5 * pre * (1.0 + tanh_of(pre))).astype(BF16)
 
 
-def project_down(hidden, weight, **ties):
-    return launch(
-        down_kernel, "down", [(hidden, VMEM), (weight, VMEM)],
-        [(array((TOK, R), F32), VMEM), (array((TOK, R), BF16), VMEM)], **ties,
-    )
-
-
-def pick_half_kernel(weight_ref, out_ref, sem):
+def project_down(messages, stats, staged, **ties):
+    return launch(
+        functools.partial(down_kernel, len(messages)), "down",
+        [(value, VMEM) for value in (staged, *messages, *stats)],
+        [
+            (array((TOK, D), BF16), VMEM), (array((TOK, R), F32), VMEM),
+            (array((TOK, R), BF16), VMEM),
+        ],
+        [pltpu.VMEM((D // 128, 128), F32)], **ties,
+    )
+
+
+def stage_kernel(weight_hbm, whole_ref, half_ref, sems):
     half = lax.rem(lax.axis_index("dp"), 2)
     rows = pl.ds(pl.multiple_of(half * HALF, HALF), HALF)
-    copy = pltpu.make_async_copy(weight_ref.at[rows], out_ref, sem.at[0])
-    copy.start()
-    copy.wait()
-
-
-def pick_half(weight):
-    return launch(
-        pick_half_kernel, "pick_half", [(weight, ANY)], [(array((HALF, R), BF16), VMEM)],
-        [pltpu.SemaphoreType.DMA((1,))],
-    )[0]
+    copies = [
+        pltpu.make_async_copy(weight_hbm.at[rows], half_ref, sems.at[0]),
+        pltpu.make_async_copy(weight_hbm, whole_ref, sems.at[1]),
+    ]
+    for copy in copies:
+        copy.start()
+    for copy in copies:
+        copy.wait()
+
+
+def stage(weight):
+    return launch(
+        stage_kernel, "stage", [(weight, ANY)],
+        [(array((D, R), BF16), VMEM), (array((HALF, R), BF16), VMEM)],
+        [pltpu.SemaphoreType.DMA((2,))],
+    )
 
 
 def back_kernel(grad_ref, chip_ref, mine_ref, other_ref, out_ref):
@@ -408,34 +446,31 @@
                 pairs.append((s * replicas + source, goal))
         return lax.ppermute(value, both, pairs)
 
-    up = w_up[0]
+    down_next = along(stage_down(w_down[0], norm_gain), -1)
+    up, up_half = stage(w_up[0])
     odd_to_even = [(s, (s + 1) % sections) for s in range(1, sections, 2)]
     even_to_odd = [(s, s + 1) for s in range(0, sections, 2)]
-    up_mine = lax.ppermute(pick_half(up), "section", odd_to_even)
+    up_mine = lax.ppermute(up_half, "section", odd_to_even)
     up_chip = lax.ppermute(up, "section", even_to_odd)
-    down_next = along(w_down[0], -1)
-    gain_next = along(norm_gain, -1)
+    up_other = among(up_mine, 1, stride=2)
 
     codes, base = forward_codes[0], stored_base[0]
     scales = forward_scales[0].T
     firsts = [sum(SPANS[:k]) for k in range(len(SPANS))]
     message0, stats0 = make_messages(codes, scales, base, sample_ids, 0, SPANS[:1])
-    message1, stats1 = make_messages(
-        codes, scales, base, sample_ids, firsts[1], SPANS[1:2], needs=[message0]
-    )
-    up_mine = hand_on(up_mine, message1)
-    up_other = among(up_mine, 1, stride=2)
-    *later, stats2 = make_messages(
-        codes, scales, base, sample_ids, firsts[2], SPANS[2:], needs=[message1]
-    )
-    messages = [message0, message1, *later]
+    *later, stats1 = make_messages(
+        codes, scales, base, sample_ids, firsts[1], SPANS[1:], needs=[message0]
+    )
+    messages = [message0, *later]
     gradient = make_gradient(backward_codes[0], backward_scales[0].T, needs=[later[0]])
-    hidden = make_hidden(messages, [stats0, stats1, stats2], gain_next, needs=[gradient])
-
-    pre_next, act_next = project_down(hidden, down_next, needs=[up_chip, up_other])
+
+    hidden, pre_next, act_next = project_down(
+        messages, [stats0, stats1], down_next, needs=[up_chip, gradient]
+    )
     act_before = along(act_next, 2)
     act_own = along(act_next, 1)
     arrived0 = along(messages[0], 1)
+    arrived1 = along(messages[1], 1)
     dact_before = project_back(
         gradient, up_chip, up_mine, up_other, needs=[act_next]
     )[0]
@@ -444,28 +479,29 @@
     def feedback_of(own, x, at, before, marked=False):
         return make_feedback(x, own, act_own, up, firsts[at], before, marked)
 
-    up_kept, up_sent, message1, message2 = partial_grad(
+    up_kept, up_sent, message2, message3 = partial_grad(
         read_act, "grad_up", (0, 1, 3, 2), gradient, act_before,
-        needs=[act_own, arrived0, dact_next], carried=messages[1:3],
-    )
-    arrived1 = along(message1, 1)
+        needs=[act_own, arrived0, arrived1, dact_next], carried=messages[2:4],
+    )
     arrived2 = along(message2, 1)
+    arrived3 = along(message3, 1)
     down_kept, down_sent = partial_grad(
         make_dpre, "grad_down", (0, 3, 1, 2), hidden, pre_next, dact_next,
     )
-    feedback, done = feedback_of(messages[0], arrived0, 0, None, True)
-    up_kept, up_sent, message3 = halve(
-        up_kept, among(up_sent, 3), needs=[arrived1], carried=messages[3:4]
-    )
-    arrived3 = along(message3, 1)
+    feedback = feedback_of(messages[0], arrived0, 0, None)[0]
+    feedback, done = feedback_of(messages[1], arrived1, 1, feedback, True)
+    up_kept, up_sent, message4 = halve(
+        up_kept, among(up_sent, 3), needs=[arrived2], carried=messages[4:5]
+    )
+    arrived4 = along(message4, 1)
     down_kept, down_sent = halve(down_kept, among(down_sent, 1), needs=[done])
-    feedback, done = feedback_of(message1, arrived1, 1, feedback, True)
-    up_parts = split(up_kept, among(up_sent, 1), needs=[arrived2])
+    feedback, done = feedback_of(message2, arrived2, 2, feedback, True)
+    up_parts = split(up_kept, among(up_sent, 1), needs=[arrived3])
     down_parts = split(down_kept, among(down_sent, 3), needs=[done])
     grad_up = finish([among(up_parts[half], 0, half, -1) for half in range(2)])
     grad_down = finish([among(down_parts[half], 0, half, 1) for half in range(2)])
-    feedback = feedback_of(message2, arrived2, 2, feedback)[0]
     feedback = feedback_of(message3, arrived3, 3, feedback)[0]
+    feedback = feedback_of(message4, arrived4, 4, feedback)[0]
     return (feedback[None], grad_down[None], grad_up[None])
 
 

time: 112 us -> 111 us (level)
  Pallas kernels: 42.4 us -> 30.9 us
  starting transfers between devices: 31.7 us -> 39.7 us
  local copies, waits for them, and re-layouts: 1.93 us -> 5.47 us
  waiting for transfers between devices: 34.8 us -> 33.5 us
    pallas_call x21 -> x20, Pallas kernels: 42.4 us -> 30.9 us  [launch(): pl.pallas_call(wrapped, grid=grid, in_specs=[spec for _, spec in ins] + [...]
    ppermute x9, starting transfers between devices: 10.2 us -> 19.2 us  [along(): return lax.ppermute(value, 'section', pairs)]
    ppermute x1, waiting for transfers between devices: 0.01 us -> 4.37 us  [body(): up_mine = lax.ppermute(up_half, 'section', odd_to_even)]
    unnamed x18 -> x20, local copies, waits for them, and re-layouts: 1.93 us -> 5.47 us
    ppermute x9, waiting for transfers between devices: 27 us -> 23.6 us  [among(): return lax.ppermute(value, both, pairs)]
    ppermute x9, waiting for transfers between devices: 7.74 us -> 5.57 us  [along(): return lax.ppermute(value, 'section', pairs)]
    ppermute x1, starting transfers between devices: 4.98 us -> 3.02 us  [body(): up_mine = lax.ppermute(up_half, 'section', odd_to_even)]
  transfers between devices with their start and end apart: 20 -> 20, of which waited for: 5 -> 6; matrix products, arithmetic and copies ran while one was open for 0% -> 0% of each run, Pallas kernels for 35% -> 26%
where the time goes in v6:
time: 111 us
  starting transfers between devices  39.7 us (36%)
  waiting for transfers between devices  33.5 us (30%)
  Pallas kernels  30.9 us (28%)
  local copies, waits for them, and re-layouts  5.47 us (5%)
    pallas_call x20, Pallas kernels, launch(): pl.pallas_call(wrapped, grid=grid, in_specs=[spec for _, spec in ins] + [...  30.9 us
    ppermute x9, waiting for transfers between devices, among(): return lax.ppermute(value, both, pairs)  23.6 us
    ppermute x9, starting transfers between devices, along(): return lax.ppermute(value, 'section', pairs)  19.2 us
    ppermute x9, starting transfers between devices, among(): return lax.ppermute(value, both, pairs)  16 us
    ppermute x9, waiting for transfers between devices, along(): return lax.ppermute(value, 'section', pairs)  5.57 us
    unnamed x20, local copies, waits for them, and re-layouts  5.47 us
    ppermute x1, waiting for transfers between devices, body(): up_mine = lax.ppermute(up_half, 'section', odd_to_even)  4.37 us
    ppermute x1, starting transfers between devices, body(): up_mine = lax.ppermute(up_half, 'section', odd_to_even)  3.02 us
  transfers between devices with their start and end apart: 20, of which 6 were waited for; matrix products, arithmetic and copies ran while one was open for 0% of the time, Pallas kernels for 26%

profile of v6, /device:TPU:1, one launch (start us, length us, event | category | flops | bytes accessed | tf_op | source)
XLA Modules:
  0.0 110.6 jit_solution(9148116618272901728)
XLA Ops:
  0.6 1.4 %copy-done.1 = bf16[1,6144,128]{2,1,0:T(8,128)(2,1)S(1)} copy-done((bf16[1,6144,128]{2,1,0:T(8,128)(2,1)S(1)}, bf16[1,6144,128]{2,1,0:T(8,128)(2,1)}, u32[]{:S(2)}) %copy-start.1) | copy-done | bytes 1572888
  2.9 3.3 %collective-permute-start = (bf16[6240,128]{1,0:T(8,128)(2,1)S(1)}, bf16[6240,128]{1,0:T(8,128)(2,1)S(1)}, u32[]{:S(2)}, u32[]{:S(2)}) collective-permute-start(bf16[6240,128]{1,0:T(8,128)(2,1)S(1)} %stage_down.1), channel_id=1, source_target_pairs={{0,248},{8,0},{16,8},{24,16},{32,24},{40,32},{48,40},{56,48},{64,5... | collective-permute-start | bytes 4792328 | tf_op jit(solution)/shard_map/ppermute | solution.py:437
  6.2 1.4 %copy-done.2 = bf16[1,6144,128]{2,1,0:T(8,128)(2,1)S(1)} copy-done((bf16[1,6144,128]{2,1,0:T(8,128)(2,1)S(1)}, bf16[1,6144,128]{2,1,0:T(8,128)(2,1)}, u32[]{:S(2)}) %copy-start.2) | copy-done | bytes 1572888
  7.8 1.6 %collective-permute-start.1 = (bf16[6144,128]{1,0:T(8,128)(2,1)S(1)}, bf16[6144,128]{1,0:T(8,128)(2,1)S(1)}, u32[]{:S(2)}, u32[]{:S(2)}) collective-permute-start(bf16[6144,128]{1,0:T(8,128)(2,1)S(1)} %get-tuple-element.41.refs_3_), channel_id=1, source_target_pairs={{0,8},{16,24},{32,40},{48,56},{64,72},{80,88},{96,104},{112,120},{... | collective-permute-start | bytes 4718600 | tf_op jit(solution)/shard_map/ppermute | solution.py:454
  9.4 3.0 %collective-permute-start.6 = (bf16[3072,128]{1,0:T(8,128)(2,1)S(1)}, bf16[3072,128]{1,0:T(8,128)(2,1)S(1)}, u32[]{:S(2)}, u32[]{:S(2)}) collective-permute-start(bf16[3072,128]{1,0:T(8,128)(2,1)S(1)} %get-tuple-element.43), channel_id=1, source_target_pairs={{8,16},{24,32},{40,48},{56,64},{72,80},{88,96},{104,112},{120,128}... | collective-permute-start | bytes 2359304 | tf_op jit(solution)/shard_map/ppermute | solution.py:453
  12.5 1.0 copy-done.3
  14.4 2.5 %message.2 = (bf16[96,6144]{1,0:T(8,128)(2,1)S(1)}, f32[96,256]{1,0:T(8,128)S(1)}) custom-call(s32[384,2048]{1,0:T(8,128)S(1)} %bitcast.14, bf16[192,384]{1,0:T(8,128)(2,1)S(1)} %bitcast.23, bf16[32,6144]{1,0:T(8,128)(2,1)S(1)} %bitcast.21, s32[1,384]{1,0:T(1,128)S(1)} %copy-done.7), custom_call_target="tpu_custom_call" | custom-call | flops 1 | bytes 1 | tf_op jit(solution)/shard_map/message/pallas_call | solution.py:47
  16.9 4.4 %collective-permute-done.6.refs_2_ = bf16[3072,128]{1,0:T(8,128)(2,1)S(1)} collective-permute-done((bf16[3072,128]{1,0:T(8,128)(2,1)S(1)}, bf16[3072,128]{1,0:T(8,128)(2,1)S(1)}, u32[]{:S(2)}, u32[]{:S(2)}) %collective-permute-start.6) | collective-permute-done | bytes 786464 | tf_op jit(solution)/shard_map/ppermute | solution.py:453
  22.0 5.3 %message.3 = (bf16[48,6144]{1,0:T(8,128)(2,1)S(1)}, bf16[96,6144]{1,0:T(8,128)(2,1)S(1)}, bf16[96,6144]{1,0:T(8,128)(2,1)S(1)}, bf16[48,6144]{1,0:T(8,128)(2,1)S(1)}, f32[288,256]{1,0:T(8,128)S(1)}) custom-call(s32[384,2048]{1,0:T(8,128)S(1)} %bitcast.15, bf16[192,384]{1,0:T(8,128)(2,1)S(1)} %bitcast.24, bf16[32,6144]{1,0:T(8,128)(2,1)S(1)} %bitcast.22, ...), custom_call_target="tpu_custom_call" | custom-call | flops 1 | bytes 1 | tf_op jit(solution)/shard_map/message/pallas_call | solution.py:47
  27.3 5.2 %collective-permute-start.5 = (bf16[48,6144]{1,0:T(8,128)(2,1)S(1)}, bf16[48,6144]{1,0:T(8,128)(2,1)S(1)}, u32[]{:S(2)}, u32[]{:S(2)}) collective-permute-start(bf16[48,6144]{1,0:T(8,128)(2,1)S(1)} %get-tuple-element.35.refs_2_.refs_1_), channel_id=1, source_target_pairs={{0,8},{8,16},{16,24},{24,32},{32,40},{40,48},{48,56},{56,64},{64,7... | collective-permute-start | bytes 1769480 | tf_op jit(solution)/shard_map/ppermute | solution.py:437
  32.5 2.6 %gradient.1.refs_9_.refs_0_ = bf16[384,6144]{1,0:T(8,128)(2,1)S(1)} custom-call(bf16[384,6144]{1,0:T(8,128)(2,1)S(1)} %bitcast.18, bf16[192,384]{1,0:T(8,128)(2,1)S(1)} %bitcast.25, bf16[48,6144]{1,0:T(8,128)(2,1)S(1)} %get-tuple-element.35.refs_2_.refs_1_), custom_call_target="tpu_custom_call" | custom-call | flops 1 | bytes 1 | tf_op jit(solution)/shard_map/gradient/pallas_call | solution.py:47
  35.1 5.4 %down.1 = (bf16[384,6144]{1,0:T(8,128)(2,1)S(1)}, f32[384,128]{1,0:T(8,128)S(1)}, bf16[384,128]{1,0:T(8,128)(2,1)S(1)}) custom-call(bf16[6240,128]{1,0:T(8,128)(2,1)S(1)} %collective-permute-done.refs_0_, bf16[96,6144]{1,0:T(8,128)(2,1)S(1)} %get-tuple-element.34.refs_4_.refs_1_, bf16[48,6144]{1,0:T(8,128)(2,1)S(1)} %get-tuple-element.35.refs_2_.refs_1_, ...), custom_call_target="tpu_custom_call" | custom-call | flops 1 | bytes 1 | tf_op jit(solution)/shard_map/down/pallas_call | solution.py:47
  40.5 1.5 %back.1 = bf16[384,128]{1,0:T(8,128)(2,1)S(1)} custom-call(bf16[384,6144]{1,0:T(8,128)(2,1)S(1)} %gradient.1.refs_9_.refs_0_, bf16[6144,128]{1,0:T(8,128)(2,1)S(1)} %collective-permute-done.1.refs_8_.refs_1_, bf16[3072,128]{1,0:T(8,128)(2,1)S(1)} %collective-permute-done.6.refs_2_, bf16[3072,128]{1,0:T(8,128)(2,1)S(1)} %collective-permute-done.7.refs_3_, ...), custom_call_target="tpu_custom_call" | custom-call | flops 1 | bytes 1 | tf_op jit(solution)/shard_map/back/pallas_call | solution.py:47
  42.0 9.2 %collective-permute-start.8 = (bf16[384,128]{1,0:T(8,128)(2,1)S(1)}, bf16[384,128]{1,0:T(8,128)(2,1)S(1)}, u32[]{:S(2)}, u32[]{:S(2)}) collective-permute-start(bf16[384,128]{1,0:T(8,128)(2,1)S(1)} %back.1), channel_id=1, source_target_pairs={{0,240},{8,248},{16,0},{24,8},{32,16},{40,24},{48,32},{56,40},{64,... | collective-permute-start | bytes 294920 | tf_op jit(solution)/shard_map/ppermute | solution.py:437
  51.2 1.6 %collective-permute-done.8.refs_5_.refs_2_ = bf16[384,128]{1,0:T(8,128)(2,1)S(1)} collective-permute-done((bf16[384,128]{1,0:T(8,128)(2,1)S(1)}, bf16[384,128]{1,0:T(8,128)(2,1)S(1)}, u32[]{:S(2)}, u32[]{:S(2)}) %collective-permute-start.8) | collective-permute-done | bytes 98336 | tf_op jit(solution)/shard_map/ppermute | solution.py:437
  52.9 3.9 %collective-permute-done.2.refs_1_ = bf16[384,128]{1,0:T(8,128)(2,1)S(1)} collective-permute-done((bf16[384,128]{1,0:T(8,128)(2,1)S(1)}, bf16[384,128]{1,0:T(8,128)(2,1)S(1)}, u32[]{:S(2)}, u32[]{:S(2)}) %collective-permute-start.2) | collective-permute-done | bytes 98336 | tf_op jit(solution)/shard_map/ppermute | solution.py:437
  56.8 1.0 grad_up.1
  58.1 1.1 grad_down.1
  59.5 2.5 %collective-permute-start.9 = (bf16[4,128,768]{2,1,0:T(8,128)(2,1)S(1)}, bf16[4,128,768]{2,1,0:T(8,128)(2,1)S(1)}, u32[]{:S(2)}, u32[]{:S(2)}) collective-permute-start(bf16[4,128,768]{2,1,0:T(8,128)(2,1)S(1)} %get-tuple-element.45), channel_id=1, source_target_pairs={{3,0},{2,1},{1,2},{0,3},{7,4},{6,5},{5,6},{4,7},{11,8},{10,9},{9,1... | collective-permute-start | bytes 2359304 | tf_op jit(solution)/shard_map/ppermute | solution.py:447
  62.1 2.0 %feedback.5.refs_4_ = bf16[384,6144]{1,0:T(8,128)(2,1)} custom-call(bf16[96,6144]{1,0:T(8,128)(2,1)S(1)} %collective-permute-done.4.refs_3_.refs_0_, bf16[96,6144]{1,0:T(8,128)(2,1)S(1)} %get-tuple-element.34.refs_4_.refs_1_, bf16[384,128]{1,0:T(8,128)(2,1)S(1)} %collective-permute-done.3.refs_2_, bf16[6144,128]{1,0:T(8,128)(2,1)S(1)} %get-tuple-element.41.refs_3_), custom_call_target="tpu_custom_call" | custom-call | flops 1 | bytes 1 | tf_op jit(solution)/shard_map/feedback/pallas_call | solution.py:47
  64.1 1.5 %feedback.6 = (bf16[384,6144]{1,0:T(8,128)(2,1)}, f32[8,128]{1,0:T(8,128)S(1)}) custom-call(bf16[48,6144]{1,0:T(8,128)(2,1)S(1)} %collective-permute-done.5.refs_4_.refs_0_, bf16[48,6144]{1,0:T(8,128)(2,1)S(1)} %get-tuple-element.35.refs_2_.refs_1_, bf16[384,128]{1,0:T(8,128)(2,1)S(1)} %collective-permute-done.3.refs_2_, ...), custom_call_target="tpu_custom_call", output_to_operand_aliasing={{0}: (4, {})} | custom-call | flops 1 | bytes 1 | tf_op jit(solution)/shard_map/feedback/pallas_call | solution.py:47
  65.6 10.9 %collective-permute-done.13.refs_1_ = bf16[4,128,768]{2,1,0:T(8,128)(2,1)S(1)} collective-permute-done((bf16[4,128,768]{2,1,0:T(8,128)(2,1)S(1)}, bf16[4,128,768]{2,1,0:T(8,128)(2,1)S(1)}, u32[]{:S(2)}, u32[]{:S(2)}) %collective-permute-start.13) | collective-permute-done | bytes 786464 | tf_op jit(solution)/shard_map/ppermute | solution.py:447
  76.7 1.9 %collective-permute-start.14 = (bf16[2,128,768]{2,1,0:T(8,128)(2,1)S(1)}, bf16[2,128,768]{2,1,0:T(8,128)(2,1)S(1)}, u32[]{:S(2)}, u32[]{:S(2)}) collective-permute-start(bf16[2,128,768]{2,1,0:T(8,128)(2,1)S(1)} %get-tuple-element.57), channel_id=1, source_target_pairs={{3,0},{2,1},{1,2},{0,3},{7,4},{6,5},{5,6},{4,7},{11,8},{10,9},{9,1... | collective-permute-start | bytes 1179656 | tf_op jit(solution)/shard_map/ppermute | solution.py:447
  79.2 1.0 collective-permute-start.11
  80.2 2.1 %feedback.7 = (bf16[384,6144]{1,0:T(8,128)(2,1)}, f32[8,128]{1,0:T(8,128)S(1)}) custom-call(bf16[96,6144]{1,0:T(8,128)(2,1)S(1)} %collective-permute-done.10.refs_2_.refs_0_, bf16[96,6144]{1,0:T(8,128)(2,1)S(1)} %get-tuple-element.46.refs_1_, bf16[384,128]{1,0:T(8,128)(2,1)S(1)} %collective-permute-done.3.refs_2_, ...), custom_call_target="tpu_custom_call", output_to_operand_aliasing={{0}: (4, {})} | custom-call | flops 1 | bytes 1 | tf_op jit(solution)/shard_map/feedback/pallas_call | solution.py:47
  82.3 3.7 %collective-permute-done.14.refs_1_ = bf16[2,128,768]{2,1,0:T(8,128)(2,1)S(1)} collective-permute-done((bf16[2,128,768]{2,1,0:T(8,128)(2,1)S(1)}, bf16[2,128,768]{2,1,0:T(8,128)(2,1)S(1)}, u32[]{:S(2)}, u32[]{:S(2)}) %collective-permute-start.14) | collective-permute-done | bytes 393248 | tf_op jit(solution)/shard_map/ppermute | solution.py:447
  86.0 1.4 %collective-permute-start.15 = (bf16[128,768]{1,0:T(8,128)(2,1)S(1)}, bf16[128,768]{1,0:T(8,128)(2,1)S(1)}, u32[]{:S(2)}, u32[]{:S(2)}) collective-permute-start(bf16[128,768]{1,0:T(8,128)(2,1)S(1)} %get-tuple-element.59), channel_id=1, source_target_pairs={{0,8},{1,9},{2,10},{3,11},{4,12},{5,13},{6,14},{7,15},{8,16},{9,17... | collective-permute-start | bytes 589832 | tf_op jit(solution)/shard_map/ppermute | solution.py:447
  87.4 2.4 %collective-permute-start.16 = (bf16[128,768]{1,0:T(8,128)(2,1)S(1)}, bf16[128,768]{1,0:T(8,128)(2,1)S(1)}, u32[]{:S(2)}, u32[]{:S(2)}) collective-permute-start(bf16[128,768]{1,0:T(8,128)(2,1)S(1)} %get-tuple-element.60), channel_id=1, source_target_pairs={{4,8},{5,9},{6,10},{7,11},{0,12},{1,13},{2,14},{3,15},{12,16},{13,... | collective-permute-start | bytes 589832 | tf_op jit(solution)/shard_map/ppermute | solution.py:447
  90.6 5.6 %collective-permute-start.19 = (bf16[128,768]{1,0:T(8,128)(2,1)S(1)}, bf16[128,768]{1,0:T(8,128)(2,1)S(1)}, u32[]{:S(2)}, u32[]{:S(2)}) collective-permute-start(bf16[128,768]{1,0:T(8,128)(2,1)S(1)} %get-tuple-element.64), channel_id=1, source_target_pairs={{4,248},{5,249},{6,250},{7,251},{0,252},{1,253},{2,254},{3,255},{1... | collective-permute-start | bytes 589832 | tf_op jit(solution)/shard_map/ppermute | solution.py:447
  96.2 2.0 %feedback.8.refs_4_ = bf16[384,6144]{1,0:T(8,128)(2,1)} custom-call(bf16[96,6144]{1,0:T(8,128)(2,1)S(1)} %collective-permute-done.12.refs_0_.refs_2_, bf16[96,6144]{1,0:T(8,128)(2,1)S(1)} %get-tuple-element.48.refs_1_, bf16[384,128]{1,0:T(8,128)(2,1)S(1)} %collective-permute-done.3.refs_2_, ...), custom_call_target="tpu_custom_call", output_to_operand_aliasing={{}: (4, {})} | custom-call | flops 1 | bytes 1 | tf_op jit(solution)/shard_map/feedback/pallas_call | solution.py:47
  98.3 8.9 %collective-permute-done.16.refs_1_ = bf16[128,768]{1,0:T(8,128)(2,1)S(1)} collective-permute-done((bf16[128,768]{1,0:T(8,128)(2,1)S(1)}, bf16[128,768]{1,0:T(8,128)(2,1)S(1)}, u32[]{:S(2)}, u32[]{:S(2)}) %collective-permute-start.16) | collective-permute-done | bytes 196640 | tf_op jit(solution)/shard_map/ppermute | solution.py:447
  108.1 1.5 %feedback.9 = bf16[384,6144]{1,0:T(8,128)(2,1)} custom-call(bf16[48,6144]{1,0:T(8,128)(2,1)S(1)} %collective-permute-done.11.refs_0_, bf16[48,6144]{1,0:T(8,128)(2,1)S(1)} %get-tuple-element.47.refs_1_, bf16[384,128]{1,0:T(8,128)(2,1)S(1)} %collective-permute-done.3.refs_2_, ...), custom_call_target="tpu_custom_call", output_to_operand_aliasing={{}: (4, {})} | custom-call | flops 1 | bytes 1 | tf_op jit(solution)/shard_map/feedback/pallas_call | solution.py:47
  (49 shorter events, 6.8 us)
Async XLA Ops:
  0.6 1.4 %copy-start.1 = (bf16[1,6144,128]{2,1,0:T(8,128)(2,1)S(1)}, bf16[1,6144,128]{2,1,0:T(8,128)(2,1)}, u32[]{:S(2)}) copy-start(bf16[1,6144,128]{2,1,0:T(8,128)(2,1)} %param.16) | copy-start | bytes 4718596
  2.0 0.7 copy-start.6
  2.8 9.7 %copy-start = (s32[1,384,2048]{2,1,0:T(8,128)S(1)}, s32[1,384,2048]{2,1,0:T(8,128)}, u32[]{:S(2)}) copy-start(s32[1,384,2048]{2,1,0:T(8,128)} %param.9) | copy-start | bytes 9437188
  2.9 9.5 %copy-start.7 = (s32[1,384]{1,0:T(1,128)S(1)}, s32[1,384]{1,0:T(1,128)}, u32[]{:S(2)}) copy-start(s32[1,384]{1,0:T(1,128)} %refs_3_.3) | copy-start | bytes 4612
  2.9 32.2 %collective-permute-start = (bf16[6240,128]{1,0:T(8,128)(2,1)S(1)}, bf16[6240,128]{1,0:T(8,128)(2,1)S(1)}, u32[]{:S(2)}, u32[]{:S(2)}) collective-permute-start(bf16[6240,128]{1,0:T(8,128)(2,1)S(1)} %stage_down.1), channel_id=1, source_target_pairs={{0,248},{8,0},{16,8},{24,16},{32,24},{40,32},{48,40},{56,48},{64,5... | collective-permute-start | bytes 4792328 | tf_op jit(solution)/shard_map/ppermute | solution.py:437
  6.2 1.4 %copy-start.2 = (bf16[1,6144,128]{2,1,0:T(8,128)(2,1)S(1)}, bf16[1,6144,128]{2,1,0:T(8,128)(2,1)}, u32[]{:S(2)}) copy-start(bf16[1,6144,128]{2,1,0:T(8,128)(2,1)} %param.17) | copy-start | bytes 4718596
  7.7 24.9 %slice-start = ((s8[4718592]{0:T(1024)(128)(4,1)}), s8[4194304]{0:T(1024)(128)(4,1)S(1)}, s32[]{:S(2)}) async-start(s8[4718592]{0:T(1024)(128)(4,1)} %bitcast.16), calls=%async_computation | async-start | bytes 8388608
  7.8 27.3 %collective-permute-start.1 = (bf16[6144,128]{1,0:T(8,128)(2,1)S(1)}, bf16[6144,128]{1,0:T(8,128)(2,1)S(1)}, u32[]{:S(2)}, u32[]{:S(2)}) collective-permute-start(bf16[6144,128]{1,0:T(8,128)(2,1)S(1)} %get-tuple-element.41.refs_3_), channel_id=1, source_target_pairs={{0,8},{16,24},{32,40},{48,56},{64,72},{80,88},{96,104},{112,120},{... | collective-permute-start | bytes 4718600 | tf_op jit(solution)/shard_map/ppermute | solution.py:454
  9.4 11.9 %collective-permute-start.6 = (bf16[3072,128]{1,0:T(8,128)(2,1)S(1)}, bf16[3072,128]{1,0:T(8,128)(2,1)S(1)}, u32[]{:S(2)}, u32[]{:S(2)}) collective-permute-start(bf16[3072,128]{1,0:T(8,128)(2,1)S(1)} %get-tuple-element.43), channel_id=1, source_target_pairs={{8,16},{24,32},{40,48},{56,64},{72,80},{88,96},{104,112},{120,128}... | collective-permute-start | bytes 2359304 | tf_op jit(solution)/shard_map/ppermute | solution.py:453
  12.5 1.0 copy-start.3
  13.5 0.9 copy-start.4
  14.4 18.2 %slice-start.1 = ((s8[4718592]{0:T(1024)(128)(4,1)}), s8[524288]{0:T(1024)(128)(4,1)S(1)}, s32[]{:S(2)}) async-start(s8[4718592]{0:T(1024)(128)(4,1)} %bitcast.16), calls=%async_computation.1 | async-start | bytes 1048576
  16.8 15.7 %copy-start.5 = (bf16[1,384,192]{1,2,0:T(8,128)(2,1)S(1)}, bf16[1,384,192]{1,2,0:T(8,128)(2,1)}, u32[]{:S(2)}) copy-start(bf16[1,384,192]{1,2,0:T(8,128)(2,1)} %param.14) | copy-start | bytes 442372
  16.8 34.4 %collective-permute-start.4 = (bf16[96,6144]{1,0:T(8,128)(2,1)S(1)}, bf16[96,6144]{1,0:T(8,128)(2,1)S(1)}, u32[]{:S(2)}, u32[]{:S(2)}) collective-permute-start(bf16[96,6144]{1,0:T(8,128)(2,1)S(1)} %get-tuple-element.34.refs_4_.refs_1_), channel_id=1, source_target_pairs={{0,8},{8,16},{16,24},{24,32},{32,40},{40,48},{48,56},{56,64},{64,7... | collective-permute-start | bytes 3538952 | tf_op jit(solution)/shard_map/ppermute | solution.py:437
  21.3 19.2 %collective-permute-start.7 = (bf16[3072,128]{1,0:T(8,128)(2,1)S(1)}, bf16[3072,128]{1,0:T(8,128)(2,1)S(1)}, u32[]{:S(2)}, u32[]{:S(2)}) collective-permute-start(bf16[3072,128]{1,0:T(8,128)(2,1)S(1)} %collective-permute-done.6.refs_2_), channel_id=1, source_target_pairs={{1,0},{0,1},{3,2},{2,3},{5,4},{4,5},{7,6},{6,7},{17,16},{16,17},{1... | collective-permute-start | bytes 2359304 | tf_op jit(solution)/shard_map/ppermute | solution.py:447
  27.3 23.9 %collective-permute-start.5 = (bf16[48,6144]{1,0:T(8,128)(2,1)S(1)}, bf16[48,6144]{1,0:T(8,128)(2,1)S(1)}, u32[]{:S(2)}, u32[]{:S(2)}) collective-permute-start(bf16[48,6144]{1,0:T(8,128)(2,1)S(1)} %get-tuple-element.35.refs_2_.refs_1_), channel_id=1, source_target_pairs={{0,8},{8,16},{16,24},{24,32},{32,40},{40,48},{48,56},{56,64},{64,7... | collective-permute-start | bytes 1769480 | tf_op jit(solution)/shard_map/ppermute | solution.py:437
  42.0 10.9 %collective-permute-start.8 = (bf16[384,128]{1,0:T(8,128)(2,1)S(1)}, bf16[384,128]{1,0:T(8,128)(2,1)S(1)}, u32[]{:S(2)}, u32[]{:S(2)}) collective-permute-start(bf16[384,128]{1,0:T(8,128)(2,1)S(1)} %back.1), channel_id=1, source_target_pairs={{0,240},{8,248},{16,0},{24,8},{32,16},{40,24},{48,32},{56,40},{64,... | collective-permute-start | bytes 294920 | tf_op jit(solution)/shard_map/ppermute | solution.py:437
  51.2 5.6 %collective-permute-start.2 = (bf16[384,128]{1,0:T(8,128)(2,1)S(1)}, bf16[384,128]{1,0:T(8,128)(2,1)S(1)}, u32[]{:S(2)}, u32[]{:S(2)}) collective-permute-start(bf16[384,128]{1,0:T(8,128)(2,1)S(1)} %get-tuple-element.42.refs_4_), channel_id=1, source_target_pairs={{0,16},{8,24},{16,32},{24,40},{32,48},{40,56},{48,64},{56,72},{64,... | collective-permute-start | bytes 294920 | tf_op jit(solution)/shard_map/ppermute | solution.py:437
  51.2 5.6 %collective-permute-start.3 = (bf16[384,128]{1,0:T(8,128)(2,1)S(1)}, bf16[384,128]{1,0:T(8,128)(2,1)S(1)}, u32[]{:S(2)}, u32[]{:S(2)}) collective-permute-start(bf16[384,128]{1,0:T(8,128)(2,1)S(1)} %get-tuple-element.42.refs_4_), channel_id=1, source_target_pairs={{0,8},{8,16},{16,24},{24,32},{32,40},{40,48},{48,56},{56,64},{64,7... | collective-permute-start | bytes 294920 | tf_op jit(solution)/shard_map/ppermute | solution.py:437
  57.8 20.8 %collective-permute-start.10 = (bf16[96,6144]{1,0:T(8,128)(2,1)S(1)}, bf16[96,6144]{1,0:T(8,128)(2,1)S(1)}, u32[]{:S(2)}, u32[]{:S(2)}) collective-permute-start(bf16[96,6144]{1,0:T(8,128)(2,1)S(1)} %get-tuple-element.46.refs_1_), channel_id=1, source_target_pairs={{0,8},{8,16},{16,24},{24,32},{32,40},{40,48},{48,56},{56,64},{64,7... | collective-permute-start | bytes 3538952 | tf_op jit(solution)/shard_map/ppermute | solution.py:437
  59.2 17.4 %collective-permute-start.13 = (bf16[4,128,768]{2,1,0:T(8,128)(2,1)S(1)}, bf16[4,128,768]{2,1,0:T(8,128)(2,1)S(1)}, u32[]{:S(2)}, u32[]{:S(2)}) collective-permute-start(bf16[4,128,768]{2,1,0:T(8,128)(2,1)S(1)} %get-tuple-element.54), channel_id=1, source_target_pairs={{1,0},{0,1},{3,2},{2,3},{5,4},{4,5},{7,6},{6,7},{9,8},{8,9},{11,10... | collective-permute-start | bytes 2359304 | tf_op jit(solution)/shard_map/ppermute | solution.py:447
  59.5 19.1 %collective-permute-start.9 = (bf16[4,128,768]{2,1,0:T(8,128)(2,1)S(1)}, bf16[4,128,768]{2,1,0:T(8,128)(2,1)S(1)}, u32[]{:S(2)}, u32[]{:S(2)}) collective-permute-start(bf16[4,128,768]{2,1,0:T(8,128)(2,1)S(1)} %get-tuple-element.45), channel_id=1, source_target_pairs={{3,0},{2,1},{1,2},{0,3},{7,4},{6,5},{5,6},{4,7},{11,8},{10,9},{9,1... | collective-permute-start | bytes 2359304 | tf_op jit(solution)/shard_map/ppermute | solution.py:447
  62.0 27.8 %collective-permute-start.12 = (bf16[96,6144]{1,0:T(8,128)(2,1)S(1)}, bf16[96,6144]{1,0:T(8,128)(2,1)S(1)}, u32[]{:S(2)}, u32[]{:S(2)}) collective-permute-start(bf16[96,6144]{1,0:T(8,128)(2,1)S(1)} %get-tuple-element.48.refs_1_), channel_id=1, source_target_pairs={{0,8},{8,16},{16,24},{24,32},{32,40},{40,48},{48,56},{56,64},{64,7... | collective-permute-start | bytes 3538952 | tf_op jit(solution)/shard_map/ppermute | solution.py:437
  76.7 9.3 %collective-permute-start.14 = (bf16[2,128,768]{2,1,0:T(8,128)(2,1)S(1)}, bf16[2,128,768]{2,1,0:T(8,128)(2,1)S(1)}, u32[]{:S(2)}, u32[]{:S(2)}) collective-permute-start(bf16[2,128,768]{2,1,0:T(8,128)(2,1)S(1)} %get-tuple-element.57), channel_id=1, source_target_pairs={{3,0},{2,1},{1,2},{0,3},{7,4},{6,5},{5,6},{4,7},{11,8},{10,9},{9,1... | collective-permute-start | bytes 1179656 | tf_op jit(solution)/shard_map/ppermute | solution.py:447
  78.8 11.0 %collective-permute-start.17 = (bf16[2,128,768]{2,1,0:T(8,128)(2,1)S(1)}, bf16[2,128,768]{2,1,0:T(8,128)(2,1)S(1)}, u32[]{:S(2)}, u32[]{:S(2)}) collective-permute-start(bf16[2,128,768]{2,1,0:T(8,128)(2,1)S(1)} %get-tuple-element.62), channel_id=1, source_target_pairs={{1,0},{0,1},{3,2},{2,3},{5,4},{4,5},{7,6},{6,7},{9,8},{8,9},{11,10... | collective-permute-start | bytes 1179656 | tf_op jit(solution)/shard_map/ppermute | solution.py:447
  79.2 28.9 %collective-permute-start.11 = (bf16[48,6144]{1,0:T(8,128)(2,1)S(1)}, bf16[48,6144]{1,0:T(8,128)(2,1)S(1)}, u32[]{:S(2)}, u32[]{:S(2)}) collective-permute-start(bf16[48,6144]{1,0:T(8,128)(2,1)S(1)} %get-tuple-element.47.refs_1_), channel_id=1, source_target_pairs={{0,8},{8,16},{16,24},{24,32},{32,40},{40,48},{48,56},{56,64},{64,7... | collective-permute-start | bytes 1769480 | tf_op jit(solution)/shard_map/ppermute | solution.py:437
  86.0 12.2 %collective-permute-start.15 = (bf16[128,768]{1,0:T(8,128)(2,1)S(1)}, bf16[128,768]{1,0:T(8,128)(2,1)S(1)}, u32[]{:S(2)}, u32[]{:S(2)}) collective-permute-start(bf16[128,768]{1,0:T(8,128)(2,1)S(1)} %get-tuple-element.59), channel_id=1, source_target_pairs={{0,8},{1,9},{2,10},{3,11},{4,12},{5,13},{6,14},{7,15},{8,16},{9,17... | collective-permute-start | bytes 589832 | tf_op jit(solution)/shard_map/ppermute | solution.py:447
  87.4 19.8 %collective-permute-start.16 = (bf16[128,768]{1,0:T(8,128)(2,1)S(1)}, bf16[128,768]{1,0:T(8,128)(2,1)S(1)}, u32[]{:S(2)}, u32[]{:S(2)}) collective-permute-start(bf16[128,768]{1,0:T(8,128)(2,1)S(1)} %get-tuple-element.60), channel_id=1, source_target_pairs={{4,8},{5,9},{6,10},{7,11},{0,12},{1,13},{2,14},{3,15},{12,16},{13,... | collective-permute-start | bytes 589832 | tf_op jit(solution)/shard_map/ppermute | solution.py:447
  89.9 19.7 %collective-permute-start.18 = (bf16[128,768]{1,0:T(8,128)(2,1)S(1)}, bf16[128,768]{1,0:T(8,128)(2,1)S(1)}, u32[]{:S(2)}, u32[]{:S(2)}) collective-permute-start(bf16[128,768]{1,0:T(8,128)(2,1)S(1)} %get-tuple-element.63), channel_id=1, source_target_pairs={{0,248},{1,249},{2,250},{3,251},{4,252},{5,253},{6,254},{7,255},{8... | collective-permute-start | bytes 589832 | tf_op jit(solution)/shard_map/ppermute | solution.py:447
  90.6 19.0 %collective-permute-start.19 = (bf16[128,768]{1,0:T(8,128)(2,1)S(1)}, bf16[128,768]{1,0:T(8,128)(2,1)S(1)}, u32[]{:S(2)}, u32[]{:S(2)}) collective-permute-start(bf16[128,768]{1,0:T(8,128)(2,1)S(1)} %get-tuple-element.64), channel_id=1, source_target_pairs={{4,248},{5,249},{6,250},{7,251},{0,252},{1,253},{2,254},{3,255},{1... | collective-permute-start | bytes 589832 | tf_op jit(solution)/shard_map/ppermute | solution.py:447

commit v7 on v6

--- a/solution.py
+++ b/solution.py
@@ -18,8 +18,7 @@
 BLOCK = 768
 WORDS = BLOCK // 3
 CODES = BLOCK // 32
-HALF = D // 2
-SPANS = (96, 48, 96, 96, 48)
+SPANS = (96, 144, 96, 48)
 MIB = 1 << 20
 ROOT_2_PI = math.sqrt(2.0 / math.pi)
 VMEM = pl.BlockSpec(memory_space=pltpu.VMEM)
@@ -193,106 +192,57 @@
     return jnp.tanh(ROOT_2_PI * (pre + 0.044715 * (pre * pre * pre)))
 
 
-def stage_down_kernel(weight_hbm, gain_ref, out_ref, rows_ref, sems):
-    copy = pltpu.make_async_copy(weight_hbm, out_ref.at[pl.ds(0, D)], sems.at[0])
-    copy.start()
-    for k in range(D // 128):
-        rows_ref[k : k + 1, :] = gain_ref[:, k * 128 : (k + 1) * 128]
-    gain = rows_ref[...]
-    high = gain.astype(BF16)
-    out_ref[D : D + D // 128, :] = high
-    out_ref[D + D // 128 :, :] = (gain - high.astype(F32)).astype(BF16)
-    copy.wait()
-
-
-def stage_down(weight, gain):
-    return launch(
-        stage_down_kernel, "stage_down", [(weight, ANY), (gain, VMEM)],
-        [(array((D + D // 64, R), BF16), VMEM)],
-        [pltpu.VMEM((D // 128, 128), F32), pltpu.SemaphoreType.DMA((1,))],
-    )[0]
-
-
-def down_kernel(n, weight_ref, *refs):
-    message_refs, stats_refs = refs[:n], refs[n:-4]
-    hidden_ref, pre_ref, act_ref, gain_ref = refs[-4:]
-    gain_ref[...] = weight_ref[D : D + D // 128, :].astype(F32) + weight_ref[
-        D + D // 128 :, :
-    ].astype(F32)
+def hidden_kernel(n, gain_ref, *refs):
+    message_refs, stats_refs, out_ref = refs[:n], refs[n:-1], refs[-1]
     messages, stats = [
         [(ref, at) for ref, row, _, rows in chunks_of(found) for at in range(row, row + rows, TILE)]
         for found in (message_refs, stats_refs)
     ]
-
-    def one_block(b, carry):
-        for c in range(BLOCK // 128):
-            at = pl.ds(pl.multiple_of(b * BLOCK + c * 128, 128), 128)
-            gain = gain_ref[pl.ds(b * (BLOCK // 128) + c, 1), :]
-            for t, ((ref, row), (stats_ref, stats_row)) in enumerate(zip(messages, stats)):
+    for t, ((ref, row), (stats_ref, stats_row)) in enumerate(zip(messages, stats)):
+        rows = slice(stats_row, stats_row + TILE)
+        mean, scale = stats_ref[rows, :128], stats_ref[rows, 128:]
+
+        def one_block(b, carry, ref=ref, row=row, t=t, mean=mean, scale=scale):
+            for c in range(BLOCK // 128):
+                at = pl.ds(pl.multiple_of(b * BLOCK + c * 128, 128), 128)
                 x = ref[row : row + TILE, at].astype(F32)
-                mean = stats_ref[stats_row : stats_row + TILE, :128]
-                scale = stats_ref[stats_row : stats_row + TILE, 128:]
-                hidden_ref[t * TILE : (t + 1) * TILE, at] = (gain * (x - mean) * scale).astype(
-                    BF16
-                )
-        weight = weight_ref[pl.ds(pl.multiple_of(b * BLOCK, 128), BLOCK), :]
-        pre_ref[...] += jnp.dot(
-            hidden_ref[:, block_at(b)], weight, preferred_element_type=F32
-        )
-        return carry
-
-    pre_ref[...] = jnp.zeros_like(pre_ref)
-    lax.fori_loop(0, D // BLOCK, one_block, 0)
-    pre = pre_ref[...]
+                value = gain_ref[:, at] * (x - mean) * scale
+                out_ref[t * TILE : (t + 1) * TILE, at] = value.astype(BF16)
+            return carry
+
+        lax.fori_loop(0, D // BLOCK, one_block, 0)
+
+
+def make_hidden(messages, stats, gain, **ties):
+    return launch(
+        functools.partial(hidden_kernel, len(messages)), "hidden",
+        [(value, VMEM) for value in (gain, *messages, *stats)],
+        [(array((TOK, D), BF16), VMEM)], **ties,
+    )[0]
+
+
+def down_kernel(hidden_ref, weight_ref, pre_ref, act_ref):
+    pre = jnp.dot(hidden_ref[...], weight_ref[...], preferred_element_type=F32)
+    pre_ref[...] = pre
     act_ref[...] = (0.5 * pre * (1.0 + tanh_of(pre))).astype(BF16)
 
 
-def project_down(messages, stats, staged, **ties):
-    return launch(
-        functools.partial(down_kernel, len(messages)), "down",
-        [(value, VMEM) for value in (staged, *messages, *stats)],
-        [
-            (array((TOK, D), BF16), VMEM), (array((TOK, R), F32), VMEM),
-            (array((TOK, R), BF16), VMEM),
-        ],
-        [pltpu.VMEM((D // 128, 128), F32)], **ties,
-    )
-
-
-def stage_kernel(weight_hbm, whole_ref, half_ref, sems):
-    half = lax.rem(lax.axis_index("dp"), 2)
-    rows = pl.ds(pl.multiple_of(half * HALF, HALF), HALF)
-    copies = [
-        pltpu.make_async_copy(weight_hbm.at[rows], half_ref, sems.at[0]),
-        pltpu.make_async_copy(weight_hbm, whole_ref, sems.at[1]),
-    ]
-    for copy in copies:
-        copy.start()
-    for copy in copies:
-        copy.wait()
-
-
-def stage(weight):
-    return launch(
-        stage_kernel, "stage", [(weight, ANY)],
-        [(array((D, R), BF16), VMEM), (array((HALF, R), BF16), VMEM)],
-        [pltpu.SemaphoreType.DMA((2,))],
-    )
-
-
-def back_kernel(grad_ref, chip_ref, mine_ref, other_ref, out_ref):
-    half = lax.rem(lax.axis_index("dp"), 2)
-    total = jnp.zeros((TOK, R), F32)
-    for where, part_ref in ((half, mine_ref), (1 - half, other_ref)):
-        at = pl.ds(pl.multiple_of(where * HALF, HALF), HALF)
-        weight = part_ref[...] + chip_ref[at, :]
-        total += jnp.dot(grad_ref[:, at], weight, preferred_element_type=F32)
-    out_ref[...] = total.astype(BF16)
-
-
-def project_back(grad, chip, mine, other, **ties):
-    return launch(
-        back_kernel, "back", [(value, VMEM) for value in (grad, chip, mine, other)],
+def project_down(hidden, weight, **ties):
+    return launch(
+        down_kernel, "down", [(hidden, VMEM), (weight, VMEM)],
+        [(array((TOK, R), F32), VMEM), (array((TOK, R), BF16), VMEM)], **ties,
+    )
+
+
+def back_kernel(grad_ref, weight_ref, out_ref):
+    out_ref[...] = jnp.dot(
+        grad_ref[...], weight_ref[...], preferred_element_type=F32
+    ).astype(BF16)
+
+
+def project_back(grad, weight, **ties):
+    return launch(
+        back_kernel, "back", [(grad, VMEM), (weight, VMEM)],
         [(array((TOK, R), BF16), VMEM)], **ties,
     )
 
@@ -436,9 +386,9 @@
         pairs = [(s, (s + distance) % sections) for s in range(sections)]
         return lax.ppermute(value, "section", pairs)
 
-    def among(value, flip_x, flip_y=0, section_step=0, stride=1):
+    def among(value, flip_x, flip_y=0, section_step=0):
         pairs = []
-        for s in range(0, sections, stride):
+        for s in range(sections):
             for d in range(replicas):
                 y, x = divmod(d, across)
                 source = (y ^ flip_y) * across + (x ^ flip_x)
@@ -446,13 +396,10 @@
                 pairs.append((s * replicas + source, goal))
         return lax.ppermute(value, both, pairs)
 
-    down_next = along(stage_down(w_down[0], norm_gain), -1)
-    up, up_half = stage(w_up[0])
-    odd_to_even = [(s, (s + 1) % sections) for s in range(1, sections, 2)]
-    even_to_odd = [(s, s + 1) for s in range(0, sections, 2)]
-    up_mine = lax.ppermute(up_half, "section", odd_to_even)
-    up_chip = lax.ppermute(up, "section", even_to_odd)
-    up_other = among(up_mine, 1, stride=2)
+    up = w_up[0]
+    up_before = along(up, 1)
+    down_next = along(w_down[0], -1)
+    gain_next = along(norm_gain, -1)
 
     codes, base = forward_codes[0], stored_base[0]
     scales = forward_scales[0].T
@@ -464,44 +411,39 @@
     messages = [message0, *later]
     gradient = make_gradient(backward_codes[0], backward_scales[0].T, needs=[later[0]])
 
-    hidden, pre_next, act_next = project_down(
-        messages, [stats0, stats1], down_next, needs=[up_chip, gradient]
-    )
+    hidden = make_hidden(messages, [stats0, stats1], gain_next, needs=[gradient])
+    pre_next, act_next = project_down(hidden, down_next, needs=[up_before])
     act_before = along(act_next, 2)
     act_own = along(act_next, 1)
     arrived0 = along(messages[0], 1)
-    arrived1 = along(messages[1], 1)
-    dact_before = project_back(
-        gradient, up_chip, up_mine, up_other, needs=[act_next]
-    )[0]
+    dact_before = project_back(gradient, up_before, needs=[act_next])[0]
     dact_next = along(dact_before, -2)
 
     def feedback_of(own, x, at, before, marked=False):
         return make_feedback(x, own, act_own, up, firsts[at], before, marked)
 
-    up_kept, up_sent, message2, message3 = partial_grad(
+    up_kept, up_sent, message1, message2 = partial_grad(
         read_act, "grad_up", (0, 1, 3, 2), gradient, act_before,
-        needs=[act_own, arrived0, arrived1, dact_next], carried=messages[2:4],
-    )
+        needs=[act_own, arrived0, dact_next], carried=messages[1:3],
+    )
+    arrived1 = along(message1, 1)
     arrived2 = along(message2, 1)
-    arrived3 = along(message3, 1)
     down_kept, down_sent = partial_grad(
         make_dpre, "grad_down", (0, 3, 1, 2), hidden, pre_next, dact_next,
     )
-    feedback = feedback_of(messages[0], arrived0, 0, None)[0]
-    feedback, done = feedback_of(messages[1], arrived1, 1, feedback, True)
-    up_kept, up_sent, message4 = halve(
-        up_kept, among(up_sent, 3), needs=[arrived2], carried=messages[4:5]
-    )
-    arrived4 = along(message4, 1)
+    feedback, done = feedback_of(messages[0], arrived0, 0, None, True)
+    up_kept, up_sent, message3 = halve(
+        up_kept, among(up_sent, 3), needs=[arrived1], carried=messages[3:4]
+    )
+    arrived3 = along(message3, 1)
     down_kept, down_sent = halve(down_kept, among(down_sent, 1), needs=[done])
-    feedback, done = feedback_of(message2, arrived2, 2, feedback, True)
-    up_parts = split(up_kept, among(up_sent, 1), needs=[arrived3])
+    feedback, done = feedback_of(message1, arrived1, 1, feedback, True)
+    up_parts = split(up_kept, among(up_sent, 1), needs=[arrived2])
     down_parts = split(down_kept, among(down_sent, 3), needs=[done])
     grad_up = finish([among(up_parts[half], 0, half, -1) for half in range(2)])
     grad_down = finish([among(down_parts[half], 0, half, 1) for half in range(2)])
+    feedback = feedback_of(message2, arrived2, 2, feedback)[0]
     feedback = feedback_of(message3, arrived3, 3, feedback)[0]
-    feedback = feedback_of(message4, arrived4, 4, feedback)[0]
     return (feedback[None], grad_down[None], grad_up[None])
 
 

time: 111 us -> 104 us (0.937)
  starting transfers between devices: 39.7 us -> 29.4 us
  waiting for transfers between devices: 33.5 us -> 40.9 us
  Pallas kernels: 30.9 us -> 28.1 us
    ppermute x9 -> x8, waiting for transfers between devices: 23.6 us -> 29.5 us  [among(): return lax.ppermute(value, both, pairs)]
    ppermute x9 -> x10, waiting for transfers between devices: 5.57 us -> 11.4 us  [along(): return lax.ppermute(value, 'section', pairs)]
    ppermute x2 -> x0, starting transfers between devices: 4.58 us -> none  [the longest x1 3.02 us: body(): up_mine = lax.ppermute(up_half, 'section', odd_to_even)]
    ppermute x2 -> x0, waiting for transfers between devices: 4.37 us -> none  [the longest x1 4.37 us: body(): up_mine = lax.ppermute(up_half, 'section', odd_to_even)]
    ppermute x9 -> x10, starting transfers between devices: 19.2 us -> 16.2 us  [along(): return lax.ppermute(value, 'section', pairs)]
    pallas_call x20 -> x18, Pallas kernels: 30.9 us -> 28.1 us  [launch(): pl.pallas_call(wrapped, grid=grid, in_specs=[spec for _, spec in ins] + [...]
    ppermute x9 -> x8, starting transfers between devices: 16 us -> 13.3 us  [among(): return lax.ppermute(value, both, pairs)]
    unnamed x20 -> x18, local copies, waits for them, and re-layouts: 5.47 us -> 4.5 us
  transfers between devices with their start and end apart: 20 -> 18, of which waited for: 6 -> 7; matrix products, arithmetic and copies ran while one was open for 0% -> 0% of each run, Pallas kernels for 26% -> 25%
where the time goes in v7:
time: 104 us
  waiting for transfers between devices  40.9 us (39%)
  starting transfers between devices  29.4 us (28%)
  Pallas kernels  28.1 us (27%)
  local copies, waits for them, and re-layouts  4.5 us (4%)
    ppermute x8, waiting for transfers between devices, among(): return lax.ppermute(value, both, pairs)  29.5 us
    pallas_call x18, Pallas kernels, launch(): pl.pallas_call(wrapped, grid=grid, in_specs=[spec for _, spec in ins] + [...  28.1 us
    ppermute x10, starting transfers between devices, along(): return lax.ppermute(value, 'section', pairs)  16.2 us
    ppermute x8, starting transfers between devices, among(): return lax.ppermute(value, both, pairs)  13.3 us
    ppermute x10, waiting for transfers between devices, along(): return lax.ppermute(value, 'section', pairs)  11.4 us
    unnamed x18, local copies, waits for them, and re-layouts  4.5 us
  transfers between devices with their start and end apart: 18, of which 7 were waited for; matrix products, arithmetic and copies ran while one was open for 0% of the time, Pallas kernels for 25%

profile of v7, /device:TPU:1, one launch (start us, length us, event | category | flops | bytes accessed | tf_op | source)
XLA Modules:
  0.0 103.8 jit_solution(3708809176995250690)
XLA Ops:
  0.6 3.3 %collective-permute-start.1 = (bf16[6144,128]{1,0:T(8,128)(2,1)}, bf16[6144,128]{1,0:T(8,128)(2,1)S(1)}, u32[]{:S(2)}, u32[]{:S(2)}) collective-permute-start(bf16[6144,128]{1,0:T(8,128)(2,1)} %bitcast.30), channel_id=1, source_target_pairs={{0,248},{8,0},{16,8},{24,16},{32,24},{40,32},{48,40},{56,48},{64,5... | collective-permute-start | bytes 4718600 | tf_op jit(solution)/shard_map/ppermute | solution.py:387
  4.0 1.9 %copy-done.1 = s32[1,384,2048]{2,1,0:T(8,128)S(1)} copy-done((s32[1,384,2048]{2,1,0:T(8,128)S(1)}, s32[1,384,2048]{2,1,0:T(8,128)}, u32[]{:S(2)}) %copy-start.1) | copy-done | bytes 3145752
  5.8 1.0 copy-done.3
  6.8 0.9 copy-done.4
  8.4 2.5 %message.2 = (bf16[96,6144]{1,0:T(8,128)(2,1)S(1)}, f32[96,256]{1,0:T(8,128)S(1)}) custom-call(s32[384,2048]{1,0:T(8,128)S(1)} %bitcast.19, bf16[192,384]{1,0:T(8,128)(2,1)S(1)} %bitcast.24, bf16[32,6144]{1,0:T(8,128)(2,1)S(1)} %bitcast.22, s32[1,384]{1,0:T(1,128)S(1)} %copy-done.6), custom_call_target="tpu_custom_call" | custom-call | flops 1 | bytes 1 | tf_op jit(solution)/shard_map/message/pallas_call | solution.py:46
  11.3 4.4 %collective-permute-start = (f32[1,6144]{1,0:T(1,128)S(1)}, f32[1,6144]{1,0:T(1,128)S(1)}, u32[]{:S(2)}, u32[]{:S(2)}) collective-permute-start(f32[1,6144]{1,0:T(1,128)S(1)} %copy-done.8), channel_id=1, source_target_pairs={{0,248},{8,0},{16,8},{24,16},{32,24},{40,32},{48,40},{56,48},{64,5... | collective-permute-start | bytes 73736 | tf_op jit(solution)/shard_map/ppermute | solution.py:387
  15.7 5.4 %message.3 = (bf16[144,6144]{1,0:T(8,128)(2,1)S(1)}, bf16[96,6144]{1,0:T(8,128)(2,1)S(1)}, bf16[48,6144]{1,0:T(8,128)(2,1)S(1)}, f32[288,256]{1,0:T(8,128)S(1)}) custom-call(s32[384,2048]{1,0:T(8,128)S(1)} %bitcast.20, bf16[192,384]{1,0:T(8,128)(2,1)S(1)} %bitcast.25, bf16[32,6144]{1,0:T(8,128)(2,1)S(1)} %bitcast.23, s32[1,384]{1,0:T(1,128)S(1)} %copy-done.7, ...), custom_call_target="tpu_custom_call" | custom-call | flops 1 | bytes 1 | tf_op jit(solution)/shard_map/message/pallas_call | solution.py:46
  21.1 2.6 %gradient.1.refs_7_.refs_0_ = bf16[384,6144]{1,0:T(8,128)(2,1)S(1)} custom-call(bf16[384,6144]{1,0:T(8,128)(2,1)S(1)} %bitcast.21, bf16[192,384]{1,0:T(8,128)(2,1)S(1)} %bitcast.26, bf16[144,6144]{1,0:T(8,128)(2,1)S(1)} %get-tuple-element.31.refs_2_.refs_5_), custom_call_target="tpu_custom_call" | custom-call | flops 1 | bytes 1 | tf_op jit(solution)/shard_map/gradient/pallas_call | solution.py:46
  23.7 2.3 %hidden.1.refs_0_ = bf16[384,6144]{1,0:T(8,128)(2,1)S(1)} custom-call(f32[1,6144]{1,0:T(1,128)S(1)} %collective-permute-done.refs_0_, bf16[96,6144]{1,0:T(8,128)(2,1)S(1)} %get-tuple-element.30.refs_4_.refs_1_, bf16[144,6144]{1,0:T(8,128)(2,1)S(1)} %get-tuple-element.31.refs_2_.refs_5_, bf16[96,6144]{1,0:T(8,128)(2,1)S(1)} %get-tuple-element.32.refs_3_.refs_6_, ...), custom_call_target="tpu_custom_call" | custom-call | flops 1 | bytes 1 | tf_op jit(solution)/shard_map/hidden/pallas_call | solution.py:46
  26.0 1.4 %down.1 = (f32[384,128]{1,0:T(8,128)S(1)}, bf16[384,128]{1,0:T(8,128)(2,1)S(1)}) custom-call(bf16[384,6144]{1,0:T(8,128)(2,1)S(1)} %hidden.1.refs_0_, bf16[6144,128]{1,0:T(8,128)(2,1)S(1)} %collective-permute-done.1.refs_1_, bf16[6144,128]{1,0:T(8,128)(2,1)S(1)} %collective-permute-done.2.refs_2_.refs_1_), custom_call_target="tpu_custom_call" | custom-call | flops 1 | bytes 1 | tf_op jit(solution)/shard_map/down/pallas_call | solution.py:46
  27.4 1.4 %back.1 = bf16[384,128]{1,0:T(8,128)(2,1)S(1)} custom-call(bf16[384,6144]{1,0:T(8,128)(2,1)S(1)} %gradient.1.refs_7_.refs_0_, bf16[6144,128]{1,0:T(8,128)(2,1)S(1)} %collective-permute-done.2.refs_2_.refs_1_, bf16[384,128]{1,0:T(8,128)(2,1)S(1)} %get-tuple-element.36.refs_2_), custom_call_target="tpu_custom_call" | custom-call | flops 1 | bytes 1 | tf_op jit(solution)/shard_map/back/pallas_call | solution.py:46
  28.8 6.9 %collective-permute-start.6 = (bf16[384,128]{1,0:T(8,128)(2,1)S(1)}, bf16[384,128]{1,0:T(8,128)(2,1)S(1)}, u32[]{:S(2)}, u32[]{:S(2)}) collective-permute-start(bf16[384,128]{1,0:T(8,128)(2,1)S(1)} %back.1), channel_id=1, source_target_pairs={{0,240},{8,248},{16,0},{24,8},{32,16},{40,24},{48,32},{56,40},{64,... | collective-permute-start | bytes 294920 | tf_op jit(solution)/shard_map/ppermute | solution.py:387
  35.8 1.6 %collective-permute-done.6.refs_4_.refs_2_ = bf16[384,128]{1,0:T(8,128)(2,1)S(1)} collective-permute-done((bf16[384,128]{1,0:T(8,128)(2,1)S(1)}, bf16[384,128]{1,0:T(8,128)(2,1)S(1)}, u32[]{:S(2)}, u32[]{:S(2)}) %collective-permute-start.6) | collective-permute-done | bytes 98336 | tf_op jit(solution)/shard_map/ppermute | solution.py:387
  37.7 8.1 %collective-permute-done.3.refs_1_ = bf16[384,128]{1,0:T(8,128)(2,1)S(1)} collective-permute-done((bf16[384,128]{1,0:T(8,128)(2,1)S(1)}, bf16[384,128]{1,0:T(8,128)(2,1)S(1)}, u32[]{:S(2)}, u32[]{:S(2)}) %collective-permute-start.3) | collective-permute-done | bytes 98336 | tf_op jit(solution)/shard_map/ppermute | solution.py:387
  45.8 1.0 grad_up.1
  47.1 1.1 %grad_down.1 = (f32[4,128,768]{2,1,0:T(8,128)S(1)}, bf16[4,128,768]{2,1,0:T(8,128)(2,1)S(1)}) custom-call(bf16[384,6144]{1,0:T(8,128)(2,1)S(1)} %hidden.1.refs_0_, f32[384,128]{1,0:T(8,128)S(1)} %get-tuple-element.44.refs_1_, bf16[384,128]{1,0:T(8,128)(2,1)S(1)} %collective-permute-done.6.refs_4_.refs_2_), custom_call_target="tpu_custom_call" | custom-call | flops 1 | bytes 1 | tf_op jit(solution)/shard_map/grad_down/pallas_call | solution.py:46
  48.2 1.3 %collective-permute-start.11 = (bf16[4,128,768]{2,1,0:T(8,128)(2,1)S(1)}, bf16[4,128,768]{2,1,0:T(8,128)(2,1)S(1)}, u32[]{:S(2)}, u32[]{:S(2)}) collective-permute-start(bf16[4,128,768]{2,1,0:T(8,128)(2,1)S(1)} %get-tuple-element.46), channel_id=1, source_target_pairs={{1,0},{0,1},{3,2},{2,3},{5,4},{4,5},{7,6},{6,7},{9,8},{8,9},{11,10... | collective-permute-start | bytes 2359304 | tf_op jit(solution)/shard_map/ppermute | solution.py:397
  49.5 1.8 %collective-permute-start.7 = (bf16[4,128,768]{2,1,0:T(8,128)(2,1)S(1)}, bf16[4,128,768]{2,1,0:T(8,128)(2,1)S(1)}, u32[]{:S(2)}, u32[]{:S(2)}) collective-permute-start(bf16[4,128,768]{2,1,0:T(8,128)(2,1)S(1)} %get-tuple-element.38), channel_id=1, source_target_pairs={{3,0},{2,1},{1,2},{0,3},{7,4},{6,5},{5,6},{4,7},{11,8},{10,9},{9,1... | collective-permute-start | bytes 2359304 | tf_op jit(solution)/shard_map/ppermute | solution.py:397
  51.3 2.1 %feedback.4 = (bf16[384,6144]{1,0:T(8,128)(2,1)}, f32[8,128]{1,0:T(8,128)S(1)}) custom-call(bf16[96,6144]{1,0:T(8,128)(2,1)S(1)} %collective-permute-done.5.refs_3_.refs_0_, bf16[96,6144]{1,0:T(8,128)(2,1)S(1)} %get-tuple-element.30.refs_4_.refs_1_, bf16[384,128]{1,0:T(8,128)(2,1)S(1)} %collective-permute-done.4.refs_2_, bf16[6144,128]{1,0:T(8,128)(2,1)S(1)} %bitcast.15), custom_call_target="tpu_custom_call" | custom-call | flops 1 | bytes 1 | tf_op jit(solution)/shard_map/feedback/pallas_call | solution.py:46
  53.4 13.5 %collective-permute-done.11.refs_1_ = bf16[4,128,768]{2,1,0:T(8,128)(2,1)S(1)} collective-permute-done((bf16[4,128,768]{2,1,0:T(8,128)(2,1)S(1)}, bf16[4,128,768]{2,1,0:T(8,128)(2,1)S(1)}, u32[]{:S(2)}, u32[]{:S(2)}) %collective-permute-start.11) | collective-permute-done | bytes 786464 | tf_op jit(solution)/shard_map/ppermute | solution.py:397
  67.0 2.6 %collective-permute-start.12 = (bf16[2,128,768]{2,1,0:T(8,128)(2,1)S(1)}, bf16[2,128,768]{2,1,0:T(8,128)(2,1)S(1)}, u32[]{:S(2)}, u32[]{:S(2)}) collective-permute-start(bf16[2,128,768]{2,1,0:T(8,128)(2,1)S(1)} %get-tuple-element.49), channel_id=1, source_target_pairs={{3,0},{2,1},{1,2},{0,3},{7,4},{6,5},{5,6},{4,7},{11,8},{10,9},{9,1... | collective-permute-start | bytes 1179656 | tf_op jit(solution)/shard_map/ppermute | solution.py:397
  69.9 0.9 collective-permute-start.9
  70.8 2.6 %feedback.5 = (bf16[384,6144]{1,0:T(8,128)(2,1)}, f32[8,128]{1,0:T(8,128)S(1)}) custom-call(bf16[144,6144]{1,0:T(8,128)(2,1)S(1)} %collective-permute-done.8.refs_2_.refs_0_, bf16[144,6144]{1,0:T(8,128)(2,1)S(1)} %get-tuple-element.39.refs_1_, bf16[384,128]{1,0:T(8,128)(2,1)S(1)} %collective-permute-done.4.refs_2_, ...), custom_call_target="tpu_custom_call", output_to_operand_aliasing={{0}: (4, {})} | custom-call | flops 1 | bytes 1 | tf_op jit(solution)/shard_map/feedback/pallas_call | solution.py:46
  73.4 4.2 %collective-permute-done.12.refs_1_ = bf16[2,128,768]{2,1,0:T(8,128)(2,1)S(1)} collective-permute-done((bf16[2,128,768]{2,1,0:T(8,128)(2,1)S(1)}, bf16[2,128,768]{2,1,0:T(8,128)(2,1)S(1)}, u32[]{:S(2)}, u32[]{:S(2)}) %collective-permute-start.12) | collective-permute-done | bytes 393248 | tf_op jit(solution)/shard_map/ppermute | solution.py:397
  77.9 1.3 %collective-permute-done.10.refs_0_.refs_2_ = bf16[96,6144]{1,0:T(8,128)(2,1)S(1)} collective-permute-done((bf16[96,6144]{1,0:T(8,128)(2,1)S(1)}, bf16[96,6144]{1,0:T(8,128)(2,1)S(1)}, u32[]{:S(2)}, u32[]{:S(2)}) %collective-permute-start.10) | collective-permute-done | bytes 1179680 | tf_op jit(solution)/shard_map/ppermute | solution.py:387
  79.3 4.4 %collective-permute-start.16 = (bf16[128,768]{1,0:T(8,128)(2,1)S(1)}, bf16[128,768]{1,0:T(8,128)(2,1)S(1)}, u32[]{:S(2)}, u32[]{:S(2)}) collective-permute-start(bf16[128,768]{1,0:T(8,128)(2,1)S(1)} %get-tuple-element.55), channel_id=1, source_target_pairs={{0,248},{1,249},{2,250},{3,251},{4,252},{5,253},{6,254},{7,255},{8... | collective-permute-start | bytes 589832 | tf_op jit(solution)/shard_map/ppermute | solution.py:397
  83.7 2.9 %collective-permute-start.17 = (bf16[128,768]{1,0:T(8,128)(2,1)S(1)}, bf16[128,768]{1,0:T(8,128)(2,1)S(1)}, u32[]{:S(2)}, u32[]{:S(2)}) collective-permute-start(bf16[128,768]{1,0:T(8,128)(2,1)S(1)} %get-tuple-element.56), channel_id=1, source_target_pairs={{4,248},{5,249},{6,250},{7,251},{0,252},{1,253},{2,254},{3,255},{1... | collective-permute-start | bytes 589832 | tf_op jit(solution)/shard_map/ppermute | solution.py:397
  86.5 2.0 %feedback.6.refs_4_ = bf16[384,6144]{1,0:T(8,128)(2,1)} custom-call(bf16[96,6144]{1,0:T(8,128)(2,1)S(1)} %collective-permute-done.10.refs_0_.refs_2_, bf16[96,6144]{1,0:T(8,128)(2,1)S(1)} %get-tuple-element.41.refs_1_, bf16[384,128]{1,0:T(8,128)(2,1)S(1)} %collective-permute-done.4.refs_2_, ...), custom_call_target="tpu_custom_call", output_to_operand_aliasing={{}: (4, {})} | custom-call | flops 1 | bytes 1 | tf_op jit(solution)/shard_map/feedback/pallas_call | solution.py:46
  88.6 11.8 %collective-permute-done.14.refs_1_ = bf16[128,768]{1,0:T(8,128)(2,1)S(1)} collective-permute-done((bf16[128,768]{1,0:T(8,128)(2,1)S(1)}, bf16[128,768]{1,0:T(8,128)(2,1)S(1)}, u32[]{:S(2)}, u32[]{:S(2)}) %collective-permute-start.14) | collective-permute-done | bytes 196640 | tf_op jit(solution)/shard_map/ppermute | solution.py:397
  100.4 0.9 finish.2
  101.3 1.5 %feedback.7 = bf16[384,6144]{1,0:T(8,128)(2,1)} custom-call(bf16[48,6144]{1,0:T(8,128)(2,1)S(1)} %collective-permute-done.9.refs_0_, bf16[48,6144]{1,0:T(8,128)(2,1)S(1)} %get-tuple-element.40.refs_1_, bf16[384,128]{1,0:T(8,128)(2,1)S(1)} %collective-permute-done.4.refs_2_, bf16[6144,128]{1,0:T(8,128)(2,1)S(1)} %bitcast.18, ...), custom_call_target="tpu_custom_call", output_to_operand_aliasing={{}: (4, {})} | custom-call | flops 1 | bytes 1 | tf_op jit(solution)/shard_map/feedback/pallas_call | solution.py:46
  102.9 0.9 finish.3
  (40 shorter events, 2.5 us)
Async XLA Ops:
  0.6 25.4 %collective-permute-start.1 = (bf16[6144,128]{1,0:T(8,128)(2,1)}, bf16[6144,128]{1,0:T(8,128)(2,1)S(1)}, u32[]{:S(2)}, u32[]{:S(2)}) collective-permute-start(bf16[6144,128]{1,0:T(8,128)(2,1)} %bitcast.30), channel_id=1, source_target_pairs={{0,248},{8,0},{16,8},{24,16},{32,24},{40,32},{48,40},{56,48},{64,5... | collective-permute-start | bytes 4718600 | tf_op jit(solution)/shard_map/ppermute | solution.py:387
  4.0 22.1 %collective-permute-start.2 = (bf16[6144,128]{1,0:T(8,128)(2,1)}, bf16[6144,128]{1,0:T(8,128)(2,1)S(1)}, u32[]{:S(2)}, u32[]{:S(2)}) collective-permute-start(bf16[6144,128]{1,0:T(8,128)(2,1)} %bitcast.14), channel_id=1, source_target_pairs={{0,8},{8,16},{16,24},{24,32},{32,40},{40,48},{48,56},{56,64},{64,7... | collective-permute-start | bytes 4718600 | tf_op jit(solution)/shard_map/ppermute | solution.py:387
  4.0 1.9 %copy-start.1 = (s32[1,384,2048]{2,1,0:T(8,128)S(1)}, s32[1,384,2048]{2,1,0:T(8,128)}, u32[]{:S(2)}) copy-start(s32[1,384,2048]{2,1,0:T(8,128)} %param.9) | copy-start | bytes 9437188
  5.8 1.0 copy-start.3
  6.8 0.9 copy-start.4
  7.8 0.7 copy-start.6
  8.4 2.9 %copy-start.8 = (f32[1,6144]{1,0:T(1,128)S(1)}, f32[1,6144]{1,0:T(1,128)}, u32[]{:S(2)}) copy-start(f32[1,6144]{1,0:T(1,128)} %param.15) | copy-start | bytes 73732
  8.4 7.2 %copy-start.7 = (s32[1,384]{1,0:T(1,128)S(1)}, s32[1,384]{1,0:T(1,128)}, u32[]{:S(2)}) copy-start(s32[1,384]{1,0:T(1,128)} %refs_3_.3) | copy-start | bytes 4612
  10.9 10.2 %copy-start.2 = (bf16[1,384,6144]{2,1,0:T(8,128)(2,1)S(1)}, bf16[1,384,6144]{2,1,0:T(8,128)(2,1)}, u32[]{:S(2)}) copy-start(bf16[1,384,6144]{2,1,0:T(8,128)(2,1)} %param.13) | copy-start | bytes 14155780
  10.9 10.2 %copy-start.5 = (bf16[1,384,192]{1,2,0:T(8,128)(2,1)S(1)}, bf16[1,384,192]{1,2,0:T(8,128)(2,1)}, u32[]{:S(2)}) copy-start(bf16[1,384,192]{1,2,0:T(8,128)(2,1)} %param.14) | copy-start | bytes 442372
  10.9 24.9 %collective-permute-start.5 = (bf16[96,6144]{1,0:T(8,128)(2,1)S(1)}, bf16[96,6144]{1,0:T(8,128)(2,1)S(1)}, u32[]{:S(2)}, u32[]{:S(2)}) collective-permute-start(bf16[96,6144]{1,0:T(8,128)(2,1)S(1)} %get-tuple-element.30.refs_4_.refs_1_), channel_id=1, source_target_pairs={{0,8},{8,16},{16,24},{24,32},{32,40},{40,48},{48,56},{56,64},{64,7... | collective-permute-start | bytes 3538952 | tf_op jit(solution)/shard_map/ppermute | solution.py:387
  11.3 12.4 %collective-permute-start = (f32[1,6144]{1,0:T(1,128)S(1)}, f32[1,6144]{1,0:T(1,128)S(1)}, u32[]{:S(2)}, u32[]{:S(2)}) collective-permute-start(f32[1,6144]{1,0:T(1,128)S(1)} %copy-done.8), channel_id=1, source_target_pairs={{0,248},{8,0},{16,8},{24,16},{32,24},{40,32},{48,40},{56,48},{64,5... | collective-permute-start | bytes 73736 | tf_op jit(solution)/shard_map/ppermute | solution.py:387
  28.8 8.6 %collective-permute-start.6 = (bf16[384,128]{1,0:T(8,128)(2,1)S(1)}, bf16[384,128]{1,0:T(8,128)(2,1)S(1)}, u32[]{:S(2)}, u32[]{:S(2)}) collective-permute-start(bf16[384,128]{1,0:T(8,128)(2,1)S(1)} %back.1), channel_id=1, source_target_pairs={{0,240},{8,248},{16,0},{24,8},{32,16},{40,24},{48,32},{56,40},{64,... | collective-permute-start | bytes 294920 | tf_op jit(solution)/shard_map/ppermute | solution.py:387
  35.8 2.0 %collective-permute-start.4 = (bf16[384,128]{1,0:T(8,128)(2,1)S(1)}, bf16[384,128]{1,0:T(8,128)(2,1)S(1)}, u32[]{:S(2)}, u32[]{:S(2)}) collective-permute-start(bf16[384,128]{1,0:T(8,128)(2,1)S(1)} %get-tuple-element.36.refs_2_), channel_id=1, source_target_pairs={{0,8},{8,16},{16,24},{24,32},{32,40},{40,48},{48,56},{56,64},{64,7... | collective-permute-start | bytes 294920 | tf_op jit(solution)/shard_map/ppermute | solution.py:387
  35.8 10.0 %collective-permute-start.3 = (bf16[384,128]{1,0:T(8,128)(2,1)S(1)}, bf16[384,128]{1,0:T(8,128)(2,1)S(1)}, u32[]{:S(2)}, u32[]{:S(2)}) collective-permute-start(bf16[384,128]{1,0:T(8,128)(2,1)S(1)} %get-tuple-element.36.refs_2_), channel_id=1, source_target_pairs={{0,16},{8,24},{16,32},{24,40},{32,48},{40,56},{48,64},{56,72},{64,... | collective-permute-start | bytes 294920 | tf_op jit(solution)/shard_map/ppermute | solution.py:387
  46.8 22.8 %collective-permute-start.8 = (bf16[144,6144]{1,0:T(8,128)(2,1)S(1)}, bf16[144,6144]{1,0:T(8,128)(2,1)S(1)}, u32[]{:S(2)}, u32[]{:S(2)}) collective-permute-start(bf16[144,6144]{1,0:T(8,128)(2,1)S(1)} %get-tuple-element.39.refs_1_), channel_id=1, source_target_pairs={{0,8},{8,16},{16,24},{24,32},{32,40},{40,48},{48,56},{56,64},{64,7... | collective-permute-start | bytes 5308424 | tf_op jit(solution)/shard_map/ppermute | solution.py:387
  47.1 4.2 %copy-start = (bf16[1,6144,128]{2,1,0:T(8,128)(2,1)S(1)}, bf16[1,6144,128]{2,1,0:T(8,128)(2,1)}, u32[]{:S(2)}) copy-start(bf16[1,6144,128]{2,1,0:T(8,128)(2,1)} %param.17) | copy-start | bytes 4718596
  48.2 18.7 %collective-permute-start.11 = (bf16[4,128,768]{2,1,0:T(8,128)(2,1)S(1)}, bf16[4,128,768]{2,1,0:T(8,128)(2,1)S(1)}, u32[]{:S(2)}, u32[]{:S(2)}) collective-permute-start(bf16[4,128,768]{2,1,0:T(8,128)(2,1)S(1)} %get-tuple-element.46), channel_id=1, source_target_pairs={{1,0},{0,1},{3,2},{2,3},{5,4},{4,5},{7,6},{6,7},{9,8},{8,9},{11,10... | collective-permute-start | bytes 2359304 | tf_op jit(solution)/shard_map/ppermute | solution.py:397
  49.5 20.1 %collective-permute-start.7 = (bf16[4,128,768]{2,1,0:T(8,128)(2,1)S(1)}, bf16[4,128,768]{2,1,0:T(8,128)(2,1)S(1)}, u32[]{:S(2)}, u32[]{:S(2)}) collective-permute-start(bf16[4,128,768]{2,1,0:T(8,128)(2,1)S(1)} %get-tuple-element.38), channel_id=1, source_target_pairs={{3,0},{2,1},{1,2},{0,3},{7,4},{6,5},{5,6},{4,7},{11,8},{10,9},{9,1... | collective-permute-start | bytes 2359304 | tf_op jit(solution)/shard_map/ppermute | solution.py:397
  51.3 27.9 %collective-permute-start.10 = (bf16[96,6144]{1,0:T(8,128)(2,1)S(1)}, bf16[96,6144]{1,0:T(8,128)(2,1)S(1)}, u32[]{:S(2)}, u32[]{:S(2)}) collective-permute-start(bf16[96,6144]{1,0:T(8,128)(2,1)S(1)} %get-tuple-element.41.refs_1_), channel_id=1, source_target_pairs={{0,8},{8,16},{16,24},{24,32},{32,40},{40,48},{48,56},{56,64},{64,7... | collective-permute-start | bytes 3538952 | tf_op jit(solution)/shard_map/ppermute | solution.py:387
  67.0 10.6 %collective-permute-start.12 = (bf16[2,128,768]{2,1,0:T(8,128)(2,1)S(1)}, bf16[2,128,768]{2,1,0:T(8,128)(2,1)S(1)}, u32[]{:S(2)}, u32[]{:S(2)}) collective-permute-start(bf16[2,128,768]{2,1,0:T(8,128)(2,1)S(1)} %get-tuple-element.49), channel_id=1, source_target_pairs={{3,0},{2,1},{1,2},{0,3},{7,4},{6,5},{5,6},{4,7},{11,8},{10,9},{9,1... | collective-permute-start | bytes 1179656 | tf_op jit(solution)/shard_map/ppermute | solution.py:397
  69.8 9.4 %collective-permute-start.15 = (bf16[2,128,768]{2,1,0:T(8,128)(2,1)S(1)}, bf16[2,128,768]{2,1,0:T(8,128)(2,1)S(1)}, u32[]{:S(2)}, u32[]{:S(2)}) collective-permute-start(bf16[2,128,768]{2,1,0:T(8,128)(2,1)S(1)} %get-tuple-element.54), channel_id=1, source_target_pairs={{1,0},{0,1},{3,2},{2,3},{5,4},{4,5},{7,6},{6,7},{9,8},{8,9},{11,10... | collective-permute-start | bytes 1179656 | tf_op jit(solution)/shard_map/ppermute | solution.py:397
  69.9 31.5 %collective-permute-start.9 = (bf16[48,6144]{1,0:T(8,128)(2,1)S(1)}, bf16[48,6144]{1,0:T(8,128)(2,1)S(1)}, u32[]{:S(2)}, u32[]{:S(2)}) collective-permute-start(bf16[48,6144]{1,0:T(8,128)(2,1)S(1)} %get-tuple-element.40.refs_1_), channel_id=1, source_target_pairs={{0,8},{8,16},{16,24},{24,32},{32,40},{40,48},{48,56},{56,64},{64,7... | collective-permute-start | bytes 1769480 | tf_op jit(solution)/shard_map/ppermute | solution.py:387
  77.7 10.9 %collective-permute-start.13 = (bf16[128,768]{1,0:T(8,128)(2,1)S(1)}, bf16[128,768]{1,0:T(8,128)(2,1)S(1)}, u32[]{:S(2)}, u32[]{:S(2)}) collective-permute-start(bf16[128,768]{1,0:T(8,128)(2,1)S(1)} %get-tuple-element.51), channel_id=1, source_target_pairs={{0,8},{1,9},{2,10},{3,11},{4,12},{5,13},{6,14},{7,15},{8,16},{9,17... | collective-permute-start | bytes 589832 | tf_op jit(solution)/shard_map/ppermute | solution.py:397
  77.8 22.7 %collective-permute-start.14 = (bf16[128,768]{1,0:T(8,128)(2,1)S(1)}, bf16[128,768]{1,0:T(8,128)(2,1)S(1)}, u32[]{:S(2)}, u32[]{:S(2)}) collective-permute-start(bf16[128,768]{1,0:T(8,128)(2,1)S(1)} %get-tuple-element.52), channel_id=1, source_target_pairs={{4,8},{5,9},{6,10},{7,11},{0,12},{1,13},{2,14},{3,15},{12,16},{13,... | collective-permute-start | bytes 589832 | tf_op jit(solution)/shard_map/ppermute | solution.py:397
  79.3 23.6 %collective-permute-start.16 = (bf16[128,768]{1,0:T(8,128)(2,1)S(1)}, bf16[128,768]{1,0:T(8,128)(2,1)S(1)}, u32[]{:S(2)}, u32[]{:S(2)}) collective-permute-start(bf16[128,768]{1,0:T(8,128)(2,1)S(1)} %get-tuple-element.55), channel_id=1, source_target_pairs={{0,248},{1,249},{2,250},{3,251},{4,252},{5,253},{6,254},{7,255},{8... | collective-permute-start | bytes 589832 | tf_op jit(solution)/shard_map/ppermute | solution.py:397
  83.7 19.2 %collective-permute-start.17 = (bf16[128,768]{1,0:T(8,128)(2,1)S(1)}, bf16[128,768]{1,0:T(8,128)(2,1)S(1)}, u32[]{:S(2)}, u32[]{:S(2)}) collective-permute-start(bf16[128,768]{1,0:T(8,128)(2,1)S(1)} %get-tuple-element.56), channel_id=1, source_target_pairs={{4,248},{5,249},{6,250},{7,251},{0,252},{1,253},{2,254},{3,255},{1... | collective-permute-start | bytes 589832 | tf_op jit(solution)/shard_map/ppermute | solution.py:397

commit v8 on v7

--- a/solution.py
+++ b/solution.py
@@ -18,7 +18,7 @@
 BLOCK = 768
 WORDS = BLOCK // 3
 CODES = BLOCK // 32
-SPANS = (96, 144, 96, 48)
+SPANS = (48, 144, 96, 96)
 MIB = 1 << 20
 ROOT_2_PI = math.sqrt(2.0 / math.pi)
 VMEM = pl.BlockSpec(memory_space=pltpu.VMEM)

time: 104 us -> 109 us (1.048)
  starting transfers between devices: 29.4 us -> 34.8 us
    ppermute x10, waiting for transfers between devices: 11.4 us -> 6.29 us  [along(): return lax.ppermute(value, 'section', pairs)]
    ppermute x8, starting transfers between devices: 13.3 us -> 17.5 us  [among(): return lax.ppermute(value, both, pairs)]
    ppermute x8, waiting for transfers between devices: 29.5 us -> 33.7 us  [among(): return lax.ppermute(value, both, pairs)]
    ppermute x10, starting transfers between devices: 16.2 us -> 17.3 us  [along(): return lax.ppermute(value, 'section', pairs)]
    unnamed x18 -> x16, local copies, waits for them, and re-layouts: 4.5 us -> 5.17 us
  transfers between devices with their start and end apart: 18 -> 18, of which waited for: 7 -> 8; matrix products, arithmetic and copies ran while one was open for 0% -> 0% of each run, Pallas kernels for 25% -> 23%
where the time goes in v8:
time: 109 us
  waiting for transfers between devices  40 us (37%)
  starting transfers between devices  34.8 us (32%)
  Pallas kernels  28 us (26%)
  local copies, waits for them, and re-layouts  5.17 us (5%)
    ppermute x8, waiting for transfers between devices, among(): return lax.ppermute(value, both, pairs)  33.7 us
    pallas_call x18, Pallas kernels, launch(): pl.pallas_call(wrapped, grid=grid, in_specs=[spec for _, spec in ins] + [...  28 us
    ppermute x8, starting transfers between devices, among(): return lax.ppermute(value, both, pairs)  17.5 us
    ppermute x10, starting transfers between devices, along(): return lax.ppermute(value, 'section', pairs)  17.3 us
    ppermute x10, waiting for transfers between devices, along(): return lax.ppermute(value, 'section', pairs)  6.29 us
    unnamed x16, local copies, waits for them, and re-layouts  5.17 us
  transfers between devices with their start and end apart: 18, of which 8 were waited for; matrix products, arithmetic and copies ran while one was open for 0% of the time, Pallas kernels for 23%

profile of v8, /device:TPU:1, one launch (start us, length us, event | category | flops | bytes accessed | tf_op | source)
XLA Modules:
  0.0 109.0 jit_solution(17570359711431204897)
XLA Ops:
  0.6 3.3 %collective-permute-start.1 = (bf16[6144,128]{1,0:T(8,128)(2,1)}, bf16[6144,128]{1,0:T(8,128)(2,1)S(1)}, u32[]{:S(2)}, u32[]{:S(2)}) collective-permute-start(bf16[6144,128]{1,0:T(8,128)(2,1)} %bitcast.30), channel_id=1, source_target_pairs={{0,248},{8,0},{16,8},{24,16},{32,24},{40,32},{48,40},{56,48},{64,5... | collective-permute-start | bytes 4718600 | tf_op jit(solution)/shard_map/ppermute | solution.py:387
  4.0 1.9 %copy-done.1 = s32[1,384,2048]{2,1,0:T(8,128)S(1)} copy-done((s32[1,384,2048]{2,1,0:T(8,128)S(1)}, s32[1,384,2048]{2,1,0:T(8,128)}, u32[]{:S(2)}) %copy-start.1) | copy-done | bytes 3145752
  5.8 1.0 copy-done.3
  6.8 0.9 copy-done.4
  7.8 0.7 copy-done.6
  8.4 1.8 %message.2 = (bf16[48,6144]{1,0:T(8,128)(2,1)S(1)}, f32[48,256]{1,0:T(8,128)S(1)}) custom-call(s32[384,2048]{1,0:T(8,128)S(1)} %bitcast.19, bf16[192,384]{1,0:T(8,128)(2,1)S(1)} %bitcast.24, bf16[32,6144]{1,0:T(8,128)(2,1)S(1)} %bitcast.22, s32[1,384]{1,0:T(1,128)S(1)} %copy-done.6), custom_call_target="tpu_custom_call" | custom-call | flops 1 | bytes 1 | tf_op jit(solution)/shard_map/message/pallas_call | solution.py:46
  10.7 4.4 %collective-permute-start = (f32[1,6144]{1,0:T(1,128)}, f32[1,6144]{1,0:T(1,128)S(1)}, u32[]{:S(2)}, u32[]{:S(2)}) collective-permute-start(f32[1,6144]{1,0:T(1,128)} %param.15), channel_id=1, source_target_pairs={{0,248},{8,0},{16,8},{24,16},{32,24},{40,32},{48,40},{56,48},{64,5... | collective-permute-start | bytes 73736 | tf_op jit(solution)/shard_map/ppermute | solution.py:387
  15.7 5.9 %message.3 = (bf16[144,6144]{1,0:T(8,128)(2,1)S(1)}, bf16[96,6144]{1,0:T(8,128)(2,1)S(1)}, bf16[96,6144]{1,0:T(8,128)(2,1)S(1)}, f32[336,256]{1,0:T(8,128)S(1)}) custom-call(s32[384,2048]{1,0:T(8,128)S(1)} %bitcast.20, bf16[192,384]{1,0:T(8,128)(2,1)S(1)} %bitcast.25, bf16[32,6144]{1,0:T(8,128)(2,1)S(1)} %bitcast.23, s32[1,384]{1,0:T(1,128)S(1)} %copy-done.7, ...), custom_call_target="tpu_custom_call" | custom-call | flops 1 | bytes 1 | tf_op jit(solution)/shard_map/message/pallas_call | solution.py:46
  21.7 2.6 %gradient.1.refs_7_.refs_0_ = bf16[384,6144]{1,0:T(8,128)(2,1)S(1)} custom-call(bf16[384,6144]{1,0:T(8,128)(2,1)S(1)} %bitcast.21, bf16[192,384]{1,0:T(8,128)(2,1)S(1)} %bitcast.26, bf16[144,6144]{1,0:T(8,128)(2,1)S(1)} %get-tuple-element.31.refs_2_.refs_5_), custom_call_target="tpu_custom_call" | custom-call | flops 1 | bytes 1 | tf_op jit(solution)/shard_map/gradient/pallas_call | solution.py:46
  24.3 2.3 %hidden.1.refs_0_ = bf16[384,6144]{1,0:T(8,128)(2,1)S(1)} custom-call(f32[1,6144]{1,0:T(1,128)S(1)} %collective-permute-done.refs_0_, bf16[48,6144]{1,0:T(8,128)(2,1)S(1)} %get-tuple-element.30.refs_4_.refs_1_, bf16[144,6144]{1,0:T(8,128)(2,1)S(1)} %get-tuple-element.31.refs_2_.refs_5_, bf16[96,6144]{1,0:T(8,128)(2,1)S(1)} %get-tuple-element.32.refs_3_.refs_6_, ...), custom_call_target="tpu_custom_call" | custom-call | flops 1 | bytes 1 | tf_op jit(solution)/shard_map/hidden/pallas_call | solution.py:46
  26.6 1.4 %down.1 = (f32[384,128]{1,0:T(8,128)S(1)}, bf16[384,128]{1,0:T(8,128)(2,1)S(1)}) custom-call(bf16[384,6144]{1,0:T(8,128)(2,1)S(1)} %hidden.1.refs_0_, bf16[6144,128]{1,0:T(8,128)(2,1)S(1)} %collective-permute-done.1.refs_1_, bf16[6144,128]{1,0:T(8,128)(2,1)S(1)} %collective-permute-done.2.refs_2_.refs_1_), custom_call_target="tpu_custom_call" | custom-call | flops 1 | bytes 1 | tf_op jit(solution)/shard_map/down/pallas_call | solution.py:46
  28.0 1.4 %back.1 = bf16[384,128]{1,0:T(8,128)(2,1)S(1)} custom-call(bf16[384,6144]{1,0:T(8,128)(2,1)S(1)} %gradient.1.refs_7_.refs_0_, bf16[6144,128]{1,0:T(8,128)(2,1)S(1)} %collective-permute-done.2.refs_2_.refs_1_, bf16[384,128]{1,0:T(8,128)(2,1)S(1)} %get-tuple-element.36.refs_2_), custom_call_target="tpu_custom_call" | custom-call | flops 1 | bytes 1 | tf_op jit(solution)/shard_map/back/pallas_call | solution.py:46
  29.4 6.4 %collective-permute-start.6 = (bf16[384,128]{1,0:T(8,128)(2,1)S(1)}, bf16[384,128]{1,0:T(8,128)(2,1)S(1)}, u32[]{:S(2)}, u32[]{:S(2)}) collective-permute-start(bf16[384,128]{1,0:T(8,128)(2,1)S(1)} %back.1), channel_id=1, source_target_pairs={{0,240},{8,248},{16,0},{24,8},{32,16},{40,24},{48,32},{56,40},{64,... | collective-permute-start | bytes 294920 | tf_op jit(solution)/shard_map/ppermute | solution.py:387
  35.8 1.6 %collective-permute-done.6.refs_4_.refs_2_ = bf16[384,128]{1,0:T(8,128)(2,1)S(1)} collective-permute-done((bf16[384,128]{1,0:T(8,128)(2,1)S(1)}, bf16[384,128]{1,0:T(8,128)(2,1)S(1)}, u32[]{:S(2)}, u32[]{:S(2)}) %collective-permute-start.6) | collective-permute-done | bytes 98336 | tf_op jit(solution)/shard_map/ppermute | solution.py:387
  37.7 4.0 %collective-permute-done.3.refs_1_ = bf16[384,128]{1,0:T(8,128)(2,1)S(1)} collective-permute-done((bf16[384,128]{1,0:T(8,128)(2,1)S(1)}, bf16[384,128]{1,0:T(8,128)(2,1)S(1)}, u32[]{:S(2)}, u32[]{:S(2)}) %collective-permute-start.3) | collective-permute-done | bytes 98336 | tf_op jit(solution)/shard_map/ppermute | solution.py:387
  41.7 1.0 grad_up.1
  42.8 2.7 %collective-permute-start.7 = (bf16[4,128,768]{2,1,0:T(8,128)(2,1)S(1)}, bf16[4,128,768]{2,1,0:T(8,128)(2,1)S(1)}, u32[]{:S(2)}, u32[]{:S(2)}) collective-permute-start(bf16[4,128,768]{2,1,0:T(8,128)(2,1)S(1)} %get-tuple-element.38), channel_id=1, source_target_pairs={{3,0},{2,1},{1,2},{0,3},{7,4},{6,5},{5,6},{4,7},{11,8},{10,9},{9,1... | collective-permute-start | bytes 2359304 | tf_op jit(solution)/shard_map/ppermute | solution.py:397
  45.6 1.1 grad_down.1
  47.0 14.9 %collective-permute-done.7.refs_1_ = bf16[4,128,768]{2,1,0:T(8,128)(2,1)S(1)} collective-permute-done((bf16[4,128,768]{2,1,0:T(8,128)(2,1)S(1)}, bf16[4,128,768]{2,1,0:T(8,128)(2,1)S(1)}, u32[]{:S(2)}, u32[]{:S(2)}) %collective-permute-start.7) | collective-permute-done | bytes 786464 | tf_op jit(solution)/shard_map/ppermute | solution.py:397
  62.4 2.6 %collective-permute-start.9 = (bf16[96,6144]{1,0:T(8,128)(2,1)S(1)}, bf16[96,6144]{1,0:T(8,128)(2,1)S(1)}, u32[]{:S(2)}, u32[]{:S(2)}) collective-permute-start(bf16[96,6144]{1,0:T(8,128)(2,1)S(1)} %get-tuple-element.40.refs_1_), channel_id=1, source_target_pairs={{0,8},{8,16},{16,24},{24,32},{32,40},{40,48},{48,56},{56,64},{64,7... | collective-permute-start | bytes 3538952 | tf_op jit(solution)/shard_map/ppermute | solution.py:387
  65.0 1.5 %feedback.4 = (bf16[384,6144]{1,0:T(8,128)(2,1)}, f32[8,128]{1,0:T(8,128)S(1)}) custom-call(bf16[48,6144]{1,0:T(8,128)(2,1)S(1)} %collective-permute-done.5.refs_3_.refs_0_, bf16[48,6144]{1,0:T(8,128)(2,1)S(1)} %get-tuple-element.30.refs_4_.refs_1_, bf16[384,128]{1,0:T(8,128)(2,1)S(1)} %collective-permute-done.4.refs_2_, bf16[6144,128]{1,0:T(8,128)(2,1)S(1)} %bitcast.15), custom_call_target="tpu_custom_call" | custom-call | flops 1 | bytes 1 | tf_op jit(solution)/shard_map/feedback/pallas_call | solution.py:46
  66.7 2.6 %collective-permute-start.12 = (bf16[2,128,768]{2,1,0:T(8,128)(2,1)S(1)}, bf16[2,128,768]{2,1,0:T(8,128)(2,1)S(1)}, u32[]{:S(2)}, u32[]{:S(2)}) collective-permute-start(bf16[2,128,768]{2,1,0:T(8,128)(2,1)S(1)} %get-tuple-element.49), channel_id=1, source_target_pairs={{3,0},{2,1},{1,2},{0,3},{7,4},{6,5},{5,6},{4,7},{11,8},{10,9},{9,1... | collective-permute-start | bytes 1179656 | tf_op jit(solution)/shard_map/ppermute | solution.py:397
  69.2 2.6 %feedback.5 = (bf16[384,6144]{1,0:T(8,128)(2,1)}, f32[8,128]{1,0:T(8,128)S(1)}) custom-call(bf16[144,6144]{1,0:T(8,128)(2,1)S(1)} %collective-permute-done.8.refs_2_.refs_0_, bf16[144,6144]{1,0:T(8,128)(2,1)S(1)} %get-tuple-element.39.refs_1_, bf16[384,128]{1,0:T(8,128)(2,1)S(1)} %collective-permute-done.4.refs_2_, ...), custom_call_target="tpu_custom_call", output_to_operand_aliasing={{0}: (4, {})} | custom-call | flops 1 | bytes 1 | tf_op jit(solution)/shard_map/feedback/pallas_call | solution.py:46
  71.8 3.1 %collective-permute-done.12.refs_1_ = bf16[2,128,768]{2,1,0:T(8,128)(2,1)S(1)} collective-permute-done((bf16[2,128,768]{2,1,0:T(8,128)(2,1)S(1)}, bf16[2,128,768]{2,1,0:T(8,128)(2,1)S(1)}, u32[]{:S(2)}, u32[]{:S(2)}) %collective-permute-start.12) | collective-permute-done | bytes 393248 | tf_op jit(solution)/shard_map/ppermute | solution.py:397
  75.0 4.2 %collective-permute-start.13 = (bf16[128,768]{1,0:T(8,128)(2,1)S(1)}, bf16[128,768]{1,0:T(8,128)(2,1)S(1)}, u32[]{:S(2)}, u32[]{:S(2)}) collective-permute-start(bf16[128,768]{1,0:T(8,128)(2,1)S(1)} %get-tuple-element.51), channel_id=1, source_target_pairs={{0,8},{1,9},{2,10},{3,11},{4,12},{5,13},{6,14},{7,15},{8,16},{9,17... | collective-permute-start | bytes 589832 | tf_op jit(solution)/shard_map/ppermute | solution.py:397
  79.2 2.4 %collective-permute-start.14 = (bf16[128,768]{1,0:T(8,128)(2,1)S(1)}, bf16[128,768]{1,0:T(8,128)(2,1)S(1)}, u32[]{:S(2)}, u32[]{:S(2)}) collective-permute-start(bf16[128,768]{1,0:T(8,128)(2,1)S(1)} %get-tuple-element.52), channel_id=1, source_target_pairs={{4,8},{5,9},{6,10},{7,11},{0,12},{1,13},{2,14},{3,15},{12,16},{13,... | collective-permute-start | bytes 589832 | tf_op jit(solution)/shard_map/ppermute | solution.py:397
  82.3 4.8 %collective-permute-start.17 = (bf16[128,768]{1,0:T(8,128)(2,1)S(1)}, bf16[128,768]{1,0:T(8,128)(2,1)S(1)}, u32[]{:S(2)}, u32[]{:S(2)}) collective-permute-start(bf16[128,768]{1,0:T(8,128)(2,1)S(1)} %get-tuple-element.56), channel_id=1, source_target_pairs={{4,248},{5,249},{6,250},{7,251},{0,252},{1,253},{2,254},{3,255},{1... | collective-permute-start | bytes 589832 | tf_op jit(solution)/shard_map/ppermute | solution.py:397
  87.1 2.1 %feedback.6.refs_4_ = bf16[384,6144]{1,0:T(8,128)(2,1)} custom-call(bf16[96,6144]{1,0:T(8,128)(2,1)S(1)} %collective-permute-done.10.refs_0_.refs_2_, bf16[96,6144]{1,0:T(8,128)(2,1)S(1)} %get-tuple-element.41.refs_1_, bf16[384,128]{1,0:T(8,128)(2,1)S(1)} %collective-permute-done.4.refs_2_, ...), custom_call_target="tpu_custom_call", output_to_operand_aliasing={{}: (4, {})} | custom-call | flops 1 | bytes 1 | tf_op jit(solution)/shard_map/feedback/pallas_call | solution.py:46
  89.7 15.2 %collective-permute-done.14.refs_1_ = bf16[128,768]{1,0:T(8,128)(2,1)S(1)} collective-permute-done((bf16[128,768]{1,0:T(8,128)(2,1)S(1)}, bf16[128,768]{1,0:T(8,128)(2,1)S(1)}, u32[]{:S(2)}, u32[]{:S(2)}) %collective-permute-start.14) | collective-permute-done | bytes 196640 | tf_op jit(solution)/shard_map/ppermute | solution.py:397
  104.9 0.9 finish.2
  105.8 0.9 finish.3
  106.7 2.1 %feedback.7 = bf16[384,6144]{1,0:T(8,128)(2,1)} custom-call(bf16[96,6144]{1,0:T(8,128)(2,1)S(1)} %collective-permute-done.9.refs_0_, bf16[96,6144]{1,0:T(8,128)(2,1)S(1)} %get-tuple-element.40.refs_1_, bf16[384,128]{1,0:T(8,128)(2,1)S(1)} %collective-permute-done.4.refs_2_, bf16[6144,128]{1,0:T(8,128)(2,1)S(1)} %bitcast.18, ...), custom_call_target="tpu_custom_call", output_to_operand_aliasing={{}: (4, {})} | custom-call | flops 1 | bytes 1 | tf_op jit(solution)/shard_map/feedback/pallas_call | solution.py:46
  (38 shorter events, 3.9 us)
Async XLA Ops:
  0.6 26.0 %collective-permute-start.1 = (bf16[6144,128]{1,0:T(8,128)(2,1)}, bf16[6144,128]{1,0:T(8,128)(2,1)S(1)}, u32[]{:S(2)}, u32[]{:S(2)}) collective-permute-start(bf16[6144,128]{1,0:T(8,128)(2,1)} %bitcast.30), channel_id=1, source_target_pairs={{0,248},{8,0},{16,8},{24,16},{32,24},{40,32},{48,40},{56,48},{64,5... | collective-permute-start | bytes 4718600 | tf_op jit(solution)/shard_map/ppermute | solution.py:387
  3.9 22.7 %collective-permute-start.2 = (bf16[6144,128]{1,0:T(8,128)(2,1)}, bf16[6144,128]{1,0:T(8,128)(2,1)S(1)}, u32[]{:S(2)}, u32[]{:S(2)}) collective-permute-start(bf16[6144,128]{1,0:T(8,128)(2,1)} %bitcast.14), channel_id=1, source_target_pairs={{0,8},{8,16},{16,24},{24,32},{32,40},{40,48},{48,56},{56,64},{64,7... | collective-permute-start | bytes 4718600 | tf_op jit(solution)/shard_map/ppermute | solution.py:387
  4.0 1.9 %copy-start.1 = (s32[1,384,2048]{2,1,0:T(8,128)S(1)}, s32[1,384,2048]{2,1,0:T(8,128)}, u32[]{:S(2)}) copy-start(s32[1,384,2048]{2,1,0:T(8,128)} %param.9) | copy-start | bytes 9437188
  5.8 1.0 copy-start.3
  6.8 0.9 copy-start.4
  7.8 0.7 copy-start.6
  8.4 13.2 %copy-start.2 = (bf16[1,384,6144]{2,1,0:T(8,128)(2,1)S(1)}, bf16[1,384,6144]{2,1,0:T(8,128)(2,1)}, u32[]{:S(2)}) copy-start(bf16[1,384,6144]{2,1,0:T(8,128)(2,1)} %param.13) | copy-start | bytes 14155780
  10.3 11.4 %copy-start.5 = (bf16[1,384,192]{1,2,0:T(8,128)(2,1)S(1)}, bf16[1,384,192]{1,2,0:T(8,128)(2,1)}, u32[]{:S(2)}) copy-start(bf16[1,384,192]{1,2,0:T(8,128)(2,1)} %param.14) | copy-start | bytes 442372
  10.3 25.5 %collective-permute-start.5 = (bf16[48,6144]{1,0:T(8,128)(2,1)S(1)}, bf16[48,6144]{1,0:T(8,128)(2,1)S(1)}, u32[]{:S(2)}, u32[]{:S(2)}) collective-permute-start(bf16[48,6144]{1,0:T(8,128)(2,1)S(1)} %get-tuple-element.30.refs_4_.refs_1_), channel_id=1, source_target_pairs={{0,8},{8,16},{16,24},{24,32},{32,40},{40,48},{48,56},{56,64},{64,7... | collective-permute-start | bytes 1769480 | tf_op jit(solution)/shard_map/ppermute | solution.py:387
  10.7 13.6 %collective-permute-start = (f32[1,6144]{1,0:T(1,128)}, f32[1,6144]{1,0:T(1,128)S(1)}, u32[]{:S(2)}, u32[]{:S(2)}) collective-permute-start(f32[1,6144]{1,0:T(1,128)} %param.15), channel_id=1, source_target_pairs={{0,248},{8,0},{16,8},{24,16},{32,24},{40,32},{48,40},{56,48},{64,5... | collective-permute-start | bytes 73736 | tf_op jit(solution)/shard_map/ppermute | solution.py:387
  15.0 0.7 copy-start.7
  29.4 8.0 %collective-permute-start.6 = (bf16[384,128]{1,0:T(8,128)(2,1)S(1)}, bf16[384,128]{1,0:T(8,128)(2,1)S(1)}, u32[]{:S(2)}, u32[]{:S(2)}) collective-permute-start(bf16[384,128]{1,0:T(8,128)(2,1)S(1)} %back.1), channel_id=1, source_target_pairs={{0,240},{8,248},{16,0},{24,8},{32,16},{40,24},{48,32},{56,40},{64,... | collective-permute-start | bytes 294920 | tf_op jit(solution)/shard_map/ppermute | solution.py:387
  35.8 2.0 %collective-permute-start.4 = (bf16[384,128]{1,0:T(8,128)(2,1)S(1)}, bf16[384,128]{1,0:T(8,128)(2,1)S(1)}, u32[]{:S(2)}, u32[]{:S(2)}) collective-permute-start(bf16[384,128]{1,0:T(8,128)(2,1)S(1)} %get-tuple-element.36.refs_2_), channel_id=1, source_target_pairs={{0,8},{8,16},{16,24},{24,32},{32,40},{40,48},{48,56},{56,64},{64,7... | collective-permute-start | bytes 294920 | tf_op jit(solution)/shard_map/ppermute | solution.py:387
  35.8 6.0 %collective-permute-start.3 = (bf16[384,128]{1,0:T(8,128)(2,1)S(1)}, bf16[384,128]{1,0:T(8,128)(2,1)S(1)}, u32[]{:S(2)}, u32[]{:S(2)}) collective-permute-start(bf16[384,128]{1,0:T(8,128)(2,1)S(1)} %get-tuple-element.36.refs_2_), channel_id=1, source_target_pairs={{0,16},{8,24},{16,32},{24,40},{32,48},{40,56},{48,64},{56,72},{64,... | collective-permute-start | bytes 294920 | tf_op jit(solution)/shard_map/ppermute | solution.py:387
  42.7 19.6 %collective-permute-start.8 = (bf16[144,6144]{1,0:T(8,128)(2,1)S(1)}, bf16[144,6144]{1,0:T(8,128)(2,1)S(1)}, u32[]{:S(2)}, u32[]{:S(2)}) collective-permute-start(bf16[144,6144]{1,0:T(8,128)(2,1)S(1)} %get-tuple-element.39.refs_1_), channel_id=1, source_target_pairs={{0,8},{8,16},{16,24},{24,32},{32,40},{40,48},{48,56},{56,64},{64,7... | collective-permute-start | bytes 5308424 | tf_op jit(solution)/shard_map/ppermute | solution.py:387
  42.8 19.1 %collective-permute-start.7 = (bf16[4,128,768]{2,1,0:T(8,128)(2,1)S(1)}, bf16[4,128,768]{2,1,0:T(8,128)(2,1)S(1)}, u32[]{:S(2)}, u32[]{:S(2)}) collective-permute-start(bf16[4,128,768]{2,1,0:T(8,128)(2,1)S(1)} %get-tuple-element.38), channel_id=1, source_target_pairs={{3,0},{2,1},{1,2},{0,3},{7,4},{6,5},{5,6},{4,7},{11,8},{10,9},{9,1... | collective-permute-start | bytes 2359304 | tf_op jit(solution)/shard_map/ppermute | solution.py:397
  46.7 19.8 %collective-permute-start.11 = (bf16[4,128,768]{2,1,0:T(8,128)(2,1)S(1)}, bf16[4,128,768]{2,1,0:T(8,128)(2,1)S(1)}, u32[]{:S(2)}, u32[]{:S(2)}) collective-permute-start(bf16[4,128,768]{2,1,0:T(8,128)(2,1)S(1)} %get-tuple-element.46), channel_id=1, source_target_pairs={{1,0},{0,1},{3,2},{2,3},{5,4},{4,5},{7,6},{6,7},{9,8},{8,9},{11,10... | collective-permute-start | bytes 2359304 | tf_op jit(solution)/shard_map/ppermute | solution.py:397
  46.8 34.8 %collective-permute-start.10 = (bf16[96,6144]{1,0:T(8,128)(2,1)S(1)}, bf16[96,6144]{1,0:T(8,128)(2,1)S(1)}, u32[]{:S(2)}, u32[]{:S(2)}) collective-permute-start(bf16[96,6144]{1,0:T(8,128)(2,1)S(1)} %get-tuple-element.41.refs_1_), channel_id=1, source_target_pairs={{0,8},{8,16},{16,24},{24,32},{32,40},{40,48},{48,56},{56,64},{64,7... | collective-permute-start | bytes 3538952 | tf_op jit(solution)/shard_map/ppermute | solution.py:387
  62.3 2.7 %copy-start = (bf16[1,6144,128]{2,1,0:T(8,128)(2,1)S(1)}, bf16[1,6144,128]{2,1,0:T(8,128)(2,1)}, u32[]{:S(2)}) copy-start(bf16[1,6144,128]{2,1,0:T(8,128)(2,1)} %param.17) | copy-start | bytes 4718596
  62.4 44.3 %collective-permute-start.9 = (bf16[96,6144]{1,0:T(8,128)(2,1)S(1)}, bf16[96,6144]{1,0:T(8,128)(2,1)S(1)}, u32[]{:S(2)}, u32[]{:S(2)}) collective-permute-start(bf16[96,6144]{1,0:T(8,128)(2,1)S(1)} %get-tuple-element.40.refs_1_), channel_id=1, source_target_pairs={{0,8},{8,16},{16,24},{24,32},{32,40},{40,48},{48,56},{56,64},{64,7... | collective-permute-start | bytes 3538952 | tf_op jit(solution)/shard_map/ppermute | solution.py:387
  66.7 8.2 %collective-permute-start.12 = (bf16[2,128,768]{2,1,0:T(8,128)(2,1)S(1)}, bf16[2,128,768]{2,1,0:T(8,128)(2,1)S(1)}, u32[]{:S(2)}, u32[]{:S(2)}) collective-permute-start(bf16[2,128,768]{2,1,0:T(8,128)(2,1)S(1)} %get-tuple-element.49), channel_id=1, source_target_pairs={{3,0},{2,1},{1,2},{0,3},{7,4},{6,5},{5,6},{4,7},{11,8},{10,9},{9,1... | collective-permute-start | bytes 1179656 | tf_op jit(solution)/shard_map/ppermute | solution.py:397
  69.2 12.3 %collective-permute-start.15 = (bf16[2,128,768]{2,1,0:T(8,128)(2,1)S(1)}, bf16[2,128,768]{2,1,0:T(8,128)(2,1)S(1)}, u32[]{:S(2)}, u32[]{:S(2)}) collective-permute-start(bf16[2,128,768]{2,1,0:T(8,128)(2,1)S(1)} %get-tuple-element.54), channel_id=1, source_target_pairs={{1,0},{0,1},{3,2},{2,3},{5,4},{4,5},{7,6},{6,7},{9,8},{8,9},{11,10... | collective-permute-start | bytes 1179656 | tf_op jit(solution)/shard_map/ppermute | solution.py:397
  75.0 14.7 %collective-permute-start.13 = (bf16[128,768]{1,0:T(8,128)(2,1)S(1)}, bf16[128,768]{1,0:T(8,128)(2,1)S(1)}, u32[]{:S(2)}, u32[]{:S(2)}) collective-permute-start(bf16[128,768]{1,0:T(8,128)(2,1)S(1)} %get-tuple-element.51), channel_id=1, source_target_pairs={{0,8},{1,9},{2,10},{3,11},{4,12},{5,13},{6,14},{7,15},{8,16},{9,17... | collective-permute-start | bytes 589832 | tf_op jit(solution)/shard_map/ppermute | solution.py:397
  79.2 25.7 %collective-permute-start.14 = (bf16[128,768]{1,0:T(8,128)(2,1)S(1)}, bf16[128,768]{1,0:T(8,128)(2,1)S(1)}, u32[]{:S(2)}, u32[]{:S(2)}) collective-permute-start(bf16[128,768]{1,0:T(8,128)(2,1)S(1)} %get-tuple-element.52), channel_id=1, source_target_pairs={{4,8},{5,9},{6,10},{7,11},{0,12},{1,13},{2,14},{3,15},{12,16},{13,... | collective-permute-start | bytes 589832 | tf_op jit(solution)/shard_map/ppermute | solution.py:397
  81.7 24.1 %collective-permute-start.16 = (bf16[128,768]{1,0:T(8,128)(2,1)S(1)}, bf16[128,768]{1,0:T(8,128)(2,1)S(1)}, u32[]{:S(2)}, u32[]{:S(2)}) collective-permute-start(bf16[128,768]{1,0:T(8,128)(2,1)S(1)} %get-tuple-element.55), channel_id=1, source_target_pairs={{0,248},{1,249},{2,250},{3,251},{4,252},{5,253},{6,254},{7,255},{8... | collective-permute-start | bytes 589832 | tf_op jit(solution)/shard_map/ppermute | solution.py:397
  82.3 23.5 %collective-permute-start.17 = (bf16[128,768]{1,0:T(8,128)(2,1)S(1)}, bf16[128,768]{1,0:T(8,128)(2,1)S(1)}, u32[]{:S(2)}, u32[]{:S(2)}) collective-permute-start(bf16[128,768]{1,0:T(8,128)(2,1)S(1)} %get-tuple-element.56), channel_id=1, source_target_pairs={{4,248},{5,249},{6,250},{7,251},{0,252},{1,253},{2,254},{3,255},{1... | collective-permute-start | bytes 589832 | tf_op jit(solution)/shard_map/ppermute | solution.py:397

commit v9 on v8

--- a/solution.py
+++ b/solution.py
@@ -18,7 +18,7 @@
 BLOCK = 768
 WORDS = BLOCK // 3
 CODES = BLOCK // 32
-SPANS = (48, 144, 96, 96)
+SPANS = (48, 96, 96, 96, 48)
 MIB = 1 << 20
 ROOT_2_PI = math.sqrt(2.0 / math.pi)
 VMEM = pl.BlockSpec(memory_space=pltpu.VMEM)
@@ -433,17 +433,21 @@
     )
     feedback, done = feedback_of(messages[0], arrived0, 0, None, True)
     up_kept, up_sent, message3 = halve(
-        up_kept, among(up_sent, 3), needs=[arrived1], carried=messages[3:4]
+        up_kept, among(up_sent, 3), needs=[arrived1, done], carried=messages[3:4]
     )
     arrived3 = along(message3, 1)
-    down_kept, down_sent = halve(down_kept, among(down_sent, 1), needs=[done])
+    down_kept, down_sent = halve(down_kept, among(down_sent, 1), needs=[up_sent])
     feedback, done = feedback_of(message1, arrived1, 1, feedback, True)
-    up_parts = split(up_kept, among(up_sent, 1), needs=[arrived2])
-    down_parts = split(down_kept, among(down_sent, 3), needs=[done])
+    *up_parts, message4 = split(
+        up_kept, among(up_sent, 1), needs=[arrived2, done], carried=messages[4:5]
+    )
+    arrived4 = along(message4, 1)
+    down_parts = split(down_kept, among(down_sent, 3), needs=[up_parts[0]])
     grad_up = finish([among(up_parts[half], 0, half, -1) for half in range(2)])
     grad_down = finish([among(down_parts[half], 0, half, 1) for half in range(2)])
     feedback = feedback_of(message2, arrived2, 2, feedback)[0]
     feedback = feedback_of(message3, arrived3, 3, feedback)[0]
+    feedback = feedback_of(message4, arrived4, 4, feedback)[0]
     return (feedback[None], grad_down[None], grad_up[None])
 
 

time: 109 us -> 111 us (1.018)
  starting transfers between devices: 34.8 us -> 36.6 us
  waiting for transfers between devices: 40 us -> 38.4 us
    ppermute x8, starting transfers between devices: 17.5 us -> 19.6 us  [among(): return lax.ppermute(value, both, pairs)]
    ppermute x8, waiting for transfers between devices: 33.7 us -> 32.4 us  [among(): return lax.ppermute(value, both, pairs)]
    pallas_call x18 -> x19, Pallas kernels: 28 us -> 29.1 us  [launch(): pl.pallas_call(wrapped, grid=grid, in_specs=[spec for _, spec in ins] + [...]
    ppermute x10 -> x11, starting transfers between devices: 17.3 us -> 17 us  [along(): return lax.ppermute(value, 'section', pairs)]
    ppermute x10 -> x11, waiting for transfers between devices: 6.29 us -> 5.97 us  [along(): return lax.ppermute(value, 'section', pairs)]
  transfers between devices with their start and end apart: 18 -> 19, of which waited for: 8 -> 8; matrix products, arithmetic and copies ran while one was open for 0% -> 0% of each run, Pallas kernels for 23% -> 24%
where the time goes in v9:
time: 111 us; the launch traced here: 110 us
  waiting for transfers between devices  38.4 us (35%)
  starting transfers between devices  36.6 us (33%)
  Pallas kernels  29.1 us (26%)
  local copies, waits for them, and re-layouts  5.39 us (5%)
    ppermute x8, waiting for transfers between devices, among(): return lax.ppermute(value, both, pairs)  32.4 us
    pallas_call x19, Pallas kernels, launch(): pl.pallas_call(wrapped, grid=grid, in_specs=[spec for _, spec in ins] + [...  29.1 us
    ppermute x8, starting transfers between devices, among(): return lax.ppermute(value, both, pairs)  19.6 us
    ppermute x11, starting transfers between devices, along(): return lax.ppermute(value, 'section', pairs)  17 us
    ppermute x11, waiting for transfers between devices, along(): return lax.ppermute(value, 'section', pairs)  5.97 us
    unnamed x16, local copies, waits for them, and re-layouts  5.39 us
  transfers between devices with their start and end apart: 19, of which 8 were waited for; matrix products, arithmetic and copies ran while one was open for 0% of the time, Pallas kernels for 24%

profile of v9, /device:TPU:1, one launch (start us, length us, event | category | flops | bytes accessed | tf_op | source)
XLA Modules:
  0.0 110.5 jit_solution(17751036320615744984)
XLA Ops:
  0.6 3.3 %collective-permute-start.1 = (bf16[6144,128]{1,0:T(8,128)(2,1)}, bf16[6144,128]{1,0:T(8,128)(2,1)S(1)}, u32[]{:S(2)}, u32[]{:S(2)}) collective-permute-start(bf16[6144,128]{1,0:T(8,128)(2,1)} %bitcast.31), channel_id=1, source_target_pairs={{0,248},{8,0},{16,8},{24,16},{32,24},{40,32},{48,40},{56,48},{64,5... | collective-permute-start | bytes 4718600 | tf_op jit(solution)/shard_map/ppermute | solution.py:387
  4.0 1.9 %copy-done.1 = s32[1,384,2048]{2,1,0:T(8,128)S(1)} copy-done((s32[1,384,2048]{2,1,0:T(8,128)S(1)}, s32[1,384,2048]{2,1,0:T(8,128)}, u32[]{:S(2)}) %copy-start.1) | copy-done | bytes 3145752
  5.8 1.0 copy-done.3
  8.4 1.8 %message.2 = (bf16[48,6144]{1,0:T(8,128)(2,1)S(1)}, f32[48,256]{1,0:T(8,128)S(1)}) custom-call(s32[384,2048]{1,0:T(8,128)S(1)} %bitcast.20, bf16[192,384]{1,0:T(8,128)(2,1)S(1)} %bitcast.25, bf16[32,6144]{1,0:T(8,128)(2,1)S(1)} %bitcast.23, s32[1,384]{1,0:T(1,128)S(1)} %copy-done.6), custom_call_target="tpu_custom_call" | custom-call | flops 1 | bytes 1 | tf_op jit(solution)/shard_map/message/pallas_call | solution.py:46
  10.7 4.4 %collective-permute-start = (f32[1,6144]{1,0:T(1,128)}, f32[1,6144]{1,0:T(1,128)S(1)}, u32[]{:S(2)}, u32[]{:S(2)}) collective-permute-start(f32[1,6144]{1,0:T(1,128)} %param.15), channel_id=1, source_target_pairs={{0,248},{8,0},{16,8},{24,16},{32,24},{40,32},{48,40},{56,48},{64,5... | collective-permute-start | bytes 73736 | tf_op jit(solution)/shard_map/ppermute | solution.py:387
  15.7 6.1 %message.3 = (bf16[96,6144]{1,0:T(8,128)(2,1)S(1)}, bf16[96,6144]{1,0:T(8,128)(2,1)S(1)}, bf16[96,6144]{1,0:T(8,128)(2,1)S(1)}, bf16[48,6144]{1,0:T(8,128)(2,1)S(1)}, f32[336,256]{1,0:T(8,128)S(1)}) custom-call(s32[384,2048]{1,0:T(8,128)S(1)} %bitcast.21, bf16[192,384]{1,0:T(8,128)(2,1)S(1)} %bitcast.26, bf16[32,6144]{1,0:T(8,128)(2,1)S(1)} %bitcast.24, ...), custom_call_target="tpu_custom_call" | custom-call | flops 1 | bytes 1 | tf_op jit(solution)/shard_map/message/pallas_call | solution.py:46
  21.8 2.6 %gradient.1.refs_8_.refs_0_ = bf16[384,6144]{1,0:T(8,128)(2,1)S(1)} custom-call(bf16[384,6144]{1,0:T(8,128)(2,1)S(1)} %bitcast.22, bf16[192,384]{1,0:T(8,128)(2,1)S(1)} %bitcast.27, bf16[96,6144]{1,0:T(8,128)(2,1)S(1)} %get-tuple-element.33.refs_2_.refs_5_), custom_call_target="tpu_custom_call" | custom-call | flops 1 | bytes 1 | tf_op jit(solution)/shard_map/gradient/pallas_call | solution.py:46
  24.4 2.3 %hidden.1.refs_0_ = bf16[384,6144]{1,0:T(8,128)(2,1)S(1)} custom-call(f32[1,6144]{1,0:T(1,128)S(1)} %collective-permute-done.refs_0_, bf16[48,6144]{1,0:T(8,128)(2,1)S(1)} %get-tuple-element.32.refs_4_.refs_1_, bf16[96,6144]{1,0:T(8,128)(2,1)S(1)} %get-tuple-element.33.refs_2_.refs_5_, bf16[96,6144]{1,0:T(8,128)(2,1)S(1)} %get-tuple-element.34.refs_3_.refs_6_, ...), custom_call_target="tpu_custom_call" | custom-call | flops 1 | bytes 1 | tf_op jit(solution)/shard_map/hidden/pallas_call | solution.py:46
  26.8 1.4 %down.1 = (f32[384,128]{1,0:T(8,128)S(1)}, bf16[384,128]{1,0:T(8,128)(2,1)S(1)}) custom-call(bf16[384,6144]{1,0:T(8,128)(2,1)S(1)} %hidden.1.refs_0_, bf16[6144,128]{1,0:T(8,128)(2,1)S(1)} %collective-permute-done.1.refs_1_, bf16[6144,128]{1,0:T(8,128)(2,1)S(1)} %collective-permute-done.2.refs_2_.refs_1_), custom_call_target="tpu_custom_call" | custom-call | flops 1 | bytes 1 | tf_op jit(solution)/shard_map/down/pallas_call | solution.py:46
  28.2 1.4 %back.1 = bf16[384,128]{1,0:T(8,128)(2,1)S(1)} custom-call(bf16[384,6144]{1,0:T(8,128)(2,1)S(1)} %gradient.1.refs_8_.refs_0_, bf16[6144,128]{1,0:T(8,128)(2,1)S(1)} %collective-permute-done.2.refs_2_.refs_1_, bf16[384,128]{1,0:T(8,128)(2,1)S(1)} %get-tuple-element.39.refs_2_), custom_call_target="tpu_custom_call" | custom-call | flops 1 | bytes 1 | tf_op jit(solution)/shard_map/back/pallas_call | solution.py:46
  29.6 6.2 %collective-permute-start.6 = (bf16[384,128]{1,0:T(8,128)(2,1)S(1)}, bf16[384,128]{1,0:T(8,128)(2,1)S(1)}, u32[]{:S(2)}, u32[]{:S(2)}) collective-permute-start(bf16[384,128]{1,0:T(8,128)(2,1)S(1)} %back.1), channel_id=1, source_target_pairs={{0,240},{8,248},{16,0},{24,8},{32,16},{40,24},{48,32},{56,40},{64,... | collective-permute-start | bytes 294920 | tf_op jit(solution)/shard_map/ppermute | solution.py:387
  35.8 1.6 %collective-permute-done.6.refs_4_.refs_2_ = bf16[384,128]{1,0:T(8,128)(2,1)S(1)} collective-permute-done((bf16[384,128]{1,0:T(8,128)(2,1)S(1)}, bf16[384,128]{1,0:T(8,128)(2,1)S(1)}, u32[]{:S(2)}, u32[]{:S(2)}) %collective-permute-start.6) | collective-permute-done | bytes 98336 | tf_op jit(solution)/shard_map/ppermute | solution.py:387
  37.7 4.0 %collective-permute-done.3.refs_1_ = bf16[384,128]{1,0:T(8,128)(2,1)S(1)} collective-permute-done((bf16[384,128]{1,0:T(8,128)(2,1)S(1)}, bf16[384,128]{1,0:T(8,128)(2,1)S(1)}, u32[]{:S(2)}, u32[]{:S(2)}) %collective-permute-start.3) | collective-permute-done | bytes 98336 | tf_op jit(solution)/shard_map/ppermute | solution.py:387
  41.7 1.0 grad_up.1
  42.8 2.7 %collective-permute-start.7 = (bf16[4,128,768]{2,1,0:T(8,128)(2,1)S(1)}, bf16[4,128,768]{2,1,0:T(8,128)(2,1)S(1)}, u32[]{:S(2)}, u32[]{:S(2)}) collective-permute-start(bf16[4,128,768]{2,1,0:T(8,128)(2,1)S(1)} %get-tuple-element.41), channel_id=1, source_target_pairs={{3,0},{2,1},{1,2},{0,3},{7,4},{6,5},{5,6},{4,7},{11,8},{10,9},{9,1... | collective-permute-start | bytes 2359304 | tf_op jit(solution)/shard_map/ppermute | solution.py:397
  45.6 1.1 grad_down.1
  47.0 1.5 %feedback.5 = (bf16[384,6144]{1,0:T(8,128)(2,1)}, f32[8,128]{1,0:T(8,128)S(1)}) custom-call(bf16[48,6144]{1,0:T(8,128)(2,1)S(1)} %collective-permute-done.5.refs_3_.refs_0_, bf16[48,6144]{1,0:T(8,128)(2,1)S(1)} %get-tuple-element.32.refs_4_.refs_1_, bf16[384,128]{1,0:T(8,128)(2,1)S(1)} %collective-permute-done.4.refs_2_, bf16[6144,128]{1,0:T(8,128)(2,1)S(1)} %bitcast.15), custom_call_target="tpu_custom_call" | custom-call | flops 1 | bytes 1 | tf_op jit(solution)/shard_map/feedback/pallas_call | solution.py:46
  48.5 13.4 %collective-permute-done.7.refs_1_ = bf16[4,128,768]{2,1,0:T(8,128)(2,1)S(1)} collective-permute-done((bf16[4,128,768]{2,1,0:T(8,128)(2,1)S(1)}, bf16[4,128,768]{2,1,0:T(8,128)(2,1)S(1)}, u32[]{:S(2)}, u32[]{:S(2)}) %collective-permute-start.7) | collective-permute-done | bytes 786464 | tf_op jit(solution)/shard_map/ppermute | solution.py:397
  62.1 1.9 %collective-permute-start.12 = (bf16[96,6144]{1,0:T(8,128)(2,1)S(1)}, bf16[96,6144]{1,0:T(8,128)(2,1)S(1)}, u32[]{:S(2)}, u32[]{:S(2)}) collective-permute-start(bf16[96,6144]{1,0:T(8,128)(2,1)S(1)} %get-tuple-element.50.refs_1_), channel_id=1, source_target_pairs={{0,8},{8,16},{16,24},{24,32},{32,40},{40,48},{48,56},{56,64},{64,7... | collective-permute-start | bytes 3538952 | tf_op jit(solution)/shard_map/ppermute | solution.py:387
  64.4 2.3 %collective-permute-start.14 = (bf16[2,128,768]{2,1,0:T(8,128)(2,1)S(1)}, bf16[2,128,768]{2,1,0:T(8,128)(2,1)S(1)}, u32[]{:S(2)}, u32[]{:S(2)}) collective-permute-start(bf16[2,128,768]{2,1,0:T(8,128)(2,1)S(1)} %get-tuple-element.56), channel_id=1, source_target_pairs={{3,0},{2,1},{1,2},{0,3},{7,4},{6,5},{5,6},{4,7},{11,8},{10,9},{9,1... | collective-permute-start | bytes 1179656 | tf_op jit(solution)/shard_map/ppermute | solution.py:397
  66.7 2.1 %feedback.6 = (bf16[384,6144]{1,0:T(8,128)(2,1)}, f32[8,128]{1,0:T(8,128)S(1)}) custom-call(bf16[96,6144]{1,0:T(8,128)(2,1)S(1)} %collective-permute-done.8.refs_2_.refs_0_, bf16[96,6144]{1,0:T(8,128)(2,1)S(1)} %get-tuple-element.42.refs_1_, bf16[384,128]{1,0:T(8,128)(2,1)S(1)} %collective-permute-done.4.refs_2_, ...), custom_call_target="tpu_custom_call", output_to_operand_aliasing={{0}: (4, {})} | custom-call | flops 1 | bytes 1 | tf_op jit(solution)/shard_map/feedback/pallas_call | solution.py:46
  68.8 5.3 %collective-permute-done.9.refs_1_ = bf16[2,128,768]{2,1,0:T(8,128)(2,1)S(1)} collective-permute-done((bf16[2,128,768]{2,1,0:T(8,128)(2,1)S(1)}, bf16[2,128,768]{2,1,0:T(8,128)(2,1)S(1)}, u32[]{:S(2)}, u32[]{:S(2)}) %collective-permute-start.9) | collective-permute-done | bytes 393248 | tf_op jit(solution)/shard_map/ppermute | solution.py:397
  74.9 3.0 %collective-permute-start.15 = (bf16[128,768]{1,0:T(8,128)(2,1)S(1)}, bf16[128,768]{1,0:T(8,128)(2,1)S(1)}, u32[]{:S(2)}, u32[]{:S(2)}) collective-permute-start(bf16[128,768]{1,0:T(8,128)(2,1)S(1)} %get-tuple-element.58), channel_id=1, source_target_pairs={{0,8},{1,9},{2,10},{3,11},{4,12},{5,13},{6,14},{7,15},{8,16},{9,17... | collective-permute-start | bytes 589832 | tf_op jit(solution)/shard_map/ppermute | solution.py:397
  77.9 2.4 %collective-permute-start.16 = (bf16[128,768]{1,0:T(8,128)(2,1)S(1)}, bf16[128,768]{1,0:T(8,128)(2,1)S(1)}, u32[]{:S(2)}, u32[]{:S(2)}) collective-permute-start(bf16[128,768]{1,0:T(8,128)(2,1)S(1)} %get-tuple-element.59), channel_id=1, source_target_pairs={{4,8},{5,9},{6,10},{7,11},{0,12},{1,13},{2,14},{3,15},{12,16},{13,... | collective-permute-start | bytes 589832 | tf_op jit(solution)/shard_map/ppermute | solution.py:397
  81.2 8.5 %collective-permute-done.15.refs_0_ = bf16[128,768]{1,0:T(8,128)(2,1)S(1)} collective-permute-done((bf16[128,768]{1,0:T(8,128)(2,1)S(1)}, bf16[128,768]{1,0:T(8,128)(2,1)S(1)}, u32[]{:S(2)}, u32[]{:S(2)}) %collective-permute-start.15) | collective-permute-done | bytes 196640 | tf_op jit(solution)/shard_map/ppermute | solution.py:397
  89.7 8.2 %collective-permute-start.17 = (bf16[128,768]{1,0:T(8,128)(2,1)S(1)}, bf16[128,768]{1,0:T(8,128)(2,1)S(1)}, u32[]{:S(2)}, u32[]{:S(2)}) collective-permute-start(bf16[128,768]{1,0:T(8,128)(2,1)S(1)} %get-tuple-element.57.refs_2_), channel_id=1, source_target_pairs={{0,248},{1,249},{2,250},{3,251},{4,252},{5,253},{6,254},{7,255},{8... | collective-permute-start | bytes 589832 | tf_op jit(solution)/shard_map/ppermute | solution.py:397
  97.8 2.0 %feedback.7.refs_4_ = bf16[384,6144]{1,0:T(8,128)(2,1)} custom-call(bf16[96,6144]{1,0:T(8,128)(2,1)S(1)} %collective-permute-done.10.refs_2_.refs_0_, bf16[96,6144]{1,0:T(8,128)(2,1)S(1)} %get-tuple-element.46.refs_1_, bf16[384,128]{1,0:T(8,128)(2,1)S(1)} %collective-permute-done.4.refs_2_, ...), custom_call_target="tpu_custom_call", output_to_operand_aliasing={{}: (4, {})} | custom-call | flops 1 | bytes 1 | tf_op jit(solution)/shard_map/feedback/pallas_call | solution.py:46
  99.9 5.0 %collective-permute-done.16.refs_1_ = bf16[128,768]{1,0:T(8,128)(2,1)S(1)} collective-permute-done((bf16[128,768]{1,0:T(8,128)(2,1)S(1)}, bf16[128,768]{1,0:T(8,128)(2,1)S(1)}, u32[]{:S(2)}, u32[]{:S(2)}) %collective-permute-start.16) | collective-permute-done | bytes 196640 | tf_op jit(solution)/shard_map/ppermute | solution.py:397
  104.9 0.9 finish.2
  105.8 0.9 finish.3
  106.7 2.1 %feedback.8.refs_4_ = bf16[384,6144]{1,0:T(8,128)(2,1)} custom-call(bf16[96,6144]{1,0:T(8,128)(2,1)S(1)} %collective-permute-done.12.refs_0_, bf16[96,6144]{1,0:T(8,128)(2,1)S(1)} %get-tuple-element.50.refs_1_, bf16[384,128]{1,0:T(8,128)(2,1)S(1)} %collective-permute-done.4.refs_2_, bf16[6144,128]{1,0:T(8,128)(2,1)S(1)} %bitcast.18, ...), custom_call_target="tpu_custom_call", output_to_operand_aliasing={{}: (4, {})} | custom-call | flops 1 | bytes 1 | tf_op jit(solution)/shard_map/feedback/pallas_call | solution.py:46
  108.8 1.5 %feedback.9 = bf16[384,6144]{1,0:T(8,128)(2,1)} custom-call(bf16[48,6144]{1,0:T(8,128)(2,1)S(1)} %collective-permute-done.11.refs_0_, bf16[48,6144]{1,0:T(8,128)(2,1)S(1)} %get-tuple-element.49.refs_1_, bf16[384,128]{1,0:T(8,128)(2,1)S(1)} %collective-permute-done.4.refs_2_, bf16[6144,128]{1,0:T(8,128)(2,1)S(1)} %bitcast.19, ...), custom_call_target="tpu_custom_call", output_to_operand_aliasing={{}: (4, {})} | custom-call | flops 1 | bytes 1 | tf_op jit(solution)/shard_map/feedback/pallas_call | solution.py:46
  (41 shorter events, 5.7 us)
Async XLA Ops:
  0.6 26.1 %collective-permute-start.1 = (bf16[6144,128]{1,0:T(8,128)(2,1)}, bf16[6144,128]{1,0:T(8,128)(2,1)S(1)}, u32[]{:S(2)}, u32[]{:S(2)}) collective-permute-start(bf16[6144,128]{1,0:T(8,128)(2,1)} %bitcast.31), channel_id=1, source_target_pairs={{0,248},{8,0},{16,8},{24,16},{32,24},{40,32},{48,40},{56,48},{64,5... | collective-permute-start | bytes 4718600 | tf_op jit(solution)/shard_map/ppermute | solution.py:387
  3.9 22.8 %collective-permute-start.2 = (bf16[6144,128]{1,0:T(8,128)(2,1)}, bf16[6144,128]{1,0:T(8,128)(2,1)S(1)}, u32[]{:S(2)}, u32[]{:S(2)}) collective-permute-start(bf16[6144,128]{1,0:T(8,128)(2,1)} %bitcast.14), channel_id=1, source_target_pairs={{0,8},{8,16},{16,24},{24,32},{32,40},{40,48},{48,56},{56,64},{64,7... | collective-permute-start | bytes 4718600 | tf_op jit(solution)/shard_map/ppermute | solution.py:387
  4.0 1.9 %copy-start.1 = (s32[1,384,2048]{2,1,0:T(8,128)S(1)}, s32[1,384,2048]{2,1,0:T(8,128)}, u32[]{:S(2)}) copy-start(s32[1,384,2048]{2,1,0:T(8,128)} %param.9) | copy-start | bytes 9437188
  5.8 1.0 copy-start.3
  6.8 0.9 copy-start.4
  7.8 0.7 copy-start.6
  8.4 13.4 %copy-start.2 = (bf16[1,384,6144]{2,1,0:T(8,128)(2,1)S(1)}, bf16[1,384,6144]{2,1,0:T(8,128)(2,1)}, u32[]{:S(2)}) copy-start(bf16[1,384,6144]{2,1,0:T(8,128)(2,1)} %param.13) | copy-start | bytes 14155780
  10.3 11.5 %copy-start.5 = (bf16[1,384,192]{1,2,0:T(8,128)(2,1)S(1)}, bf16[1,384,192]{1,2,0:T(8,128)(2,1)}, u32[]{:S(2)}) copy-start(bf16[1,384,192]{1,2,0:T(8,128)(2,1)} %param.14) | copy-start | bytes 442372
  10.3 25.5 %collective-permute-start.5 = (bf16[48,6144]{1,0:T(8,128)(2,1)S(1)}, bf16[48,6144]{1,0:T(8,128)(2,1)S(1)}, u32[]{:S(2)}, u32[]{:S(2)}) collective-permute-start(bf16[48,6144]{1,0:T(8,128)(2,1)S(1)} %get-tuple-element.32.refs_4_.refs_1_), channel_id=1, source_target_pairs={{0,8},{8,16},{16,24},{24,32},{32,40},{40,48},{48,56},{56,64},{64,7... | collective-permute-start | bytes 1769480 | tf_op jit(solution)/shard_map/ppermute | solution.py:387
  10.7 13.7 %collective-permute-start = (f32[1,6144]{1,0:T(1,128)}, f32[1,6144]{1,0:T(1,128)S(1)}, u32[]{:S(2)}, u32[]{:S(2)}) collective-permute-start(f32[1,6144]{1,0:T(1,128)} %param.15), channel_id=1, source_target_pairs={{0,248},{8,0},{16,8},{24,16},{32,24},{40,32},{48,40},{56,48},{64,5... | collective-permute-start | bytes 73736 | tf_op jit(solution)/shard_map/ppermute | solution.py:387
  15.0 0.7 copy-start.7
  29.6 7.9 %collective-permute-start.6 = (bf16[384,128]{1,0:T(8,128)(2,1)S(1)}, bf16[384,128]{1,0:T(8,128)(2,1)S(1)}, u32[]{:S(2)}, u32[]{:S(2)}) collective-permute-start(bf16[384,128]{1,0:T(8,128)(2,1)S(1)} %back.1), channel_id=1, source_target_pairs={{0,240},{8,248},{16,0},{24,8},{32,16},{40,24},{48,32},{56,40},{64,... | collective-permute-start | bytes 294920 | tf_op jit(solution)/shard_map/ppermute | solution.py:387
  35.8 2.0 %collective-permute-start.4 = (bf16[384,128]{1,0:T(8,128)(2,1)S(1)}, bf16[384,128]{1,0:T(8,128)(2,1)S(1)}, u32[]{:S(2)}, u32[]{:S(2)}) collective-permute-start(bf16[384,128]{1,0:T(8,128)(2,1)S(1)} %get-tuple-element.39.refs_2_), channel_id=1, source_target_pairs={{0,8},{8,16},{16,24},{24,32},{32,40},{40,48},{48,56},{56,64},{64,7... | collective-permute-start | bytes 294920 | tf_op jit(solution)/shard_map/ppermute | solution.py:387
  35.8 6.0 %collective-permute-start.3 = (bf16[384,128]{1,0:T(8,128)(2,1)S(1)}, bf16[384,128]{1,0:T(8,128)(2,1)S(1)}, u32[]{:S(2)}, u32[]{:S(2)}) collective-permute-start(bf16[384,128]{1,0:T(8,128)(2,1)S(1)} %get-tuple-element.39.refs_2_), channel_id=1, source_target_pairs={{0,16},{8,24},{16,32},{24,40},{32,48},{40,56},{48,64},{56,72},{64,... | collective-permute-start | bytes 294920 | tf_op jit(solution)/shard_map/ppermute | solution.py:387
  42.7 19.2 %collective-permute-start.8 = (bf16[96,6144]{1,0:T(8,128)(2,1)S(1)}, bf16[96,6144]{1,0:T(8,128)(2,1)S(1)}, u32[]{:S(2)}, u32[]{:S(2)}) collective-permute-start(bf16[96,6144]{1,0:T(8,128)(2,1)S(1)} %get-tuple-element.42.refs_1_), channel_id=1, source_target_pairs={{0,8},{8,16},{16,24},{24,32},{32,40},{40,48},{48,56},{56,64},{64,7... | collective-permute-start | bytes 3538952 | tf_op jit(solution)/shard_map/ppermute | solution.py:387
  42.8 19.1 %collective-permute-start.7 = (bf16[4,128,768]{2,1,0:T(8,128)(2,1)S(1)}, bf16[4,128,768]{2,1,0:T(8,128)(2,1)S(1)}, u32[]{:S(2)}, u32[]{:S(2)}) collective-permute-start(bf16[4,128,768]{2,1,0:T(8,128)(2,1)S(1)} %get-tuple-element.41), channel_id=1, source_target_pairs={{3,0},{2,1},{1,2},{0,3},{7,4},{6,5},{5,6},{4,7},{11,8},{10,9},{9,1... | collective-permute-start | bytes 2359304 | tf_op jit(solution)/shard_map/ppermute | solution.py:397
  45.6 23.2 %collective-permute-start.10 = (bf16[96,6144]{1,0:T(8,128)(2,1)S(1)}, bf16[96,6144]{1,0:T(8,128)(2,1)S(1)}, u32[]{:S(2)}, u32[]{:S(2)}) collective-permute-start(bf16[96,6144]{1,0:T(8,128)(2,1)S(1)} %get-tuple-element.46.refs_1_), channel_id=1, source_target_pairs={{0,8},{8,16},{16,24},{24,32},{32,40},{40,48},{48,56},{56,64},{64,7... | collective-permute-start | bytes 3538952 | tf_op jit(solution)/shard_map/ppermute | solution.py:387
  45.6 1.4 %copy-start = (bf16[1,6144,128]{2,1,0:T(8,128)(2,1)S(1)}, bf16[1,6144,128]{2,1,0:T(8,128)(2,1)}, u32[]{:S(2)}) copy-start(bf16[1,6144,128]{2,1,0:T(8,128)(2,1)} %param.17) | copy-start | bytes 4718596
  46.7 17.5 %collective-permute-start.13 = (bf16[4,128,768]{2,1,0:T(8,128)(2,1)S(1)}, bf16[4,128,768]{2,1,0:T(8,128)(2,1)S(1)}, u32[]{:S(2)}, u32[]{:S(2)}) collective-permute-start(bf16[4,128,768]{2,1,0:T(8,128)(2,1)S(1)} %get-tuple-element.54), channel_id=1, source_target_pairs={{1,0},{0,1},{3,2},{2,3},{5,4},{4,5},{7,6},{6,7},{9,8},{8,9},{11,10... | collective-permute-start | bytes 2359304 | tf_op jit(solution)/shard_map/ppermute | solution.py:397
  62.1 44.6 %collective-permute-start.12 = (bf16[96,6144]{1,0:T(8,128)(2,1)S(1)}, bf16[96,6144]{1,0:T(8,128)(2,1)S(1)}, u32[]{:S(2)}, u32[]{:S(2)}) collective-permute-start(bf16[96,6144]{1,0:T(8,128)(2,1)S(1)} %get-tuple-element.50.refs_1_), channel_id=1, source_target_pairs={{0,8},{8,16},{16,24},{24,32},{32,40},{40,48},{48,56},{56,64},{64,7... | collective-permute-start | bytes 3538952 | tf_op jit(solution)/shard_map/ppermute | solution.py:387
  64.0 10.1 %collective-permute-start.9 = (bf16[2,128,768]{2,1,0:T(8,128)(2,1)S(1)}, bf16[2,128,768]{2,1,0:T(8,128)(2,1)S(1)}, u32[]{:S(2)}, u32[]{:S(2)}) collective-permute-start(bf16[2,128,768]{2,1,0:T(8,128)(2,1)S(1)} %get-tuple-element.45.refs_2_), channel_id=1, source_target_pairs={{1,0},{0,1},{3,2},{2,3},{5,4},{4,5},{7,6},{6,7},{9,8},{8,9},{11,10... | collective-permute-start | bytes 1179656 | tf_op jit(solution)/shard_map/ppermute | solution.py:397
  64.4 10.4 %collective-permute-start.14 = (bf16[2,128,768]{2,1,0:T(8,128)(2,1)S(1)}, bf16[2,128,768]{2,1,0:T(8,128)(2,1)S(1)}, u32[]{:S(2)}, u32[]{:S(2)}) collective-permute-start(bf16[2,128,768]{2,1,0:T(8,128)(2,1)S(1)} %get-tuple-element.56), channel_id=1, source_target_pairs={{3,0},{2,1},{1,2},{0,3},{7,4},{6,5},{5,6},{4,7},{11,8},{10,9},{9,1... | collective-permute-start | bytes 1179656 | tf_op jit(solution)/shard_map/ppermute | solution.py:397
  74.1 34.7 %collective-permute-start.11 = (bf16[48,6144]{1,0:T(8,128)(2,1)S(1)}, bf16[48,6144]{1,0:T(8,128)(2,1)S(1)}, u32[]{:S(2)}, u32[]{:S(2)}) collective-permute-start(bf16[48,6144]{1,0:T(8,128)(2,1)S(1)} %get-tuple-element.49.refs_1_), channel_id=1, source_target_pairs={{0,8},{8,16},{16,24},{24,32},{32,40},{40,48},{48,56},{56,64},{64,7... | collective-permute-start | bytes 1769480 | tf_op jit(solution)/shard_map/ppermute | solution.py:387
  74.9 14.8 %collective-permute-start.15 = (bf16[128,768]{1,0:T(8,128)(2,1)S(1)}, bf16[128,768]{1,0:T(8,128)(2,1)S(1)}, u32[]{:S(2)}, u32[]{:S(2)}) collective-permute-start(bf16[128,768]{1,0:T(8,128)(2,1)S(1)} %get-tuple-element.58), channel_id=1, source_target_pairs={{0,8},{1,9},{2,10},{3,11},{4,12},{5,13},{6,14},{7,15},{8,16},{9,17... | collective-permute-start | bytes 589832 | tf_op jit(solution)/shard_map/ppermute | solution.py:397
  77.9 26.9 %collective-permute-start.16 = (bf16[128,768]{1,0:T(8,128)(2,1)S(1)}, bf16[128,768]{1,0:T(8,128)(2,1)S(1)}, u32[]{:S(2)}, u32[]{:S(2)}) collective-permute-start(bf16[128,768]{1,0:T(8,128)(2,1)S(1)} %get-tuple-element.59), channel_id=1, source_target_pairs={{4,8},{5,9},{6,10},{7,11},{0,12},{1,13},{2,14},{3,15},{12,16},{13,... | collective-permute-start | bytes 589832 | tf_op jit(solution)/shard_map/ppermute | solution.py:397
  80.4 25.4 %collective-permute-start.18 = (bf16[128,768]{1,0:T(8,128)(2,1)S(1)}, bf16[128,768]{1,0:T(8,128)(2,1)S(1)}, u32[]{:S(2)}, u32[]{:S(2)}) collective-permute-start(bf16[128,768]{1,0:T(8,128)(2,1)S(1)} %get-tuple-element.60), channel_id=1, source_target_pairs={{4,248},{5,249},{6,250},{7,251},{0,252},{1,253},{2,254},{3,255},{1... | collective-permute-start | bytes 589832 | tf_op jit(solution)/shard_map/ppermute | solution.py:397
  89.7 16.1 %collective-permute-start.17 = (bf16[128,768]{1,0:T(8,128)(2,1)S(1)}, bf16[128,768]{1,0:T(8,128)(2,1)S(1)}, u32[]{:S(2)}, u32[]{:S(2)}) collective-permute-start(bf16[128,768]{1,0:T(8,128)(2,1)S(1)} %get-tuple-element.57.refs_2_), channel_id=1, source_target_pairs={{0,248},{1,249},{2,250},{3,251},{4,252},{5,253},{6,254},{7,255},{8... | collective-permute-start | bytes 589832 | tf_op jit(solution)/shard_map/ppermute | solution.py:397

commit v10 on v9

--- a/solution.py
+++ b/solution.py
@@ -16,9 +16,10 @@
 BF16 = jnp.bfloat16
 TILE = 48
 BLOCK = 768
+HALF = D // 2
 WORDS = BLOCK // 3
 CODES = BLOCK // 32
-SPANS = (48, 96, 96, 96, 48)
+SPANS = (96, 96, 96, 96)
 MIB = 1 << 20
 ROOT_2_PI = math.sqrt(2.0 / math.pi)
 VMEM = pl.BlockSpec(memory_space=pltpu.VMEM)
@@ -55,6 +56,10 @@
         cost_estimate=pl.CostEstimate(flops=1, bytes_accessed=1, transcendentals=0),
         name=name,
     )(*[value for value, _ in ins], *needs, *carried)
+
+
+def hand_on(value, after):
+    return launch(lambda: None, "hand_on", [], [], needs=[after], carried=[value], grant=1)[0]
 
 
 def lanes(shape):
@@ -234,15 +239,34 @@
     )
 
 
-def back_kernel(grad_ref, weight_ref, out_ref):
-    out_ref[...] = jnp.dot(
-        grad_ref[...], weight_ref[...], preferred_element_type=F32
-    ).astype(BF16)
-
-
-def project_back(grad, weight, **ties):
-    return launch(
-        back_kernel, "back", [(grad, VMEM), (weight, VMEM)],
+def pick_half_kernel(weight_ref, out_ref, sem):
+    half = lax.rem(lax.axis_index("dp"), 2)
+    rows = pl.ds(pl.multiple_of(half * HALF, HALF), HALF)
+    copy = pltpu.make_async_copy(weight_ref.at[rows], out_ref, sem.at[0])
+    copy.start()
+    copy.wait()
+
+
+def pick_half(weight):
+    return launch(
+        pick_half_kernel, "pick_half", [(weight, ANY)], [(array((HALF, R), BF16), VMEM)],
+        [pltpu.SemaphoreType.DMA((1,))],
+    )[0]
+
+
+def back_kernel(grad_ref, chip_ref, mine_ref, other_ref, out_ref):
+    half = lax.rem(lax.axis_index("dp"), 2)
+    total = jnp.zeros((TOK, R), F32)
+    for where, part_ref in ((half, mine_ref), (1 - half, other_ref)):
+        at = pl.ds(pl.multiple_of(where * HALF, HALF), HALF)
+        weight = part_ref[...] + chip_ref[at, :]
+        total += jnp.dot(grad_ref[:, at], weight, preferred_element_type=F32)
+    out_ref[...] = total.astype(BF16)
+
+
+def project_back(grad, chip, mine, other, **ties):
+    return launch(
+        back_kernel, "back", [(value, VMEM) for value in (grad, chip, mine, other)],
         [(array((TOK, R), BF16), VMEM)], **ties,
     )
 
@@ -386,9 +410,9 @@
         pairs = [(s, (s + distance) % sections) for s in range(sections)]
         return lax.ppermute(value, "section", pairs)
 
-    def among(value, flip_x, flip_y=0, section_step=0):
+    def among(value, flip_x, flip_y=0, section_step=0, stride=1):
         pairs = []
-        for s in range(sections):
+        for s in range(0, sections, stride):
             for d in range(replicas):
                 y, x = divmod(d, across)
                 source = (y ^ flip_y) * across + (x ^ flip_x)
@@ -397,7 +421,10 @@
         return lax.ppermute(value, both, pairs)
 
     up = w_up[0]
-    up_before = along(up, 1)
+    odd_to_even = [(s, (s + 1) % sections) for s in range(1, sections, 2)]
+    even_to_odd = [(s, s + 1) for s in range(0, sections, 2)]
+    up_chip = lax.ppermute(up, "section", even_to_odd)
+    up_mine = lax.ppermute(pick_half(up), "section", odd_to_even)
     down_next = along(w_down[0], -1)
     gain_next = along(norm_gain, -1)
 
@@ -409,14 +436,18 @@
         codes, scales, base, sample_ids, firsts[1], SPANS[1:], needs=[message0]
     )
     messages = [message0, *later]
+    up_mine = hand_on(up_mine, stats1)
+    up_other = among(up_mine, 1, stride=2)
     gradient = make_gradient(backward_codes[0], backward_scales[0].T, needs=[later[0]])
 
     hidden = make_hidden(messages, [stats0, stats1], gain_next, needs=[gradient])
-    pre_next, act_next = project_down(hidden, down_next, needs=[up_before])
+    pre_next, act_next = project_down(hidden, down_next, needs=[up_chip])
     act_before = along(act_next, 2)
     act_own = along(act_next, 1)
     arrived0 = along(messages[0], 1)
-    dact_before = project_back(gradient, up_before, needs=[act_next])[0]
+    dact_before = project_back(
+        gradient, up_chip, up_mine, up_other, needs=[act_before, act_own]
+    )[0]
     dact_next = along(dact_before, -2)
 
     def feedback_of(own, x, at, before, marked=False):
@@ -424,7 +455,7 @@
 
     up_kept, up_sent, message1, message2 = partial_grad(
         read_act, "grad_up", (0, 1, 3, 2), gradient, act_before,
-        needs=[act_own, arrived0, dact_next], carried=messages[1:3],
+        needs=[arrived0, dact_before], carried=messages[1:3],
     )
     arrived1 = along(message1, 1)
     arrived2 = along(message2, 1)
@@ -438,16 +469,12 @@
     arrived3 = along(message3, 1)
     down_kept, down_sent = halve(down_kept, among(down_sent, 1), needs=[up_sent])
     feedback, done = feedback_of(message1, arrived1, 1, feedback, True)
-    *up_parts, message4 = split(
-        up_kept, among(up_sent, 1), needs=[arrived2, done], carried=messages[4:5]
-    )
-    arrived4 = along(message4, 1)
+    up_parts = split(up_kept, among(up_sent, 1), needs=[arrived2, done])
     down_parts = split(down_kept, among(down_sent, 3), needs=[up_parts[0]])
     grad_up = finish([among(up_parts[half], 0, half, -1) for half in range(2)])
     grad_down = finish([among(down_parts[half], 0, half, 1) for half in range(2)])
     feedback = feedback_of(message2, arrived2, 2, feedback)[0]
     feedback = feedback_of(message3, arrived3, 3, feedback)[0]
-    feedback = feedback_of(message4, arrived4, 4, feedback)[0]
     return (feedback[None], grad_down[None], grad_up[None])
 
 

time: 111 us -> 106 us (0.955)
  starting transfers between devices: 36.6 us -> 33.1 us
  local copies, waits for them, and re-layouts: 5.39 us -> 3.32 us
  waiting for transfers between devices: 38.4 us -> 39.7 us
    ppermute x8 -> x9, starting transfers between devices: 19.6 us -> 11.3 us  [among(): return lax.ppermute(value, both, pairs)]
    ppermute x0 -> x2, starting transfers between devices: none -> 4.38 us  [the longest x1 3.1 us: body(): up_mine = lax.ppermute(pick_half(up), 'section', odd_to_even)]
    ppermute x11 -> x9, waiting for transfers between devices: 5.97 us -> 9.41 us  [along(): return lax.ppermute(value, 'section', pairs)]
    ppermute x8 -> x9, waiting for transfers between devices: 32.4 us -> 30.3 us  [among(): return lax.ppermute(value, both, pairs)]
    unnamed x16 -> x18, local copies, waits for them, and re-layouts: 5.39 us -> 3.32 us
    pallas_call x19 -> x20, Pallas kernels: 29.1 us -> 28.2 us  [launch(): pl.pallas_call(wrapped, grid=grid, in_specs=[spec for _, spec in ins] + [...]
    ppermute x11 -> x9, starting transfers between devices: 17 us -> 17.3 us  [along(): return lax.ppermute(value, 'section', pairs)]
  transfers between devices with their start and end apart: 19 -> 20, of which waited for: 8 -> 8; matrix products, arithmetic and copies ran while one was open for 0% -> 0% of each run, Pallas kernels for 24% -> 24%
where the time goes in v10:
time: 106 us; the launch traced here: 105 us
  waiting for transfers between devices  39.7 us (37%)
  starting transfers between devices  33.1 us (31%)
  Pallas kernels  28.2 us (27%)
  local copies, waits for them, and re-layouts  3.32 us (3%)
  between operations  1.14 us (1%)
    ppermute x9, waiting for transfers between devices, among(): return lax.ppermute(value, both, pairs)  30.3 us
    pallas_call x20, Pallas kernels, launch(): pl.pallas_call(wrapped, grid=grid, in_specs=[spec for _, spec in ins] + [...  28.2 us
    ppermute x9, starting transfers between devices, along(): return lax.ppermute(value, 'section', pairs)  17.3 us
    ppermute x9, starting transfers between devices, among(): return lax.ppermute(value, both, pairs)  11.3 us
    ppermute x9, waiting for transfers between devices, along(): return lax.ppermute(value, 'section', pairs)  9.41 us
    unnamed x18, local copies, waits for them, and re-layouts  3.32 us
    ppermute x1, starting transfers between devices, body(): up_mine = lax.ppermute(pick_half(up), 'section', odd_to_even)  3.1 us
  transfers between devices with their start and end apart: 20, of which 8 were waited for; matrix products, arithmetic and copies ran while one was open for 0% of the time, Pallas kernels for 24%

profile of v10, /device:TPU:1, one launch (start us, length us, event | category | flops | bytes accessed | tf_op | source)
XLA Modules:
  0.0 105.5 jit_solution(2976885161767551421)
XLA Ops:
  0.6 3.3 %collective-permute-start.1 = (bf16[6144,128]{1,0:T(8,128)(2,1)}, bf16[6144,128]{1,0:T(8,128)(2,1)S(1)}, u32[]{:S(2)}, u32[]{:S(2)}) collective-permute-start(bf16[6144,128]{1,0:T(8,128)(2,1)} %bitcast.31), channel_id=1, source_target_pairs={{0,248},{8,0},{16,8},{24,16},{32,24},{40,32},{48,40},{56,48},{64,5... | collective-permute-start | bytes 4718600 | tf_op jit(solution)/shard_map/ppermute | solution.py:411
  4.0 1.3 %collective-permute-start.2 = (bf16[6144,128]{1,0:T(8,128)(2,1)}, bf16[6144,128]{1,0:T(8,128)(2,1)S(1)}, u32[]{:S(2)}, u32[]{:S(2)}) collective-permute-start(bf16[6144,128]{1,0:T(8,128)(2,1)} %bitcast.14), channel_id=1, source_target_pairs={{0,8},{16,24},{32,40},{48,56},{64,72},{80,88},{96,104},{112,120},{... | collective-permute-start | bytes 4718600 | tf_op jit(solution)/shard_map/ppermute | solution.py:426
  5.3 1.4 %copy-done = bf16[1,6144,128]{2,1,0:T(8,128)(2,1)S(1)} copy-done((bf16[1,6144,128]{2,1,0:T(8,128)(2,1)S(1)}, bf16[1,6144,128]{2,1,0:T(8,128)(2,1)}, u32[]{:S(2)}) %copy-start) | copy-done | bytes 1572888
  6.7 3.1 %collective-permute-start.5 = (bf16[3072,128]{1,0:T(8,128)(2,1)S(1)}, bf16[3072,128]{1,0:T(8,128)(2,1)S(1)}, u32[]{:S(2)}, u32[]{:S(2)}) collective-permute-start(bf16[3072,128]{1,0:T(8,128)(2,1)S(1)} %pick_half.1), channel_id=1, source_target_pairs={{8,16},{24,32},{40,48},{56,64},{72,80},{88,96},{104,112},{120,128}... | collective-permute-start | bytes 2359304 | tf_op jit(solution)/shard_map/ppermute | solution.py:427
  9.9 1.9 %copy-done.2 = s32[1,384,2048]{2,1,0:T(8,128)S(1)} copy-done((s32[1,384,2048]{2,1,0:T(8,128)S(1)}, s32[1,384,2048]{2,1,0:T(8,128)}, u32[]{:S(2)}) %copy-start.2) | copy-done | bytes 3145752
  11.8 2.5 %message.2 = (bf16[96,6144]{1,0:T(8,128)(2,1)S(1)}, f32[96,256]{1,0:T(8,128)S(1)}) custom-call(s32[384,2048]{1,0:T(8,128)S(1)} %bitcast.20, bf16[192,384]{1,0:T(8,128)(2,1)S(1)} %bitcast.25, bf16[32,6144]{1,0:T(8,128)(2,1)S(1)} %bitcast.23, s32[1,384]{1,0:T(1,128)S(1)} %copy-done.7), custom_call_target="tpu_custom_call" | custom-call | flops 1 | bytes 1 | tf_op jit(solution)/shard_map/message/pallas_call | solution.py:47
  14.3 5.4 %message.3 = (bf16[96,6144]{1,0:T(8,128)(2,1)S(1)}, bf16[96,6144]{1,0:T(8,128)(2,1)S(1)}, bf16[96,6144]{1,0:T(8,128)(2,1)S(1)}, f32[288,256]{1,0:T(8,128)S(1)}) custom-call(s32[384,2048]{1,0:T(8,128)S(1)} %bitcast.21, bf16[192,384]{1,0:T(8,128)(2,1)S(1)} %bitcast.26, bf16[32,6144]{1,0:T(8,128)(2,1)S(1)} %bitcast.24, s32[1,384]{1,0:T(1,128)S(1)} %copy-done.7, ...), custom_call_target="tpu_custom_call" | custom-call | flops 1 | bytes 1 | tf_op jit(solution)/shard_map/message/pallas_call | solution.py:47
  20.6 9.8 %collective-permute-start = (f32[1,6144]{1,0:T(1,128)S(1)}, f32[1,6144]{1,0:T(1,128)S(1)}, u32[]{:S(2)}, u32[]{:S(2)}) collective-permute-start(f32[1,6144]{1,0:T(1,128)S(1)} %copy-done.8), channel_id=1, source_target_pairs={{0,248},{8,0},{16,8},{24,16},{32,24},{40,32},{48,40},{56,48},{64,5... | collective-permute-start | bytes 73736 | tf_op jit(solution)/shard_map/ppermute | solution.py:411
  30.4 2.6 %gradient.1.refs_7_.refs_0_ = bf16[384,6144]{1,0:T(8,128)(2,1)S(1)} custom-call(bf16[384,6144]{1,0:T(8,128)(2,1)S(1)} %bitcast.22, bf16[192,384]{1,0:T(8,128)(2,1)S(1)} %bitcast.27, bf16[96,6144]{1,0:T(8,128)(2,1)S(1)} %get-tuple-element.31.refs_2_.refs_4_), custom_call_target="tpu_custom_call" | custom-call | flops 1 | bytes 1 | tf_op jit(solution)/shard_map/gradient/pallas_call | solution.py:47
  33.0 2.3 %hidden.1.refs_0_ = bf16[384,6144]{1,0:T(8,128)(2,1)S(1)} custom-call(f32[1,6144]{1,0:T(1,128)S(1)} %collective-permute-done.refs_0_, bf16[96,6144]{1,0:T(8,128)(2,1)S(1)} %get-tuple-element.30.refs_4_.refs_1_, bf16[96,6144]{1,0:T(8,128)(2,1)S(1)} %get-tuple-element.31.refs_2_.refs_4_, bf16[96,6144]{1,0:T(8,128)(2,1)S(1)} %get-tuple-element.32.refs_3_.refs_5_, ...), custom_call_target="tpu_custom_call" | custom-call | flops 1 | bytes 1 | tf_op jit(solution)/shard_map/hidden/pallas_call | solution.py:47
  35.4 1.4 %down.1 = (f32[384,128]{1,0:T(8,128)S(1)}, bf16[384,128]{1,0:T(8,128)(2,1)S(1)}) custom-call(bf16[384,6144]{1,0:T(8,128)(2,1)S(1)} %hidden.1.refs_0_, bf16[6144,128]{1,0:T(8,128)(2,1)S(1)} %collective-permute-done.1.refs_1_, bf16[6144,128]{1,0:T(8,128)(2,1)S(1)} %collective-permute-done.2.refs_2_.refs_1_), custom_call_target="tpu_custom_call" | custom-call | flops 1 | bytes 1 | tf_op jit(solution)/shard_map/down/pallas_call | solution.py:47
  37.0 1.9 %collective-permute-done.7.refs_5_.refs_2_ = bf16[384,128]{1,0:T(8,128)(2,1)S(1)} collective-permute-done((bf16[384,128]{1,0:T(8,128)(2,1)S(1)}, bf16[384,128]{1,0:T(8,128)(2,1)S(1)}, u32[]{:S(2)}, u32[]{:S(2)}) %collective-permute-start.7) | collective-permute-done | bytes 98336 | tf_op jit(solution)/shard_map/ppermute | solution.py:411
  38.9 5.9 %collective-permute-done.3.refs_4_.refs_1_ = bf16[384,128]{1,0:T(8,128)(2,1)S(1)} collective-permute-done((bf16[384,128]{1,0:T(8,128)(2,1)S(1)}, bf16[384,128]{1,0:T(8,128)(2,1)S(1)}, u32[]{:S(2)}, u32[]{:S(2)}) %collective-permute-start.3) | collective-permute-done | bytes 98336 | tf_op jit(solution)/shard_map/ppermute | solution.py:411
  44.8 1.4 %back.1.refs_3_ = bf16[384,128]{1,0:T(8,128)(2,1)S(1)} custom-call(bf16[384,6144]{1,0:T(8,128)(2,1)S(1)} %gradient.1.refs_7_.refs_0_, bf16[6144,128]{1,0:T(8,128)(2,1)S(1)} %collective-permute-done.2.refs_2_.refs_1_, bf16[3072,128]{1,0:T(8,128)(2,1)S(1)} %hand_on.1.refs_2_, bf16[3072,128]{1,0:T(8,128)(2,1)S(1)} %collective-permute-done.6.refs_3_, ...), custom_call_target="tpu_custom_call" | custom-call | flops 1 | bytes 1 | tf_op jit(solution)/shard_map/back/pallas_call | solution.py:47
  46.2 1.0 grad_up.1
  47.3 1.9 %collective-permute-start.8 = (bf16[4,128,768]{2,1,0:T(8,128)(2,1)S(1)}, bf16[4,128,768]{2,1,0:T(8,128)(2,1)S(1)}, u32[]{:S(2)}, u32[]{:S(2)}) collective-permute-start(bf16[4,128,768]{2,1,0:T(8,128)(2,1)S(1)} %get-tuple-element.38), channel_id=1, source_target_pairs={{3,0},{2,1},{1,2},{0,3},{7,4},{6,5},{5,6},{4,7},{11,8},{10,9},{9,1... | collective-permute-start | bytes 2359304 | tf_op jit(solution)/shard_map/ppermute | solution.py:421
  49.2 3.8 %collective-permute-start.12 = (bf16[384,128]{1,0:T(8,128)(2,1)S(1)}, bf16[384,128]{1,0:T(8,128)(2,1)S(1)}, u32[]{:S(2)}, u32[]{:S(2)}) collective-permute-start(bf16[384,128]{1,0:T(8,128)(2,1)S(1)} %back.1.refs_3_), channel_id=1, source_target_pairs={{0,240},{8,248},{16,0},{24,8},{32,16},{40,24},{48,32},{56,40},{64,... | collective-permute-start | bytes 294920 | tf_op jit(solution)/shard_map/ppermute | solution.py:411
  53.0 1.6 %collective-permute-done.12.refs_2_ = bf16[384,128]{1,0:T(8,128)(2,1)S(1)} collective-permute-done((bf16[384,128]{1,0:T(8,128)(2,1)S(1)}, bf16[384,128]{1,0:T(8,128)(2,1)S(1)}, u32[]{:S(2)}, u32[]{:S(2)}) %collective-permute-start.12) | collective-permute-done | bytes 98336 | tf_op jit(solution)/shard_map/ppermute | solution.py:411
  54.6 1.1 %grad_down.1 = (f32[4,128,768]{2,1,0:T(8,128)S(1)}, bf16[4,128,768]{2,1,0:T(8,128)(2,1)S(1)}) custom-call(bf16[384,6144]{1,0:T(8,128)(2,1)S(1)} %hidden.1.refs_0_, f32[384,128]{1,0:T(8,128)S(1)} %get-tuple-element.45.refs_1_, bf16[384,128]{1,0:T(8,128)(2,1)S(1)} %collective-permute-done.12.refs_2_), custom_call_target="tpu_custom_call" | custom-call | flops 1 | bytes 1 | tf_op jit(solution)/shard_map/grad_down/pallas_call | solution.py:47
  56.1 2.1 %feedback.4 = (bf16[384,6144]{1,0:T(8,128)(2,1)}, f32[8,128]{1,0:T(8,128)S(1)}) custom-call(bf16[96,6144]{1,0:T(8,128)(2,1)S(1)} %collective-permute-done.4.refs_2_.refs_0_, bf16[96,6144]{1,0:T(8,128)(2,1)S(1)} %get-tuple-element.30.refs_4_.refs_1_, bf16[384,128]{1,0:T(8,128)(2,1)S(1)} %collective-permute-done.7.refs_5_.refs_2_, bf16[6144,128]{1,0:T(8,128)(2,1)S(1)} %bitcast.16), custom_call_target="tpu_custom_call" | custom-call | flops 1 | bytes 1 | tf_op jit(solution)/shard_map/feedback/pallas_call | solution.py:47
  58.2 9.1 %collective-permute-done.8.refs_1_ = bf16[4,128,768]{2,1,0:T(8,128)(2,1)S(1)} collective-permute-done((bf16[4,128,768]{2,1,0:T(8,128)(2,1)S(1)}, bf16[4,128,768]{2,1,0:T(8,128)(2,1)S(1)}, u32[]{:S(2)}, u32[]{:S(2)}) %collective-permute-start.8) | collective-permute-done | bytes 786464 | tf_op jit(solution)/shard_map/ppermute | solution.py:421
  67.7 7.4 %collective-permute-done.13.refs_1_ = bf16[4,128,768]{2,1,0:T(8,128)(2,1)S(1)} collective-permute-done((bf16[4,128,768]{2,1,0:T(8,128)(2,1)S(1)}, bf16[4,128,768]{2,1,0:T(8,128)(2,1)S(1)}, u32[]{:S(2)}, u32[]{:S(2)}) %collective-permute-start.13) | collective-permute-done | bytes 786464 | tf_op jit(solution)/shard_map/ppermute | solution.py:421
  75.2 0.9 collective-permute-start.14
  76.2 2.0 %feedback.5 = (bf16[384,6144]{1,0:T(8,128)(2,1)}, f32[8,128]{1,0:T(8,128)S(1)}) custom-call(bf16[96,6144]{1,0:T(8,128)(2,1)S(1)} %collective-permute-done.9.refs_2_.refs_0_, bf16[96,6144]{1,0:T(8,128)(2,1)S(1)} %get-tuple-element.39.refs_1_, bf16[384,128]{1,0:T(8,128)(2,1)S(1)} %collective-permute-done.7.refs_5_.refs_2_, ...), custom_call_target="tpu_custom_call", output_to_operand_aliasing={{0}: (4, {})} | custom-call | flops 1 | bytes 1 | tf_op jit(solution)/shard_map/feedback/pallas_call | solution.py:47
  78.2 5.3 %collective-permute-done.15.refs_1_ = bf16[2,128,768]{2,1,0:T(8,128)(2,1)S(1)} collective-permute-done((bf16[2,128,768]{2,1,0:T(8,128)(2,1)S(1)}, bf16[2,128,768]{2,1,0:T(8,128)(2,1)S(1)}, u32[]{:S(2)}, u32[]{:S(2)}) %collective-permute-start.15) | collective-permute-done | bytes 393248 | tf_op jit(solution)/shard_map/ppermute | solution.py:421
  83.6 2.6 %collective-permute-done.14.refs_1_ = bf16[2,128,768]{2,1,0:T(8,128)(2,1)S(1)} collective-permute-done((bf16[2,128,768]{2,1,0:T(8,128)(2,1)S(1)}, bf16[2,128,768]{2,1,0:T(8,128)(2,1)S(1)}, u32[]{:S(2)}, u32[]{:S(2)}) %collective-permute-start.14) | collective-permute-done | bytes 393248 | tf_op jit(solution)/shard_map/ppermute | solution.py:421
  87.2 3.7 %collective-permute-start.19 = (bf16[128,768]{1,0:T(8,128)(2,1)S(1)}, bf16[128,768]{1,0:T(8,128)(2,1)S(1)}, u32[]{:S(2)}, u32[]{:S(2)}) collective-permute-start(bf16[128,768]{1,0:T(8,128)(2,1)S(1)} %get-tuple-element.56), channel_id=1, source_target_pairs={{4,248},{5,249},{6,250},{7,251},{0,252},{1,253},{2,254},{3,255},{1... | collective-permute-start | bytes 589832 | tf_op jit(solution)/shard_map/ppermute | solution.py:421
  90.9 2.6 %collective-permute-start.18 = (bf16[128,768]{1,0:T(8,128)(2,1)S(1)}, bf16[128,768]{1,0:T(8,128)(2,1)S(1)}, u32[]{:S(2)}, u32[]{:S(2)}) collective-permute-start(bf16[128,768]{1,0:T(8,128)(2,1)S(1)} %get-tuple-element.53.refs_2_), channel_id=1, source_target_pairs={{0,248},{1,249},{2,250},{3,251},{4,252},{5,253},{6,254},{7,255},{8... | collective-permute-start | bytes 589832 | tf_op jit(solution)/shard_map/ppermute | solution.py:421
  93.5 2.0 %feedback.6.refs_4_ = bf16[384,6144]{1,0:T(8,128)(2,1)} custom-call(bf16[96,6144]{1,0:T(8,128)(2,1)S(1)} %collective-permute-done.11.refs_0_.refs_2_, bf16[96,6144]{1,0:T(8,128)(2,1)S(1)} %get-tuple-element.42.refs_1_, bf16[384,128]{1,0:T(8,128)(2,1)S(1)} %collective-permute-done.7.refs_5_.refs_2_, ...), custom_call_target="tpu_custom_call", output_to_operand_aliasing={{}: (4, {})} | custom-call | flops 1 | bytes 1 | tf_op jit(solution)/shard_map/feedback/pallas_call | solution.py:47
  95.6 5.9 %collective-permute-done.17.refs_1_ = bf16[128,768]{1,0:T(8,128)(2,1)S(1)} collective-permute-done((bf16[128,768]{1,0:T(8,128)(2,1)S(1)}, bf16[128,768]{1,0:T(8,128)(2,1)S(1)}, u32[]{:S(2)}, u32[]{:S(2)}) %collective-permute-start.17) | collective-permute-done | bytes 196640 | tf_op jit(solution)/shard_map/ppermute | solution.py:421
  102.3 0.9 finish.3
  103.3 2.1 %feedback.7 = bf16[384,6144]{1,0:T(8,128)(2,1)} custom-call(bf16[96,6144]{1,0:T(8,128)(2,1)S(1)} %collective-permute-done.10.refs_0_, bf16[96,6144]{1,0:T(8,128)(2,1)S(1)} %get-tuple-element.41.refs_1_, bf16[384,128]{1,0:T(8,128)(2,1)S(1)} %collective-permute-done.7.refs_5_.refs_2_, bf16[6144,128]{1,0:T(8,128)(2,1)S(1)} %bitcast.19, ...), custom_call_target="tpu_custom_call", output_to_operand_aliasing={{}: (4, {})} | custom-call | flops 1 | bytes 1 | tf_op jit(solution)/shard_map/feedback/pallas_call | solution.py:47
  (46 shorter events, 4.1 us)
Async XLA Ops:
  0.6 9.2 %copy-start.7 = (s32[1,384]{1,0:T(1,128)S(1)}, s32[1,384]{1,0:T(1,128)}, u32[]{:S(2)}) copy-start(s32[1,384]{1,0:T(1,128)} %refs_3_.3) | copy-start | bytes 4612
  0.6 34.7 %collective-permute-start.1 = (bf16[6144,128]{1,0:T(8,128)(2,1)}, bf16[6144,128]{1,0:T(8,128)(2,1)S(1)}, u32[]{:S(2)}, u32[]{:S(2)}) collective-permute-start(bf16[6144,128]{1,0:T(8,128)(2,1)} %bitcast.31), channel_id=1, source_target_pairs={{0,248},{8,0},{16,8},{24,16},{32,24},{40,32},{48,40},{56,48},{64,5... | collective-permute-start | bytes 4718600 | tf_op jit(solution)/shard_map/ppermute | solution.py:411
  4.0 31.4 %collective-permute-start.2 = (bf16[6144,128]{1,0:T(8,128)(2,1)}, bf16[6144,128]{1,0:T(8,128)(2,1)S(1)}, u32[]{:S(2)}, u32[]{:S(2)}) collective-permute-start(bf16[6144,128]{1,0:T(8,128)(2,1)} %bitcast.14), channel_id=1, source_target_pairs={{0,8},{16,24},{32,40},{48,56},{64,72},{80,88},{96,104},{112,120},{... | collective-permute-start | bytes 4718600 | tf_op jit(solution)/shard_map/ppermute | solution.py:426
  5.2 1.4 %copy-start = (bf16[1,6144,128]{2,1,0:T(8,128)(2,1)S(1)}, bf16[1,6144,128]{2,1,0:T(8,128)(2,1)}, u32[]{:S(2)}) copy-start(bf16[1,6144,128]{2,1,0:T(8,128)(2,1)} %param.17) | copy-start | bytes 4718596
  6.7 3.2 %copy-start.4 = (bf16[1,32,6144]{2,1,0:T(8,128)(2,1)S(1)}, bf16[1,32,6144]{2,1,0:T(8,128)(2,1)}, u32[]{:S(2)}) copy-start(bf16[1,32,6144]{2,1,0:T(8,128)(2,1)} %param.11) | copy-start | bytes 1179652
  6.7 3.2 %copy-start.5 = (bf16[1,384,192]{1,2,0:T(8,128)(2,1)S(1)}, bf16[1,384,192]{1,2,0:T(8,128)(2,1)}, u32[]{:S(2)}) copy-start(bf16[1,384,192]{1,2,0:T(8,128)(2,1)} %param.10) | copy-start | bytes 442372
  6.7 13.0 %collective-permute-start.5 = (bf16[3072,128]{1,0:T(8,128)(2,1)S(1)}, bf16[3072,128]{1,0:T(8,128)(2,1)S(1)}, u32[]{:S(2)}, u32[]{:S(2)}) collective-permute-start(bf16[3072,128]{1,0:T(8,128)(2,1)S(1)} %pick_half.1), channel_id=1, source_target_pairs={{8,16},{24,32},{40,48},{56,64},{72,80},{88,96},{104,112},{120,128}... | collective-permute-start | bytes 2359304 | tf_op jit(solution)/shard_map/ppermute | solution.py:427
  9.9 1.9 %copy-start.2 = (s32[1,384,2048]{2,1,0:T(8,128)S(1)}, s32[1,384,2048]{2,1,0:T(8,128)}, u32[]{:S(2)}) copy-start(s32[1,384,2048]{2,1,0:T(8,128)} %param.9) | copy-start | bytes 9437188
  14.2 32.0 %collective-permute-start.4 = (bf16[96,6144]{1,0:T(8,128)(2,1)S(1)}, bf16[96,6144]{1,0:T(8,128)(2,1)S(1)}, u32[]{:S(2)}, u32[]{:S(2)}) collective-permute-start(bf16[96,6144]{1,0:T(8,128)(2,1)S(1)} %get-tuple-element.30.refs_4_.refs_1_), channel_id=1, source_target_pairs={{0,8},{8,16},{16,24},{24,32},{32,40},{40,48},{48,56},{56,64},{64,7... | collective-permute-start | bytes 3538952 | tf_op jit(solution)/shard_map/ppermute | solution.py:411
  14.3 16.1 %copy-start.3 = (bf16[1,384,6144]{2,1,0:T(8,128)(2,1)S(1)}, bf16[1,384,6144]{2,1,0:T(8,128)(2,1)}, u32[]{:S(2)}) copy-start(bf16[1,384,6144]{2,1,0:T(8,128)(2,1)} %param.13) | copy-start | bytes 14155780
  19.7 0.9 copy-start.8
  19.7 10.7 %copy-start.6 = (bf16[1,384,192]{1,2,0:T(8,128)(2,1)S(1)}, bf16[1,384,192]{1,2,0:T(8,128)(2,1)}, u32[]{:S(2)}) copy-start(bf16[1,384,192]{1,2,0:T(8,128)(2,1)} %param.14) | copy-start | bytes 442372
  19.8 17.2 %collective-permute-start.6 = (bf16[3072,128]{1,0:T(8,128)(2,1)S(1)}, bf16[3072,128]{1,0:T(8,128)(2,1)S(1)}, u32[]{:S(2)}, u32[]{:S(2)}) collective-permute-start(bf16[3072,128]{1,0:T(8,128)(2,1)S(1)} %hand_on.1.refs_2_), channel_id=1, source_target_pairs={{1,0},{0,1},{3,2},{2,3},{5,4},{4,5},{7,6},{6,7},{17,16},{16,17},{1... | collective-permute-start | bytes 2359304 | tf_op jit(solution)/shard_map/ppermute | solution.py:421
  20.6 12.4 %collective-permute-start = (f32[1,6144]{1,0:T(1,128)S(1)}, f32[1,6144]{1,0:T(1,128)S(1)}, u32[]{:S(2)}, u32[]{:S(2)}) collective-permute-start(f32[1,6144]{1,0:T(1,128)S(1)} %copy-done.8), channel_id=1, source_target_pairs={{0,248},{8,0},{16,8},{24,16},{32,24},{40,32},{48,40},{56,48},{64,5... | collective-permute-start | bytes 73736 | tf_op jit(solution)/shard_map/ppermute | solution.py:411
  36.8 2.1 %collective-permute-start.7 = (bf16[384,128]{1,0:T(8,128)(2,1)S(1)}, bf16[384,128]{1,0:T(8,128)(2,1)S(1)}, u32[]{:S(2)}, u32[]{:S(2)}) collective-permute-start(bf16[384,128]{1,0:T(8,128)(2,1)S(1)} %get-tuple-element.36), channel_id=1, source_target_pairs={{0,8},{8,16},{16,24},{24,32},{32,40},{40,48},{48,56},{56,64},{64,7... | collective-permute-start | bytes 294920 | tf_op jit(solution)/shard_map/ppermute | solution.py:411
  36.9 7.9 %collective-permute-start.3 = (bf16[384,128]{1,0:T(8,128)(2,1)S(1)}, bf16[384,128]{1,0:T(8,128)(2,1)S(1)}, u32[]{:S(2)}, u32[]{:S(2)}) collective-permute-start(bf16[384,128]{1,0:T(8,128)(2,1)S(1)} %get-tuple-element.36), channel_id=1, source_target_pairs={{0,16},{8,24},{16,32},{24,40},{32,48},{40,56},{48,64},{56,72},{64,... | collective-permute-start | bytes 294920 | tf_op jit(solution)/shard_map/ppermute | solution.py:411
  47.2 20.1 %collective-permute-start.9 = (bf16[96,6144]{1,0:T(8,128)(2,1)S(1)}, bf16[96,6144]{1,0:T(8,128)(2,1)S(1)}, u32[]{:S(2)}, u32[]{:S(2)}) collective-permute-start(bf16[96,6144]{1,0:T(8,128)(2,1)S(1)} %get-tuple-element.39.refs_1_), channel_id=1, source_target_pairs={{0,8},{8,16},{16,24},{24,32},{32,40},{40,48},{48,56},{56,64},{64,7... | collective-permute-start | bytes 3538952 | tf_op jit(solution)/shard_map/ppermute | solution.py:411
  47.3 20.0 %collective-permute-start.8 = (bf16[4,128,768]{2,1,0:T(8,128)(2,1)S(1)}, bf16[4,128,768]{2,1,0:T(8,128)(2,1)S(1)}, u32[]{:S(2)}, u32[]{:S(2)}) collective-permute-start(bf16[4,128,768]{2,1,0:T(8,128)(2,1)S(1)} %get-tuple-element.38), channel_id=1, source_target_pairs={{3,0},{2,1},{1,2},{0,3},{7,4},{6,5},{5,6},{4,7},{11,8},{10,9},{9,1... | collective-permute-start | bytes 2359304 | tf_op jit(solution)/shard_map/ppermute | solution.py:421
  49.2 5.4 %collective-permute-start.12 = (bf16[384,128]{1,0:T(8,128)(2,1)S(1)}, bf16[384,128]{1,0:T(8,128)(2,1)S(1)}, u32[]{:S(2)}, u32[]{:S(2)}) collective-permute-start(bf16[384,128]{1,0:T(8,128)(2,1)S(1)} %back.1.refs_3_), channel_id=1, source_target_pairs={{0,240},{8,248},{16,0},{24,8},{32,16},{40,24},{48,32},{56,40},{64,... | collective-permute-start | bytes 294920 | tf_op jit(solution)/shard_map/ppermute | solution.py:411
  53.0 25.3 %collective-permute-start.11 = (bf16[96,6144]{1,0:T(8,128)(2,1)S(1)}, bf16[96,6144]{1,0:T(8,128)(2,1)S(1)}, u32[]{:S(2)}, u32[]{:S(2)}) collective-permute-start(bf16[96,6144]{1,0:T(8,128)(2,1)S(1)} %get-tuple-element.42.refs_1_), channel_id=1, source_target_pairs={{0,8},{8,16},{16,24},{24,32},{32,40},{40,48},{48,56},{56,64},{64,7... | collective-permute-start | bytes 3538952 | tf_op jit(solution)/shard_map/ppermute | solution.py:411
  54.6 1.5 %copy-start.1 = (bf16[1,6144,128]{2,1,0:T(8,128)(2,1)S(1)}, bf16[1,6144,128]{2,1,0:T(8,128)(2,1)}, u32[]{:S(2)}) copy-start(bf16[1,6144,128]{2,1,0:T(8,128)(2,1)} %param.17) | copy-start | bytes 4718596
  55.7 19.4 %collective-permute-start.13 = (bf16[4,128,768]{2,1,0:T(8,128)(2,1)S(1)}, bf16[4,128,768]{2,1,0:T(8,128)(2,1)S(1)}, u32[]{:S(2)}, u32[]{:S(2)}) collective-permute-start(bf16[4,128,768]{2,1,0:T(8,128)(2,1)S(1)} %get-tuple-element.47), channel_id=1, source_target_pairs={{1,0},{0,1},{3,2},{2,3},{5,4},{4,5},{7,6},{6,7},{9,8},{8,9},{11,10... | collective-permute-start | bytes 2359304 | tf_op jit(solution)/shard_map/ppermute | solution.py:421
  67.5 35.8 %collective-permute-start.10 = (bf16[96,6144]{1,0:T(8,128)(2,1)S(1)}, bf16[96,6144]{1,0:T(8,128)(2,1)S(1)}, u32[]{:S(2)}, u32[]{:S(2)}) collective-permute-start(bf16[96,6144]{1,0:T(8,128)(2,1)S(1)} %get-tuple-element.41.refs_1_), channel_id=1, source_target_pairs={{0,8},{8,16},{16,24},{24,32},{32,40},{40,48},{48,56},{56,64},{64,7... | collective-permute-start | bytes 3538952 | tf_op jit(solution)/shard_map/ppermute | solution.py:411
  67.6 16.0 %collective-permute-start.15 = (bf16[2,128,768]{2,1,0:T(8,128)(2,1)S(1)}, bf16[2,128,768]{2,1,0:T(8,128)(2,1)S(1)}, u32[]{:S(2)}, u32[]{:S(2)}) collective-permute-start(bf16[2,128,768]{2,1,0:T(8,128)(2,1)S(1)} %get-tuple-element.48.refs_2_), channel_id=1, source_target_pairs={{1,0},{0,1},{3,2},{2,3},{5,4},{4,5},{7,6},{6,7},{9,8},{8,9},{11,10... | collective-permute-start | bytes 1179656 | tf_op jit(solution)/shard_map/ppermute | solution.py:421
  75.2 11.0 %collective-permute-start.14 = (bf16[2,128,768]{2,1,0:T(8,128)(2,1)S(1)}, bf16[2,128,768]{2,1,0:T(8,128)(2,1)S(1)}, u32[]{:S(2)}, u32[]{:S(2)}) collective-permute-start(bf16[2,128,768]{2,1,0:T(8,128)(2,1)S(1)} %get-tuple-element.50), channel_id=1, source_target_pairs={{3,0},{2,1},{1,2},{0,3},{7,4},{6,5},{5,6},{4,7},{11,8},{10,9},{9,1... | collective-permute-start | bytes 1179656 | tf_op jit(solution)/shard_map/ppermute | solution.py:421
  86.3 9.2 %collective-permute-start.16 = (bf16[128,768]{1,0:T(8,128)(2,1)S(1)}, bf16[128,768]{1,0:T(8,128)(2,1)S(1)}, u32[]{:S(2)}, u32[]{:S(2)}) collective-permute-start(bf16[128,768]{1,0:T(8,128)(2,1)S(1)} %get-tuple-element.54), channel_id=1, source_target_pairs={{0,8},{1,9},{2,10},{3,11},{4,12},{5,13},{6,14},{7,15},{8,16},{9,17... | collective-permute-start | bytes 589832 | tf_op jit(solution)/shard_map/ppermute | solution.py:421
  86.4 15.0 %collective-permute-start.17 = (bf16[128,768]{1,0:T(8,128)(2,1)S(1)}, bf16[128,768]{1,0:T(8,128)(2,1)S(1)}, u32[]{:S(2)}, u32[]{:S(2)}) collective-permute-start(bf16[128,768]{1,0:T(8,128)(2,1)S(1)} %get-tuple-element.55), channel_id=1, source_target_pairs={{4,8},{5,9},{6,10},{7,11},{0,12},{1,13},{2,14},{3,15},{12,16},{13,... | collective-permute-start | bytes 589832 | tf_op jit(solution)/shard_map/ppermute | solution.py:421
  87.2 15.2 %collective-permute-start.19 = (bf16[128,768]{1,0:T(8,128)(2,1)S(1)}, bf16[128,768]{1,0:T(8,128)(2,1)S(1)}, u32[]{:S(2)}, u32[]{:S(2)}) collective-permute-start(bf16[128,768]{1,0:T(8,128)(2,1)S(1)} %get-tuple-element.56), channel_id=1, source_target_pairs={{4,248},{5,249},{6,250},{7,251},{0,252},{1,253},{2,254},{3,255},{1... | collective-permute-start | bytes 589832 | tf_op jit(solution)/shard_map/ppermute | solution.py:421
  90.9 11.5 %collective-permute-start.18 = (bf16[128,768]{1,0:T(8,128)(2,1)S(1)}, bf16[128,768]{1,0:T(8,128)(2,1)S(1)}, u32[]{:S(2)}, u32[]{:S(2)}) collective-permute-start(bf16[128,768]{1,0:T(8,128)(2,1)S(1)} %get-tuple-element.53.refs_2_), channel_id=1, source_target_pairs={{0,248},{1,249},{2,250},{3,251},{4,252},{5,253},{6,254},{7,255},{8... | collective-permute-start | bytes 589832 | tf_op jit(solution)/shard_map/ppermute | solution.py:421

commit v11 on v10

--- a/solution.py
+++ b/solution.py
@@ -14,12 +14,12 @@
 PIECE = D // 8
 F32 = jnp.float32
 BF16 = jnp.bfloat16
-TILE = 48
+TILE = 64
 BLOCK = 768
 HALF = D // 2
 WORDS = BLOCK // 3
 CODES = BLOCK // 32
-SPANS = (96, 96, 96, 96)
+SPANS = (128, 128, 64, 64)
 MIB = 1 << 20
 ROOT_2_PI = math.sqrt(2.0 / math.pi)
 VMEM = pl.BlockSpec(memory_space=pltpu.VMEM)
@@ -58,10 +58,6 @@
     )(*[value for value, _ in ins], *needs, *carried)
 
 
-def hand_on(value, after):
-    return launch(lambda: None, "hand_on", [], [], needs=[after], carried=[value], grant=1)[0]
-
-
 def lanes(shape):
     return lax.broadcasted_iota(jnp.int32, shape, 1)
 
@@ -92,8 +88,8 @@
     found, start = [], 0
     for ref in out_refs:
         count = ref.shape[0]
-        for row in range(0, count, 96):
-            found.append((ref, row, start + row, min(96, count - row)))
+        for row in range(0, count, TILE):
+            found.append((ref, row, start + row, TILE))
         start += count
     return found
 
@@ -336,15 +332,20 @@
     )
 
 
-def finish_kernel(one_ref, two_ref, out_ref):
+def finish_kernel(one_ref, two_ref, out_ref, done_ref):
     out_ref[...] = (one_ref[...].astype(F32) + two_ref[...].astype(F32)).T
-
-
-def finish(parts):
+    done_ref[...] = jnp.zeros_like(done_ref)
+
+
+def finish(parts, **ties):
     return launch(
         finish_kernel, "finish", [(part, VMEM) for part in parts],
-        [(array((PIECE, R), F32), pl.BlockSpec((PIECE, R)))],
-    )[0]
+        [
+            (array((PIECE, R), F32), pl.BlockSpec((PIECE, R))),
+            (array((8, 128), F32), VMEM),
+        ],
+        **ties,
+    )
 
 
 def feedback_kernel(first, count, before, x_ref, own_ref, act_ref, weight_ref, *refs):
@@ -425,6 +426,7 @@
     even_to_odd = [(s, s + 1) for s in range(0, sections, 2)]
     up_chip = lax.ppermute(up, "section", even_to_odd)
     up_mine = lax.ppermute(pick_half(up), "section", odd_to_even)
+    up_other = among(up_mine, 1, stride=2)
     down_next = along(w_down[0], -1)
     gain_next = along(norm_gain, -1)
 
@@ -436,8 +438,6 @@
         codes, scales, base, sample_ids, firsts[1], SPANS[1:], needs=[message0]
     )
     messages = [message0, *later]
-    up_mine = hand_on(up_mine, stats1)
-    up_other = among(up_mine, 1, stride=2)
     gradient = make_gradient(backward_codes[0], backward_scales[0].T, needs=[later[0]])
 
     hidden = make_hidden(messages, [stats0, stats1], gain_next, needs=[gradient])
@@ -446,7 +446,7 @@
     act_own = along(act_next, 1)
     arrived0 = along(messages[0], 1)
     dact_before = project_back(
-        gradient, up_chip, up_mine, up_other, needs=[act_before, act_own]
+        gradient, up_chip, up_mine, up_other, needs=[act_next]
     )[0]
     dact_next = along(dact_before, -2)
 
@@ -455,7 +455,7 @@
 
     up_kept, up_sent, message1, message2 = partial_grad(
         read_act, "grad_up", (0, 1, 3, 2), gradient, act_before,
-        needs=[arrived0, dact_before], carried=messages[1:3],
+        needs=[act_own, arrived0, dact_next], carried=messages[1:3],
     )
     arrived1 = along(message1, 1)
     arrived2 = along(message2, 1)
@@ -471,10 +471,12 @@
     feedback, done = feedback_of(message1, arrived1, 1, feedback, True)
     up_parts = split(up_kept, among(up_sent, 1), needs=[arrived2, done])
     down_parts = split(down_kept, among(down_sent, 3), needs=[up_parts[0]])
-    grad_up = finish([among(up_parts[half], 0, half, -1) for half in range(2)])
-    grad_down = finish([among(down_parts[half], 0, half, 1) for half in range(2)])
     feedback = feedback_of(message2, arrived2, 2, feedback)[0]
-    feedback = feedback_of(message3, arrived3, 3, feedback)[0]
+    feedback, done = feedback_of(message3, arrived3, 3, feedback, True)
+    grad_up, done_up = finish([among(up_parts[half], 0, half, -1) for half in range(2)])
+    grad_down = finish(
+        [among(down_parts[half], 0, half, 1) for half in range(2)], needs=[done, done_up]
+    )[0]
     return (feedback[None], grad_down[None], grad_up[None])
 
 

time: 106 us -> 105 us (level); the launches traced: 105 us -> 103 us
    ppermute x1, waiting for transfers between devices: 0.01 us -> 3.92 us  [body(): up_mine = lax.ppermute(pick_half(up), 'section', odd_to_even)]
    ppermute x9, waiting for transfers between devices: 9.41 us -> 6.57 us  [along(): return lax.ppermute(value, 'section', pairs)]
    ppermute x9, waiting for transfers between devices: 30.3 us -> 28.5 us  [among(): return lax.ppermute(value, both, pairs)]
    pallas_call x20 -> x19, Pallas kernels: 28.2 us -> 27.2 us  [launch(): pl.pallas_call(wrapped, grid=grid, in_specs=[spec for _, spec in ins] + [...]
  transfers between devices with their start and end apart: 20 -> 20, of which waited for: 8 -> 9; matrix products, arithmetic and copies ran while one was open for 0% -> 0% of each run, Pallas kernels for 24% -> 24%
where the time goes in v11:
time: 105 us; the launch traced here: 103 us
  waiting for transfers between devices  39 us (37%)
  starting transfers between devices  32.7 us (31%)
  Pallas kernels  27.2 us (26%)
  local copies, waits for them, and re-layouts  3.32 us (3%)
    ppermute x9, waiting for transfers between devices, among(): return lax.ppermute(value, both, pairs)  28.5 us
    pallas_call x19, Pallas kernels, launch(): pl.pallas_call(wrapped, grid=grid, in_specs=[spec for _, spec in ins] + [...  27.2 us
    ppermute x9, starting transfers between devices, along(): return lax.ppermute(value, 'section', pairs)  17.1 us
    ppermute x9, starting transfers between devices, among(): return lax.ppermute(value, both, pairs)  11.2 us
    ppermute x9, waiting for transfers between devices, along(): return lax.ppermute(value, 'section', pairs)  6.57 us
    ppermute x1, waiting for transfers between devices, body(): up_mine = lax.ppermute(pick_half(up), 'section', odd_to_even)  3.92 us
    unnamed x18, local copies, waits for them, and re-layouts  3.32 us
    ppermute x1, starting transfers between devices, body(): up_mine = lax.ppermute(pick_half(up), 'section', odd_to_even)  3.1 us
  transfers between devices with their start and end apart: 20, of which 9 were waited for; matrix products, arithmetic and copies ran while one was open for 0% of the time, Pallas kernels for 24%

profile of v11, /device:TPU:1, one launch (start us, length us, event | category | flops | bytes accessed | tf_op | source)
XLA Modules:
  0.0 103.1 jit_solution(5900977975991532911)
XLA Ops:
  0.6 3.3 %collective-permute-start.1 = (bf16[6144,128]{1,0:T(8,128)(2,1)}, bf16[6144,128]{1,0:T(8,128)(2,1)S(1)}, u32[]{:S(2)}, u32[]{:S(2)}) collective-permute-start(bf16[6144,128]{1,0:T(8,128)(2,1)} %bitcast.29), channel_id=1, source_target_pairs={{0,248},{8,0},{16,8},{24,16},{32,24},{40,32},{48,40},{56,48},{64,5... | collective-permute-start | bytes 4718600 | tf_op jit(solution)/shard_map/ppermute | solution.py:412
  4.0 1.3 %collective-permute-start.2 = (bf16[6144,128]{1,0:T(8,128)(2,1)}, bf16[6144,128]{1,0:T(8,128)(2,1)S(1)}, u32[]{:S(2)}, u32[]{:S(2)}) collective-permute-start(bf16[6144,128]{1,0:T(8,128)(2,1)} %bitcast.14), channel_id=1, source_target_pairs={{0,8},{16,24},{32,40},{48,56},{64,72},{80,88},{96,104},{112,120},{... | collective-permute-start | bytes 4718600 | tf_op jit(solution)/shard_map/ppermute | solution.py:427
  5.3 1.4 %copy-done = bf16[1,6144,128]{2,1,0:T(8,128)(2,1)S(1)} copy-done((bf16[1,6144,128]{2,1,0:T(8,128)(2,1)S(1)}, bf16[1,6144,128]{2,1,0:T(8,128)(2,1)}, u32[]{:S(2)}) %copy-start) | copy-done | bytes 1572888
  6.7 3.1 %collective-permute-start.6 = (bf16[3072,128]{1,0:T(8,128)(2,1)S(1)}, bf16[3072,128]{1,0:T(8,128)(2,1)S(1)}, u32[]{:S(2)}, u32[]{:S(2)}) collective-permute-start(bf16[3072,128]{1,0:T(8,128)(2,1)S(1)} %pick_half.1), channel_id=1, source_target_pairs={{8,16},{24,32},{40,48},{56,64},{72,80},{88,96},{104,112},{120,128}... | collective-permute-start | bytes 2359304 | tf_op jit(solution)/shard_map/ppermute | solution.py:428
  9.9 1.9 %copy-done.2 = s32[1,384,2048]{2,1,0:T(8,128)S(1)} copy-done((s32[1,384,2048]{2,1,0:T(8,128)S(1)}, s32[1,384,2048]{2,1,0:T(8,128)}, u32[]{:S(2)}) %copy-start.2) | copy-done | bytes 3145752
  11.8 2.9 %message.2 = (bf16[128,6144]{1,0:T(8,128)(2,1)S(1)}, f32[128,256]{1,0:T(8,128)S(1)}) custom-call(s32[384,2048]{1,0:T(8,128)S(1)} %bitcast.20, bf16[192,384]{1,0:T(8,128)(2,1)S(1)} %bitcast.25, bf16[32,6144]{1,0:T(8,128)(2,1)S(1)} %bitcast.23, s32[1,384]{1,0:T(1,128)S(1)} %copy-done.7), custom_call_target="tpu_custom_call" | custom-call | flops 1 | bytes 1 | tf_op jit(solution)/shard_map/message/pallas_call | solution.py:47
  14.8 3.9 %collective-permute-done.6.refs_2_ = bf16[3072,128]{1,0:T(8,128)(2,1)S(1)} collective-permute-done((bf16[3072,128]{1,0:T(8,128)(2,1)S(1)}, bf16[3072,128]{1,0:T(8,128)(2,1)S(1)}, u32[]{:S(2)}, u32[]{:S(2)}) %collective-permute-start.6) | collective-permute-done | bytes 786464 | tf_op jit(solution)/shard_map/ppermute | solution.py:428
  19.4 11.0 %collective-permute-start = (f32[1,6144]{1,0:T(1,128)S(1)}, f32[1,6144]{1,0:T(1,128)S(1)}, u32[]{:S(2)}, u32[]{:S(2)}) collective-permute-start(f32[1,6144]{1,0:T(1,128)S(1)} %copy-done.8), channel_id=1, source_target_pairs={{0,248},{8,0},{16,8},{24,16},{32,24},{40,32},{48,40},{56,48},{64,5... | collective-permute-start | bytes 73736 | tf_op jit(solution)/shard_map/ppermute | solution.py:412
  30.4 4.8 %message.3 = (bf16[128,6144]{1,0:T(8,128)(2,1)S(1)}, bf16[64,6144]{1,0:T(8,128)(2,1)S(1)}, bf16[64,6144]{1,0:T(8,128)(2,1)S(1)}, f32[256,256]{1,0:T(8,128)S(1)}) custom-call(s32[384,2048]{1,0:T(8,128)S(1)} %bitcast.21, bf16[192,384]{1,0:T(8,128)(2,1)S(1)} %bitcast.26, bf16[32,6144]{1,0:T(8,128)(2,1)S(1)} %bitcast.24, s32[1,384]{1,0:T(1,128)S(1)} %copy-done.7, ...), custom_call_target="tpu_custom_call" | custom-call | flops 1 | bytes 1 | tf_op jit(solution)/shard_map/message/pallas_call | solution.py:47
  35.3 2.6 %gradient.1.refs_7_.refs_0_ = bf16[384,6144]{1,0:T(8,128)(2,1)S(1)} custom-call(bf16[384,6144]{1,0:T(8,128)(2,1)S(1)} %bitcast.22, bf16[192,384]{1,0:T(8,128)(2,1)S(1)} %bitcast.27, bf16[128,6144]{1,0:T(8,128)(2,1)S(1)} %get-tuple-element.36.refs_2_.refs_5_), custom_call_target="tpu_custom_call" | custom-call | flops 1 | bytes 1 | tf_op jit(solution)/shard_map/gradient/pallas_call | solution.py:47
  37.8 2.3 %hidden.1.refs_0_ = bf16[384,6144]{1,0:T(8,128)(2,1)S(1)} custom-call(f32[1,6144]{1,0:T(1,128)S(1)} %collective-permute-done.refs_0_, bf16[128,6144]{1,0:T(8,128)(2,1)S(1)} %get-tuple-element.35.refs_4_.refs_1_, bf16[128,6144]{1,0:T(8,128)(2,1)S(1)} %get-tuple-element.36.refs_2_.refs_5_, bf16[64,6144]{1,0:T(8,128)(2,1)S(1)} %get-tuple-element.37.refs_3_.refs_6_, ...), custom_call_target="tpu_custom_call" | custom-call | flops 1 | bytes 1 | tf_op jit(solution)/shard_map/hidden/pallas_call | solution.py:47
  40.2 1.4 %down.1 = (f32[384,128]{1,0:T(8,128)S(1)}, bf16[384,128]{1,0:T(8,128)(2,1)S(1)}) custom-call(bf16[384,6144]{1,0:T(8,128)(2,1)S(1)} %hidden.1.refs_0_, bf16[6144,128]{1,0:T(8,128)(2,1)S(1)} %collective-permute-done.1.refs_1_, bf16[6144,128]{1,0:T(8,128)(2,1)S(1)} %collective-permute-done.2.refs_2_.refs_1_), custom_call_target="tpu_custom_call" | custom-call | flops 1 | bytes 1 | tf_op jit(solution)/shard_map/down/pallas_call | solution.py:47
  41.6 1.5 %back.1 = bf16[384,128]{1,0:T(8,128)(2,1)S(1)} custom-call(bf16[384,6144]{1,0:T(8,128)(2,1)S(1)} %gradient.1.refs_7_.refs_0_, bf16[6144,128]{1,0:T(8,128)(2,1)S(1)} %collective-permute-done.2.refs_2_.refs_1_, bf16[3072,128]{1,0:T(8,128)(2,1)S(1)} %collective-permute-done.6.refs_2_, bf16[3072,128]{1,0:T(8,128)(2,1)S(1)} %collective-permute-done.7.refs_3_, ...), custom_call_target="tpu_custom_call" | custom-call | flops 1 | bytes 1 | tf_op jit(solution)/shard_map/back/pallas_call | solution.py:47
  43.1 1.6 %collective-permute-start.4 = (bf16[384,128]{1,0:T(8,128)(2,1)S(1)}, bf16[384,128]{1,0:T(8,128)(2,1)S(1)}, u32[]{:S(2)}, u32[]{:S(2)}) collective-permute-start(bf16[384,128]{1,0:T(8,128)(2,1)S(1)} %get-tuple-element.41.refs_4_), channel_id=1, source_target_pairs={{0,8},{8,16},{16,24},{24,32},{32,40},{40,48},{48,56},{56,64},{64,7... | collective-permute-start | bytes 294920 | tf_op jit(solution)/shard_map/ppermute | solution.py:412
  44.8 2.8 %collective-permute-done.8.refs_4_.refs_2_ = bf16[384,128]{1,0:T(8,128)(2,1)S(1)} collective-permute-done((bf16[384,128]{1,0:T(8,128)(2,1)S(1)}, bf16[384,128]{1,0:T(8,128)(2,1)S(1)}, u32[]{:S(2)}, u32[]{:S(2)}) %collective-permute-start.8) | collective-permute-done | bytes 98336 | tf_op jit(solution)/shard_map/ppermute | solution.py:412
  47.5 3.3 %collective-permute-done.3.refs_1_ = bf16[384,128]{1,0:T(8,128)(2,1)S(1)} collective-permute-done((bf16[384,128]{1,0:T(8,128)(2,1)S(1)}, bf16[384,128]{1,0:T(8,128)(2,1)S(1)}, u32[]{:S(2)}, u32[]{:S(2)}) %collective-permute-start.3) | collective-permute-done | bytes 98336 | tf_op jit(solution)/shard_map/ppermute | solution.py:412
  50.8 1.0 grad_up.1
  51.9 2.1 %collective-permute-start.9 = (bf16[4,128,768]{2,1,0:T(8,128)(2,1)S(1)}, bf16[4,128,768]{2,1,0:T(8,128)(2,1)S(1)}, u32[]{:S(2)}, u32[]{:S(2)}) collective-permute-start(bf16[4,128,768]{2,1,0:T(8,128)(2,1)S(1)} %get-tuple-element.43), channel_id=1, source_target_pairs={{3,0},{2,1},{1,2},{0,3},{7,4},{6,5},{5,6},{4,7},{11,8},{10,9},{9,1... | collective-permute-start | bytes 2359304 | tf_op jit(solution)/shard_map/ppermute | solution.py:422
  54.0 1.1 %grad_down.1 = (f32[4,128,768]{2,1,0:T(8,128)S(1)}, bf16[4,128,768]{2,1,0:T(8,128)(2,1)S(1)}) custom-call(bf16[384,6144]{1,0:T(8,128)(2,1)S(1)} %hidden.1.refs_0_, f32[384,128]{1,0:T(8,128)S(1)} %get-tuple-element.51.refs_1_, bf16[384,128]{1,0:T(8,128)(2,1)S(1)} %collective-permute-done.8.refs_4_.refs_2_), custom_call_target="tpu_custom_call" | custom-call | flops 1 | bytes 1 | tf_op jit(solution)/shard_map/grad_down/pallas_call | solution.py:47
  55.9 2.1 %feedback.4 = (bf16[384,6144]{1,0:T(8,128)(2,1)}, f32[8,128]{1,0:T(8,128)S(1)}) custom-call(bf16[128,6144]{1,0:T(8,128)(2,1)S(1)} %collective-permute-done.5.refs_3_.refs_0_, bf16[128,6144]{1,0:T(8,128)(2,1)S(1)} %get-tuple-element.35.refs_4_.refs_1_, bf16[384,128]{1,0:T(8,128)(2,1)S(1)} %collective-permute-done.4.refs_2_, bf16[6144,128]{1,0:T(8,128)(2,1)S(1)} %bitcast.16), custom_call_target="tpu_custom_call" | custom-call | flops 1 | bytes 1 | tf_op jit(solution)/shard_map/feedback/pallas_call | solution.py:47
  58.0 14.3 %collective-permute-done.9.refs_1_ = bf16[4,128,768]{2,1,0:T(8,128)(2,1)S(1)} collective-permute-done((bf16[4,128,768]{2,1,0:T(8,128)(2,1)S(1)}, bf16[4,128,768]{2,1,0:T(8,128)(2,1)S(1)}, u32[]{:S(2)}, u32[]{:S(2)}) %collective-permute-start.9) | collective-permute-done | bytes 786464 | tf_op jit(solution)/shard_map/ppermute | solution.py:422
  73.9 1.1 %collective-permute-start.14 = (bf16[2,128,768]{2,1,0:T(8,128)(2,1)S(1)}, bf16[2,128,768]{2,1,0:T(8,128)(2,1)S(1)}, u32[]{:S(2)}, u32[]{:S(2)}) collective-permute-start(bf16[2,128,768]{2,1,0:T(8,128)(2,1)S(1)} %get-tuple-element.56), channel_id=1, source_target_pairs={{3,0},{2,1},{1,2},{0,3},{7,4},{6,5},{5,6},{4,7},{11,8},{10,9},{9,1... | collective-permute-start | bytes 1179656 | tf_op jit(solution)/shard_map/ppermute | solution.py:422
  75.1 2.1 %feedback.5 = (bf16[384,6144]{1,0:T(8,128)(2,1)}, f32[8,128]{1,0:T(8,128)S(1)}) custom-call(bf16[128,6144]{1,0:T(8,128)(2,1)S(1)} %collective-permute-done.10.refs_2_.refs_0_, bf16[128,6144]{1,0:T(8,128)(2,1)S(1)} %get-tuple-element.44.refs_1_, bf16[384,128]{1,0:T(8,128)(2,1)S(1)} %collective-permute-done.4.refs_2_, ...), custom_call_target="tpu_custom_call", output_to_operand_aliasing={{0}: (4, {})} | custom-call | flops 1 | bytes 1 | tf_op jit(solution)/shard_map/feedback/pallas_call | solution.py:47
  77.7 4.5 %collective-permute-done.15.refs_1_ = bf16[2,128,768]{2,1,0:T(8,128)(2,1)S(1)} collective-permute-done((bf16[2,128,768]{2,1,0:T(8,128)(2,1)S(1)}, bf16[2,128,768]{2,1,0:T(8,128)(2,1)S(1)}, u32[]{:S(2)}, u32[]{:S(2)}) %collective-permute-start.15) | collective-permute-done | bytes 393248 | tf_op jit(solution)/shard_map/ppermute | solution.py:422
  82.3 4.9 %collective-permute-start.19 = (bf16[128,768]{1,0:T(8,128)(2,1)S(1)}, bf16[128,768]{1,0:T(8,128)(2,1)S(1)}, u32[]{:S(2)}, u32[]{:S(2)}) collective-permute-start(bf16[128,768]{1,0:T(8,128)(2,1)S(1)} %get-tuple-element.63), channel_id=1, source_target_pairs={{4,248},{5,249},{6,250},{7,251},{0,252},{1,253},{2,254},{3,255},{1... | collective-permute-start | bytes 589832 | tf_op jit(solution)/shard_map/ppermute | solution.py:422
  87.3 1.8 %collective-permute-start.16 = (bf16[128,768]{1,0:T(8,128)(2,1)S(1)}, bf16[128,768]{1,0:T(8,128)(2,1)S(1)}, u32[]{:S(2)}, u32[]{:S(2)}) collective-permute-start(bf16[128,768]{1,0:T(8,128)(2,1)S(1)} %get-tuple-element.60), channel_id=1, source_target_pairs={{0,8},{1,9},{2,10},{3,11},{4,12},{5,13},{6,14},{7,15},{8,16},{9,17... | collective-permute-start | bytes 589832 | tf_op jit(solution)/shard_map/ppermute | solution.py:422
  89.2 1.6 %feedback.6.refs_4_ = bf16[384,6144]{1,0:T(8,128)(2,1)} custom-call(bf16[64,6144]{1,0:T(8,128)(2,1)S(1)} %collective-permute-done.12.refs_0_.refs_2_, bf16[64,6144]{1,0:T(8,128)(2,1)S(1)} %get-tuple-element.47.refs_1_, bf16[384,128]{1,0:T(8,128)(2,1)S(1)} %collective-permute-done.4.refs_2_, ...), custom_call_target="tpu_custom_call", output_to_operand_aliasing={{}: (4, {})} | custom-call | flops 1 | bytes 1 | tf_op jit(solution)/shard_map/feedback/pallas_call | solution.py:47
  90.8 8.0 %collective-permute-done.19.refs_1_ = bf16[128,768]{1,0:T(8,128)(2,1)S(1)} collective-permute-done((bf16[128,768]{1,0:T(8,128)(2,1)S(1)}, bf16[128,768]{1,0:T(8,128)(2,1)S(1)}, u32[]{:S(2)}, u32[]{:S(2)}) %collective-permute-start.19) | collective-permute-done | bytes 196640 | tf_op jit(solution)/shard_map/ppermute | solution.py:422
  98.8 0.9 finish.2
  99.7 1.6 %feedback.7 = (bf16[384,6144]{1,0:T(8,128)(2,1)}, f32[8,128]{1,0:T(8,128)S(1)}) custom-call(bf16[64,6144]{1,0:T(8,128)(2,1)S(1)} %collective-permute-done.11.refs_0_, bf16[64,6144]{1,0:T(8,128)(2,1)S(1)} %get-tuple-element.46.refs_1_, bf16[384,128]{1,0:T(8,128)(2,1)S(1)} %collective-permute-done.4.refs_2_, ...), custom_call_target="tpu_custom_call", output_to_operand_aliasing={{0}: (4, {})} | custom-call | flops 1 | bytes 1 | tf_op jit(solution)/shard_map/feedback/pallas_call | solution.py:47
  101.3 0.9 collective-permute-done.17.refs_1_
  102.2 0.9 finish.3
  (45 shorter events, 4.4 us)
Async XLA Ops:
  0.6 9.2 %copy-start.7 = (s32[1,384]{1,0:T(1,128)S(1)}, s32[1,384]{1,0:T(1,128)}, u32[]{:S(2)}) copy-start(s32[1,384]{1,0:T(1,128)} %refs_3_.3) | copy-start | bytes 4612
  0.6 39.5 %collective-permute-start.1 = (bf16[6144,128]{1,0:T(8,128)(2,1)}, bf16[6144,128]{1,0:T(8,128)(2,1)S(1)}, u32[]{:S(2)}, u32[]{:S(2)}) collective-permute-start(bf16[6144,128]{1,0:T(8,128)(2,1)} %bitcast.29), channel_id=1, source_target_pairs={{0,248},{8,0},{16,8},{24,16},{32,24},{40,32},{48,40},{56,48},{64,5... | collective-permute-start | bytes 4718600 | tf_op jit(solution)/shard_map/ppermute | solution.py:412
  4.0 36.2 %collective-permute-start.2 = (bf16[6144,128]{1,0:T(8,128)(2,1)}, bf16[6144,128]{1,0:T(8,128)(2,1)S(1)}, u32[]{:S(2)}, u32[]{:S(2)}) collective-permute-start(bf16[6144,128]{1,0:T(8,128)(2,1)} %bitcast.14), channel_id=1, source_target_pairs={{0,8},{16,24},{32,40},{48,56},{64,72},{80,88},{96,104},{112,120},{... | collective-permute-start | bytes 4718600 | tf_op jit(solution)/shard_map/ppermute | solution.py:427
  5.2 1.4 %copy-start = (bf16[1,6144,128]{2,1,0:T(8,128)(2,1)S(1)}, bf16[1,6144,128]{2,1,0:T(8,128)(2,1)}, u32[]{:S(2)}) copy-start(bf16[1,6144,128]{2,1,0:T(8,128)(2,1)} %param.17) | copy-start | bytes 4718596
  6.7 3.2 %copy-start.4 = (bf16[1,32,6144]{2,1,0:T(8,128)(2,1)S(1)}, bf16[1,32,6144]{2,1,0:T(8,128)(2,1)}, u32[]{:S(2)}) copy-start(bf16[1,32,6144]{2,1,0:T(8,128)(2,1)} %param.11) | copy-start | bytes 1179652
  6.7 3.2 %copy-start.5 = (bf16[1,384,192]{1,2,0:T(8,128)(2,1)S(1)}, bf16[1,384,192]{1,2,0:T(8,128)(2,1)}, u32[]{:S(2)}) copy-start(bf16[1,384,192]{1,2,0:T(8,128)(2,1)} %param.10) | copy-start | bytes 442372
  6.7 12.0 %collective-permute-start.6 = (bf16[3072,128]{1,0:T(8,128)(2,1)S(1)}, bf16[3072,128]{1,0:T(8,128)(2,1)S(1)}, u32[]{:S(2)}, u32[]{:S(2)}) collective-permute-start(bf16[3072,128]{1,0:T(8,128)(2,1)S(1)} %pick_half.1), channel_id=1, source_target_pairs={{8,16},{24,32},{40,48},{56,64},{72,80},{88,96},{104,112},{120,128}... | collective-permute-start | bytes 2359304 | tf_op jit(solution)/shard_map/ppermute | solution.py:428
  9.9 1.9 %copy-start.2 = (s32[1,384,2048]{2,1,0:T(8,128)S(1)}, s32[1,384,2048]{2,1,0:T(8,128)}, u32[]{:S(2)}) copy-start(s32[1,384,2048]{2,1,0:T(8,128)} %param.9) | copy-start | bytes 9437188
  11.8 7.7 %copy-start.8 = (f32[1,6144]{1,0:T(1,128)S(1)}, f32[1,6144]{1,0:T(1,128)}, u32[]{:S(2)}) copy-start(f32[1,6144]{1,0:T(1,128)} %param.15) | copy-start | bytes 73732
  14.7 20.6 %copy-start.3 = (bf16[1,384,6144]{2,1,0:T(8,128)(2,1)S(1)}, bf16[1,384,6144]{2,1,0:T(8,128)(2,1)}, u32[]{:S(2)}) copy-start(bf16[1,384,6144]{2,1,0:T(8,128)(2,1)} %param.13) | copy-start | bytes 14155780
  14.7 20.6 %copy-start.6 = (bf16[1,384,192]{1,2,0:T(8,128)(2,1)S(1)}, bf16[1,384,192]{1,2,0:T(8,128)(2,1)}, u32[]{:S(2)}) copy-start(bf16[1,384,192]{1,2,0:T(8,128)(2,1)} %param.14) | copy-start | bytes 442372
  14.7 30.1 %collective-permute-start.5 = (bf16[128,6144]{1,0:T(8,128)(2,1)S(1)}, bf16[128,6144]{1,0:T(8,128)(2,1)S(1)}, u32[]{:S(2)}, u32[]{:S(2)}) collective-permute-start(bf16[128,6144]{1,0:T(8,128)(2,1)S(1)} %get-tuple-element.35.refs_4_.refs_1_), channel_id=1, source_target_pairs={{0,8},{8,16},{16,24},{24,32},{32,40},{40,48},{48,56},{56,64},{64,7... | collective-permute-start | bytes 4718600 | tf_op jit(solution)/shard_map/ppermute | solution.py:412
  18.7 22.9 %collective-permute-start.7 = (bf16[3072,128]{1,0:T(8,128)(2,1)S(1)}, bf16[3072,128]{1,0:T(8,128)(2,1)S(1)}, u32[]{:S(2)}, u32[]{:S(2)}) collective-permute-start(bf16[3072,128]{1,0:T(8,128)(2,1)S(1)} %collective-permute-done.6.refs_2_), channel_id=1, source_target_pairs={{1,0},{0,1},{3,2},{2,3},{5,4},{4,5},{7,6},{6,7},{17,16},{16,17},{1... | collective-permute-start | bytes 2359304 | tf_op jit(solution)/shard_map/ppermute | solution.py:422
  19.4 18.4 %collective-permute-start = (f32[1,6144]{1,0:T(1,128)S(1)}, f32[1,6144]{1,0:T(1,128)S(1)}, u32[]{:S(2)}, u32[]{:S(2)}) collective-permute-start(f32[1,6144]{1,0:T(1,128)S(1)} %copy-done.8), channel_id=1, source_target_pairs={{0,248},{8,0},{16,8},{24,16},{32,24},{40,32},{48,40},{56,48},{64,5... | collective-permute-start | bytes 73736 | tf_op jit(solution)/shard_map/ppermute | solution.py:412
  43.0 4.5 %collective-permute-start.8 = (bf16[384,128]{1,0:T(8,128)(2,1)S(1)}, bf16[384,128]{1,0:T(8,128)(2,1)S(1)}, u32[]{:S(2)}, u32[]{:S(2)}) collective-permute-start(bf16[384,128]{1,0:T(8,128)(2,1)S(1)} %back.1), channel_id=1, source_target_pairs={{0,240},{8,248},{16,0},{24,8},{32,16},{40,24},{48,32},{56,40},{64,... | collective-permute-start | bytes 294920 | tf_op jit(solution)/shard_map/ppermute | solution.py:412
  43.1 4.4 %collective-permute-start.4 = (bf16[384,128]{1,0:T(8,128)(2,1)S(1)}, bf16[384,128]{1,0:T(8,128)(2,1)S(1)}, u32[]{:S(2)}, u32[]{:S(2)}) collective-permute-start(bf16[384,128]{1,0:T(8,128)(2,1)S(1)} %get-tuple-element.41.refs_4_), channel_id=1, source_target_pairs={{0,8},{8,16},{16,24},{24,32},{32,40},{40,48},{48,56},{56,64},{64,7... | collective-permute-start | bytes 294920 | tf_op jit(solution)/shard_map/ppermute | solution.py:412
  44.8 6.0 %collective-permute-start.3 = (bf16[384,128]{1,0:T(8,128)(2,1)S(1)}, bf16[384,128]{1,0:T(8,128)(2,1)S(1)}, u32[]{:S(2)}, u32[]{:S(2)}) collective-permute-start(bf16[384,128]{1,0:T(8,128)(2,1)S(1)} %get-tuple-element.41.refs_4_), channel_id=1, source_target_pairs={{0,16},{8,24},{16,32},{24,40},{32,48},{40,56},{48,64},{56,72},{64,... | collective-permute-start | bytes 294920 | tf_op jit(solution)/shard_map/ppermute | solution.py:412
  51.8 20.5 %collective-permute-start.10 = (bf16[128,6144]{1,0:T(8,128)(2,1)S(1)}, bf16[128,6144]{1,0:T(8,128)(2,1)S(1)}, u32[]{:S(2)}, u32[]{:S(2)}) collective-permute-start(bf16[128,6144]{1,0:T(8,128)(2,1)S(1)} %get-tuple-element.44.refs_1_), channel_id=1, source_target_pairs={{0,8},{8,16},{16,24},{24,32},{32,40},{40,48},{48,56},{56,64},{64,7... | collective-permute-start | bytes 4718600 | tf_op jit(solution)/shard_map/ppermute | solution.py:412
  51.9 20.4 %collective-permute-start.9 = (bf16[4,128,768]{2,1,0:T(8,128)(2,1)S(1)}, bf16[4,128,768]{2,1,0:T(8,128)(2,1)S(1)}, u32[]{:S(2)}, u32[]{:S(2)}) collective-permute-start(bf16[4,128,768]{2,1,0:T(8,128)(2,1)S(1)} %get-tuple-element.43), channel_id=1, source_target_pairs={{3,0},{2,1},{1,2},{0,3},{7,4},{6,5},{5,6},{4,7},{11,8},{10,9},{9,1... | collective-permute-start | bytes 2359304 | tf_op jit(solution)/shard_map/ppermute | solution.py:422
  54.0 1.9 %copy-start.1 = (bf16[1,6144,128]{2,1,0:T(8,128)(2,1)S(1)}, bf16[1,6144,128]{2,1,0:T(8,128)(2,1)}, u32[]{:S(2)}) copy-start(bf16[1,6144,128]{2,1,0:T(8,128)(2,1)} %param.17) | copy-start | bytes 4718596
  55.1 18.7 %collective-permute-start.13 = (bf16[4,128,768]{2,1,0:T(8,128)(2,1)S(1)}, bf16[4,128,768]{2,1,0:T(8,128)(2,1)S(1)}, u32[]{:S(2)}, u32[]{:S(2)}) collective-permute-start(bf16[4,128,768]{2,1,0:T(8,128)(2,1)S(1)} %get-tuple-element.53), channel_id=1, source_target_pairs={{1,0},{0,1},{3,2},{2,3},{5,4},{4,5},{7,6},{6,7},{9,8},{8,9},{11,10... | collective-permute-start | bytes 2359304 | tf_op jit(solution)/shard_map/ppermute | solution.py:422
  55.5 22.2 %collective-permute-start.12 = (bf16[64,6144]{1,0:T(8,128)(2,1)S(1)}, bf16[64,6144]{1,0:T(8,128)(2,1)S(1)}, u32[]{:S(2)}, u32[]{:S(2)}) collective-permute-start(bf16[64,6144]{1,0:T(8,128)(2,1)S(1)} %get-tuple-element.47.refs_1_), channel_id=1, source_target_pairs={{0,8},{8,16},{16,24},{24,32},{32,40},{40,48},{48,56},{56,64},{64,7... | collective-permute-start | bytes 2359304 | tf_op jit(solution)/shard_map/ppermute | solution.py:412
  72.4 27.3 %collective-permute-start.11 = (bf16[64,6144]{1,0:T(8,128)(2,1)S(1)}, bf16[64,6144]{1,0:T(8,128)(2,1)S(1)}, u32[]{:S(2)}, u32[]{:S(2)}) collective-permute-start(bf16[64,6144]{1,0:T(8,128)(2,1)S(1)} %get-tuple-element.46.refs_1_), channel_id=1, source_target_pairs={{0,8},{8,16},{16,24},{24,32},{32,40},{40,48},{48,56},{56,64},{64,7... | collective-permute-start | bytes 2359304 | tf_op jit(solution)/shard_map/ppermute | solution.py:412
  73.0 9.2 %collective-permute-start.15 = (bf16[2,128,768]{2,1,0:T(8,128)(2,1)S(1)}, bf16[2,128,768]{2,1,0:T(8,128)(2,1)S(1)}, u32[]{:S(2)}, u32[]{:S(2)}) collective-permute-start(bf16[2,128,768]{2,1,0:T(8,128)(2,1)S(1)} %get-tuple-element.54.refs_2_), channel_id=1, source_target_pairs={{1,0},{0,1},{3,2},{2,3},{5,4},{4,5},{7,6},{6,7},{9,8},{8,9},{11,10... | collective-permute-start | bytes 1179656 | tf_op jit(solution)/shard_map/ppermute | solution.py:422
  73.9 13.3 %collective-permute-start.14 = (bf16[2,128,768]{2,1,0:T(8,128)(2,1)S(1)}, bf16[2,128,768]{2,1,0:T(8,128)(2,1)S(1)}, u32[]{:S(2)}, u32[]{:S(2)}) collective-permute-start(bf16[2,128,768]{2,1,0:T(8,128)(2,1)S(1)} %get-tuple-element.56), channel_id=1, source_target_pairs={{3,0},{2,1},{1,2},{0,3},{7,4},{6,5},{5,6},{4,7},{11,8},{10,9},{9,1... | collective-permute-start | bytes 1179656 | tf_op jit(solution)/shard_map/ppermute | solution.py:422
  82.3 16.5 %collective-permute-start.19 = (bf16[128,768]{1,0:T(8,128)(2,1)S(1)}, bf16[128,768]{1,0:T(8,128)(2,1)S(1)}, u32[]{:S(2)}, u32[]{:S(2)}) collective-permute-start(bf16[128,768]{1,0:T(8,128)(2,1)S(1)} %get-tuple-element.63), channel_id=1, source_target_pairs={{4,248},{5,249},{6,250},{7,251},{0,252},{1,253},{2,254},{3,255},{1... | collective-permute-start | bytes 589832 | tf_op jit(solution)/shard_map/ppermute | solution.py:422
  87.2 11.7 %collective-permute-start.18 = (bf16[128,768]{1,0:T(8,128)(2,1)S(1)}, bf16[128,768]{1,0:T(8,128)(2,1)S(1)}, u32[]{:S(2)}, u32[]{:S(2)}) collective-permute-start(bf16[128,768]{1,0:T(8,128)(2,1)S(1)} %get-tuple-element.59.refs_2_), channel_id=1, source_target_pairs={{0,248},{1,249},{2,250},{3,251},{4,252},{5,253},{6,254},{7,255},{8... | collective-permute-start | bytes 589832 | tf_op jit(solution)/shard_map/ppermute | solution.py:422
  87.3 14.0 %collective-permute-start.16 = (bf16[128,768]{1,0:T(8,128)(2,1)S(1)}, bf16[128,768]{1,0:T(8,128)(2,1)S(1)}, u32[]{:S(2)}, u32[]{:S(2)}) collective-permute-start(bf16[128,768]{1,0:T(8,128)(2,1)S(1)} %get-tuple-element.60), channel_id=1, source_target_pairs={{0,8},{1,9},{2,10},{3,11},{4,12},{5,13},{6,14},{7,15},{8,16},{9,17... | collective-permute-start | bytes 589832 | tf_op jit(solution)/shard_map/ppermute | solution.py:422
  89.1 13.2 %collective-permute-start.17 = (bf16[128,768]{1,0:T(8,128)(2,1)S(1)}, bf16[128,768]{1,0:T(8,128)(2,1)S(1)}, u32[]{:S(2)}, u32[]{:S(2)}) collective-permute-start(bf16[128,768]{1,0:T(8,128)(2,1)S(1)} %get-tuple-element.61), channel_id=1, source_target_pairs={{4,8},{5,9},{6,10},{7,11},{0,12},{1,13},{2,14},{3,15},{12,16},{13,... | collective-permute-start | bytes 589832 | tf_op jit(solution)/shard_map/ppermute | solution.py:422

commit v12 on v7

--- a/solution.py
+++ b/solution.py
@@ -312,15 +312,20 @@
     )
 
 
-def finish_kernel(one_ref, two_ref, out_ref):
+def finish_kernel(one_ref, two_ref, out_ref, done_ref):
     out_ref[...] = (one_ref[...].astype(F32) + two_ref[...].astype(F32)).T
-
-
-def finish(parts):
+    done_ref[...] = jnp.zeros_like(done_ref)
+
+
+def finish(parts, **ties):
     return launch(
         finish_kernel, "finish", [(part, VMEM) for part in parts],
-        [(array((PIECE, R), F32), pl.BlockSpec((PIECE, R)))],
-    )[0]
+        [
+            (array((PIECE, R), F32), pl.BlockSpec((PIECE, R))),
+            (array((8, 128), F32), VMEM),
+        ],
+        **ties,
+    )
 
 
 def feedback_kernel(first, count, before, x_ref, own_ref, act_ref, weight_ref, *refs):
@@ -433,17 +438,19 @@
     )
     feedback, done = feedback_of(messages[0], arrived0, 0, None, True)
     up_kept, up_sent, message3 = halve(
-        up_kept, among(up_sent, 3), needs=[arrived1], carried=messages[3:4]
+        up_kept, among(up_sent, 3), needs=[arrived1, done], carried=messages[3:4]
     )
     arrived3 = along(message3, 1)
-    down_kept, down_sent = halve(down_kept, among(down_sent, 1), needs=[done])
+    down_kept, down_sent = halve(down_kept, among(down_sent, 1), needs=[up_sent])
     feedback, done = feedback_of(message1, arrived1, 1, feedback, True)
-    up_parts = split(up_kept, among(up_sent, 1), needs=[arrived2])
-    down_parts = split(down_kept, among(down_sent, 3), needs=[done])
-    grad_up = finish([among(up_parts[half], 0, half, -1) for half in range(2)])
-    grad_down = finish([among(down_parts[half], 0, half, 1) for half in range(2)])
+    up_parts = split(up_kept, among(up_sent, 1), needs=[done])
+    down_parts = split(down_kept, among(down_sent, 3), needs=[up_parts[0], arrived2])
     feedback = feedback_of(message2, arrived2, 2, feedback)[0]
-    feedback = feedback_of(message3, arrived3, 3, feedback)[0]
+    feedback, done = feedback_of(message3, arrived3, 3, feedback, True)
+    grad_up, done_up = finish([among(up_parts[half], 0, half, -1) for half in range(2)])
+    grad_down = finish(
+        [among(down_parts[half], 0, half, 1) for half in range(2)], needs=[done, done_up]
+    )[0]
     return (feedback[None], grad_down[None], grad_up[None])
 
 

time: 104 us -> 102 us (0.981)
  waiting for transfers between devices: 40.9 us -> 38.1 us
    ppermute x10, starting transfers between devices: 16.2 us -> 17.8 us  [along(): return lax.ppermute(value, 'section', pairs)]
    ppermute x8, waiting for transfers between devices: 29.5 us -> 28.1 us  [among(): return lax.ppermute(value, both, pairs)]
    ppermute x10, waiting for transfers between devices: 11.4 us -> 10 us  [along(): return lax.ppermute(value, 'section', pairs)]
  transfers between devices with their start and end apart: 18 -> 18, of which waited for: 7 -> 7; matrix products, arithmetic and copies ran while one was open for 0% -> 0% of each run, Pallas kernels for 25% -> 26%
where the time goes in v12:
time: 102 us
  waiting for transfers between devices  38.1 us (37%)
  starting transfers between devices  30.1 us (30%)
  Pallas kernels  28.1 us (28%)
  local copies, waits for them, and re-layouts  4.63 us (5%)
    pallas_call x18, Pallas kernels, launch(): pl.pallas_call(wrapped, grid=grid, in_specs=[spec for _, spec in ins] + [...  28.1 us
    ppermute x8, waiting for transfers between devices, among(): return lax.ppermute(value, both, pairs)  28.1 us
    ppermute x10, starting transfers between devices, along(): return lax.ppermute(value, 'section', pairs)  17.8 us
    ppermute x8, starting transfers between devices, among(): return lax.ppermute(value, both, pairs)  12.3 us
    ppermute x10, waiting for transfers between devices, along(): return lax.ppermute(value, 'section', pairs)  10 us
    unnamed x18, local copies, waits for them, and re-layouts  4.63 us
  transfers between devices with their start and end apart: 18, of which 7 were waited for; matrix products, arithmetic and copies ran while one was open for 0% of the time, Pallas kernels for 26%

profile of v12, /device:TPU:1, one launch (start us, length us, event | category | flops | bytes accessed | tf_op | source)
XLA Modules:
  0.0 101.8 jit_solution(9789945352697914635)
XLA Ops:
  0.6 3.3 %collective-permute-start.1 = (bf16[6144,128]{1,0:T(8,128)(2,1)}, bf16[6144,128]{1,0:T(8,128)(2,1)S(1)}, u32[]{:S(2)}, u32[]{:S(2)}) collective-permute-start(bf16[6144,128]{1,0:T(8,128)(2,1)} %bitcast.28), channel_id=1, source_target_pairs={{0,248},{8,0},{16,8},{24,16},{32,24},{40,32},{48,40},{56,48},{64,5... | collective-permute-start | bytes 4718600 | tf_op jit(solution)/shard_map/ppermute | solution.py:392
  4.0 1.9 %copy-done.1 = s32[1,384,2048]{2,1,0:T(8,128)S(1)} copy-done((s32[1,384,2048]{2,1,0:T(8,128)S(1)}, s32[1,384,2048]{2,1,0:T(8,128)}, u32[]{:S(2)}) %copy-start.1) | copy-done | bytes 3145752
  5.8 1.0 copy-done.3
  6.8 0.9 copy-done.4
  8.4 2.5 %message.2 = (bf16[96,6144]{1,0:T(8,128)(2,1)S(1)}, f32[96,256]{1,0:T(8,128)S(1)}) custom-call(s32[384,2048]{1,0:T(8,128)S(1)} %bitcast.19, bf16[192,384]{1,0:T(8,128)(2,1)S(1)} %bitcast.24, bf16[32,6144]{1,0:T(8,128)(2,1)S(1)} %bitcast.22, s32[1,384]{1,0:T(1,128)S(1)} %copy-done.6), custom_call_target="tpu_custom_call" | custom-call | flops 1 | bytes 1 | tf_op jit(solution)/shard_map/message/pallas_call | solution.py:46
  11.3 4.4 %collective-permute-start = (f32[1,6144]{1,0:T(1,128)S(1)}, f32[1,6144]{1,0:T(1,128)S(1)}, u32[]{:S(2)}, u32[]{:S(2)}) collective-permute-start(f32[1,6144]{1,0:T(1,128)S(1)} %copy-done.8), channel_id=1, source_target_pairs={{0,248},{8,0},{16,8},{24,16},{32,24},{40,32},{48,40},{56,48},{64,5... | collective-permute-start | bytes 73736 | tf_op jit(solution)/shard_map/ppermute | solution.py:392
  15.7 5.4 %message.3 = (bf16[144,6144]{1,0:T(8,128)(2,1)S(1)}, bf16[96,6144]{1,0:T(8,128)(2,1)S(1)}, bf16[48,6144]{1,0:T(8,128)(2,1)S(1)}, f32[288,256]{1,0:T(8,128)S(1)}) custom-call(s32[384,2048]{1,0:T(8,128)S(1)} %bitcast.20, bf16[192,384]{1,0:T(8,128)(2,1)S(1)} %bitcast.25, bf16[32,6144]{1,0:T(8,128)(2,1)S(1)} %bitcast.23, s32[1,384]{1,0:T(1,128)S(1)} %copy-done.7, ...), custom_call_target="tpu_custom_call" | custom-call | flops 1 | bytes 1 | tf_op jit(solution)/shard_map/message/pallas_call | solution.py:46
  21.1 2.6 %gradient.1.refs_7_.refs_0_ = bf16[384,6144]{1,0:T(8,128)(2,1)S(1)} custom-call(bf16[384,6144]{1,0:T(8,128)(2,1)S(1)} %bitcast.21, bf16[192,384]{1,0:T(8,128)(2,1)S(1)} %bitcast.26, bf16[144,6144]{1,0:T(8,128)(2,1)S(1)} %get-tuple-element.36.refs_2_.refs_5_), custom_call_target="tpu_custom_call" | custom-call | flops 1 | bytes 1 | tf_op jit(solution)/shard_map/gradient/pallas_call | solution.py:46
  23.7 2.3 %hidden.1.refs_0_ = bf16[384,6144]{1,0:T(8,128)(2,1)S(1)} custom-call(f32[1,6144]{1,0:T(1,128)S(1)} %collective-permute-done.refs_0_, bf16[96,6144]{1,0:T(8,128)(2,1)S(1)} %get-tuple-element.35.refs_4_.refs_1_, bf16[144,6144]{1,0:T(8,128)(2,1)S(1)} %get-tuple-element.36.refs_2_.refs_5_, bf16[96,6144]{1,0:T(8,128)(2,1)S(1)} %get-tuple-element.37.refs_3_.refs_6_, ...), custom_call_target="tpu_custom_call" | custom-call | flops 1 | bytes 1 | tf_op jit(solution)/shard_map/hidden/pallas_call | solution.py:46
  26.0 1.4 %down.1 = (f32[384,128]{1,0:T(8,128)S(1)}, bf16[384,128]{1,0:T(8,128)(2,1)S(1)}) custom-call(bf16[384,6144]{1,0:T(8,128)(2,1)S(1)} %hidden.1.refs_0_, bf16[6144,128]{1,0:T(8,128)(2,1)S(1)} %collective-permute-done.1.refs_1_, bf16[6144,128]{1,0:T(8,128)(2,1)S(1)} %collective-permute-done.2.refs_2_.refs_1_), custom_call_target="tpu_custom_call" | custom-call | flops 1 | bytes 1 | tf_op jit(solution)/shard_map/down/pallas_call | solution.py:46
  27.4 1.4 %back.1 = bf16[384,128]{1,0:T(8,128)(2,1)S(1)} custom-call(bf16[384,6144]{1,0:T(8,128)(2,1)S(1)} %gradient.1.refs_7_.refs_0_, bf16[6144,128]{1,0:T(8,128)(2,1)S(1)} %collective-permute-done.2.refs_2_.refs_1_, bf16[384,128]{1,0:T(8,128)(2,1)S(1)} %get-tuple-element.41.refs_2_), custom_call_target="tpu_custom_call" | custom-call | flops 1 | bytes 1 | tf_op jit(solution)/shard_map/back/pallas_call | solution.py:46
  28.8 6.9 %collective-permute-start.6 = (bf16[384,128]{1,0:T(8,128)(2,1)S(1)}, bf16[384,128]{1,0:T(8,128)(2,1)S(1)}, u32[]{:S(2)}, u32[]{:S(2)}) collective-permute-start(bf16[384,128]{1,0:T(8,128)(2,1)S(1)} %back.1), channel_id=1, source_target_pairs={{0,240},{8,248},{16,0},{24,8},{32,16},{40,24},{48,32},{56,40},{64,... | collective-permute-start | bytes 294920 | tf_op jit(solution)/shard_map/ppermute | solution.py:392
  35.8 1.6 %collective-permute-done.6.refs_4_.refs_2_ = bf16[384,128]{1,0:T(8,128)(2,1)S(1)} collective-permute-done((bf16[384,128]{1,0:T(8,128)(2,1)S(1)}, bf16[384,128]{1,0:T(8,128)(2,1)S(1)}, u32[]{:S(2)}, u32[]{:S(2)}) %collective-permute-start.6) | collective-permute-done | bytes 98336 | tf_op jit(solution)/shard_map/ppermute | solution.py:392
  37.7 8.1 %collective-permute-done.3.refs_1_ = bf16[384,128]{1,0:T(8,128)(2,1)S(1)} collective-permute-done((bf16[384,128]{1,0:T(8,128)(2,1)S(1)}, bf16[384,128]{1,0:T(8,128)(2,1)S(1)}, u32[]{:S(2)}, u32[]{:S(2)}) %collective-permute-start.3) | collective-permute-done | bytes 98336 | tf_op jit(solution)/shard_map/ppermute | solution.py:392
  45.8 1.0 grad_up.1
  46.9 2.7 %collective-permute-start.7 = (bf16[4,128,768]{2,1,0:T(8,128)(2,1)S(1)}, bf16[4,128,768]{2,1,0:T(8,128)(2,1)S(1)}, u32[]{:S(2)}, u32[]{:S(2)}) collective-permute-start(bf16[4,128,768]{2,1,0:T(8,128)(2,1)S(1)} %get-tuple-element.43), channel_id=1, source_target_pairs={{3,0},{2,1},{1,2},{0,3},{7,4},{6,5},{5,6},{4,7},{11,8},{10,9},{9,1... | collective-permute-start | bytes 2359304 | tf_op jit(solution)/shard_map/ppermute | solution.py:402
  49.6 1.1 %grad_down.1 = (f32[4,128,768]{2,1,0:T(8,128)S(1)}, bf16[4,128,768]{2,1,0:T(8,128)(2,1)S(1)}) custom-call(bf16[384,6144]{1,0:T(8,128)(2,1)S(1)} %hidden.1.refs_0_, f32[384,128]{1,0:T(8,128)S(1)} %get-tuple-element.51.refs_1_, bf16[384,128]{1,0:T(8,128)(2,1)S(1)} %collective-permute-done.6.refs_4_.refs_2_), custom_call_target="tpu_custom_call" | custom-call | flops 1 | bytes 1 | tf_op jit(solution)/shard_map/grad_down/pallas_call | solution.py:46
  51.0 2.1 %feedback.4 = (bf16[384,6144]{1,0:T(8,128)(2,1)}, f32[8,128]{1,0:T(8,128)S(1)}) custom-call(bf16[96,6144]{1,0:T(8,128)(2,1)S(1)} %collective-permute-done.5.refs_3_.refs_0_, bf16[96,6144]{1,0:T(8,128)(2,1)S(1)} %get-tuple-element.35.refs_4_.refs_1_, bf16[384,128]{1,0:T(8,128)(2,1)S(1)} %collective-permute-done.4.refs_2_, bf16[6144,128]{1,0:T(8,128)(2,1)S(1)} %bitcast.15), custom_call_target="tpu_custom_call" | custom-call | flops 1 | bytes 1 | tf_op jit(solution)/shard_map/feedback/pallas_call | solution.py:46
  53.1 14.2 %collective-permute-done.7.refs_1_ = bf16[4,128,768]{2,1,0:T(8,128)(2,1)S(1)} collective-permute-done((bf16[4,128,768]{2,1,0:T(8,128)(2,1)S(1)}, bf16[4,128,768]{2,1,0:T(8,128)(2,1)S(1)}, u32[]{:S(2)}, u32[]{:S(2)}) %collective-permute-start.7) | collective-permute-done | bytes 786464 | tf_op jit(solution)/shard_map/ppermute | solution.py:402
  67.8 1.6 %collective-permute-done.11.refs_1_ = bf16[4,128,768]{2,1,0:T(8,128)(2,1)S(1)} collective-permute-done((bf16[4,128,768]{2,1,0:T(8,128)(2,1)S(1)}, bf16[4,128,768]{2,1,0:T(8,128)(2,1)S(1)}, u32[]{:S(2)}, u32[]{:S(2)}) %collective-permute-start.11) | collective-permute-done | bytes 786464 | tf_op jit(solution)/shard_map/ppermute | solution.py:402
  69.5 0.7 collective-permute-start.12
  70.3 2.6 %collective-permute-start.9 = (bf16[48,6144]{1,0:T(8,128)(2,1)S(1)}, bf16[48,6144]{1,0:T(8,128)(2,1)S(1)}, u32[]{:S(2)}, u32[]{:S(2)}) collective-permute-start(bf16[48,6144]{1,0:T(8,128)(2,1)S(1)} %get-tuple-element.46.refs_1_), channel_id=1, source_target_pairs={{0,8},{8,16},{16,24},{24,32},{32,40},{40,48},{48,56},{56,64},{64,7... | collective-permute-start | bytes 1769480 | tf_op jit(solution)/shard_map/ppermute | solution.py:392
  72.9 2.6 %feedback.5 = (bf16[384,6144]{1,0:T(8,128)(2,1)}, f32[8,128]{1,0:T(8,128)S(1)}) custom-call(bf16[144,6144]{1,0:T(8,128)(2,1)S(1)} %collective-permute-done.8.refs_2_.refs_0_, bf16[144,6144]{1,0:T(8,128)(2,1)S(1)} %get-tuple-element.44.refs_1_, bf16[384,128]{1,0:T(8,128)(2,1)S(1)} %collective-permute-done.4.refs_2_, ...), custom_call_target="tpu_custom_call", output_to_operand_aliasing={{0}: (4, {})} | custom-call | flops 1 | bytes 1 | tf_op jit(solution)/shard_map/feedback/pallas_call | solution.py:46
  75.6 6.2 %collective-permute-start.17 = (bf16[128,768]{1,0:T(8,128)(2,1)S(1)}, bf16[128,768]{1,0:T(8,128)(2,1)S(1)}, u32[]{:S(2)}, u32[]{:S(2)}) collective-permute-start(bf16[128,768]{1,0:T(8,128)(2,1)S(1)} %get-tuple-element.63), channel_id=1, source_target_pairs={{4,248},{5,249},{6,250},{7,251},{0,252},{1,253},{2,254},{3,255},{1... | collective-permute-start | bytes 589832 | tf_op jit(solution)/shard_map/ppermute | solution.py:402
  81.8 0.9 collective-permute-start.16
  82.8 1.0 collective-permute-start.14
  84.1 2.1 %feedback.6.refs_4_ = bf16[384,6144]{1,0:T(8,128)(2,1)} custom-call(bf16[96,6144]{1,0:T(8,128)(2,1)S(1)} %collective-permute-done.10.refs_0_.refs_3_, bf16[96,6144]{1,0:T(8,128)(2,1)S(1)} %get-tuple-element.47.refs_1_, bf16[384,128]{1,0:T(8,128)(2,1)S(1)} %collective-permute-done.4.refs_2_, ...), custom_call_target="tpu_custom_call", output_to_operand_aliasing={{}: (4, {})} | custom-call | flops 1 | bytes 1 | tf_op jit(solution)/shard_map/feedback/pallas_call | solution.py:46
  86.1 1.5 %feedback.7 = (bf16[384,6144]{1,0:T(8,128)(2,1)}, f32[8,128]{1,0:T(8,128)S(1)}) custom-call(bf16[48,6144]{1,0:T(8,128)(2,1)S(1)} %collective-permute-done.9.refs_0_, bf16[48,6144]{1,0:T(8,128)(2,1)S(1)} %get-tuple-element.46.refs_1_, bf16[384,128]{1,0:T(8,128)(2,1)S(1)} %collective-permute-done.4.refs_2_, ...), custom_call_target="tpu_custom_call", output_to_operand_aliasing={{0}: (4, {})} | custom-call | flops 1 | bytes 1 | tf_op jit(solution)/shard_map/feedback/pallas_call | solution.py:46
  87.6 9.8 %collective-permute-done.17.refs_1_ = bf16[128,768]{1,0:T(8,128)(2,1)S(1)} collective-permute-done((bf16[128,768]{1,0:T(8,128)(2,1)S(1)}, bf16[128,768]{1,0:T(8,128)(2,1)S(1)}, u32[]{:S(2)}, u32[]{:S(2)}) %collective-permute-start.17) | collective-permute-done | bytes 196640 | tf_op jit(solution)/shard_map/ppermute | solution.py:402
  97.5 0.9 finish.2
  98.4 2.5 %collective-permute-done.15.refs_1_ = bf16[128,768]{1,0:T(8,128)(2,1)S(1)} collective-permute-done((bf16[128,768]{1,0:T(8,128)(2,1)S(1)}, bf16[128,768]{1,0:T(8,128)(2,1)S(1)}, u32[]{:S(2)}, u32[]{:S(2)}) %collective-permute-start.15) | collective-permute-done | bytes 196640 | tf_op jit(solution)/shard_map/ppermute | solution.py:402
  100.9 0.9 finish.3
  (40 shorter events, 2.9 us)
Async XLA Ops:
  0.6 25.4 %collective-permute-start.1 = (bf16[6144,128]{1,0:T(8,128)(2,1)}, bf16[6144,128]{1,0:T(8,128)(2,1)S(1)}, u32[]{:S(2)}, u32[]{:S(2)}) collective-permute-start(bf16[6144,128]{1,0:T(8,128)(2,1)} %bitcast.28), channel_id=1, source_target_pairs={{0,248},{8,0},{16,8},{24,16},{32,24},{40,32},{48,40},{56,48},{64,5... | collective-permute-start | bytes 4718600 | tf_op jit(solution)/shard_map/ppermute | solution.py:392
  4.0 22.1 %collective-permute-start.2 = (bf16[6144,128]{1,0:T(8,128)(2,1)}, bf16[6144,128]{1,0:T(8,128)(2,1)S(1)}, u32[]{:S(2)}, u32[]{:S(2)}) collective-permute-start(bf16[6144,128]{1,0:T(8,128)(2,1)} %bitcast.14), channel_id=1, source_target_pairs={{0,8},{8,16},{16,24},{24,32},{32,40},{40,48},{48,56},{56,64},{64,7... | collective-permute-start | bytes 4718600 | tf_op jit(solution)/shard_map/ppermute | solution.py:392
  4.0 1.9 %copy-start.1 = (s32[1,384,2048]{2,1,0:T(8,128)S(1)}, s32[1,384,2048]{2,1,0:T(8,128)}, u32[]{:S(2)}) copy-start(s32[1,384,2048]{2,1,0:T(8,128)} %param.9) | copy-start | bytes 9437188
  5.8 1.0 copy-start.3
  6.8 0.9 copy-start.4
  7.8 0.7 copy-start.6
  8.4 2.9 %copy-start.8 = (f32[1,6144]{1,0:T(1,128)S(1)}, f32[1,6144]{1,0:T(1,128)}, u32[]{:S(2)}) copy-start(f32[1,6144]{1,0:T(1,128)} %param.15) | copy-start | bytes 73732
  8.4 7.2 %copy-start.7 = (s32[1,384]{1,0:T(1,128)S(1)}, s32[1,384]{1,0:T(1,128)}, u32[]{:S(2)}) copy-start(s32[1,384]{1,0:T(1,128)} %refs_3_.3) | copy-start | bytes 4612
  10.9 10.2 %copy-start.2 = (bf16[1,384,6144]{2,1,0:T(8,128)(2,1)S(1)}, bf16[1,384,6144]{2,1,0:T(8,128)(2,1)}, u32[]{:S(2)}) copy-start(bf16[1,384,6144]{2,1,0:T(8,128)(2,1)} %param.13) | copy-start | bytes 14155780
  10.9 10.2 %copy-start.5 = (bf16[1,384,192]{1,2,0:T(8,128)(2,1)S(1)}, bf16[1,384,192]{1,2,0:T(8,128)(2,1)}, u32[]{:S(2)}) copy-start(bf16[1,384,192]{1,2,0:T(8,128)(2,1)} %param.14) | copy-start | bytes 442372
  10.9 24.9 %collective-permute-start.5 = (bf16[96,6144]{1,0:T(8,128)(2,1)S(1)}, bf16[96,6144]{1,0:T(8,128)(2,1)S(1)}, u32[]{:S(2)}, u32[]{:S(2)}) collective-permute-start(bf16[96,6144]{1,0:T(8,128)(2,1)S(1)} %get-tuple-element.35.refs_4_.refs_1_), channel_id=1, source_target_pairs={{0,8},{8,16},{16,24},{24,32},{32,40},{40,48},{48,56},{56,64},{64,7... | collective-permute-start | bytes 3538952 | tf_op jit(solution)/shard_map/ppermute | solution.py:392
  11.3 12.4 %collective-permute-start = (f32[1,6144]{1,0:T(1,128)S(1)}, f32[1,6144]{1,0:T(1,128)S(1)}, u32[]{:S(2)}, u32[]{:S(2)}) collective-permute-start(f32[1,6144]{1,0:T(1,128)S(1)} %copy-done.8), channel_id=1, source_target_pairs={{0,248},{8,0},{16,8},{24,16},{32,24},{40,32},{48,40},{56,48},{64,5... | collective-permute-start | bytes 73736 | tf_op jit(solution)/shard_map/ppermute | solution.py:392
  28.8 8.6 %collective-permute-start.6 = (bf16[384,128]{1,0:T(8,128)(2,1)S(1)}, bf16[384,128]{1,0:T(8,128)(2,1)S(1)}, u32[]{:S(2)}, u32[]{:S(2)}) collective-permute-start(bf16[384,128]{1,0:T(8,128)(2,1)S(1)} %back.1), channel_id=1, source_target_pairs={{0,240},{8,248},{16,0},{24,8},{32,16},{40,24},{48,32},{56,40},{64,... | collective-permute-start | bytes 294920 | tf_op jit(solution)/shard_map/ppermute | solution.py:392
  35.8 2.0 %collective-permute-start.4 = (bf16[384,128]{1,0:T(8,128)(2,1)S(1)}, bf16[384,128]{1,0:T(8,128)(2,1)S(1)}, u32[]{:S(2)}, u32[]{:S(2)}) collective-permute-start(bf16[384,128]{1,0:T(8,128)(2,1)S(1)} %get-tuple-element.41.refs_2_), channel_id=1, source_target_pairs={{0,8},{8,16},{16,24},{24,32},{32,40},{40,48},{48,56},{56,64},{64,7... | collective-permute-start | bytes 294920 | tf_op jit(solution)/shard_map/ppermute | solution.py:392
  35.8 10.0 %collective-permute-start.3 = (bf16[384,128]{1,0:T(8,128)(2,1)S(1)}, bf16[384,128]{1,0:T(8,128)(2,1)S(1)}, u32[]{:S(2)}, u32[]{:S(2)}) collective-permute-start(bf16[384,128]{1,0:T(8,128)(2,1)S(1)} %get-tuple-element.41.refs_2_), channel_id=1, source_target_pairs={{0,16},{8,24},{16,32},{24,40},{32,48},{40,56},{48,64},{56,72},{64,... | collective-permute-start | bytes 294920 | tf_op jit(solution)/shard_map/ppermute | solution.py:392
  46.8 20.5 %collective-permute-start.8 = (bf16[144,6144]{1,0:T(8,128)(2,1)S(1)}, bf16[144,6144]{1,0:T(8,128)(2,1)S(1)}, u32[]{:S(2)}, u32[]{:S(2)}) collective-permute-start(bf16[144,6144]{1,0:T(8,128)(2,1)S(1)} %get-tuple-element.44.refs_1_), channel_id=1, source_target_pairs={{0,8},{8,16},{16,24},{24,32},{32,40},{40,48},{48,56},{56,64},{64,7... | collective-permute-start | bytes 5308424 | tf_op jit(solution)/shard_map/ppermute | solution.py:392
  46.9 20.4 %collective-permute-start.7 = (bf16[4,128,768]{2,1,0:T(8,128)(2,1)S(1)}, bf16[4,128,768]{2,1,0:T(8,128)(2,1)S(1)}, u32[]{:S(2)}, u32[]{:S(2)}) collective-permute-start(bf16[4,128,768]{2,1,0:T(8,128)(2,1)S(1)} %get-tuple-element.43), channel_id=1, source_target_pairs={{3,0},{2,1},{1,2},{0,3},{7,4},{6,5},{5,6},{4,7},{11,8},{10,9},{9,1... | collective-permute-start | bytes 2359304 | tf_op jit(solution)/shard_map/ppermute | solution.py:402
  49.6 1.4 %copy-start = (bf16[1,6144,128]{2,1,0:T(8,128)(2,1)S(1)}, bf16[1,6144,128]{2,1,0:T(8,128)(2,1)}, u32[]{:S(2)}) copy-start(bf16[1,6144,128]{2,1,0:T(8,128)(2,1)} %param.17) | copy-start | bytes 4718596
  50.7 18.7 %collective-permute-start.11 = (bf16[4,128,768]{2,1,0:T(8,128)(2,1)S(1)}, bf16[4,128,768]{2,1,0:T(8,128)(2,1)S(1)}, u32[]{:S(2)}, u32[]{:S(2)}) collective-permute-start(bf16[4,128,768]{2,1,0:T(8,128)(2,1)S(1)} %get-tuple-element.53), channel_id=1, source_target_pairs={{1,0},{0,1},{3,2},{2,3},{5,4},{4,5},{7,6},{6,7},{9,8},{8,9},{11,10... | collective-permute-start | bytes 2359304 | tf_op jit(solution)/shard_map/ppermute | solution.py:402
  50.8 31.9 %collective-permute-start.10 = (bf16[96,6144]{1,0:T(8,128)(2,1)S(1)}, bf16[96,6144]{1,0:T(8,128)(2,1)S(1)}, u32[]{:S(2)}, u32[]{:S(2)}) collective-permute-start(bf16[96,6144]{1,0:T(8,128)(2,1)S(1)} %get-tuple-element.47.refs_1_), channel_id=1, source_target_pairs={{0,8},{8,16},{16,24},{24,32},{32,40},{40,48},{48,56},{56,64},{64,7... | collective-permute-start | bytes 3538952 | tf_op jit(solution)/shard_map/ppermute | solution.py:392
  67.5 8.1 %collective-permute-start.13 = (bf16[2,128,768]{2,1,0:T(8,128)(2,1)S(1)}, bf16[2,128,768]{2,1,0:T(8,128)(2,1)S(1)}, u32[]{:S(2)}, u32[]{:S(2)}) collective-permute-start(bf16[2,128,768]{2,1,0:T(8,128)(2,1)S(1)} %get-tuple-element.54.refs_2_), channel_id=1, source_target_pairs={{1,0},{0,1},{3,2},{2,3},{5,4},{4,5},{7,6},{6,7},{9,8},{8,9},{11,10... | collective-permute-start | bytes 1179656 | tf_op jit(solution)/shard_map/ppermute | solution.py:402
  69.5 13.2 %collective-permute-start.12 = (bf16[2,128,768]{2,1,0:T(8,128)(2,1)S(1)}, bf16[2,128,768]{2,1,0:T(8,128)(2,1)S(1)}, u32[]{:S(2)}, u32[]{:S(2)}) collective-permute-start(bf16[2,128,768]{2,1,0:T(8,128)(2,1)S(1)} %get-tuple-element.56), channel_id=1, source_target_pairs={{3,0},{2,1},{1,2},{0,3},{7,4},{6,5},{5,6},{4,7},{11,8},{10,9},{9,1... | collective-permute-start | bytes 1179656 | tf_op jit(solution)/shard_map/ppermute | solution.py:402
  70.3 15.9 %collective-permute-start.9 = (bf16[48,6144]{1,0:T(8,128)(2,1)S(1)}, bf16[48,6144]{1,0:T(8,128)(2,1)S(1)}, u32[]{:S(2)}, u32[]{:S(2)}) collective-permute-start(bf16[48,6144]{1,0:T(8,128)(2,1)S(1)} %get-tuple-element.46.refs_1_), channel_id=1, source_target_pairs={{0,8},{8,16},{16,24},{24,32},{32,40},{40,48},{48,56},{56,64},{64,7... | collective-permute-start | bytes 1769480 | tf_op jit(solution)/shard_map/ppermute | solution.py:392
  75.6 21.9 %collective-permute-start.17 = (bf16[128,768]{1,0:T(8,128)(2,1)S(1)}, bf16[128,768]{1,0:T(8,128)(2,1)S(1)}, u32[]{:S(2)}, u32[]{:S(2)}) collective-permute-start(bf16[128,768]{1,0:T(8,128)(2,1)S(1)} %get-tuple-element.63), channel_id=1, source_target_pairs={{4,248},{5,249},{6,250},{7,251},{0,252},{1,253},{2,254},{3,255},{1... | collective-permute-start | bytes 589832 | tf_op jit(solution)/shard_map/ppermute | solution.py:402
  81.8 15.6 %collective-permute-start.16 = (bf16[128,768]{1,0:T(8,128)(2,1)S(1)}, bf16[128,768]{1,0:T(8,128)(2,1)S(1)}, u32[]{:S(2)}, u32[]{:S(2)}) collective-permute-start(bf16[128,768]{1,0:T(8,128)(2,1)S(1)} %get-tuple-element.59.refs_2_), channel_id=1, source_target_pairs={{0,248},{1,249},{2,250},{3,251},{4,252},{5,253},{6,254},{7,255},{8... | collective-permute-start | bytes 589832 | tf_op jit(solution)/shard_map/ppermute | solution.py:402
  82.8 15.6 %collective-permute-start.14 = (bf16[128,768]{1,0:T(8,128)(2,1)S(1)}, bf16[128,768]{1,0:T(8,128)(2,1)S(1)}, u32[]{:S(2)}, u32[]{:S(2)}) collective-permute-start(bf16[128,768]{1,0:T(8,128)(2,1)S(1)} %get-tuple-element.60), channel_id=1, source_target_pairs={{0,8},{1,9},{2,10},{3,11},{4,12},{5,13},{6,14},{7,15},{8,16},{9,17... | collective-permute-start | bytes 589832 | tf_op jit(solution)/shard_map/ppermute | solution.py:402
  83.8 17.2 %collective-permute-start.15 = (bf16[128,768]{1,0:T(8,128)(2,1)S(1)}, bf16[128,768]{1,0:T(8,128)(2,1)S(1)}, u32[]{:S(2)}, u32[]{:S(2)}) collective-permute-start(bf16[128,768]{1,0:T(8,128)(2,1)S(1)} %get-tuple-element.61), channel_id=1, source_target_pairs={{4,8},{5,9},{6,10},{7,11},{0,12},{1,13},{2,14},{3,15},{12,16},{13,... | collective-permute-start | bytes 589832 | tf_op jit(solution)/shard_map/ppermute | solution.py:402
